TPU v7x, 32 devices: a whole 2x2x4 slice. The times are simulated.
32 devices in a mesh: fsdp: 16 (over z, y, core), tensor: 2 (over x).
Axes of the slice: x: 2, y: 2, z: 4, core: 2. Of those that a mesh axis runs over, the one named last changes fastest.
Arguments:
- tokens: bfloat16 [2048, 8192], P('fsdp'), may hold values from -6 to 6
- cotangent: bfloat16 [2048, 8192], P('fsdp'), may hold values from -1.5 to 1.5
- gate_blocks: bfloat16 [2, 32, 128, 128], P('tensor', 'fsdp'), may hold values from -0.75 to 0.75
- up_blocks: bfloat16 [2, 32, 128, 128], P('tensor', 'fsdp'), may hold values from -0.75 to 0.75
- down_blocks: bfloat16 [2, 32, 128, 128], P('tensor', 'fsdp'), may hold values from -0.75 to 0.75
- gate_where: int32 [2, 32], P('tensor'), may hold values from 0 to 3583, as said below
- up_where: int32 [2, 32], P('tensor'), may hold values from 0 to 3583, as said below
- down_where: int32 [2, 32], P('tensor'), may hold values from 0 to 3583, as said below
- block_counts: int32 [3, 2], P(None, 'tensor'), may hold values from 16 to 32, as said below
Outputs:
- outputs: bfloat16 [2048, 8192], P('fsdp', 'tensor')
- input_grads: bfloat16 [2048, 8192], P('fsdp', 'tensor')
- gate_grads: bfloat16 [2, 32, 128, 128], P('tensor', 'fsdp')
- up_grads: bfloat16 [2, 32, 128, 128], P('tensor', 'fsdp')
- down_grads: bfloat16 [2, 32, 128, 128], P('tensor', 'fsdp')
Inputs may be any that keep to these rules, and one draw needn't show every extreme that they name: Within one group of hidden units the 32 positions of gate_where are distinct. Within one group of hidden units the 32 positions of up_where are distinct. Within one group of hidden units the 32 positions of down_where are distinct. `block_counts`: for each matrix some group has all 32 slots live.
All inputs are finite; a program needn't handle non-finite values.
Results may differ from a plain program's by a relative error of at most 0.015.
Values may be sent and summed in bfloat16 or wider, within the bound.
No kernel may reach another device: no remote copies, remote signals or barrier semaphores. Data moves between devices by JAX's collectives and lax.ppermute only.
A program may use at most 128 MiB of HBM per device.

v0:
```python
import functools

import jax
import jax.numpy as jnp
from jax import lax
from jax.experimental import pallas as pl
from jax.experimental.pallas import tpu as pltpu
from jax.sharding import PartitionSpec as P

FF = 14336
BLK = 128
GROUP = 4
FIRST_SEND = 18
LEAN_SLOTS = 4
SMALL = 4 * 1024 * 1024
PART, STRIP, CIDX, CWAS, OIDX, OWAS = range(6)
FIELDS = 6
COLS_ROW = 3 * FIELDS
HEAD_ROW = COLS_ROW + 1
MINE_ROW = COLS_ROW + 2
LISTS_ROW = COLS_ROW + 3
HEAD_COLS, HEAD_OVER, HEAD_LISTS = 3, 4, 8


class Sizes:
    def __init__(self, tokens, gate_blocks, slots, n_fsdp, n_tensor, lean):
        self.tok, self.width = tokens.shape
        self.n_fsdp, self.n_tensor = n_fsdp, n_tensor
        self.rb = self.width // BLK
        self.cb = FF // (BLK * n_tensor)
        self.slots = slots
        self.all = 3 * slots
        self.lanes = -(-(self.all + GROUP) // 128) * 128
        self.nb = gate_blocks.shape[1]
        self.owned = 3 * self.nb
        self.ring = n_fsdp // 2
        self.top = self.ring // 2
        self.rbt = self.rb // n_tensor
        self.order = [self.top]
        for d in range(1, self.top):
            self.order += [self.top + d, self.top - d]
        self.order.append(0)
        self.far = min(4, self.ring - 1)
        self.keep = min(LEAN_SLOTS, self.owned) if lean else self.owned
        self.send_all = 2 * self.rbt
        self.first = min(FIRST_SEND, self.send_all) if lean else self.send_all
        self.blocks = 2 * self.ring * self.keep
        self.plan_rows = -(-(LISTS_ROW + 2 * n_tensor) // 8) * 8
        self.note_n, self.note_over = self.lanes - 1, self.lanes - 2
        self.room = slots + GROUP


def permutations(sz):
    seq = list(range(0, sz.ring, 2)) + list(range(sz.ring - 1, 0, -2))
    ahead, behind, swap = [], [], []
    for i, q in enumerate(seq):
        up, down = seq[(i + 1) % sz.ring], seq[i - 1]
        ahead += [(q * 2, up * 2), (q * 2 + 1, down * 2 + 1)]
        behind += [(q * 2, down * 2), (q * 2 + 1, up * 2 + 1)]
        swap += [(q * 2, q * 2 + 1), (q * 2 + 1, q * 2)]
    return ahead, behind, swap


def ratio(x, d):
    return jnp.floor((x + 0.5) * (1.0 / d))


def rest_of(x, d):
    return x - d * ratio(x, d)


def ring_position(sz, chip):
    return jnp.where(rest_of(chip, 2) == 0, ratio(chip, 2), sz.ring - 1 - ratio(chip, 2))


class Marks:
    def __init__(self, sz, own):
        N, L, S = sz.all, sz.lanes, sz.slots
        f32 = jnp.float32
        self.sz = sz
        self.sub = lax.broadcasted_iota(jnp.int32, (N, L), 0)
        self.lane = lax.broadcasted_iota(jnp.int32, (N, L), 1)
        self.same = self.sub == self.lane
        sub_c = self.sub[:, :1].astype(f32)
        lane_r = lax.broadcasted_iota(jnp.int32, (1, L), 1).astype(f32)
        self.sub_c, self.lane_r = sub_c, lane_r
        raw_r = own[...].astype(f32)

        def single(row, at):
            return jnp.sum(jnp.where(lane_r == at, row, 0.0), axis=1, keepdims=True)

        self.f, self.rank = single(raw_r, N + 3), single(raw_r, N + 4)

        def kind(x):
            return (x >= S).astype(f32) + (x >= 2 * S).astype(f32)

        self.kind_c, self.kind_r = kind(sub_c), kind(lane_r)
        self.n_r = lane_r - S * self.kind_r
        self.n_c = sub_c - S * self.kind_c
        limit = jnp.zeros((1, L), f32)
        for k in range(3):
            limit = limit + jnp.where(self.kind_r == k, single(raw_r, N + k), 0.0)
        live_r = jnp.where((lane_r < N) & (self.n_r < limit), 1.0, 0.0)
        w_c = self.col(raw_r)
        live_c = self.col(live_r)

        def place(w, k):
            gate, down = ratio(w, sz.cb), ratio(w, sz.rb)
            is_down = k == 2
            return jnp.where(is_down, w - down * sz.rb, gate), jnp.where(is_down, down, w - gate * sz.cb)

        self.row_c, col_c = place(w_c, self.kind_c)
        self.row_r, col_r = place(raw_r, self.kind_r)
        self.chip_c, chip_r = ratio(self.n_c, 2 * sz.nb), ratio(self.n_r, 2 * sz.nb)
        self.same_chip = (self.chip_c == chip_r).astype(f32)
        self.same_col = (col_c == col_r).astype(f32)
        act_c, act_r = live_c, live_r
        for k in range(3):
            lanes = self.same_col * (live_r * (self.kind_r == k).astype(f32))
            act_c = act_c * jnp.max(lanes, axis=1, keepdims=True)
            subs = self.same_col * (live_c * (self.kind_c == k).astype(f32))
            act_r = act_r * jnp.max(subs, axis=0, keepdims=True)
        self.act_c, self.act_r = act_c, act_r
        out_c = jnp.where(self.kind_c == 2, 0.0, f32(sz.rb)) + self.row_c
        out_r = jnp.where(self.kind_r == 2, 0.0, f32(sz.rb)) + self.row_r
        self.same_out = (out_c == out_r).astype(f32)
        self.before = (self.lane < self.sub).astype(f32)
        self.after = (self.sub < self.lane).astype(f32)
        self.owas_c = jnp.max(self.same_out * self.before * act_r, axis=1, keepdims=True)
        self.owas_r = jnp.max(self.same_out * self.after * act_c, axis=0, keepdims=True)
        self.lead_c = act_c * (1.0 - self.owas_c)
        self.lead_r = act_r * (1.0 - self.owas_r)

        def shift(row):
            away = ratio(row, sz.rbt) - self.rank
            return jnp.where(away < 0, away + sz.n_tensor, away)

        self.shift_c, self.shift_r = shift(self.row_c), shift(self.row_r)
        self.local_c = jnp.where(self.kind_c == 2, 0.0, f32(sz.rbt)) + rest_of(self.row_c, sz.rbt)

    def col(self, row):
        return jnp.sum(jnp.where(self.same, row, 0.0), axis=1, keepdims=True)

    def carried(self):
        sz = self.sz
        rank = jnp.sum(self.before * self.same_chip * self.act_r, axis=1, keepdims=True)
        core = rest_of(rank, 2)
        away = ring_position(sz, self.chip_c) - ring_position(sz, ratio(self.f, 2))
        away = jnp.where(core == 0, away, -away)
        rel = jnp.where(away < 0, away + sz.ring, away)
        j = jnp.where(rel > sz.top, 2 * (rel - sz.top) - 1, 2 * (sz.top - rel))
        j = jnp.where(rel == 0, sz.ring - 1.0, j)
        return core, ratio(rank, 2), j + jnp.where(core == rest_of(self.f, 2), 0.0, float(sz.ring))

    def ranks(self, chosen_r):
        return jnp.sum(self.before * chosen_r, axis=1, keepdims=True)

    def listed(self, chosen_c, rank_c, value_c, lo=0, hi=None):
        at = rank_c[lo:hi] == self.lane[lo:hi].astype(jnp.float32)
        return jnp.sum(jnp.where(at, chosen_c[lo:hi] * value_c[lo:hi], 0.0), axis=0, keepdims=True)

    def most_on_chip(self):
        return jnp.max(jnp.sum(self.same_chip * self.act_r, axis=1, keepdims=True), axis=0, keepdims=True)


def total(x):
    return jnp.sum(x, axis=0, keepdims=True)


def head_row(sz, entries):
    lane = lax.broadcasted_iota(jnp.int32, (1, sz.lanes), 1)
    row = jnp.zeros((1, sz.lanes), jnp.float32)
    for i, value in entries:
        row = jnp.where(lane == i, value, row)
    return row


def plan_kernel(sz, own, *refs):
    mine, theirs, (plan, chunk, *notes, sems) = refs[:3], refs[3:6], refs[6:]
    S, N = sz.slots, sz.all
    m = Marks(sz, own)
    f32 = jnp.float32
    lane_r, sub_c = m.lane_r, m.sub_c
    core_c, pos_c, base_c = m.carried()
    own_core = core_c == rest_of(m.f, 2)

    pair = jnp.where(rest_of(m.f, 2) == 0, m.f + 1, m.f - 1)
    i_r = rest_of(lane_r, sz.owned)
    owner_r = jnp.where(lane_r < sz.owned, m.f, pair)
    slot_r = ratio(i_r, sz.nb) * S + owner_r * sz.nb + rest_of(i_r, sz.nb)
    at_r = jnp.sum(
        jnp.where((sub_c == slot_r) & own_core, m.act_c * (pos_c + 1.0), 0.0), axis=0, keepdims=True)
    copies = []
    for i in range(2 * sz.owned):
        side, k, a = i // sz.owned, i % sz.owned // sz.nb, i % sz.nb
        at = jnp.max(jnp.where(lane_r == i, at_r, 0.0)).astype(jnp.int32)
        fits = (at > 0) & (at <= sz.keep)
        place = jnp.minimum(jnp.maximum(at - 1, 0), sz.keep - 1)
        copy = pltpu.make_async_copy((mine, theirs)[side][k].at[0, a], chunk.at[place], sems.at[i])
        copies.append((fits, copy))
    for fits, copy in copies:
        pl.when(fits)(copy.start)

    same_kind = (m.kind_c == m.kind_r).astype(f32)
    rank_c = jnp.sum(m.before * same_kind * m.act_r, axis=1, keepdims=True)
    cwas_c = jnp.max(m.before * same_kind * m.same_col * m.act_r, axis=1, keepdims=True)
    cwas_r = jnp.max(m.after * same_kind * m.same_col * m.act_c, axis=0, keepdims=True)
    big = f32(4 * N)
    lanes_f = m.lane.astype(f32)
    gates_r = m.act_r * (m.kind_r == 0).astype(f32)
    cidx_c = jnp.min(jnp.where(m.same_col * gates_r > 0, lanes_f, big), axis=1, keepdims=True)
    oidx_c = jnp.min(jnp.where(m.same_out * m.act_r > 0, lanes_f, big), axis=1, keepdims=True)
    rank_r = jnp.sum(m.after * same_kind * m.act_c, axis=0, keepdims=True)
    turn_c = ratio(rank_c, GROUP) * 3 + m.kind_c
    turn_r = ratio(rank_r, GROUP) * 3 + m.kind_r
    ahead = ((turn_r < turn_c) | ((turn_r == turn_c) & (rank_r < rank_c))).astype(f32)
    owas_c = jnp.max(m.same_out * ahead * m.act_r, axis=1, keepdims=True)
    part_c = jnp.where(pos_c < sz.keep, base_c * sz.keep + pos_c, f32(sz.blocks))
    fields = [(part_c, sz.blocks), (m.row_c, 0), (cidx_c, S), (cwas_c, 0), (oidx_c, N), (owas_c, 0)]
    rows = []
    head = []
    for k in range(3):
        lo, hi = k * S, (k + 1) * S
        n_k = total(m.act_c[lo:hi])
        head.append((k, n_k))
        for value, spare in fields:
            row = m.listed(m.act_c, rank_c, value, lo, hi)
            rows.append(jnp.where(lane_r < n_k, row, f32(spare)))
    leader_c = m.act_c * (1.0 - cwas_c) * (m.kind_c == 0).astype(f32)
    leader_r = m.act_r * (1.0 - cwas_r) * (m.kind_r == 0).astype(f32)
    n_cols = total(leader_c)
    cols = m.listed(leader_c, m.ranks(leader_r), sub_c, 0, S)
    rows.append(jnp.where(lane_r < n_cols, cols, f32(S)))
    head.append((HEAD_COLS, n_cols))
    lists, sent = [], []
    over = (m.most_on_chip() > 2 * sz.keep).astype(f32)
    for s in range(sz.n_tensor):
        chosen_c = m.lead_c * (m.shift_c == s).astype(f32)
        chosen_r = m.lead_r * (m.shift_r == s).astype(f32)
        rank = m.ranks(chosen_r)
        lists.append(m.listed(chosen_c, rank, sub_c))
        lists.append(m.listed(chosen_c, rank, m.local_c))
        n = total(chosen_c)
        head.append((HEAD_LISTS + s, n))
        sent.append(n)
        over = jnp.maximum(over, (n > sz.first).astype(f32))
    head.append((HEAD_OVER, over))
    for s in range(1, sz.n_tensor):
        note = jnp.where(lane_r == sz.note_n, sent[s], lists[2 * s + 1])
        notes[s - 1][...] = jnp.where(lane_r == sz.note_over, over, note).astype(jnp.int32)
    rows.append(head_row(sz, head))
    held_c = pos_c + 1.0 + jnp.where(own_core, 0.0, float(sz.keep))
    rows.append(jnp.sum(
        jnp.where((sub_c == slot_r) & (lane_r < sz.owned), m.act_c * held_c, 0.0), axis=0, keepdims=True))
    rows += lists
    for i, row in enumerate(rows):
        plan[i:i + 1, :] = row.astype(jnp.int32)
    for fits, copy in copies:
        pl.when(fits)(copy.wait)


def dot(a, b, ca, cb):
    return lax.dot_general(a, b, (((ca,), (cb,)), ((), ())), preferred_element_type=jnp.float32)


def field(sz, plan, k, j, e):
    return plan[k * FIELDS + j, e]


def walk(plan, body):
    most = jnp.maximum(jnp.maximum(plan[HEAD_ROW, 0], plan[HEAD_ROW, 1]), plan[HEAD_ROW, 2])
    lax.fori_loop(0, (most + (GROUP - 1)) // GROUP, lambda p, _: body(p * GROUP), None)


def each(plan, k, body):
    lax.fori_loop(0, plan[HEAD_ROW, k], lambda e, _: body(e), None)


def compute_kernel(sz, plan, tokens, cot, *refs):
    n_chunks, T = 2 * sz.ring, sz.n_tensor
    chunks, refs = refs[:n_chunks], refs[n_chunks:]
    same, far, near = refs[:3]
    firsts, refs = refs[3:3 + T], refs[3 + T:]
    xs, wbuf, parts, gate_acc, up_acc, hg_acc, acts, out_acc, stage, strip_sems, sems = refs
    A = sz.slots + 1
    get = functools.partial(field, sz, plan)

    def strip_copy(k, e):
        src = cot if k == 2 else tokens
        cols = pl.ds(pl.multiple_of(get(k, STRIP, e) * BLK, BLK), BLK)
        return pltpu.make_async_copy(src.at[:, cols], xs.at[k * sz.room + e], strip_sems.at[k * sz.room + e])

    loads = [
        pltpu.make_async_copy(chunk, wbuf.at[pl.ds(i * sz.keep, sz.keep)], sems.at[i])
        for i, chunk in enumerate(chunks)
    ]
    for k in range(3):
        each(plan, k, lambda e, k=k: strip_copy(k, e).start())
    for c in loads:
        c.start()
    for k in range(3):
        each(plan, k, lambda e, k=k: strip_copy(k, e).wait())
    for c in loads:
        c.wait()

    group = [(k, u) for k in range(3) for u in range(GROUP)]

    def forward(e0):
        for k, u in group:
            e, acc = e0 + u, (gate_acc, up_acc, hg_acc)[k]
            prod = dot(xs[k * sz.room + e], wbuf[get(k, PART, e)], 1, 1 if k == 2 else 0)
            c = get(k, CIDX, e)
            acc[c] = prod + jnp.where(get(k, CWAS, e) == 0, 0.0, acc[c])

    walk(plan, forward)

    def columns(i, _):
        for j in range(GROUP):
            c = plan[COLS_ROW, i * GROUP + j]
            g, u, h = gate_acc[c], up_acc[c], hg_acc[c]
            s = lax.logistic(g)
            silu = g * s
            acts[c] = (h * u * s * (1.0 + g * (1.0 - s))).astype(jnp.bfloat16)
            acts[A + c] = (h * silu).astype(jnp.bfloat16)
            acts[2 * A + c] = (silu * u).astype(jnp.bfloat16)

    lax.fori_loop(0, (plan[HEAD_ROW, HEAD_COLS] + (GROUP - 1)) // GROUP, columns, None)

    def gradients(e0):
        for k, u in group:
            e = e0 + u
            a, x = acts[k * A + get(k, CIDX, e)], xs[k * sz.room + e]
            grad = dot(a, x, 0, 0) if k == 2 else dot(x, a, 0, 0)
            parts[get(k, PART, e)] = grad.astype(jnp.bfloat16)

    walk(plan, gradients)
    split = sz.ring * sz.keep
    cut = split + sz.far * sz.keep
    outs = [
        pltpu.make_async_copy(parts.at[pl.ds(split, cut - split)], far, sems.at[0]),
        pltpu.make_async_copy(parts.at[pl.ds(0, split)], same, sems.at[1]),
        pltpu.make_async_copy(parts.at[pl.ds(cut, sz.blocks - cut)], near, sems.at[2]),
    ]
    for c in outs:
        c.start()

    def terms(e0):
        for k, u in group:
            e = e0 + u
            prod = dot(acts[k * A + get(k, CIDX, e)], wbuf[get(k, PART, e)], 1, 0 if k == 2 else 1)
            at = get(k, OIDX, e)
            out_acc[at] = prod + jnp.where(get(k, OWAS, e) == 0, 0.0, out_acc[at])

    walk(plan, terms)

    for s in reversed(range(T)):
        def staged(i, _, s=s):
            stage[s * sz.first + i] = out_acc[plan[LISTS_ROW + 2 * s, i]].astype(jnp.bfloat16)

        lax.fori_loop(0, jnp.minimum(plan[HEAD_ROW, HEAD_LISTS + s], sz.first), staged, None)
        copy = pltpu.make_async_copy(stage.at[pl.ds(s * sz.first, sz.first)], firsts[s], sems.at[3 + s])
        copy.start()
        outs.append(copy)
    for c in outs:
        c.wait()


def strip_of(sz, at):
    w = jnp.where(at < sz.rbt, at, at - sz.rbt)
    return at < sz.rbt, pl.ds(pl.multiple_of(w * BLK, BLK), BLK)


def prepare_kernel(sz, plan, first, outputs, input_grads):
    outputs[...] = jnp.zeros_like(outputs)
    input_grads[...] = jnp.zeros_like(input_grads)

    def step(i, _):
        is_out, cols = strip_of(sz, plan[LISTS_ROW + 1, i])

        @pl.when(is_out)
        def _():
            outputs[:, cols] = first[i]

        @pl.when(jnp.logical_not(is_out))
        def _():
            input_grads[:, cols] = first[i]

    lax.fori_loop(0, jnp.minimum(plan[HEAD_ROW, HEAD_LISTS], sz.first), step, None)


def last_kernel(sz, plan, *refs):
    T = sz.n_tensor
    notes, refs = refs[:T - 1], refs[T - 1:]
    firsts, refs = refs[:T - 1], refs[T - 1:]
    mine, theirs, refs = refs[:3], refs[3:6], refs[8:]
    outputs, input_grads, grads, flag = refs[0], refs[1], refs[2:5], refs[5]
    strips, read_sems, write_sems = refs[6:]
    over = plan[HEAD_ROW, HEAD_OVER]
    for note in notes:
        over = jnp.maximum(over, note[0, sz.note_over])
    flag[0] = over

    def move(s, i, back, act):
        is_out, cols = strip_of(sz, notes[s][0, i])
        for ref, here in ((outputs, is_out), (input_grads, jnp.logical_not(is_out))):
            @pl.when(here)
            def _(ref=ref):
                there = ref.at[:, cols]
                if back:
                    act(pltpu.make_async_copy(strips.at[i], there, write_sems.at[i]))
                else:
                    act(pltpu.make_async_copy(there, strips.at[i], read_sems.at[i]))

    def loop(s, body):
        lax.fori_loop(0, jnp.minimum(notes[s][0, sz.note_n], sz.first), lambda i, _: body(i), None)

    def begin(s):
        loop(s, lambda i: move(s, i, False, lambda c: c.start()))

    def add(s):
        def step(i):
            move(s, i, False, lambda c: c.wait())
            value = strips[i].astype(jnp.float32) + firsts[s][i].astype(jnp.float32)
            strips[i] = value.astype(jnp.bfloat16)
            move(s, i, True, lambda c: c.start())

        loop(s, step)

    def end(s):
        loop(s, lambda i: move(s, i, True, lambda c: c.wait()))

    begin(0)
    for k in range(3):
        for a in range(sz.nb):
            at = plan[MINE_ROW, k * sz.nb + a]

            def value(terms, p):
                p = jnp.minimum(jnp.maximum(p, 0), sz.keep - 1)
                return sum(t[p].astype(jnp.float32) for t in terms)

            out = jnp.where(at > sz.keep, value(theirs, at - 1 - sz.keep), value(mine, at - 1))
            grads[k][0, a] = jnp.where(at > 0, out, 0.0).astype(jnp.bfloat16)
    add(0)
    end(0)
    for s in range(1, T - 1):
        begin(s)
        add(s)
        end(s)


def spec(space):
    return pl.BlockSpec(memory_space=space)


ANY, HBM, VMEM, SMEM = pl.ANY, pltpu.HBM, pltpu.VMEM, pltpu.SMEM


def cost(flops, moved):
    return pl.CostEstimate(flops=flops, bytes_accessed=moved, transcendentals=0)


def call_plan(sz, own, mine, theirs):
    return pl.pallas_call(
        functools.partial(plan_kernel, sz),
        out_shape=[
            jax.ShapeDtypeStruct((sz.plan_rows, sz.lanes), jnp.int32),
            jax.ShapeDtypeStruct((sz.keep, BLK, BLK), jnp.bfloat16),
        ] + [jax.ShapeDtypeStruct((1, sz.lanes), jnp.int32)] * (sz.n_tensor - 1),
        in_specs=[spec(VMEM)] + [spec(ANY)] * 6,
        out_specs=[spec(VMEM), spec(ANY)] + [spec(VMEM)] * (sz.n_tensor - 1),
        scratch_shapes=[pltpu.SemaphoreType.DMA((2 * sz.owned,))],
        compiler_params=pltpu.CompilerParams(vmem_limit_bytes=SMALL),
        cost_estimate=cost(1_000_000, 4_000_000),
        name="plan",
    )(own, *mine, *theirs)


def call_turn(handed, arrived):
    return pl.pallas_call(
        lambda *_: None,
        out_shape=[jax.ShapeDtypeStruct(x.shape, x.dtype) for x in handed],
        in_specs=[spec(ANY)] * (len(handed) + len(arrived)),
        out_specs=[spec(ANY)] * len(handed),
        input_output_aliases={i: i for i in range(len(handed))},
        compiler_params=pltpu.CompilerParams(vmem_limit_bytes=SMALL),
        cost_estimate=cost(1000, 1000),
        name="turn",
    )(*handed, *arrived)


def blocks(n):
    return jax.ShapeDtypeStruct((n, BLK, BLK), jnp.bfloat16)


def held(scratch):
    return sum(s[0] * s[1] * s[2] * jnp.dtype(t).itemsize for s, t in scratch) + 2 * 1024 * 1024


def call_compute(sz, plan, tokens, cot, chunks):
    bf, f32 = jnp.bfloat16, jnp.float32
    T, A = sz.n_tensor, sz.slots + 1
    out_shape = [blocks(sz.ring * sz.keep), blocks(sz.far * sz.keep), blocks((sz.ring - sz.far) * sz.keep)]
    out_shape += [blocks(sz.first)] * T
    scratch = [
        ((3 * sz.room, sz.tok, BLK), bf),
        ((sz.blocks + 1, BLK, BLK), bf),
        ((sz.blocks + 1, BLK, BLK), bf),
        ((A, sz.tok, BLK), f32),
        ((A, sz.tok, BLK), f32),
        ((A, sz.tok, BLK), f32),
        ((3 * A, sz.tok, BLK), bf),
        ((sz.all + 1, sz.tok, BLK), f32),
        ((T * sz.first, sz.tok, BLK), bf),
    ]
    return pl.pallas_call(
        functools.partial(compute_kernel, sz),
        out_shape=out_shape,
        in_specs=[spec(SMEM)] + [spec(HBM)] * 2 + [spec(ANY)] * len(chunks),
        out_specs=[spec(ANY)] * len(out_shape),
        scratch_shapes=[pltpu.VMEM(s, t) for s, t in scratch] + [
            pltpu.SemaphoreType.DMA((3 * sz.room,)),
            pltpu.SemaphoreType.DMA((max(len(chunks), 3 + T),)),
        ],
        compiler_params=pltpu.CompilerParams(vmem_limit_bytes=held(scratch)),
        cost_estimate=cost(1_000_000_000, 20_000_000),
        name="compute",
    )(plan, pltpu.with_memory_space_constraint(tokens, HBM), pltpu.with_memory_space_constraint(cot, HBM), *chunks)


def call_prepare(sz, plan, first):
    half = jax.ShapeDtypeStruct((sz.tok, sz.width // sz.n_tensor), jnp.bfloat16)
    return pl.pallas_call(
        functools.partial(prepare_kernel, sz),
        out_shape=[half, half],
        in_specs=[spec(SMEM), spec(VMEM)],
        out_specs=[spec(VMEM), spec(VMEM)],
        compiler_params=pltpu.CompilerParams(vmem_limit_bytes=10 * 1024 * 1024),
        cost_estimate=cost(1_000_000, 6_000_000),
        name="prepare",
    )(plan, first)


def call_last(sz, plan, notes, firsts, terms, partial):
    n = 1 + len(notes) + len(firsts) + len(terms)
    out = jax.ShapeDtypeStruct((1, sz.nb, BLK, BLK), jnp.bfloat16)
    return pl.pallas_call(
        functools.partial(last_kernel, sz),
        out_shape=[jax.ShapeDtypeStruct(p.shape, p.dtype) for p in partial] + [out] * 3 + [
            jax.ShapeDtypeStruct((1,), jnp.int32)],
        in_specs=[spec(SMEM)] * (1 + len(notes)) + [spec(VMEM)] * (len(firsts) + len(terms)) + [spec(ANY)] * 2,
        out_specs=[spec(ANY)] * 2 + [spec(VMEM)] * 3 + [spec(SMEM)],
        input_output_aliases={n: 0, n + 1: 1},
        scratch_shapes=[
            pltpu.VMEM((sz.first, sz.tok, BLK), jnp.bfloat16),
            pltpu.SemaphoreType.DMA((sz.first,)),
            pltpu.SemaphoreType.DMA((sz.first,)),
        ],
        compiler_params=pltpu.CompilerParams(vmem_limit_bytes=12 * 1024 * 1024),
        cost_estimate=cost(1_000_000, 3_000_000),
        name="last",
    )(plan, *notes, *firsts, *terms, *partial)


def gather_chunks(sz, chunk, notes):
    ahead, behind, swap = permutations(sz)
    same = {0: chunk}
    a = b = chunk
    for s in range(1, sz.top):
        a, b = lax.ppermute(a, "fsdp", ahead), lax.ppermute(b, "fsdp", behind)
        if s == 2:
            a, b = call_turn([a, b], notes)
        same[sz.ring - s], same[s] = a, b
    other = {d: lax.ppermute(same[d], "fsdp", swap) for d in same}
    same[sz.top] = lax.ppermute(a, "fsdp", ahead)
    other[sz.top] = lax.ppermute(a, "fsdp", [(i, j ^ 1) for i, j in ahead])
    return [side[d] for side in (same, other) for d in sz.order]


def reduce_parts(sz, same, far, near):
    ahead, behind, swap = permutations(sz)
    keep = sz.keep
    far, near = lax.ppermute(far, "fsdp", swap), lax.ppermute(near, "fsdp", swap)

    def term(d, *more):
        j = sz.order.index(d)
        pair = far[j * keep:(j + 1) * keep] if j < sz.far else near[(j - sz.far) * keep:][:keep]
        out = same[j * keep:(j + 1) * keep].astype(jnp.float32) + pair.astype(jnp.float32)
        for m in more:
            out = out + m.astype(jnp.float32)
        return out.astype(jnp.bfloat16)

    a, b = lax.optimization_barrier((term(sz.top), term(sz.top + 1)))
    for s in range(1, sz.top):
        a, b = lax.ppermute(a, "fsdp", ahead), lax.ppermute(b, "fsdp", behind)
        a = term(sz.top - s, a)
        if s + 1 < sz.top:
            a, b = lax.optimization_barrier((a, term(sz.top + 1 + s, b)))
    here = term(0)
    mine = [here, lax.ppermute(a, "fsdp", ahead), b]
    theirs = [
        lax.ppermute(here, "fsdp", swap),
        lax.ppermute(a, "fsdp", [(i, j ^ 1) for i, j in ahead]),
        lax.ppermute(b, "fsdp", swap),
    ]
    return mine + theirs


def program(sz, own, tokens, cotangent, mine):
    T = sz.n_tensor
    swap = permutations(sz)[-1]
    theirs = [lax.ppermute(b, "fsdp", swap) for b in mine]
    plan, chunk, *notes = call_plan(sz, own, mine, theirs)

    def exchange(array, s):
        return lax.ppermute(array, "tensor", [(i, (i + s) % T) for i in range(T)])

    notes = [exchange(note, s) for s, note in enumerate(notes, 1)]
    chunks = gather_chunks(sz, chunk, notes)
    same, far, near, *firsts = call_compute(sz, plan, tokens, cotangent, chunks)
    partial = call_prepare(sz, plan, firsts[0])
    firsts = [exchange(firsts[s], s) for s in range(1, T)]
    terms = reduce_parts(sz, same, far, near)
    *outs, flag = call_last(sz, plan, notes, firsts, terms, partial)
    return tuple(outs), flag


def shards(
    tokens,
    cotangent,
    gate_blocks,
    up_blocks,
    down_blocks,
    gate_where,
    up_where,
    down_where,
    block_counts,
):
    n_fsdp, n_tensor = lax.axis_size("fsdp"), lax.axis_size("tensor")
    f, rank = lax.axis_index("fsdp"), lax.axis_index("tensor")
    slots = gate_where.shape[1]
    full = Sizes(tokens, gate_blocks, slots, n_fsdp, n_tensor, False)
    own = jnp.concatenate([
        gate_where[0], up_where[0], down_where[0], block_counts[:, 0],
        f.astype(jnp.int32)[None], rank.astype(jnp.int32)[None]])
    own = jnp.pad(own, (0, full.lanes - own.shape[0]))[None]
    blocks_in = (gate_blocks, up_blocks, down_blocks)
    if slots >= full.cb:
        return program(full, own, tokens, cotangent, blocks_in)[0]
    lean = Sizes(tokens, gate_blocks, slots, n_fsdp, n_tensor, True)
    outs, flag = program(lean, own, tokens, cotangent, blocks_in)
    return lax.cond(
        flag[0] > 0,
        lambda outs, *args: program(full, *args)[0],
        lambda outs, *args: outs,
        outs, own, tokens, cotangent, blocks_in)


def solution(mesh):
    placed = (
        P("fsdp", None),
        P("fsdp", None),
        P("tensor", "fsdp", None, None),
        P("tensor", "fsdp", None, None),
        P("tensor", "fsdp", None, None),
        P("tensor", None),
        P("tensor", None),
        P("tensor", None),
        P(None, "tensor"),
    )
    return jax.shard_map(
        shards,
        mesh=mesh,
        in_specs=placed,
        out_specs=(
            P("fsdp", "tensor"),
            P("fsdp", "tensor"),
            P("tensor", "fsdp", None, None),
            P("tensor", "fsdp", None, None),
            P("tensor", "fsdp", None, None),
        ),
        check_vma=False,
    )
```

profile of v0, /device:TPU:0, one launch (start us, length us, event | category | flops | bytes accessed | tf_op | source)
XLA Modules:
  0.0 67.8 jit_solution(48409946691778670)
XLA Ops:
  0.6 0.5 collective-permute-start.32
  1.2 0.1 collective-permute-start.33
  1.2 0.4 collective-permute-start.34
  1.7 0.8 %concatenate.3 = s32[101]{0:T(128)S(1)} concatenate(s32[32]{0:T(128)} %bitcast.9, s32[32]{0:T(128)} %bitcast.10, s32[32]{0:T(128)} %bitcast.11, s32[3]{0:T(128)} %bitcast.12, s32[1]{0:T(128)} %bitcast.4, s32[1]{0:T(128)} %bitcast.5), dimensions={0} | concatenate | bytes 808 | tf_op jit(solution)/shard_map/concatenate | solution.py:642
  2.5 0.2 collective-permute-done.33.refs_4_
  2.6 0.2 collective-permute-done.34.refs_5_
  2.8 1.4 %plan.3 = (s32[32,128]{1,0:T(8,128)S(1)}, bf16[4,128,128]{2,1,0:T(8,128)(2,1)S(1)}, s32[1,128]{1,0:T(1,128)S(1)}) custom-call(s32[1,128]{1,0:T(1,128)S(1)} %pad_bitcast_fusion.own, bf16[1,2,128,128]{3,2,1,0:T(8,128)(2,1)} %refs_0_.1, bf16[1,2,128,128]{3,2,1,0:T(8,128)(2,1)} %refs_1_.1, bf16[1,2,128,128]{3,2,1,0:T(8,128)(2,1)} %refs_2_.1, ...), custom_call_target="tpu_custom_call" | custom-call | flops 1000000 | bytes 4000000 | tf_op jit(solution)/shard_map/plan/pallas_call | solution.py:463
  4.1 2.9 %collective-permute-start.38 = (bf16[4,128,128]{2,1,0:T(8,128)(2,1)S(1)}, bf16[4,128,128]{2,1,0:T(8,128)(2,1)S(1)}, u32[]{:S(2)}, u32[]{:S(2)}) collective-permute-start(bf16[4,128,128]{2,1,0:T(8,128)(2,1)S(1)} %get-tuple-element.82.refs_7_), channel_id=1, source_target_pairs={{0,4},{2,10},{8,0},{10,18},{16,8},{18,26},{24,16},{26,30},{28,24},... | collective-permute-start | bytes 393224 | tf_op jit(solution)/shard_map/ppermute | solution.py:569
  7.1 0.1 collective-permute-start.36
  7.2 3.9 %collective-permute-done.38.refs_6_ = bf16[4,128,128]{2,1,0:T(8,128)(2,1)S(1)} collective-permute-done((bf16[4,128,128]{2,1,0:T(8,128)(2,1)S(1)}, bf16[4,128,128]{2,1,0:T(8,128)(2,1)S(1)}, u32[]{:S(2)}, u32[]{:S(2)}) %collective-permute-start.38) | collective-permute-done | bytes 131104 | tf_op jit(solution)/shard_map/ppermute | solution.py:569
  11.1 1.1 %collective-permute-start.39 = (bf16[4,128,128]{2,1,0:T(8,128)(2,1)S(1)}, bf16[4,128,128]{2,1,0:T(8,128)(2,1)S(1)}, u32[]{:S(2)}, u32[]{:S(2)}) collective-permute-start(bf16[4,128,128]{2,1,0:T(8,128)(2,1)S(1)} %collective-permute-done.38.refs_6_), channel_id=1, source_target_pairs={{0,4},{2,10},{8,0},{10,18},{16,8},{18,26},{24,16},{26,30},{28,24},... | collective-permute-start | bytes 393224 | tf_op jit(solution)/shard_map/ppermute | solution.py:569
  12.2 1.3 %collective-permute-start.37 = (bf16[4,128,128]{2,1,0:T(8,128)(2,1)S(1)}, bf16[4,128,128]{2,1,0:T(8,128)(2,1)S(1)}, u32[]{:S(2)}, u32[]{:S(2)}) collective-permute-start(bf16[4,128,128]{2,1,0:T(8,128)(2,1)S(1)} %collective-permute-done.36.refs_5_), channel_id=1, source_target_pairs={{0,8},{2,6},{8,16},{10,2},{16,24},{18,10},{24,28},{26,18},{28,20},... | collective-permute-start | bytes 393224 | tf_op jit(solution)/shard_map/ppermute | solution.py:569
  13.5 0.0 collective-permute-start.50
  13.5 1.1 %collective-permute-start.35 = (s32[1,128]{1,0:T(1,128)S(1)}, s32[1,128]{1,0:T(1,128)S(1)}, u32[]{:S(2)}, u32[]{:S(2)}) collective-permute-start(s32[1,128]{1,0:T(1,128)S(1)} %get-tuple-element.81), channel_id=1, source_target_pairs={{0,1},{1,0},{2,3},{3,2},{4,5},{5,4},{6,7},{7,6},{8,9},{9,8},{10,11... | collective-permute-start | bytes 1544 | tf_op jit(solution)/shard_map/ppermute | solution.py:615
  14.6 0.2 collective-permute-start.49
  14.9 2.2 %collective-permute-done.35.__2_.refs_0_ = s32[1,128]{1,0:T(1,128)S(1)} collective-permute-done((s32[1,128]{1,0:T(1,128)S(1)}, s32[1,128]{1,0:T(1,128)S(1)}, u32[]{:S(2)}, u32[]{:S(2)}) %collective-permute-start.35) | collective-permute-done | bytes 544 | tf_op jit(solution)/shard_map/ppermute | solution.py:615
  17.0 0.2 collective-permute-done.39.__1_
  17.3 0.0 collective-permute-done.37.__0_
  17.3 1.9 %collective-permute-start.40 = (bf16[4,128,128]{2,1,0:T(8,128)(2,1)S(1)}, bf16[4,128,128]{2,1,0:T(8,128)(2,1)S(1)}, u32[]{:S(2)}, u32[]{:S(2)}) collective-permute-start(bf16[4,128,128]{2,1,0:T(8,128)(2,1)S(1)} %get-tuple-element.83.refs_3_), channel_id=1, source_target_pairs={{0,8},{2,6},{8,16},{10,2},{16,24},{18,10},{24,28},{26,18},{28,20},... | collective-permute-start | bytes 393224 | tf_op jit(solution)/shard_map/ppermute | solution.py:569
  19.1 0.0 collective-permute-start.48
  19.1 0.5 collective-permute-start.46
  19.6 0.2 collective-permute-start.42
  19.8 0.0 collective-permute-done.49.refs_14_
  19.8 1.1 %collective-permute-start.47 = (bf16[4,128,128]{2,1,0:T(8,128)(2,1)S(1)}, bf16[4,128,128]{2,1,0:T(8,128)(2,1)S(1)}, u32[]{:S(2)}, u32[]{:S(2)}) collective-permute-start(bf16[4,128,128]{2,1,0:T(8,128)(2,1)S(1)} %get-tuple-element.84.refs_4_), channel_id=1, source_target_pairs={{0,2},{2,0},{8,10},{10,8},{16,18},{18,16},{24,26},{26,24},{28,30},... | collective-permute-start | bytes 393224 | tf_op jit(solution)/shard_map/ppermute | solution.py:573
  20.9 1.3 %collective-permute-done.40.refs_1_ = bf16[4,128,128]{2,1,0:T(8,128)(2,1)S(1)} collective-permute-done((bf16[4,128,128]{2,1,0:T(8,128)(2,1)S(1)}, bf16[4,128,128]{2,1,0:T(8,128)(2,1)S(1)}, u32[]{:S(2)}, u32[]{:S(2)}) %collective-permute-start.40) | collective-permute-done | bytes 131104 | tf_op jit(solution)/shard_map/ppermute | solution.py:569
  22.2 0.0 collective-permute-done.48.refs_13_
  22.2 2.2 %collective-permute-start.43 = (bf16[4,128,128]{2,1,0:T(8,128)(2,1)S(1)}, bf16[4,128,128]{2,1,0:T(8,128)(2,1)S(1)}, u32[]{:S(2)}, u32[]{:S(2)}) collective-permute-start(bf16[4,128,128]{2,1,0:T(8,128)(2,1)S(1)} %collective-permute-done.40.refs_1_), channel_id=1, source_target_pairs={{0,10},{2,4},{8,18},{10,0},{16,26},{18,8},{24,30},{26,16},{28,22},... | collective-permute-start | bytes 393224 | tf_op jit(solution)/shard_map/ppermute | solution.py:575
  24.5 1.8 %collective-permute-start.41 = (bf16[4,128,128]{2,1,0:T(8,128)(2,1)S(1)}, bf16[4,128,128]{2,1,0:T(8,128)(2,1)S(1)}, u32[]{:S(2)}, u32[]{:S(2)}) collective-permute-start(bf16[4,128,128]{2,1,0:T(8,128)(2,1)S(1)} %collective-permute-done.40.refs_1_), channel_id=1, source_target_pairs={{0,8},{2,6},{8,16},{10,2},{16,24},{18,10},{24,28},{26,18},{28,20},... | collective-permute-start | bytes 393224 | tf_op jit(solution)/shard_map/ppermute | solution.py:574
  26.3 0.0 collective-permute-done.42.refs_2_
  26.3 0.8 %collective-permute-start.45 = (bf16[4,128,128]{2,1,0:T(8,128)(2,1)S(1)}, bf16[4,128,128]{2,1,0:T(8,128)(2,1)S(1)}, u32[]{:S(2)}, u32[]{:S(2)}) collective-permute-start(bf16[4,128,128]{2,1,0:T(8,128)(2,1)S(1)} %collective-permute-done.42.refs_2_), channel_id=1, source_target_pairs={{0,2},{2,0},{8,10},{10,8},{16,18},{18,16},{24,26},{26,24},{28,30},... | collective-permute-start | bytes 393224 | tf_op jit(solution)/shard_map/ppermute | solution.py:573
  27.0 0.0 collective-permute-done.47.refs_12_
  27.0 0.1 collective-permute-done.43.refs_8_
  27.1 2.7 %collective-permute-done.41.refs_0_ = bf16[4,128,128]{2,1,0:T(8,128)(2,1)S(1)} collective-permute-done((bf16[4,128,128]{2,1,0:T(8,128)(2,1)S(1)}, bf16[4,128,128]{2,1,0:T(8,128)(2,1)S(1)}, u32[]{:S(2)}, u32[]{:S(2)}) %collective-permute-start.41) | collective-permute-done | bytes 131104 | tf_op jit(solution)/shard_map/ppermute | solution.py:574
  29.8 6.8 %compute.3 = (bf16[32,128,128]{2,1,0:T(8,128)(2,1)S(1)}, bf16[16,128,128]{2,1,0:T(8,128)(2,1)S(1)}, bf16[16,128,128]{2,1,0:T(8,128)(2,1)S(1)}, bf16[18,128,128]{...) custom-call(s32[32,128]{1,0:T(8,128)S(1)} %get-tuple-element.80.plan, bf16[128,8192]{1,0:T(8,128)(2,1)} %tokens.1, ...), custom_call_target="tpu_custom_call" | custom-call | flops 1000000000 | bytes 20000000 | tf_op jit(solution)/shard_map/compute/pallas_call | solution.py:515
  36.6 0.1 collective-permute-start.53
  36.7 0.5 collective-permute-start.52
  37.2 1.4 %collective-permute-done.53 = bf16[16,128,128]{2,1,0:T(8,128)(2,1)S(1)} collective-permute-done((bf16[16,128,128]{2,1,0:T(8,128)(2,1)S(1)}, bf16[16,128,128]{2,1,0:T(8,128)(2,1)S(1)}, u32[]{:S(2)}, u32[]{:S(2)}) %collective-permute-start.53) | collective-permute-done | bytes 524320 | tf_op jit(solution)/shard_map/ppermute | solution.py:582
  38.6 0.1 add_convert_fusion.13
  38.7 1.5 %collective-permute-start.54 = (bf16[4,128,128]{2,1,0:T(8,128)(2,1)S(1)}, bf16[4,128,128]{2,1,0:T(8,128)(2,1)S(1)}, u32[]{:S(2)}, u32[]{:S(2)}) collective-permute-start(bf16[4,128,128]{2,1,0:T(8,128)(2,1)S(1)} %get-tuple-element.89), channel_id=1, source_target_pairs={{0,8},{2,6},{8,16},{10,2},{16,24},{18,10},{24,28},{26,18},{28,20},... | collective-permute-start | bytes 393224 | tf_op jit(solution)/shard_map/ppermute | solution.py:594
  40.1 0.8 %collective-permute-start.55 = (bf16[4,128,128]{2,1,0:T(8,128)(2,1)S(1)}, bf16[4,128,128]{2,1,0:T(8,128)(2,1)S(1)}, u32[]{:S(2)}, u32[]{:S(2)}) collective-permute-start(bf16[4,128,128]{2,1,0:T(8,128)(2,1)S(1)} %get-tuple-element.90), channel_id=1, source_target_pairs={{0,4},{2,10},{8,0},{10,18},{16,8},{18,26},{24,16},{26,30},{28,24},... | collective-permute-start | bytes 393224 | tf_op jit(solution)/shard_map/ppermute | solution.py:594
  40.9 3.4 %collective-permute-done.54 = bf16[4,128,128]{2,1,0:T(8,128)(2,1)S(1)} collective-permute-done((bf16[4,128,128]{2,1,0:T(8,128)(2,1)S(1)}, bf16[4,128,128]{2,1,0:T(8,128)(2,1)S(1)}, u32[]{:S(2)}, u32[]{:S(2)}) %collective-permute-start.54) | collective-permute-done | bytes 131104 | tf_op jit(solution)/shard_map/ppermute | solution.py:594
  44.3 0.8 %collective-permute-done.55 = bf16[4,128,128]{2,1,0:T(8,128)(2,1)S(1)} collective-permute-done((bf16[4,128,128]{2,1,0:T(8,128)(2,1)S(1)}, bf16[4,128,128]{2,1,0:T(8,128)(2,1)S(1)}, u32[]{:S(2)}, u32[]{:S(2)}) %collective-permute-start.55) | collective-permute-done | bytes 131104 | tf_op jit(solution)/shard_map/ppermute | solution.py:594
  45.1 0.1 add_convert_fusion.11
  45.2 2.0 %collective-permute-start.56 = (bf16[4,128,128]{2,1,0:T(8,128)(2,1)S(1)}, bf16[4,128,128]{2,1,0:T(8,128)(2,1)S(1)}, u32[]{:S(2)}, u32[]{:S(2)}) collective-permute-start(bf16[4,128,128]{2,1,0:T(8,128)(2,1)S(1)} %get-tuple-element.91), channel_id=1, source_target_pairs={{0,8},{2,6},{8,16},{10,2},{16,24},{18,10},{24,28},{26,18},{28,20},... | collective-permute-start | bytes 393224 | tf_op jit(solution)/shard_map/ppermute | solution.py:594
  47.2 0.1 collective-permute-start.57
  47.3 1.1 %collective-permute-start.51 = (bf16[18,128,128]{2,1,0:T(8,128)(2,1)S(1)}, bf16[18,128,128]{2,1,0:T(8,128)(2,1)S(1)}, u32[]{:S(2)}, u32[]{:S(2)}) collective-permute-start(bf16[18,128,128]{2,1,0:T(8,128)(2,1)S(1)} %get-tuple-element.85), channel_id=1, source_target_pairs={{0,1},{1,0},{2,3},{3,2},{4,5},{5,4},{6,7},{7,6},{8,9},{9,8},{10,11... | collective-permute-start | bytes 1769480 | tf_op jit(solution)/shard_map/ppermute | solution.py:615
  48.4 2.6 %collective-permute-done.56 = bf16[4,128,128]{2,1,0:T(8,128)(2,1)S(1)} collective-permute-done((bf16[4,128,128]{2,1,0:T(8,128)(2,1)S(1)}, bf16[4,128,128]{2,1,0:T(8,128)(2,1)S(1)}, u32[]{:S(2)}, u32[]{:S(2)}) %collective-permute-start.56) | collective-permute-done | bytes 131104 | tf_op jit(solution)/shard_map/ppermute | solution.py:594
  51.0 1.2 %collective-permute-done.57 = bf16[4,128,128]{2,1,0:T(8,128)(2,1)S(1)} collective-permute-done((bf16[4,128,128]{2,1,0:T(8,128)(2,1)S(1)}, bf16[4,128,128]{2,1,0:T(8,128)(2,1)S(1)}, u32[]{:S(2)}, u32[]{:S(2)}) %collective-permute-start.57) | collective-permute-done | bytes 131104 | tf_op jit(solution)/shard_map/ppermute | solution.py:594
  52.2 0.1 add_convert_fusion.9
  52.3 1.5 %collective-permute-start.58 = (bf16[4,128,128]{2,1,0:T(8,128)(2,1)S(1)}, bf16[4,128,128]{2,1,0:T(8,128)(2,1)S(1)}, u32[]{:S(2)}, u32[]{:S(2)}) collective-permute-start(bf16[4,128,128]{2,1,0:T(8,128)(2,1)S(1)} %get-tuple-element.93), channel_id=1, source_target_pairs={{0,8},{2,6},{8,16},{10,2},{16,24},{18,10},{24,28},{26,18},{28,20},... | collective-permute-start | bytes 393224 | tf_op jit(solution)/shard_map/ppermute | solution.py:594
  53.7 0.6 collective-permute-start.60
  54.4 4.2 %collective-permute-done.58 = bf16[4,128,128]{2,1,0:T(8,128)(2,1)S(1)} collective-permute-done((bf16[4,128,128]{2,1,0:T(8,128)(2,1)S(1)}, bf16[4,128,128]{2,1,0:T(8,128)(2,1)S(1)}, u32[]{:S(2)}, u32[]{:S(2)}) %collective-permute-start.58) | collective-permute-done | bytes 131104 | tf_op jit(solution)/shard_map/ppermute | solution.py:594
  58.6 0.1 add_convert_fusion.8
  58.7 0.0 copy-start
  58.7 0.0 copy-start.1
  58.7 0.0 copy-start.2
  58.7 0.1 collective-permute-start.62
  58.8 0.5 collective-permute-start.59
  59.3 1.5 %collective-permute-start.61 = (bf16[4,128,128]{2,1,0:T(8,128)(2,1)S(1)}, bf16[4,128,128]{2,1,0:T(8,128)(2,1)S(1)}, u32[]{:S(2)}, u32[]{:S(2)}) collective-permute-start(bf16[4,128,128]{2,1,0:T(8,128)(2,1)S(1)} %get-tuple-element.123.refs_2_), channel_id=1, source_target_pairs={{0,2},{2,0},{8,10},{10,8},{16,18},{18,16},{24,26},{26,24},{28,30},... | collective-permute-start | bytes 393224 | tf_op jit(solution)/shard_map/ppermute | solution.py:601
  60.8 0.0 collective-permute-start.63
  60.8 2.3 %prepare.3 = (bf16[128,4096]{1,0:T(8,128)(2,1)}, bf16[128,4096]{1,0:T(8,128)(2,1)}) custom-call(s32[32,128]{1,0:T(8,128)S(1)} %get-tuple-element.80.plan, bf16[18,128,128]{2,1,0:T(8,128)(2,1)S(1)} %get-tuple-element.95.first), custom_call_target="tpu_custom_call" | custom-call | flops 1000000 | bytes 6000000 | tf_op jit(solution)/shard_map/prepare/pallas_call | solution.py:532
  63.1 0.0 collective-permute-done.62.refs_6_
  63.2 0.6 collective-permute-done.59.refs_3_
  63.8 3.2 %last.3 = (bf16[128,4096]{1,0:T(8,128)(2,1)}, bf16[128,4096]{1,0:T(8,128)(2,1)}, bf16[1,2,128,128]{3,2,1,0:T(8,128)(2,1)}, bf16[1,2,128,128]{3,2,1,0:T(8,128)(2,...) custom-call(s32[32,128]{1,0:T(8,128)S(1)} %get-tuple-element.80.plan, ...), custom_call_target="tpu_custom_call", output_to_operand_aliasing={{0}: (9, {}), {1}: (10, {})} | custom-call | flops 1000000 | bytes 3000000 | tf_op jit(solution)/shard_map/last/pallas_call | solution.py:546
  (18 shorter events, 0.1 us)
Async XLA Ops:
  0.6 1.8 %collective-permute-start.32 = (bf16[1,2,128,128]{3,2,1,0:T(8,128)(2,1)}, bf16[1,2,128,128]{3,2,1,0:T(8,128)(2,1)S(1)}, u32[]{:S(2)}, u32[]{:S(2)}) collective-permute-start(bf16[1,2,128,128]{3,2,1,0:T(8,128)(2,1)} %refs_0_.1), channel_id=1, source_target_pairs={{0,2},{2,0},{8,10},{10,8},{16,18},{18,16},{24,26},{26,24},{28,30},... | collective-permute-start | bytes 196616 | tf_op jit(solution)/shard_map/ppermute | solution.py:611
  1.2 1.5 %collective-permute-start.33 = (bf16[1,2,128,128]{3,2,1,0:T(8,128)(2,1)}, bf16[1,2,128,128]{3,2,1,0:T(8,128)(2,1)S(1)}, u32[]{:S(2)}, u32[]{:S(2)}) collective-permute-start(bf16[1,2,128,128]{3,2,1,0:T(8,128)(2,1)} %refs_1_.1), channel_id=1, source_target_pairs={{0,2},{2,0},{8,10},{10,8},{16,18},{18,16},{24,26},{26,24},{28,30},... | collective-permute-start | bytes 196616 | tf_op jit(solution)/shard_map/ppermute | solution.py:611
  1.2 1.5 %collective-permute-start.34 = (bf16[1,2,128,128]{3,2,1,0:T(8,128)(2,1)}, bf16[1,2,128,128]{3,2,1,0:T(8,128)(2,1)S(1)}, u32[]{:S(2)}, u32[]{:S(2)}) collective-permute-start(bf16[1,2,128,128]{3,2,1,0:T(8,128)(2,1)} %refs_2_.1), channel_id=1, source_target_pairs={{0,2},{2,0},{8,10},{10,8},{16,18},{18,16},{24,26},{26,24},{28,30},... | collective-permute-start | bytes 196616 | tf_op jit(solution)/shard_map/ppermute | solution.py:611
  4.1 7.0 %collective-permute-start.38 = (bf16[4,128,128]{2,1,0:T(8,128)(2,1)S(1)}, bf16[4,128,128]{2,1,0:T(8,128)(2,1)S(1)}, u32[]{:S(2)}, u32[]{:S(2)}) collective-permute-start(bf16[4,128,128]{2,1,0:T(8,128)(2,1)S(1)} %get-tuple-element.82.refs_7_), channel_id=1, source_target_pairs={{0,4},{2,10},{8,0},{10,18},{16,8},{18,26},{24,16},{26,30},{28,24},... | collective-permute-start | bytes 393224 | tf_op jit(solution)/shard_map/ppermute | solution.py:569
  7.1 5.1 %collective-permute-start.36 = (bf16[4,128,128]{2,1,0:T(8,128)(2,1)S(1)}, bf16[4,128,128]{2,1,0:T(8,128)(2,1)S(1)}, u32[]{:S(2)}, u32[]{:S(2)}) collective-permute-start(bf16[4,128,128]{2,1,0:T(8,128)(2,1)S(1)} %get-tuple-element.82.refs_7_), channel_id=1, source_target_pairs={{0,8},{2,6},{8,16},{10,2},{16,24},{18,10},{24,28},{26,18},{28,20},... | collective-permute-start | bytes 393224 | tf_op jit(solution)/shard_map/ppermute | solution.py:569
  11.1 6.2 %collective-permute-start.39 = (bf16[4,128,128]{2,1,0:T(8,128)(2,1)S(1)}, bf16[4,128,128]{2,1,0:T(8,128)(2,1)S(1)}, u32[]{:S(2)}, u32[]{:S(2)}) collective-permute-start(bf16[4,128,128]{2,1,0:T(8,128)(2,1)S(1)} %collective-permute-done.38.refs_6_), channel_id=1, source_target_pairs={{0,4},{2,10},{8,0},{10,18},{16,8},{18,26},{24,16},{26,30},{28,24},... | collective-permute-start | bytes 393224 | tf_op jit(solution)/shard_map/ppermute | solution.py:569
  12.2 5.1 %collective-permute-start.37 = (bf16[4,128,128]{2,1,0:T(8,128)(2,1)S(1)}, bf16[4,128,128]{2,1,0:T(8,128)(2,1)S(1)}, u32[]{:S(2)}, u32[]{:S(2)}) collective-permute-start(bf16[4,128,128]{2,1,0:T(8,128)(2,1)S(1)} %collective-permute-done.36.refs_5_), channel_id=1, source_target_pairs={{0,8},{2,6},{8,16},{10,2},{16,24},{18,10},{24,28},{26,18},{28,20},... | collective-permute-start | bytes 393224 | tf_op jit(solution)/shard_map/ppermute | solution.py:569
  13.5 6.1 %collective-permute-start.50 = (bf16[4,128,128]{2,1,0:T(8,128)(2,1)S(1)}, bf16[4,128,128]{2,1,0:T(8,128)(2,1)S(1)}, u32[]{:S(2)}, u32[]{:S(2)}) collective-permute-start(bf16[4,128,128]{2,1,0:T(8,128)(2,1)S(1)} %get-tuple-element.82.refs_7_), channel_id=1, source_target_pairs={{0,2},{2,0},{8,10},{10,8},{16,18},{18,16},{24,26},{26,24},{28,30},... | collective-permute-start | bytes 393224 | tf_op jit(solution)/shard_map/ppermute | solution.py:573
  13.5 3.5 %collective-permute-start.35 = (s32[1,128]{1,0:T(1,128)S(1)}, s32[1,128]{1,0:T(1,128)S(1)}, u32[]{:S(2)}, u32[]{:S(2)}) collective-permute-start(s32[1,128]{1,0:T(1,128)S(1)} %get-tuple-element.81), channel_id=1, source_target_pairs={{0,1},{1,0},{2,3},{3,2},{4,5},{5,4},{6,7},{7,6},{8,9},{9,8},{10,11... | collective-permute-start | bytes 1544 | tf_op jit(solution)/shard_map/ppermute | solution.py:615
  14.6 5.2 %collective-permute-start.49 = (bf16[4,128,128]{2,1,0:T(8,128)(2,1)S(1)}, bf16[4,128,128]{2,1,0:T(8,128)(2,1)S(1)}, u32[]{:S(2)}, u32[]{:S(2)}) collective-permute-start(bf16[4,128,128]{2,1,0:T(8,128)(2,1)S(1)} %collective-permute-done.38.refs_6_), channel_id=1, source_target_pairs={{0,2},{2,0},{8,10},{10,8},{16,18},{18,16},{24,26},{26,24},{28,30},... | collective-permute-start | bytes 393224 | tf_op jit(solution)/shard_map/ppermute | solution.py:573
  17.3 5.0 %collective-permute-start.40 = (bf16[4,128,128]{2,1,0:T(8,128)(2,1)S(1)}, bf16[4,128,128]{2,1,0:T(8,128)(2,1)S(1)}, u32[]{:S(2)}, u32[]{:S(2)}) collective-permute-start(bf16[4,128,128]{2,1,0:T(8,128)(2,1)S(1)} %get-tuple-element.83.refs_3_), channel_id=1, source_target_pairs={{0,8},{2,6},{8,16},{10,2},{16,24},{18,10},{24,28},{26,18},{28,20},... | collective-permute-start | bytes 393224 | tf_op jit(solution)/shard_map/ppermute | solution.py:569
  19.1 3.1 %collective-permute-start.48 = (bf16[4,128,128]{2,1,0:T(8,128)(2,1)S(1)}, bf16[4,128,128]{2,1,0:T(8,128)(2,1)S(1)}, u32[]{:S(2)}, u32[]{:S(2)}) collective-permute-start(bf16[4,128,128]{2,1,0:T(8,128)(2,1)S(1)} %collective-permute-done.36.refs_5_), channel_id=1, source_target_pairs={{0,2},{2,0},{8,10},{10,8},{16,18},{18,16},{24,26},{26,24},{28,30},... | collective-permute-start | bytes 393224 | tf_op jit(solution)/shard_map/ppermute | solution.py:573
  19.1 5.4 %collective-permute-start.46 = (bf16[4,128,128]{2,1,0:T(8,128)(2,1)S(1)}, bf16[4,128,128]{2,1,0:T(8,128)(2,1)S(1)}, u32[]{:S(2)}, u32[]{:S(2)}) collective-permute-start(bf16[4,128,128]{2,1,0:T(8,128)(2,1)S(1)} %get-tuple-element.83.refs_3_), channel_id=1, source_target_pairs={{0,2},{2,0},{8,10},{10,8},{16,18},{18,16},{24,26},{26,24},{28,30},... | collective-permute-start | bytes 393224 | tf_op jit(solution)/shard_map/ppermute | solution.py:573
  19.6 6.6 %collective-permute-start.42 = (bf16[4,128,128]{2,1,0:T(8,128)(2,1)S(1)}, bf16[4,128,128]{2,1,0:T(8,128)(2,1)S(1)}, u32[]{:S(2)}, u32[]{:S(2)}) collective-permute-start(bf16[4,128,128]{2,1,0:T(8,128)(2,1)S(1)} %get-tuple-element.84.refs_4_), channel_id=1, source_target_pairs={{0,4},{2,10},{8,0},{10,18},{16,8},{18,26},{24,16},{26,30},{28,24},... | collective-permute-start | bytes 393224 | tf_op jit(solution)/shard_map/ppermute | solution.py:569
  19.8 7.2 %collective-permute-start.47 = (bf16[4,128,128]{2,1,0:T(8,128)(2,1)S(1)}, bf16[4,128,128]{2,1,0:T(8,128)(2,1)S(1)}, u32[]{:S(2)}, u32[]{:S(2)}) collective-permute-start(bf16[4,128,128]{2,1,0:T(8,128)(2,1)S(1)} %get-tuple-element.84.refs_4_), channel_id=1, source_target_pairs={{0,2},{2,0},{8,10},{10,8},{16,18},{18,16},{24,26},{26,24},{28,30},... | collective-permute-start | bytes 393224 | tf_op jit(solution)/shard_map/ppermute | solution.py:573
  22.2 4.8 %collective-permute-start.44 = (bf16[4,128,128]{2,1,0:T(8,128)(2,1)S(1)}, bf16[4,128,128]{2,1,0:T(8,128)(2,1)S(1)}, u32[]{:S(2)}, u32[]{:S(2)}) collective-permute-start(bf16[4,128,128]{2,1,0:T(8,128)(2,1)S(1)} %collective-permute-done.40.refs_1_), channel_id=1, source_target_pairs={{0,2},{2,0},{8,10},{10,8},{16,18},{18,16},{24,26},{26,24},{28,30},... | collective-permute-start | bytes 393224 | tf_op jit(solution)/shard_map/ppermute | solution.py:573
  22.2 4.9 %collective-permute-start.43 = (bf16[4,128,128]{2,1,0:T(8,128)(2,1)S(1)}, bf16[4,128,128]{2,1,0:T(8,128)(2,1)S(1)}, u32[]{:S(2)}, u32[]{:S(2)}) collective-permute-start(bf16[4,128,128]{2,1,0:T(8,128)(2,1)S(1)} %collective-permute-done.40.refs_1_), channel_id=1, source_target_pairs={{0,10},{2,4},{8,18},{10,0},{16,26},{18,8},{24,30},{26,16},{28,22},... | collective-permute-start | bytes 393224 | tf_op jit(solution)/shard_map/ppermute | solution.py:575
  24.5 5.3 %collective-permute-start.41 = (bf16[4,128,128]{2,1,0:T(8,128)(2,1)S(1)}, bf16[4,128,128]{2,1,0:T(8,128)(2,1)S(1)}, u32[]{:S(2)}, u32[]{:S(2)}) collective-permute-start(bf16[4,128,128]{2,1,0:T(8,128)(2,1)S(1)} %collective-permute-done.40.refs_1_), channel_id=1, source_target_pairs={{0,8},{2,6},{8,16},{10,2},{16,24},{18,10},{24,28},{26,18},{28,20},... | collective-permute-start | bytes 393224 | tf_op jit(solution)/shard_map/ppermute | solution.py:574
  26.3 3.5 %collective-permute-start.45 = (bf16[4,128,128]{2,1,0:T(8,128)(2,1)S(1)}, bf16[4,128,128]{2,1,0:T(8,128)(2,1)S(1)}, u32[]{:S(2)}, u32[]{:S(2)}) collective-permute-start(bf16[4,128,128]{2,1,0:T(8,128)(2,1)S(1)} %collective-permute-done.42.refs_2_), channel_id=1, source_target_pairs={{0,2},{2,0},{8,10},{10,8},{16,18},{18,16},{24,26},{26,24},{28,30},... | collective-permute-start | bytes 393224 | tf_op jit(solution)/shard_map/ppermute | solution.py:573
  36.6 2.0 %collective-permute-start.53 = (bf16[16,128,128]{2,1,0:T(8,128)(2,1)S(1)}, bf16[16,128,128]{2,1,0:T(8,128)(2,1)S(1)}, u32[]{:S(2)}, u32[]{:S(2)}) collective-permute-start(bf16[16,128,128]{2,1,0:T(8,128)(2,1)S(1)} %get-tuple-element.88), channel_id=1, source_target_pairs={{0,2},{2,0},{8,10},{10,8},{16,18},{18,16},{24,26},{26,24},{28,30},... | collective-permute-start | bytes 1572872 | tf_op jit(solution)/shard_map/ppermute | solution.py:582
  36.7 11.7 %collective-permute-start.52 = (bf16[16,128,128]{2,1,0:T(8,128)(2,1)S(1)}, bf16[16,128,128]{2,1,0:T(8,128)(2,1)S(1)}, u32[]{:S(2)}, u32[]{:S(2)}) collective-permute-start(bf16[16,128,128]{2,1,0:T(8,128)(2,1)S(1)} %get-tuple-element.87), channel_id=1, source_target_pairs={{0,2},{2,0},{8,10},{10,8},{16,18},{18,16},{24,26},{26,24},{28,30},... | collective-permute-start | bytes 1572872 | tf_op jit(solution)/shard_map/ppermute | solution.py:582
  38.7 5.6 %collective-permute-start.54 = (bf16[4,128,128]{2,1,0:T(8,128)(2,1)S(1)}, bf16[4,128,128]{2,1,0:T(8,128)(2,1)S(1)}, u32[]{:S(2)}, u32[]{:S(2)}) collective-permute-start(bf16[4,128,128]{2,1,0:T(8,128)(2,1)S(1)} %get-tuple-element.89), channel_id=1, source_target_pairs={{0,8},{2,6},{8,16},{10,2},{16,24},{18,10},{24,28},{26,18},{28,20},... | collective-permute-start | bytes 393224 | tf_op jit(solution)/shard_map/ppermute | solution.py:594
  40.1 5.0 %collective-permute-start.55 = (bf16[4,128,128]{2,1,0:T(8,128)(2,1)S(1)}, bf16[4,128,128]{2,1,0:T(8,128)(2,1)S(1)}, u32[]{:S(2)}, u32[]{:S(2)}) collective-permute-start(bf16[4,128,128]{2,1,0:T(8,128)(2,1)S(1)} %get-tuple-element.90), channel_id=1, source_target_pairs={{0,4},{2,10},{8,0},{10,18},{16,8},{18,26},{24,16},{26,30},{28,24},... | collective-permute-start | bytes 393224 | tf_op jit(solution)/shard_map/ppermute | solution.py:594
  45.2 5.8 %collective-permute-start.56 = (bf16[4,128,128]{2,1,0:T(8,128)(2,1)S(1)}, bf16[4,128,128]{2,1,0:T(8,128)(2,1)S(1)}, u32[]{:S(2)}, u32[]{:S(2)}) collective-permute-start(bf16[4,128,128]{2,1,0:T(8,128)(2,1)S(1)} %get-tuple-element.91), channel_id=1, source_target_pairs={{0,8},{2,6},{8,16},{10,2},{16,24},{18,10},{24,28},{26,18},{28,20},... | collective-permute-start | bytes 393224 | tf_op jit(solution)/shard_map/ppermute | solution.py:594
  47.2 5.0 %collective-permute-start.57 = (bf16[4,128,128]{2,1,0:T(8,128)(2,1)S(1)}, bf16[4,128,128]{2,1,0:T(8,128)(2,1)S(1)}, u32[]{:S(2)}, u32[]{:S(2)}) collective-permute-start(bf16[4,128,128]{2,1,0:T(8,128)(2,1)S(1)} %get-tuple-element.92), channel_id=1, source_target_pairs={{0,4},{2,10},{8,0},{10,18},{16,8},{18,26},{24,16},{26,30},{28,24},... | collective-permute-start | bytes 393224 | tf_op jit(solution)/shard_map/ppermute | solution.py:594
  47.3 15.8 %collective-permute-start.51 = (bf16[18,128,128]{2,1,0:T(8,128)(2,1)S(1)}, bf16[18,128,128]{2,1,0:T(8,128)(2,1)S(1)}, u32[]{:S(2)}, u32[]{:S(2)}) collective-permute-start(bf16[18,128,128]{2,1,0:T(8,128)(2,1)S(1)} %get-tuple-element.85), channel_id=1, source_target_pairs={{0,1},{1,0},{2,3},{3,2},{4,5},{5,4},{6,7},{7,6},{8,9},{9,8},{10,11... | collective-permute-start | bytes 1769480 | tf_op jit(solution)/shard_map/ppermute | solution.py:615
  52.3 6.3 %collective-permute-start.58 = (bf16[4,128,128]{2,1,0:T(8,128)(2,1)S(1)}, bf16[4,128,128]{2,1,0:T(8,128)(2,1)S(1)}, u32[]{:S(2)}, u32[]{:S(2)}) collective-permute-start(bf16[4,128,128]{2,1,0:T(8,128)(2,1)S(1)} %get-tuple-element.93), channel_id=1, source_target_pairs={{0,8},{2,6},{8,16},{10,2},{16,24},{18,10},{24,28},{26,18},{28,20},... | collective-permute-start | bytes 393224 | tf_op jit(solution)/shard_map/ppermute | solution.py:594
  53.7 7.0 %collective-permute-start.60 = (bf16[4,128,128]{2,1,0:T(8,128)(2,1)S(1)}, bf16[4,128,128]{2,1,0:T(8,128)(2,1)S(1)}, u32[]{:S(2)}, u32[]{:S(2)}) collective-permute-start(bf16[4,128,128]{2,1,0:T(8,128)(2,1)S(1)} %get-tuple-element.94), channel_id=1, source_target_pairs={{0,4},{2,10},{8,0},{10,18},{16,8},{18,26},{24,16},{26,30},{28,24},... | collective-permute-start | bytes 393224 | tf_op jit(solution)/shard_map/ppermute | solution.py:594
  58.7 9.0 %copy-start = (bf16[1,2,128,128]{3,2,1,0:T(8,128)(2,1)S(1)}, bf16[1,2,128,128]{3,2,1,0:T(8,128)(2,1)}, u32[]{:S(2)}) copy-start(bf16[1,2,128,128]{3,2,1,0:T(8,128)(2,1)} %refs_0_.1) | copy-start | bytes 196612
  58.7 9.0 %copy-start.1 = (bf16[1,2,128,128]{3,2,1,0:T(8,128)(2,1)S(1)}, bf16[1,2,128,128]{3,2,1,0:T(8,128)(2,1)}, u32[]{:S(2)}) copy-start(bf16[1,2,128,128]{3,2,1,0:T(8,128)(2,1)} %refs_1_.1) | copy-start | bytes 196612
  58.7 9.0 %copy-start.2 = (bf16[1,2,128,128]{3,2,1,0:T(8,128)(2,1)S(1)}, bf16[1,2,128,128]{3,2,1,0:T(8,128)(2,1)}, u32[]{:S(2)}) copy-start(bf16[1,2,128,128]{3,2,1,0:T(8,128)(2,1)} %refs_2_.1) | copy-start | bytes 196612
  58.7 4.5 %collective-permute-start.62 = (bf16[4,128,128]{2,1,0:T(8,128)(2,1)S(1)}, bf16[4,128,128]{2,1,0:T(8,128)(2,1)S(1)}, u32[]{:S(2)}, u32[]{:S(2)}) collective-permute-start(bf16[4,128,128]{2,1,0:T(8,128)(2,1)S(1)} %get-tuple-element.122), channel_id=1, source_target_pairs={{0,10},{2,4},{8,18},{10,0},{16,26},{18,8},{24,30},{26,16},{28,22},... | collective-permute-start | bytes 393224 | tf_op jit(solution)/shard_map/ppermute | solution.py:602
  58.8 5.0 %collective-permute-start.59 = (bf16[4,128,128]{2,1,0:T(8,128)(2,1)S(1)}, bf16[4,128,128]{2,1,0:T(8,128)(2,1)S(1)}, u32[]{:S(2)}, u32[]{:S(2)}) collective-permute-start(bf16[4,128,128]{2,1,0:T(8,128)(2,1)S(1)} %get-tuple-element.122), channel_id=1, source_target_pairs={{0,8},{2,6},{8,16},{10,2},{16,24},{18,10},{24,28},{26,18},{28,20},... | collective-permute-start | bytes 393224 | tf_op jit(solution)/shard_map/ppermute | solution.py:599
  59.3 4.5 %collective-permute-start.61 = (bf16[4,128,128]{2,1,0:T(8,128)(2,1)S(1)}, bf16[4,128,128]{2,1,0:T(8,128)(2,1)S(1)}, u32[]{:S(2)}, u32[]{:S(2)}) collective-permute-start(bf16[4,128,128]{2,1,0:T(8,128)(2,1)S(1)} %get-tuple-element.123.refs_2_), channel_id=1, source_target_pairs={{0,2},{2,0},{8,10},{10,8},{16,18},{18,16},{24,26},{26,24},{28,30},... | collective-permute-start | bytes 393224 | tf_op jit(solution)/shard_map/ppermute | solution.py:601
  60.8 3.0 %collective-permute-start.63 = (bf16[4,128,128]{2,1,0:T(8,128)(2,1)S(1)}, bf16[4,128,128]{2,1,0:T(8,128)(2,1)S(1)}, u32[]{:S(2)}, u32[]{:S(2)}) collective-permute-start(bf16[4,128,128]{2,1,0:T(8,128)(2,1)S(1)} %collective-permute-done.60.refs_4_), channel_id=1, source_target_pairs={{0,2},{2,0},{8,10},{10,8},{16,18},{18,16},{24,26},{26,24},{28,30},... | collective-permute-start | bytes 393224 | tf_op jit(solution)/shard_map/ppermute | solution.py:603
where the time goes:
time: 68.9 us; the launch traced here: 67.8 us
  starting transfers between devices  26.4 us (38%)
  waiting for transfers between devices  25 us (36%)
  Pallas kernels  13.7 us (20%)
  between operations  1.44 us (2%)
  local copies, waits for them, and re-layouts  0.8 us (1%)
    ppermute x6, waiting for transfers between devices, reduce_parts(): a, b = (lax.ppermute(a, 'fsdp', ahead), lax.ppermute(b, 'fsdp', behind))  12.2 us
    ppermute x6, starting transfers between devices, gather_chunks(): a, b = (lax.ppermute(a, 'fsdp', ahead), lax.ppermute(b, 'fsdp', behind))  7.45 us
    pallas_call x1, Pallas kernels, call_compute(): pl.pallas_call(functools.partial(compute_kernel, sz), out_shape=out_shape...  6.79 us
    ppermute x6, starting transfers between devices, reduce_parts(): a, b = (lax.ppermute(a, 'fsdp', ahead), lax.ppermute(b, 'fsdp', behind))  6.41 us
    ppermute x6, waiting for transfers between devices, gather_chunks(): a, b = (lax.ppermute(a, 'fsdp', ahead), lax.ppermute(b, 'fsdp', behind))  5.47 us
    pallas_call x1, Pallas kernels, call_last(): pl.pallas_call(functools.partial(last_kernel, sz), out_shape=[jax.ShapeDt...  3.22 us
    ppermute x1, waiting for transfers between devices, gather_chunks(): same[sz.top] = lax.ppermute(a, 'fsdp', ahead)  2.66 us
    ppermute x7, starting transfers between devices, gather_chunks(): other = {d: lax.ppermute(same[d], 'fsdp', swap) for d in same}  2.62 us
  transfers between devices with their start and end apart: 32, of which 15 were waited for; matrix products, arithmetic and copies ran while one was open for 2% of the time, Pallas kernels for 3%

commit v1 on v0

--- a/solution.py
+++ b/solution.py
@@ -11,7 +11,8 @@
 BLK = 128
 GROUP = 4
 FIRST_SEND = 18
-LEAN_SLOTS = 4
+LEAN_SLOTS = 7
+ROWS = BLK // 2
 SMALL = 4 * 1024 * 1024
 PART, STRIP, CIDX, CWAS, OIDX, OWAS = range(6)
 FIELDS = 6
@@ -19,7 +20,7 @@
 HEAD_ROW = COLS_ROW + 1
 MINE_ROW = COLS_ROW + 2
 LISTS_ROW = COLS_ROW + 3
-HEAD_COLS, HEAD_OVER, HEAD_LISTS = 3, 4, 8
+HEAD_COLS, HEAD_OVER, HEAD_CORE, HEAD_LISTS = 3, 4, 5, 8
 
 
 class Sizes:
@@ -40,14 +41,20 @@
         for d in range(1, self.top):
             self.order += [self.top + d, self.top - d]
         self.order.append(0)
-        self.far = min(4, self.ring - 1)
-        self.keep = min(LEAN_SLOTS, self.owned) if lean else self.owned
+        self.far = min(2, self.ring - 1)
+        self.keep = min(LEAN_SLOTS, 2 * self.owned) if lean else 2 * self.owned
         self.send_all = 2 * self.rbt
         self.first = min(FIRST_SEND, self.send_all) if lean else self.send_all
-        self.blocks = 2 * self.ring * self.keep
+        self.blocks = self.ring * self.keep
         self.plan_rows = -(-(LISTS_ROW + 2 * n_tensor) // 8) * 8
         self.note_n, self.note_over = self.lanes - 1, self.lanes - 2
         self.room = slots + GROUP
+
+    def place(self, d):
+        return self.order.index(d) * self.keep
+
+    def place_across(self, d):
+        return self.place((self.ring - d) % self.ring)
 
 
 def permutations(sz):
@@ -144,13 +151,11 @@
     def carried(self):
         sz = self.sz
         rank = jnp.sum(self.before * self.same_chip * self.act_r, axis=1, keepdims=True)
-        core = rest_of(rank, 2)
         away = ring_position(sz, self.chip_c) - ring_position(sz, ratio(self.f, 2))
-        away = jnp.where(core == 0, away, -away)
+        away = jnp.where(rest_of(self.f, 2) == 0, away, -away)
         rel = jnp.where(away < 0, away + sz.ring, away)
         j = jnp.where(rel > sz.top, 2 * (rel - sz.top) - 1, 2 * (sz.top - rel))
-        j = jnp.where(rel == 0, sz.ring - 1.0, j)
-        return core, ratio(rank, 2), j + jnp.where(core == rest_of(self.f, 2), 0.0, float(sz.ring))
+        return rank, jnp.where(rel == 0, sz.ring - 1.0, j)
 
     def ranks(self, chosen_r):
         return jnp.sum(self.before * chosen_r, axis=1, keepdims=True)
@@ -181,22 +186,22 @@
     m = Marks(sz, own)
     f32 = jnp.float32
     lane_r, sub_c = m.lane_r, m.sub_c
-    core_c, pos_c, base_c = m.carried()
-    own_core = core_c == rest_of(m.f, 2)
-
-    pair = jnp.where(rest_of(m.f, 2) == 0, m.f + 1, m.f - 1)
+    pos_c, base_c = m.carried()
+    core = rest_of(m.f, 2)
+    half = pl.ds(pl.multiple_of(jnp.max(core).astype(jnp.int32) * ROWS, ROWS), ROWS)
+
+    pair = jnp.where(core == 0, m.f + 1, m.f - 1)
     i_r = rest_of(lane_r, sz.owned)
     owner_r = jnp.where(lane_r < sz.owned, m.f, pair)
     slot_r = ratio(i_r, sz.nb) * S + owner_r * sz.nb + rest_of(i_r, sz.nb)
-    at_r = jnp.sum(
-        jnp.where((sub_c == slot_r) & own_core, m.act_c * (pos_c + 1.0), 0.0), axis=0, keepdims=True)
+    at_r = jnp.sum(jnp.where(sub_c == slot_r, m.act_c * (pos_c + 1.0), 0.0), axis=0, keepdims=True)
     copies = []
     for i in range(2 * sz.owned):
         side, k, a = i // sz.owned, i % sz.owned // sz.nb, i % sz.nb
         at = jnp.max(jnp.where(lane_r == i, at_r, 0.0)).astype(jnp.int32)
         fits = (at > 0) & (at <= sz.keep)
         place = jnp.minimum(jnp.maximum(at - 1, 0), sz.keep - 1)
-        copy = pltpu.make_async_copy((mine, theirs)[side][k].at[0, a], chunk.at[place], sems.at[i])
+        copy = pltpu.make_async_copy((mine, theirs)[side][k].at[0, a, half], chunk.at[place], sems.at[i])
         copies.append((fits, copy))
     for fits, copy in copies:
         pl.when(fits)(copy.start)
@@ -233,7 +238,7 @@
     rows.append(jnp.where(lane_r < n_cols, cols, f32(S)))
     head.append((HEAD_COLS, n_cols))
     lists, sent = [], []
-    over = (m.most_on_chip() > 2 * sz.keep).astype(f32)
+    over = (m.most_on_chip() > sz.keep).astype(f32)
     for s in range(sz.n_tensor):
         chosen_c = m.lead_c * (m.shift_c == s).astype(f32)
         chosen_r = m.lead_r * (m.shift_r == s).astype(f32)
@@ -244,14 +249,12 @@
         head.append((HEAD_LISTS + s, n))
         sent.append(n)
         over = jnp.maximum(over, (n > sz.first).astype(f32))
-    head.append((HEAD_OVER, over))
+    head += [(HEAD_OVER, over), (HEAD_CORE, core)]
     for s in range(1, sz.n_tensor):
         note = jnp.where(lane_r == sz.note_n, sent[s], lists[2 * s + 1])
         notes[s - 1][...] = jnp.where(lane_r == sz.note_over, over, note).astype(jnp.int32)
     rows.append(head_row(sz, head))
-    held_c = pos_c + 1.0 + jnp.where(own_core, 0.0, float(sz.keep))
-    rows.append(jnp.sum(
-        jnp.where((sub_c == slot_r) & (lane_r < sz.owned), m.act_c * held_c, 0.0), axis=0, keepdims=True))
+    rows.append(at_r)
     rows += lists
     for i, row in enumerate(rows):
         plan[i:i + 1, :] = row.astype(jnp.int32)
@@ -290,10 +293,14 @@
         cols = pl.ds(pl.multiple_of(get(k, STRIP, e) * BLK, BLK), BLK)
         return pltpu.make_async_copy(src.at[:, cols], xs.at[k * sz.room + e], strip_sems.at[k * sz.room + e])
 
-    loads = [
-        pltpu.make_async_copy(chunk, wbuf.at[pl.ds(i * sz.keep, sz.keep)], sems.at[i])
-        for i, chunk in enumerate(chunks)
-    ]
+    core = plan[HEAD_ROW, HEAD_CORE]
+    sides = [pl.ds(pl.multiple_of(c * ROWS, ROWS), ROWS) for c in (core, 1 - core)]
+    loads = []
+    for side, place in enumerate((sz.place, sz.place_across)):
+        for d in sz.order:
+            i = len(loads)
+            there = wbuf.at[pl.ds(place(d), sz.keep), sides[side]]
+            loads.append(pltpu.make_async_copy(chunks[i], there, sems.at[i]))
     for k in range(3):
         each(plan, k, lambda e, k=k: strip_copy(k, e).start())
     for c in loads:
@@ -334,13 +341,12 @@
             parts[get(k, PART, e)] = grad.astype(jnp.bfloat16)
 
     walk(plan, gradients)
-    split = sz.ring * sz.keep
-    cut = split + sz.far * sz.keep
-    outs = [
-        pltpu.make_async_copy(parts.at[pl.ds(split, cut - split)], far, sems.at[0]),
-        pltpu.make_async_copy(parts.at[pl.ds(0, split)], same, sems.at[1]),
-        pltpu.make_async_copy(parts.at[pl.ds(cut, sz.blocks - cut)], near, sems.at[2]),
-    ]
+    outs = []
+    for j, d in enumerate(sz.order):
+        ref, at = (far, j) if j < sz.far else (near, j - sz.far)
+        outs.append(pltpu.make_async_copy(
+            parts.at[pl.ds(sz.place_across(d), sz.keep), sides[1]], ref.at[pl.ds(at * sz.keep, sz.keep)], sems.at[j]))
+    outs.append(pltpu.make_async_copy(parts.at[pl.ds(0, sz.blocks), sides[0]], same, sems.at[sz.ring]))
     for c in outs:
         c.start()
 
@@ -358,7 +364,7 @@
             stage[s * sz.first + i] = out_acc[plan[LISTS_ROW + 2 * s, i]].astype(jnp.bfloat16)
 
         lax.fori_loop(0, jnp.minimum(plan[HEAD_ROW, HEAD_LISTS + s], sz.first), staged, None)
-        copy = pltpu.make_async_copy(stage.at[pl.ds(s * sz.first, sz.first)], firsts[s], sems.at[3 + s])
+        copy = pltpu.make_async_copy(stage.at[pl.ds(s * sz.first, sz.first)], firsts[s], sems.at[sz.ring + 1 + s])
         copy.start()
         outs.append(copy)
     for c in outs:
@@ -370,7 +376,7 @@
     return at < sz.rbt, pl.ds(pl.multiple_of(w * BLK, BLK), BLK)
 
 
-def prepare_kernel(sz, plan, first, outputs, input_grads):
+def prepare_kernel(sz, plan, note, first, outputs, input_grads, strips):
     outputs[...] = jnp.zeros_like(outputs)
     input_grads[...] = jnp.zeros_like(input_grads)
 
@@ -386,13 +392,26 @@
             input_grads[:, cols] = first[i]
 
     lax.fori_loop(0, jnp.minimum(plan[HEAD_ROW, HEAD_LISTS], sz.first), step, None)
+
+    def pick(i, _):
+        is_out, cols = strip_of(sz, note[0, i])
+
+        @pl.when(is_out)
+        def _():
+            strips[i] = outputs[:, cols]
+
+        @pl.when(jnp.logical_not(is_out))
+        def _():
+            strips[i] = input_grads[:, cols]
+
+    lax.fori_loop(0, jnp.minimum(note[0, sz.note_n], sz.first), pick, None)
 
 
 def last_kernel(sz, plan, *refs):
     T = sz.n_tensor
     notes, refs = refs[:T - 1], refs[T - 1:]
     firsts, refs = refs[:T - 1], refs[T - 1:]
-    mine, theirs, refs = refs[:3], refs[3:6], refs[8:]
+    mine, theirs, held_strips, refs = refs[:3], refs[3:6], refs[6], refs[9:]
     outputs, input_grads, grads, flag = refs[0], refs[1], refs[2:5], refs[5]
     strips, read_sems, write_sems = refs[6:]
     over = plan[HEAD_ROW, HEAD_OVER]
@@ -429,18 +448,21 @@
     def end(s):
         loop(s, lambda i: move(s, i, True, lambda c: c.wait()))
 
-    begin(0)
+    def first_add(i):
+        value = held_strips[i].astype(jnp.float32) + firsts[0][i].astype(jnp.float32)
+        strips[i] = value.astype(jnp.bfloat16)
+        move(0, i, True, lambda c: c.start())
+
+    loop(0, first_add)
+    core = plan[HEAD_ROW, HEAD_CORE]
     for k in range(3):
         for a in range(sz.nb):
             at = plan[MINE_ROW, k * sz.nb + a]
-
-            def value(terms, p):
-                p = jnp.minimum(jnp.maximum(p, 0), sz.keep - 1)
-                return sum(t[p].astype(jnp.float32) for t in terms)
-
-            out = jnp.where(at > sz.keep, value(theirs, at - 1 - sz.keep), value(mine, at - 1))
-            grads[k][0, a] = jnp.where(at > 0, out, 0.0).astype(jnp.bfloat16)
-    add(0)
+            p = jnp.minimum(jnp.maximum(at - 1, 0), sz.keep - 1)
+            for terms, c in ((mine, core), (theirs, 1 - core)):
+                value = sum(t[p].astype(jnp.float32) for t in terms)
+                rows = pl.ds(pl.multiple_of(c * ROWS, ROWS), ROWS)
+                grads[k][0, a, rows] = jnp.where(at > 0, value, 0.0).astype(jnp.bfloat16)
     end(0)
     for s in range(1, T - 1):
         begin(s)
@@ -464,7 +486,7 @@
         functools.partial(plan_kernel, sz),
         out_shape=[
             jax.ShapeDtypeStruct((sz.plan_rows, sz.lanes), jnp.int32),
-            jax.ShapeDtypeStruct((sz.keep, BLK, BLK), jnp.bfloat16),
+            halves(sz.keep),
         ] + [jax.ShapeDtypeStruct((1, sz.lanes), jnp.int32)] * (sz.n_tensor - 1),
         in_specs=[spec(VMEM)] + [spec(ANY)] * 6,
         out_specs=[spec(VMEM), spec(ANY)] + [spec(VMEM)] * (sz.n_tensor - 1),
@@ -492,6 +514,10 @@
     return jax.ShapeDtypeStruct((n, BLK, BLK), jnp.bfloat16)
 
 
+def halves(n):
+    return jax.ShapeDtypeStruct((n, ROWS, BLK), jnp.bfloat16)
+
+
 def held(scratch):
     return sum(s[0] * s[1] * s[2] * jnp.dtype(t).itemsize for s, t in scratch) + 2 * 1024 * 1024
 
@@ -499,7 +525,7 @@
 def call_compute(sz, plan, tokens, cot, chunks):
     bf, f32 = jnp.bfloat16, jnp.float32
     T, A = sz.n_tensor, sz.slots + 1
-    out_shape = [blocks(sz.ring * sz.keep), blocks(sz.far * sz.keep), blocks((sz.ring - sz.far) * sz.keep)]
+    out_shape = [halves(sz.ring * sz.keep), halves(sz.far * sz.keep), halves((sz.ring - sz.far) * sz.keep)]
     out_shape += [blocks(sz.first)] * T
     scratch = [
         ((3 * sz.room, sz.tok, BLK), bf),
@@ -519,7 +545,7 @@
         out_specs=[spec(ANY)] * len(out_shape),
         scratch_shapes=[pltpu.VMEM(s, t) for s, t in scratch] + [
             pltpu.SemaphoreType.DMA((3 * sz.room,)),
-            pltpu.SemaphoreType.DMA((max(len(chunks), 3 + T),)),
+            pltpu.SemaphoreType.DMA((max(len(chunks), sz.ring + 1 + T),)),
         ],
         compiler_params=pltpu.CompilerParams(vmem_limit_bytes=held(scratch)),
         cost_estimate=cost(1_000_000_000, 20_000_000),
@@ -527,27 +553,27 @@
     )(plan, pltpu.with_memory_space_constraint(tokens, HBM), pltpu.with_memory_space_constraint(cot, HBM), *chunks)
 
 
-def call_prepare(sz, plan, first):
+def call_prepare(sz, plan, note, first):
     half = jax.ShapeDtypeStruct((sz.tok, sz.width // sz.n_tensor), jnp.bfloat16)
     return pl.pallas_call(
         functools.partial(prepare_kernel, sz),
-        out_shape=[half, half],
-        in_specs=[spec(SMEM), spec(VMEM)],
-        out_specs=[spec(VMEM), spec(VMEM)],
-        compiler_params=pltpu.CompilerParams(vmem_limit_bytes=10 * 1024 * 1024),
+        out_shape=[half, half, blocks(sz.first)],
+        in_specs=[spec(SMEM), spec(SMEM), spec(VMEM)],
+        out_specs=[spec(VMEM)] * 3,
+        compiler_params=pltpu.CompilerParams(vmem_limit_bytes=12 * 1024 * 1024),
         cost_estimate=cost(1_000_000, 6_000_000),
         name="prepare",
-    )(plan, first)
-
-
-def call_last(sz, plan, notes, firsts, terms, partial):
-    n = 1 + len(notes) + len(firsts) + len(terms)
+    )(plan, note, first)
+
+
+def call_last(sz, plan, notes, firsts, terms, strips, partial):
+    n = 2 + len(notes) + len(firsts) + len(terms)
     out = jax.ShapeDtypeStruct((1, sz.nb, BLK, BLK), jnp.bfloat16)
     return pl.pallas_call(
         functools.partial(last_kernel, sz),
         out_shape=[jax.ShapeDtypeStruct(p.shape, p.dtype) for p in partial] + [out] * 3 + [
             jax.ShapeDtypeStruct((1,), jnp.int32)],
-        in_specs=[spec(SMEM)] * (1 + len(notes)) + [spec(VMEM)] * (len(firsts) + len(terms)) + [spec(ANY)] * 2,
+        in_specs=[spec(SMEM)] * (1 + len(notes)) + [spec(VMEM)] * (len(firsts) + len(terms) + 1) + [spec(ANY)] * 2,
         out_specs=[spec(ANY)] * 2 + [spec(VMEM)] * 3 + [spec(SMEM)],
         input_output_aliases={n: 0, n + 1: 1},
         scratch_shapes=[
@@ -558,17 +584,15 @@
         compiler_params=pltpu.CompilerParams(vmem_limit_bytes=12 * 1024 * 1024),
         cost_estimate=cost(1_000_000, 3_000_000),
         name="last",
-    )(plan, *notes, *firsts, *terms, *partial)
-
-
-def gather_chunks(sz, chunk, notes):
+    )(plan, *notes, *firsts, *terms, strips, *partial)
+
+
+def gather_chunks(sz, chunk):
     ahead, behind, swap = permutations(sz)
     same = {0: chunk}
     a = b = chunk
     for s in range(1, sz.top):
         a, b = lax.ppermute(a, "fsdp", ahead), lax.ppermute(b, "fsdp", behind)
-        if s == 2:
-            a, b = call_turn([a, b], notes)
         same[sz.ring - s], same[s] = a, b
     other = {d: lax.ppermute(same[d], "fsdp", swap) for d in same}
     same[sz.top] = lax.ppermute(a, "fsdp", ahead)
@@ -576,10 +600,11 @@
     return [side[d] for side in (same, other) for d in sz.order]
 
 
-def reduce_parts(sz, same, far, near):
+def reduce_parts(sz, same, far, near, notes):
     ahead, behind, swap = permutations(sz)
     keep = sz.keep
-    far, near = lax.ppermute(far, "fsdp", swap), lax.ppermute(near, "fsdp", swap)
+    far = lax.ppermute(far, "fsdp", swap)
+    near = lax.ppermute(call_turn([near], [far])[0], "fsdp", swap)
 
     def term(d, *more):
         j = sz.order.index(d)
@@ -591,6 +616,8 @@
 
     a, b = lax.optimization_barrier((term(sz.top), term(sz.top + 1)))
     for s in range(1, sz.top):
+        if s == 2:
+            a, b = call_turn([a, b], notes)
         a, b = lax.ppermute(a, "fsdp", ahead), lax.ppermute(b, "fsdp", behind)
         a = term(sz.top - s, a)
         if s + 1 < sz.top:
@@ -615,12 +642,12 @@
         return lax.ppermute(array, "tensor", [(i, (i + s) % T) for i in range(T)])
 
     notes = [exchange(note, s) for s, note in enumerate(notes, 1)]
-    chunks = gather_chunks(sz, chunk, notes)
+    chunks = gather_chunks(sz, chunk)
     same, far, near, *firsts = call_compute(sz, plan, tokens, cotangent, chunks)
-    partial = call_prepare(sz, plan, firsts[0])
+    *partial, strips = call_prepare(sz, plan, notes[0], firsts[0])
     firsts = [exchange(firsts[s], s) for s in range(1, T)]
-    terms = reduce_parts(sz, same, far, near)
-    *outs, flag = call_last(sz, plan, notes, firsts, terms, partial)
+    terms = reduce_parts(sz, same, far, near, notes)
+    *outs, flag = call_last(sz, plan, notes, firsts, terms, strips, partial)
     return tuple(outs), flag
 
 

time: 68.9 us -> 63.5 us (0.922); the launches traced: 67.8 us -> 63.5 us
  starting transfers between devices: 26.4 us -> 19.6 us
  waiting for transfers between devices: 25 us -> 29 us
  Pallas kernels: 13.7 us -> 12.2 us
    ppermute x6, waiting for transfers between devices: 5.47 us -> 11.3 us  [gather_chunks(): a, b = (lax.ppermute(a, 'fsdp', ahead), lax.ppermute(b, 'fsdp', behind))]
    ppermute x2, waiting for transfers between devices: 2.18 us -> 0.02 us  [exchange(): return lax.ppermute(array, 'tensor', [(i, (i + s) % T) for i in range(T)])]
    ppermute x1, starting transfers between devices: 2.25 us -> 0.12 us  [gather_chunks(): other[sz.top] = lax.ppermute(a, 'fsdp', [(i, j ^ 1) for i, j in ahead])]
    ppermute x1, waiting for transfers between devices: 0.1 us -> 2.2 us  [gather_chunks(): other[sz.top] = lax.ppermute(a, 'fsdp', [(i, j ^ 1) for i, j in ahead])]
    ppermute x2, starting transfers between devices: 2.27 us -> 0.72 us  [exchange(): return lax.ppermute(array, 'tensor', [(i, (i + s) % T) for i in range(T)])]
    ppermute x7, starting transfers between devices: 2.62 us -> 1.09 us  [gather_chunks(): other = {d: lax.ppermute(same[d], 'fsdp', swap) for d in same}]
    ppermute x6, starting transfers between devices: 7.45 us -> 6.49 us  [gather_chunks(): a, b = (lax.ppermute(a, 'fsdp', ahead), lax.ppermute(b, 'fsdp', behind))]
    ppermute x6, waiting for transfers between devices: 12.2 us -> 11.2 us  [reduce_parts(): a, b = (lax.ppermute(a, 'fsdp', ahead), lax.ppermute(b, 'fsdp', behind))]
  transfers between devices with their start and end apart: 32 -> 32, of which waited for: 15 -> 16; matrix products, arithmetic and copies ran while one was open for 2% -> 2% of each run, Pallas kernels for 3% -> 4%
where the time goes in v1:
time: 63.5 us
  waiting for transfers between devices  29 us (46%)
  starting transfers between devices  19.6 us (31%)
  Pallas kernels  12.2 us (19%)
  between operations  1.46 us (2%)
  local copies, waits for them, and re-layouts  0.8 us (1%)
    ppermute x6, waiting for transfers between devices, gather_chunks(): a, b = (lax.ppermute(a, 'fsdp', ahead), lax.ppermute(b, 'fsdp', behind))  11.3 us
    ppermute x6, waiting for transfers between devices, reduce_parts(): a, b = (lax.ppermute(a, 'fsdp', ahead), lax.ppermute(b, 'fsdp', behind))  11.2 us
    ppermute x6, starting transfers between devices, gather_chunks(): a, b = (lax.ppermute(a, 'fsdp', ahead), lax.ppermute(b, 'fsdp', behind))  6.49 us
    ppermute x6, starting transfers between devices, reduce_parts(): a, b = (lax.ppermute(a, 'fsdp', ahead), lax.ppermute(b, 'fsdp', behind))  6.23 us
    pallas_call x1, Pallas kernels, call_compute(): pl.pallas_call(functools.partial(compute_kernel, sz), out_shape=out_shape...  5.86 us
    pallas_call x1, Pallas kernels, call_prepare(): pl.pallas_call(functools.partial(prepare_kernel, sz), out_shape=[half, ha...  2.54 us
    pallas_call x1, Pallas kernels, call_last(): pl.pallas_call(functools.partial(last_kernel, sz), out_shape=[jax.ShapeDt...  2.51 us
    ppermute x1, waiting for transfers between devices, gather_chunks(): other[sz.top] = lax.ppermute(a, 'fsdp', [(i, j ^ 1) for i, j in ahead])  2.2 us
  transfers between devices with their start and end apart: 32, of which 16 were waited for; matrix products, arithmetic and copies ran while one was open for 2% of the time, Pallas kernels for 4%

profile of v1, /device:TPU:0, one launch (start us, length us, event | category | flops | bytes accessed | tf_op | source)
XLA Modules:
  0.0 63.5 jit_solution(950451381685258050)
XLA Ops:
  0.6 0.5 collective-permute-start.32
  1.2 0.1 collective-permute-start.33
  1.2 0.4 collective-permute-start.34
  1.7 0.8 %concatenate.3 = s32[101]{0:T(128)S(1)} concatenate(s32[32]{0:T(128)} %bitcast.9, s32[32]{0:T(128)} %bitcast.10, s32[32]{0:T(128)} %bitcast.11, s32[3]{0:T(128)} %bitcast.12, s32[1]{0:T(128)} %bitcast.4, s32[1]{0:T(128)} %bitcast.5), dimensions={0} | concatenate | bytes 808 | tf_op jit(solution)/shard_map/concatenate | solution.py:669
  2.4 0.0 collective-permute-done.32.refs_3_
  2.5 0.2 collective-permute-done.33.refs_4_
  2.6 0.2 collective-permute-done.34.refs_5_
  2.8 1.3 %plan.3 = (s32[32,128]{1,0:T(8,128)S(1)}, bf16[7,64,128]{2,1,0:T(8,128)(2,1)S(1)}, s32[1,128]{1,0:T(1,128)S(1)}) custom-call(s32[1,128]{1,0:T(1,128)S(1)} %pad_bitcast_fusion.own, bf16[1,2,128,128]{3,2,1,0:T(8,128)(2,1)} %refs_0_.1, bf16[1,2,128,128]{3,2,1,0:T(8,128)(2,1)} %refs_1_.1, bf16[1,2,128,128]{3,2,1,0:T(8,128)(2,1)} %refs_2_.1, ...), custom_call_target="tpu_custom_call" | custom-call | flops 1000000 | bytes 4000000 | tf_op jit(solution)/shard_map/plan/pallas_call | solution.py:485
  4.1 2.9 %collective-permute-start.40 = (bf16[7,64,128]{2,1,0:T(8,128)(2,1)S(1)}, bf16[7,64,128]{2,1,0:T(8,128)(2,1)S(1)}, u32[]{:S(2)}, u32[]{:S(2)}) collective-permute-start(bf16[7,64,128]{2,1,0:T(8,128)(2,1)S(1)} %get-tuple-element.84.refs_7_), channel_id=1, source_target_pairs={{0,4},{2,10},{8,0},{10,18},{16,8},{18,26},{24,16},{26,30},{28,24},... | collective-permute-start | bytes 344072 | tf_op jit(solution)/shard_map/ppermute | solution.py:595
  7.0 0.0 collective-permute-start.36
  7.0 2.8 %collective-permute-done.40.refs_6_ = bf16[7,64,128]{2,1,0:T(8,128)(2,1)S(1)} collective-permute-done((bf16[7,64,128]{2,1,0:T(8,128)(2,1)S(1)}, bf16[7,64,128]{2,1,0:T(8,128)(2,1)S(1)}, u32[]{:S(2)}, u32[]{:S(2)}) %collective-permute-start.40) | collective-permute-done | bytes 114720 | tf_op jit(solution)/shard_map/ppermute | solution.py:595
  9.8 2.5 %collective-permute-start.41 = (bf16[7,64,128]{2,1,0:T(8,128)(2,1)S(1)}, bf16[7,64,128]{2,1,0:T(8,128)(2,1)S(1)}, u32[]{:S(2)}, u32[]{:S(2)}) collective-permute-start(bf16[7,64,128]{2,1,0:T(8,128)(2,1)S(1)} %collective-permute-done.40.refs_6_), channel_id=1, source_target_pairs={{0,4},{2,10},{8,0},{10,18},{16,8},{18,26},{24,16},{26,30},{28,24},... | collective-permute-start | bytes 344072 | tf_op jit(solution)/shard_map/ppermute | solution.py:595
  12.3 0.0 collective-permute-done.36.refs_5_
  12.3 0.0 collective-permute-start.37
  12.3 0.0 collective-permute-start.50
  12.3 0.5 collective-permute-start.49
  12.8 3.2 %collective-permute-done.41.refs_4_ = bf16[7,64,128]{2,1,0:T(8,128)(2,1)S(1)} collective-permute-done((bf16[7,64,128]{2,1,0:T(8,128)(2,1)S(1)}, bf16[7,64,128]{2,1,0:T(8,128)(2,1)S(1)}, u32[]{:S(2)}, u32[]{:S(2)}) %collective-permute-start.41) | collective-permute-done | bytes 114720 | tf_op jit(solution)/shard_map/ppermute | solution.py:595
  16.0 1.1 %collective-permute-start.42 = (bf16[7,64,128]{2,1,0:T(8,128)(2,1)S(1)}, bf16[7,64,128]{2,1,0:T(8,128)(2,1)S(1)}, u32[]{:S(2)}, u32[]{:S(2)}) collective-permute-start(bf16[7,64,128]{2,1,0:T(8,128)(2,1)S(1)} %collective-permute-done.41.refs_4_), channel_id=1, source_target_pairs={{0,4},{2,10},{8,0},{10,18},{16,8},{18,26},{24,16},{26,30},{28,24},... | collective-permute-start | bytes 344072 | tf_op jit(solution)/shard_map/ppermute | solution.py:595
  17.1 1.1 %collective-permute-done.37.refs_3_ = bf16[7,64,128]{2,1,0:T(8,128)(2,1)S(1)} collective-permute-done((bf16[7,64,128]{2,1,0:T(8,128)(2,1)S(1)}, bf16[7,64,128]{2,1,0:T(8,128)(2,1)S(1)}, u32[]{:S(2)}, u32[]{:S(2)}) %collective-permute-start.37) | collective-permute-done | bytes 114720 | tf_op jit(solution)/shard_map/ppermute | solution.py:595
  18.2 0.0 collective-permute-start.38
  18.2 0.0 collective-permute-start.48
  18.2 0.0 collective-permute-done.50.refs_15_
  18.2 0.5 collective-permute-start.47
  18.7 0.0 collective-permute-done.49.refs_14_
  18.7 0.1 collective-permute-start.46
  18.8 2.6 %collective-permute-done.42.refs_2_ = bf16[7,64,128]{2,1,0:T(8,128)(2,1)S(1)} collective-permute-done((bf16[7,64,128]{2,1,0:T(8,128)(2,1)S(1)}, bf16[7,64,128]{2,1,0:T(8,128)(2,1)S(1)}, u32[]{:S(2)}, u32[]{:S(2)}) %collective-permute-start.42) | collective-permute-done | bytes 114720 | tf_op jit(solution)/shard_map/ppermute | solution.py:595
  21.4 0.0 collective-permute-start.45
  21.4 1.6 %collective-permute-done.38.refs_1_ = bf16[7,64,128]{2,1,0:T(8,128)(2,1)S(1)} collective-permute-done((bf16[7,64,128]{2,1,0:T(8,128)(2,1)S(1)}, bf16[7,64,128]{2,1,0:T(8,128)(2,1)S(1)}, u32[]{:S(2)}, u32[]{:S(2)}) %collective-permute-start.38) | collective-permute-done | bytes 114720 | tf_op jit(solution)/shard_map/ppermute | solution.py:595
  23.0 0.1 collective-permute-start.43
  23.1 0.0 collective-permute-done.47.refs_12_
  23.1 1.9 %collective-permute-start.39 = (bf16[7,64,128]{2,1,0:T(8,128)(2,1)S(1)}, bf16[7,64,128]{2,1,0:T(8,128)(2,1)S(1)}, u32[]{:S(2)}, u32[]{:S(2)}) collective-permute-start(bf16[7,64,128]{2,1,0:T(8,128)(2,1)S(1)} %collective-permute-done.38.refs_1_), channel_id=1, source_target_pairs={{0,8},{2,6},{8,16},{10,2},{16,24},{18,10},{24,28},{26,18},{28,20},... | collective-permute-start | bytes 344072 | tf_op jit(solution)/shard_map/ppermute | solution.py:598
  25.0 0.0 collective-permute-done.46.refs_11_
  25.0 2.2 %collective-permute-done.43.refs_8_ = bf16[7,64,128]{2,1,0:T(8,128)(2,1)S(1)} collective-permute-done((bf16[7,64,128]{2,1,0:T(8,128)(2,1)S(1)}, bf16[7,64,128]{2,1,0:T(8,128)(2,1)S(1)}, u32[]{:S(2)}, u32[]{:S(2)}) %collective-permute-start.43) | collective-permute-done | bytes 114720 | tf_op jit(solution)/shard_map/ppermute | solution.py:599
  27.2 1.9 %collective-permute-done.39.refs_0_ = bf16[7,64,128]{2,1,0:T(8,128)(2,1)S(1)} collective-permute-done((bf16[7,64,128]{2,1,0:T(8,128)(2,1)S(1)}, bf16[7,64,128]{2,1,0:T(8,128)(2,1)S(1)}, u32[]{:S(2)}, u32[]{:S(2)}) %collective-permute-start.39) | collective-permute-done | bytes 114720 | tf_op jit(solution)/shard_map/ppermute | solution.py:598
  29.1 5.9 %compute.3 = (bf16[56,64,128]{2,1,0:T(8,128)(2,1)S(1)}, bf16[14,64,128]{2,1,0:T(8,128)(2,1)S(1)}, bf16[42,64,128]{2,1,0:T(8,128)(2,1)S(1)}, bf16[18,128,128]{2,1,0:T(8,128)(2,1)S(1)}, bf16[18,128,128]{2,1,0:T(8,128)(2,1)S(1)}) custom-call(s32[32,128]{1,0:T(8,128)S(1)} %get-tuple-element.82.plan, bf16[128,8192]{1,0:T(8,128)(2,1)} %tokens.1, ...), custom_call_target="tpu_custom_call" | custom-call | flops 1000000000 | bytes 20000000 | tf_op jit(solution)/shard_map/compute/pallas_call | solution.py:541
  35.0 0.1 collective-permute-start.52
  35.1 1.5 %collective-permute-done.52.__1_ = bf16[14,64,128]{2,1,0:T(8,128)(2,1)S(1)} collective-permute-done((bf16[14,64,128]{2,1,0:T(8,128)(2,1)S(1)}, bf16[14,64,128]{2,1,0:T(8,128)(2,1)S(1)}, u32[]{:S(2)}, u32[]{:S(2)}) %collective-permute-start.52) | collective-permute-done | bytes 229408 | tf_op jit(solution)/shard_map/ppermute | solution.py:606
  36.6 0.1 collective-permute-start.53
  36.7 0.1 add_convert_fusion.13
  36.8 0.7 %collective-permute-start.54 = (bf16[7,64,128]{2,1,0:T(8,128)(2,1)S(1)}, bf16[7,64,128]{2,1,0:T(8,128)(2,1)S(1)}, u32[]{:S(2)}, u32[]{:S(2)}) collective-permute-start(bf16[7,64,128]{2,1,0:T(8,128)(2,1)S(1)} %get-tuple-element.89), channel_id=1, source_target_pairs={{0,8},{2,6},{8,16},{10,2},{16,24},{18,10},{24,28},{26,18},{28,20},... | collective-permute-start | bytes 344072 | tf_op jit(solution)/shard_map/ppermute | solution.py:621
  37.5 1.4 %collective-permute-start.55 = (bf16[7,64,128]{2,1,0:T(8,128)(2,1)S(1)}, bf16[7,64,128]{2,1,0:T(8,128)(2,1)S(1)}, u32[]{:S(2)}, u32[]{:S(2)}) collective-permute-start(bf16[7,64,128]{2,1,0:T(8,128)(2,1)S(1)} %get-tuple-element.90), channel_id=1, source_target_pairs={{0,4},{2,10},{8,0},{10,18},{16,8},{18,26},{24,16},{26,30},{28,24},... | collective-permute-start | bytes 344072 | tf_op jit(solution)/shard_map/ppermute | solution.py:621
  38.9 0.4 collective-permute-start.35
  39.2 2.8 %collective-permute-done.54 = bf16[7,64,128]{2,1,0:T(8,128)(2,1)S(1)} collective-permute-done((bf16[7,64,128]{2,1,0:T(8,128)(2,1)S(1)}, bf16[7,64,128]{2,1,0:T(8,128)(2,1)S(1)}, u32[]{:S(2)}, u32[]{:S(2)}) %collective-permute-start.54) | collective-permute-done | bytes 114720 | tf_op jit(solution)/shard_map/ppermute | solution.py:621
  42.1 0.2 collective-permute-done.55
  42.3 0.1 add_convert_fusion.11
  42.4 0.0 collective-permute-done.35.__2_.note.refs_0_
  42.4 1.8 %collective-permute-start.56 = (bf16[7,64,128]{2,1,0:T(8,128)(2,1)S(1)}, bf16[7,64,128]{2,1,0:T(8,128)(2,1)S(1)}, u32[]{:S(2)}, u32[]{:S(2)}) collective-permute-start(bf16[7,64,128]{2,1,0:T(8,128)(2,1)S(1)} %get-tuple-element.93), channel_id=1, source_target_pairs={{0,8},{2,6},{8,16},{10,2},{16,24},{18,10},{24,28},{26,18},{28,20},... | collective-permute-start | bytes 344072 | tf_op jit(solution)/shard_map/ppermute | solution.py:621
  44.2 0.2 collective-permute-start.57
  44.5 0.4 collective-permute-start.51
  44.8 2.8 %collective-permute-done.56 = bf16[7,64,128]{2,1,0:T(8,128)(2,1)S(1)} collective-permute-done((bf16[7,64,128]{2,1,0:T(8,128)(2,1)S(1)}, bf16[7,64,128]{2,1,0:T(8,128)(2,1)S(1)}, u32[]{:S(2)}, u32[]{:S(2)}) %collective-permute-start.56) | collective-permute-done | bytes 114720 | tf_op jit(solution)/shard_map/ppermute | solution.py:621
  47.7 1.4 %collective-permute-done.57 = bf16[7,64,128]{2,1,0:T(8,128)(2,1)S(1)} collective-permute-done((bf16[7,64,128]{2,1,0:T(8,128)(2,1)S(1)}, bf16[7,64,128]{2,1,0:T(8,128)(2,1)S(1)}, u32[]{:S(2)}, u32[]{:S(2)}) %collective-permute-start.57) | collective-permute-done | bytes 114720 | tf_op jit(solution)/shard_map/ppermute | solution.py:621
  49.0 0.1 add_convert_fusion.9
  49.1 2.1 %collective-permute-start.58 = (bf16[7,64,128]{2,1,0:T(8,128)(2,1)S(1)}, bf16[7,64,128]{2,1,0:T(8,128)(2,1)S(1)}, u32[]{:S(2)}, u32[]{:S(2)}) collective-permute-start(bf16[7,64,128]{2,1,0:T(8,128)(2,1)S(1)} %get-tuple-element.95), channel_id=1, source_target_pairs={{0,8},{2,6},{8,16},{10,2},{16,24},{18,10},{24,28},{26,18},{28,20},... | collective-permute-start | bytes 344072 | tf_op jit(solution)/shard_map/ppermute | solution.py:621
  51.2 4.0 %collective-permute-done.58 = bf16[7,64,128]{2,1,0:T(8,128)(2,1)S(1)} collective-permute-done((bf16[7,64,128]{2,1,0:T(8,128)(2,1)S(1)}, bf16[7,64,128]{2,1,0:T(8,128)(2,1)S(1)}, u32[]{:S(2)}, u32[]{:S(2)}) %collective-permute-start.58) | collective-permute-done | bytes 114720 | tf_op jit(solution)/shard_map/ppermute | solution.py:621
  55.2 0.1 add_convert_fusion.8
  55.3 0.1 collective-permute-start.62
  55.4 0.9 %collective-permute-start.59 = (bf16[7,64,128]{2,1,0:T(8,128)(2,1)S(1)}, bf16[7,64,128]{2,1,0:T(8,128)(2,1)S(1)}, u32[]{:S(2)}, u32[]{:S(2)}) collective-permute-start(bf16[7,64,128]{2,1,0:T(8,128)(2,1)S(1)} %get-tuple-element.125), channel_id=1, source_target_pairs={{0,8},{2,6},{8,16},{10,2},{16,24},{18,10},{24,28},{26,18},{28,20},... | collective-permute-start | bytes 344072 | tf_op jit(solution)/shard_map/ppermute | solution.py:626
  56.2 0.9 %collective-permute-start.61 = (bf16[7,64,128]{2,1,0:T(8,128)(2,1)S(1)}, bf16[7,64,128]{2,1,0:T(8,128)(2,1)S(1)}, u32[]{:S(2)}, u32[]{:S(2)}) collective-permute-start(bf16[7,64,128]{2,1,0:T(8,128)(2,1)S(1)} %get-tuple-element.126.refs_2_), channel_id=1, source_target_pairs={{0,2},{2,0},{8,10},{10,8},{16,18},{18,16},{24,26},{26,24},{28,30},... | collective-permute-start | bytes 344072 | tf_op jit(solution)/shard_map/ppermute | solution.py:628
  57.1 0.0 collective-permute-start.63
  57.1 2.5 %prepare.3 = (bf16[128,4096]{1,0:T(8,128)(2,1)}, bf16[128,4096]{1,0:T(8,128)(2,1)}, bf16[18,128,128]{2,1,0:T(8,128)(2,1)S(1)}) custom-call(s32[32,128]{1,0:T(8,128)S(1)} %get-tuple-element.82.plan, s32[1,128]{1,0:T(1,128)S(1)} %collective-permute-done.35.__2_.note.refs_0_, bf16[18,128,128]{2,1,0:T(8,128)(2,1)S(1)} %get-tuple-element.97.first), custom_call_target="tpu_custom_call" | custom-call | flops 1000000 | bytes 6000000 | tf_op jit(solution)/shard_map/prepare/pallas_call | solution.py:558
  59.7 0.5 collective-permute-done.59.refs_3_
  60.2 0.0 copy-start.1
  60.2 0.0 copy-start.2
  60.2 2.5 %last.3 = (bf16[128,4096]{1,0:T(8,128)(2,1)}, bf16[128,4096]{1,0:T(8,128)(2,1)}, bf16[1,2,128,128]{3,2,1,0:T(8,128)(2,1)}, bf16[1,2,128,128]{3,2,1,0:T(8,128)(2,...) custom-call(s32[32,128]{1,0:T(8,128)S(1)} %get-tuple-element.82.plan, ...), custom_call_target="tpu_custom_call", output_to_operand_aliasing={{0}: (10, {}), {1}: (11, {})} | custom-call | flops 1000000 | bytes 3000000 | tf_op jit(solution)/shard_map/last/pallas_call | solution.py:572
  (19 shorter events, 0.1 us)
Async XLA Ops:
  0.6 1.8 %collective-permute-start.32 = (bf16[1,2,128,128]{3,2,1,0:T(8,128)(2,1)}, bf16[1,2,128,128]{3,2,1,0:T(8,128)(2,1)S(1)}, u32[]{:S(2)}, u32[]{:S(2)}) collective-permute-start(bf16[1,2,128,128]{3,2,1,0:T(8,128)(2,1)} %refs_0_.1), channel_id=1, source_target_pairs={{0,2},{2,0},{8,10},{10,8},{16,18},{18,16},{24,26},{26,24},{28,30},... | collective-permute-start | bytes 196616 | tf_op jit(solution)/shard_map/ppermute | solution.py:638
  1.2 1.5 %collective-permute-start.33 = (bf16[1,2,128,128]{3,2,1,0:T(8,128)(2,1)}, bf16[1,2,128,128]{3,2,1,0:T(8,128)(2,1)S(1)}, u32[]{:S(2)}, u32[]{:S(2)}) collective-permute-start(bf16[1,2,128,128]{3,2,1,0:T(8,128)(2,1)} %refs_1_.1), channel_id=1, source_target_pairs={{0,2},{2,0},{8,10},{10,8},{16,18},{18,16},{24,26},{26,24},{28,30},... | collective-permute-start | bytes 196616 | tf_op jit(solution)/shard_map/ppermute | solution.py:638
  1.2 1.5 %collective-permute-start.34 = (bf16[1,2,128,128]{3,2,1,0:T(8,128)(2,1)}, bf16[1,2,128,128]{3,2,1,0:T(8,128)(2,1)S(1)}, u32[]{:S(2)}, u32[]{:S(2)}) collective-permute-start(bf16[1,2,128,128]{3,2,1,0:T(8,128)(2,1)} %refs_2_.1), channel_id=1, source_target_pairs={{0,2},{2,0},{8,10},{10,8},{16,18},{18,16},{24,26},{26,24},{28,30},... | collective-permute-start | bytes 196616 | tf_op jit(solution)/shard_map/ppermute | solution.py:638
  4.1 5.7 %collective-permute-start.40 = (bf16[7,64,128]{2,1,0:T(8,128)(2,1)S(1)}, bf16[7,64,128]{2,1,0:T(8,128)(2,1)S(1)}, u32[]{:S(2)}, u32[]{:S(2)}) collective-permute-start(bf16[7,64,128]{2,1,0:T(8,128)(2,1)S(1)} %get-tuple-element.84.refs_7_), channel_id=1, source_target_pairs={{0,4},{2,10},{8,0},{10,18},{16,8},{18,26},{24,16},{26,30},{28,24},... | collective-permute-start | bytes 344072 | tf_op jit(solution)/shard_map/ppermute | solution.py:595
  7.0 5.3 %collective-permute-start.36 = (bf16[7,64,128]{2,1,0:T(8,128)(2,1)S(1)}, bf16[7,64,128]{2,1,0:T(8,128)(2,1)S(1)}, u32[]{:S(2)}, u32[]{:S(2)}) collective-permute-start(bf16[7,64,128]{2,1,0:T(8,128)(2,1)S(1)} %get-tuple-element.84.refs_7_), channel_id=1, source_target_pairs={{0,8},{2,6},{8,16},{10,2},{16,24},{18,10},{24,28},{26,18},{28,20},... | collective-permute-start | bytes 344072 | tf_op jit(solution)/shard_map/ppermute | solution.py:595
  9.8 6.2 %collective-permute-start.41 = (bf16[7,64,128]{2,1,0:T(8,128)(2,1)S(1)}, bf16[7,64,128]{2,1,0:T(8,128)(2,1)S(1)}, u32[]{:S(2)}, u32[]{:S(2)}) collective-permute-start(bf16[7,64,128]{2,1,0:T(8,128)(2,1)S(1)} %collective-permute-done.40.refs_6_), channel_id=1, source_target_pairs={{0,4},{2,10},{8,0},{10,18},{16,8},{18,26},{24,16},{26,30},{28,24},... | collective-permute-start | bytes 344072 | tf_op jit(solution)/shard_map/ppermute | solution.py:595
  12.3 5.9 %collective-permute-start.37 = (bf16[7,64,128]{2,1,0:T(8,128)(2,1)S(1)}, bf16[7,64,128]{2,1,0:T(8,128)(2,1)S(1)}, u32[]{:S(2)}, u32[]{:S(2)}) collective-permute-start(bf16[7,64,128]{2,1,0:T(8,128)(2,1)S(1)} %collective-permute-done.36.refs_5_), channel_id=1, source_target_pairs={{0,8},{2,6},{8,16},{10,2},{16,24},{18,10},{24,28},{26,18},{28,20},... | collective-permute-start | bytes 344072 | tf_op jit(solution)/shard_map/ppermute | solution.py:595
  12.3 5.9 %collective-permute-start.50 = (bf16[7,64,128]{2,1,0:T(8,128)(2,1)S(1)}, bf16[7,64,128]{2,1,0:T(8,128)(2,1)S(1)}, u32[]{:S(2)}, u32[]{:S(2)}) collective-permute-start(bf16[7,64,128]{2,1,0:T(8,128)(2,1)S(1)} %get-tuple-element.84.refs_7_), channel_id=1, source_target_pairs={{0,2},{2,0},{8,10},{10,8},{16,18},{18,16},{24,26},{26,24},{28,30},... | collective-permute-start | bytes 344072 | tf_op jit(solution)/shard_map/ppermute | solution.py:597
  12.3 6.4 %collective-permute-start.49 = (bf16[7,64,128]{2,1,0:T(8,128)(2,1)S(1)}, bf16[7,64,128]{2,1,0:T(8,128)(2,1)S(1)}, u32[]{:S(2)}, u32[]{:S(2)}) collective-permute-start(bf16[7,64,128]{2,1,0:T(8,128)(2,1)S(1)} %collective-permute-done.40.refs_6_), channel_id=1, source_target_pairs={{0,2},{2,0},{8,10},{10,8},{16,18},{18,16},{24,26},{26,24},{28,30},... | collective-permute-start | bytes 344072 | tf_op jit(solution)/shard_map/ppermute | solution.py:597
  16.0 5.4 %collective-permute-start.42 = (bf16[7,64,128]{2,1,0:T(8,128)(2,1)S(1)}, bf16[7,64,128]{2,1,0:T(8,128)(2,1)S(1)}, u32[]{:S(2)}, u32[]{:S(2)}) collective-permute-start(bf16[7,64,128]{2,1,0:T(8,128)(2,1)S(1)} %collective-permute-done.41.refs_4_), channel_id=1, source_target_pairs={{0,4},{2,10},{8,0},{10,18},{16,8},{18,26},{24,16},{26,30},{28,24},... | collective-permute-start | bytes 344072 | tf_op jit(solution)/shard_map/ppermute | solution.py:595
  18.2 4.8 %collective-permute-start.38 = (bf16[7,64,128]{2,1,0:T(8,128)(2,1)S(1)}, bf16[7,64,128]{2,1,0:T(8,128)(2,1)S(1)}, u32[]{:S(2)}, u32[]{:S(2)}) collective-permute-start(bf16[7,64,128]{2,1,0:T(8,128)(2,1)S(1)} %collective-permute-done.37.refs_3_), channel_id=1, source_target_pairs={{0,8},{2,6},{8,16},{10,2},{16,24},{18,10},{24,28},{26,18},{28,20},... | collective-permute-start | bytes 344072 | tf_op jit(solution)/shard_map/ppermute | solution.py:595
  18.2 4.8 %collective-permute-start.48 = (bf16[7,64,128]{2,1,0:T(8,128)(2,1)S(1)}, bf16[7,64,128]{2,1,0:T(8,128)(2,1)S(1)}, u32[]{:S(2)}, u32[]{:S(2)}) collective-permute-start(bf16[7,64,128]{2,1,0:T(8,128)(2,1)S(1)} %collective-permute-done.36.refs_5_), channel_id=1, source_target_pairs={{0,2},{2,0},{8,10},{10,8},{16,18},{18,16},{24,26},{26,24},{28,30},... | collective-permute-start | bytes 344072 | tf_op jit(solution)/shard_map/ppermute | solution.py:597
  18.2 4.9 %collective-permute-start.47 = (bf16[7,64,128]{2,1,0:T(8,128)(2,1)S(1)}, bf16[7,64,128]{2,1,0:T(8,128)(2,1)S(1)}, u32[]{:S(2)}, u32[]{:S(2)}) collective-permute-start(bf16[7,64,128]{2,1,0:T(8,128)(2,1)S(1)} %collective-permute-done.41.refs_4_), channel_id=1, source_target_pairs={{0,2},{2,0},{8,10},{10,8},{16,18},{18,16},{24,26},{26,24},{28,30},... | collective-permute-start | bytes 344072 | tf_op jit(solution)/shard_map/ppermute | solution.py:597
  18.7 6.3 %collective-permute-start.46 = (bf16[7,64,128]{2,1,0:T(8,128)(2,1)S(1)}, bf16[7,64,128]{2,1,0:T(8,128)(2,1)S(1)}, u32[]{:S(2)}, u32[]{:S(2)}) collective-permute-start(bf16[7,64,128]{2,1,0:T(8,128)(2,1)S(1)} %collective-permute-done.37.refs_3_), channel_id=1, source_target_pairs={{0,2},{2,0},{8,10},{10,8},{16,18},{18,16},{24,26},{26,24},{28,30},... | collective-permute-start | bytes 344072 | tf_op jit(solution)/shard_map/ppermute | solution.py:597
  21.4 3.6 %collective-permute-start.45 = (bf16[7,64,128]{2,1,0:T(8,128)(2,1)S(1)}, bf16[7,64,128]{2,1,0:T(8,128)(2,1)S(1)}, u32[]{:S(2)}, u32[]{:S(2)}) collective-permute-start(bf16[7,64,128]{2,1,0:T(8,128)(2,1)S(1)} %collective-permute-done.42.refs_2_), channel_id=1, source_target_pairs={{0,2},{2,0},{8,10},{10,8},{16,18},{18,16},{24,26},{26,24},{28,30},... | collective-permute-start | bytes 344072 | tf_op jit(solution)/shard_map/ppermute | solution.py:597
  23.0 2.0 %collective-permute-start.44 = (bf16[7,64,128]{2,1,0:T(8,128)(2,1)S(1)}, bf16[7,64,128]{2,1,0:T(8,128)(2,1)S(1)}, u32[]{:S(2)}, u32[]{:S(2)}) collective-permute-start(bf16[7,64,128]{2,1,0:T(8,128)(2,1)S(1)} %collective-permute-done.38.refs_1_), channel_id=1, source_target_pairs={{0,2},{2,0},{8,10},{10,8},{16,18},{18,16},{24,26},{26,24},{28,30},... | collective-permute-start | bytes 344072 | tf_op jit(solution)/shard_map/ppermute | solution.py:597
  23.0 4.2 %collective-permute-start.43 = (bf16[7,64,128]{2,1,0:T(8,128)(2,1)S(1)}, bf16[7,64,128]{2,1,0:T(8,128)(2,1)S(1)}, u32[]{:S(2)}, u32[]{:S(2)}) collective-permute-start(bf16[7,64,128]{2,1,0:T(8,128)(2,1)S(1)} %collective-permute-done.38.refs_1_), channel_id=1, source_target_pairs={{0,10},{2,4},{8,18},{10,0},{16,26},{18,8},{24,30},{26,16},{28,22},... | collective-permute-start | bytes 344072 | tf_op jit(solution)/shard_map/ppermute | solution.py:599
  23.1 6.0 %collective-permute-start.39 = (bf16[7,64,128]{2,1,0:T(8,128)(2,1)S(1)}, bf16[7,64,128]{2,1,0:T(8,128)(2,1)S(1)}, u32[]{:S(2)}, u32[]{:S(2)}) collective-permute-start(bf16[7,64,128]{2,1,0:T(8,128)(2,1)S(1)} %collective-permute-done.38.refs_1_), channel_id=1, source_target_pairs={{0,8},{2,6},{8,16},{10,2},{16,24},{18,10},{24,28},{26,18},{28,20},... | collective-permute-start | bytes 344072 | tf_op jit(solution)/shard_map/ppermute | solution.py:598
  35.0 1.6 %collective-permute-start.52 = (bf16[14,64,128]{2,1,0:T(8,128)(2,1)S(1)}, bf16[14,64,128]{2,1,0:T(8,128)(2,1)S(1)}, u32[]{:S(2)}, u32[]{:S(2)}) collective-permute-start(bf16[14,64,128]{2,1,0:T(8,128)(2,1)S(1)} %get-tuple-element.88), channel_id=1, source_target_pairs={{0,2},{2,0},{8,10},{10,8},{16,18},{18,16},{24,26},{26,24},{28,30},... | collective-permute-start | bytes 688136 | tf_op jit(solution)/shard_map/ppermute | solution.py:606
  36.6 5.7 %collective-permute-start.53 = (bf16[42,64,128]{2,1,0:T(8,128)(2,1)S(1)}, bf16[42,64,128]{2,1,0:T(8,128)(2,1)S(1)}, u32[]{:S(2)}, u32[]{:S(2)}) collective-permute-start(bf16[42,64,128]{2,1,0:T(8,128)(2,1)S(1)} %turn.6), channel_id=1, source_target_pairs={{0,2},{2,0},{8,10},{10,8},{16,18},{18,16},{24,26},{26,24},{28,30},... | collective-permute-start | bytes 2064392 | tf_op jit(solution)/shard_map/ppermute | solution.py:607
  36.8 5.3 %collective-permute-start.54 = (bf16[7,64,128]{2,1,0:T(8,128)(2,1)S(1)}, bf16[7,64,128]{2,1,0:T(8,128)(2,1)S(1)}, u32[]{:S(2)}, u32[]{:S(2)}) collective-permute-start(bf16[7,64,128]{2,1,0:T(8,128)(2,1)S(1)} %get-tuple-element.89), channel_id=1, source_target_pairs={{0,8},{2,6},{8,16},{10,2},{16,24},{18,10},{24,28},{26,18},{28,20},... | collective-permute-start | bytes 344072 | tf_op jit(solution)/shard_map/ppermute | solution.py:621
  37.5 4.8 %collective-permute-start.55 = (bf16[7,64,128]{2,1,0:T(8,128)(2,1)S(1)}, bf16[7,64,128]{2,1,0:T(8,128)(2,1)S(1)}, u32[]{:S(2)}, u32[]{:S(2)}) collective-permute-start(bf16[7,64,128]{2,1,0:T(8,128)(2,1)S(1)} %get-tuple-element.90), channel_id=1, source_target_pairs={{0,4},{2,10},{8,0},{10,18},{16,8},{18,26},{24,16},{26,30},{28,24},... | collective-permute-start | bytes 344072 | tf_op jit(solution)/shard_map/ppermute | solution.py:621
  38.9 3.5 %collective-permute-start.35 = (s32[1,128]{1,0:T(1,128)S(1)}, s32[1,128]{1,0:T(1,128)S(1)}, u32[]{:S(2)}, u32[]{:S(2)}) collective-permute-start(s32[1,128]{1,0:T(1,128)S(1)} %get-tuple-element.83), channel_id=1, source_target_pairs={{0,1},{1,0},{2,3},{3,2},{4,5},{5,4},{6,7},{7,6},{8,9},{9,8},{10,11... | collective-permute-start | bytes 1544 | tf_op jit(solution)/shard_map/ppermute | solution.py:642
  42.4 5.3 %collective-permute-start.56 = (bf16[7,64,128]{2,1,0:T(8,128)(2,1)S(1)}, bf16[7,64,128]{2,1,0:T(8,128)(2,1)S(1)}, u32[]{:S(2)}, u32[]{:S(2)}) collective-permute-start(bf16[7,64,128]{2,1,0:T(8,128)(2,1)S(1)} %get-tuple-element.93), channel_id=1, source_target_pairs={{0,8},{2,6},{8,16},{10,2},{16,24},{18,10},{24,28},{26,18},{28,20},... | collective-permute-start | bytes 344072 | tf_op jit(solution)/shard_map/ppermute | solution.py:621
  44.2 4.8 %collective-permute-start.57 = (bf16[7,64,128]{2,1,0:T(8,128)(2,1)S(1)}, bf16[7,64,128]{2,1,0:T(8,128)(2,1)S(1)}, u32[]{:S(2)}, u32[]{:S(2)}) collective-permute-start(bf16[7,64,128]{2,1,0:T(8,128)(2,1)S(1)} %get-tuple-element.94), channel_id=1, source_target_pairs={{0,4},{2,10},{8,0},{10,18},{16,8},{18,26},{24,16},{26,30},{28,24},... | collective-permute-start | bytes 344072 | tf_op jit(solution)/shard_map/ppermute | solution.py:621
  44.5 15.2 %collective-permute-start.51 = (bf16[18,128,128]{2,1,0:T(8,128)(2,1)S(1)}, bf16[18,128,128]{2,1,0:T(8,128)(2,1)S(1)}, u32[]{:S(2)}, u32[]{:S(2)}) collective-permute-start(bf16[18,128,128]{2,1,0:T(8,128)(2,1)S(1)} %get-tuple-element.85), channel_id=1, source_target_pairs={{0,1},{1,0},{2,3},{3,2},{4,5},{5,4},{6,7},{7,6},{8,9},{9,8},{10,11... | collective-permute-start | bytes 1769480 | tf_op jit(solution)/shard_map/ppermute | solution.py:642
  49.1 6.0 %collective-permute-start.58 = (bf16[7,64,128]{2,1,0:T(8,128)(2,1)S(1)}, bf16[7,64,128]{2,1,0:T(8,128)(2,1)S(1)}, u32[]{:S(2)}, u32[]{:S(2)}) collective-permute-start(bf16[7,64,128]{2,1,0:T(8,128)(2,1)S(1)} %get-tuple-element.95), channel_id=1, source_target_pairs={{0,8},{2,6},{8,16},{10,2},{16,24},{18,10},{24,28},{26,18},{28,20},... | collective-permute-start | bytes 344072 | tf_op jit(solution)/shard_map/ppermute | solution.py:621
  51.2 5.9 %collective-permute-start.60 = (bf16[7,64,128]{2,1,0:T(8,128)(2,1)S(1)}, bf16[7,64,128]{2,1,0:T(8,128)(2,1)S(1)}, u32[]{:S(2)}, u32[]{:S(2)}) collective-permute-start(bf16[7,64,128]{2,1,0:T(8,128)(2,1)S(1)} %get-tuple-element.96), channel_id=1, source_target_pairs={{0,4},{2,10},{8,0},{10,18},{16,8},{18,26},{24,16},{26,30},{28,24},... | collective-permute-start | bytes 344072 | tf_op jit(solution)/shard_map/ppermute | solution.py:621
  55.3 4.4 %collective-permute-start.62 = (bf16[7,64,128]{2,1,0:T(8,128)(2,1)S(1)}, bf16[7,64,128]{2,1,0:T(8,128)(2,1)S(1)}, u32[]{:S(2)}, u32[]{:S(2)}) collective-permute-start(bf16[7,64,128]{2,1,0:T(8,128)(2,1)S(1)} %get-tuple-element.125), channel_id=1, source_target_pairs={{0,10},{2,4},{8,18},{10,0},{16,26},{18,8},{24,30},{26,16},{28,22},... | collective-permute-start | bytes 344072 | tf_op jit(solution)/shard_map/ppermute | solution.py:629
  55.4 4.8 %collective-permute-start.59 = (bf16[7,64,128]{2,1,0:T(8,128)(2,1)S(1)}, bf16[7,64,128]{2,1,0:T(8,128)(2,1)S(1)}, u32[]{:S(2)}, u32[]{:S(2)}) collective-permute-start(bf16[7,64,128]{2,1,0:T(8,128)(2,1)S(1)} %get-tuple-element.125), channel_id=1, source_target_pairs={{0,8},{2,6},{8,16},{10,2},{16,24},{18,10},{24,28},{26,18},{28,20},... | collective-permute-start | bytes 344072 | tf_op jit(solution)/shard_map/ppermute | solution.py:626
  56.2 4.0 %collective-permute-start.61 = (bf16[7,64,128]{2,1,0:T(8,128)(2,1)S(1)}, bf16[7,64,128]{2,1,0:T(8,128)(2,1)S(1)}, u32[]{:S(2)}, u32[]{:S(2)}) collective-permute-start(bf16[7,64,128]{2,1,0:T(8,128)(2,1)S(1)} %get-tuple-element.126.refs_2_), channel_id=1, source_target_pairs={{0,2},{2,0},{8,10},{10,8},{16,18},{18,16},{24,26},{26,24},{28,30},... | collective-permute-start | bytes 344072 | tf_op jit(solution)/shard_map/ppermute | solution.py:628
  57.1 3.1 %collective-permute-start.63 = (bf16[7,64,128]{2,1,0:T(8,128)(2,1)S(1)}, bf16[7,64,128]{2,1,0:T(8,128)(2,1)S(1)}, u32[]{:S(2)}, u32[]{:S(2)}) collective-permute-start(bf16[7,64,128]{2,1,0:T(8,128)(2,1)S(1)} %collective-permute-done.60.refs_4_), channel_id=1, source_target_pairs={{0,2},{2,0},{8,10},{10,8},{16,18},{18,16},{24,26},{26,24},{28,30},... | collective-permute-start | bytes 344072 | tf_op jit(solution)/shard_map/ppermute | solution.py:630
  60.2 3.2 %copy-start = (bf16[1,2,128,128]{3,2,1,0:T(8,128)(2,1)S(1)}, bf16[1,2,128,128]{3,2,1,0:T(8,128)(2,1)}, u32[]{:S(2)}) copy-start(bf16[1,2,128,128]{3,2,1,0:T(8,128)(2,1)} %refs_0_.1) | copy-start | bytes 196612
  60.2 3.2 %copy-start.1 = (bf16[1,2,128,128]{3,2,1,0:T(8,128)(2,1)S(1)}, bf16[1,2,128,128]{3,2,1,0:T(8,128)(2,1)}, u32[]{:S(2)}) copy-start(bf16[1,2,128,128]{3,2,1,0:T(8,128)(2,1)} %refs_1_.1) | copy-start | bytes 196612
  60.2 3.2 %copy-start.2 = (bf16[1,2,128,128]{3,2,1,0:T(8,128)(2,1)S(1)}, bf16[1,2,128,128]{3,2,1,0:T(8,128)(2,1)}, u32[]{:S(2)}) copy-start(bf16[1,2,128,128]{3,2,1,0:T(8,128)(2,1)} %refs_2_.1) | copy-start | bytes 196612

commit v2 on v1

--- a/solution.py
+++ b/solution.py
@@ -616,18 +616,25 @@
 
     a, b = lax.optimization_barrier((term(sz.top), term(sz.top + 1)))
     for s in range(1, sz.top):
-        if s == 2:
+        last_b = b
+        a, b = lax.ppermute(a, "fsdp", ahead), lax.ppermute(b, "fsdp", behind)
+        if s == 1:
             a, b = call_turn([a, b], notes)
-        a, b = lax.ppermute(a, "fsdp", ahead), lax.ppermute(b, "fsdp", behind)
+        else:
+            a = call_turn([a], [last_b])[0]
         a = term(sz.top - s, a)
         if s + 1 < sz.top:
-            a, b = lax.optimization_barrier((a, term(sz.top + 1 + s, b)))
+            b = term(sz.top + 1 + s, call_turn([b], [a])[0])
     here = term(0)
+
+    def across(pairs):
+        return [(i, j ^ 1) for i, j in pairs]
+
     mine = [here, lax.ppermute(a, "fsdp", ahead), b]
     theirs = [
         lax.ppermute(here, "fsdp", swap),
-        lax.ppermute(a, "fsdp", [(i, j ^ 1) for i, j in ahead]),
-        lax.ppermute(b, "fsdp", swap),
+        lax.ppermute(a, "fsdp", across(ahead)),
+        lax.ppermute(last_b, "fsdp", across(behind)),
     ]
     return mine + theirs
 

time: 63.5 us -> 63.6 us (level)
  waiting for transfers between devices: 29 us -> 22.9 us
  starting transfers between devices: 19.6 us -> 25.6 us
    ppermute x6, waiting for transfers between devices: 11.2 us -> 3.76 us  [reduce_parts(): a, b = (lax.ppermute(a, 'fsdp', ahead), lax.ppermute(b, 'fsdp', behind))]
    ppermute x6, starting transfers between devices: 6.23 us -> 8.05 us  [reduce_parts(): a, b = (lax.ppermute(a, 'fsdp', ahead), lax.ppermute(b, 'fsdp', behind))]
    ppermute x2, waiting for transfers between devices: 0.02 us -> 1.53 us  [exchange(): return lax.ppermute(array, 'tensor', [(i, (i + s) % T) for i in range(T)])]
    ppermute x2, starting transfers between devices: 0.72 us -> 2.03 us  [exchange(): return lax.ppermute(array, 'tensor', [(i, (i + s) % T) for i in range(T)])]
    ppermute x1, starting transfers between devices: 0.9 us -> 2.16 us  [reduce_parts(): lax.ppermute(here, 'fsdp', swap)]
    ppermute x2, starting transfers between devices: 0.07 us -> 1.11 us  [the longest x1 1.04 us: reduce_parts(): lax.ppermute(a, 'fsdp', across(ahead))]
    ppermute x1, starting transfers between devices: 0.87 us -> 1.72 us  [reduce_parts(): mine = [here, lax.ppermute(a, 'fsdp', ahead), b]]
  transfers between devices with their start and end apart: 32 -> 32, of which waited for: 16 -> 13; matrix products, arithmetic and copies ran while one was open for 2% -> 2% of each run, Pallas kernels for 4% -> 4%
where the time goes in v2:
time: 63.6 us; the launch traced here: 63.5 us
  starting transfers between devices  25.6 us (40%)
  waiting for transfers between devices  22.9 us (36%)
  Pallas kernels  12.4 us (19%)
  between operations  1.38 us (2%)
  local copies, waits for them, and re-layouts  0.8 us (1%)
    ppermute x6, waiting for transfers between devices, gather_chunks(): a, b = (lax.ppermute(a, 'fsdp', ahead), lax.ppermute(b, 'fsdp', behind))  11.4 us
    ppermute x6, starting transfers between devices, reduce_parts(): a, b = (lax.ppermute(a, 'fsdp', ahead), lax.ppermute(b, 'fsdp', behind))  8.05 us
    ppermute x6, starting transfers between devices, gather_chunks(): a, b = (lax.ppermute(a, 'fsdp', ahead), lax.ppermute(b, 'fsdp', behind))  6.42 us
    pallas_call x1, Pallas kernels, call_compute(): pl.pallas_call(functools.partial(compute_kernel, sz), out_shape=out_shape...  6.16 us
    ppermute x6, waiting for transfers between devices, reduce_parts(): a, b = (lax.ppermute(a, 'fsdp', ahead), lax.ppermute(b, 'fsdp', behind))  3.76 us
    pallas_call x1, Pallas kernels, call_prepare(): pl.pallas_call(functools.partial(prepare_kernel, sz), out_shape=[half, ha...  2.51 us
    pallas_call x1, Pallas kernels, call_last(): pl.pallas_call(functools.partial(last_kernel, sz), out_shape=[jax.ShapeDt...  2.45 us
    ppermute x1, waiting for transfers between devices, gather_chunks(): other[sz.top] = lax.ppermute(a, 'fsdp', [(i, j ^ 1) for i, j in ahead])  2.36 us
  transfers between devices with their start and end apart: 32, of which 13 were waited for; matrix products, arithmetic and copies ran while one was open for 2% of the time, Pallas kernels for 4%

profile of v2, /device:TPU:0, one launch (start us, length us, event | category | flops | bytes accessed | tf_op | source)
XLA Modules:
  0.0 63.5 jit_solution(18008276427475831390)
XLA Ops:
  0.6 0.5 collective-permute-start.32
  1.2 0.1 collective-permute-start.33
  1.2 0.4 collective-permute-start.34
  1.7 0.8 %concatenate.3 = s32[101]{0:T(128)S(1)} concatenate(s32[32]{0:T(128)} %bitcast.9, s32[32]{0:T(128)} %bitcast.10, s32[32]{0:T(128)} %bitcast.11, s32[3]{0:T(128)} %bitcast.12, s32[1]{0:T(128)} %bitcast.4, s32[1]{0:T(128)} %bitcast.5), dimensions={0} | concatenate | bytes 808 | tf_op jit(solution)/shard_map/concatenate | solution.py:676
  2.4 0.0 collective-permute-done.32.refs_3_
  2.5 0.2 collective-permute-done.33.refs_4_
  2.6 0.2 collective-permute-done.34.refs_5_
  2.8 1.3 %plan.3 = (s32[32,128]{1,0:T(8,128)S(1)}, bf16[7,64,128]{2,1,0:T(8,128)(2,1)S(1)}, s32[1,128]{1,0:T(1,128)S(1)}) custom-call(s32[1,128]{1,0:T(1,128)S(1)} %pad_bitcast_fusion.own, bf16[1,2,128,128]{3,2,1,0:T(8,128)(2,1)} %refs_0_.1, bf16[1,2,128,128]{3,2,1,0:T(8,128)(2,1)} %refs_1_.1, bf16[1,2,128,128]{3,2,1,0:T(8,128)(2,1)} %refs_2_.1, ...), custom_call_target="tpu_custom_call" | custom-call | flops 1000000 | bytes 4000000 | tf_op jit(solution)/shard_map/plan/pallas_call | solution.py:485
  4.1 2.9 %collective-permute-start.40 = (bf16[7,64,128]{2,1,0:T(8,128)(2,1)S(1)}, bf16[7,64,128]{2,1,0:T(8,128)(2,1)S(1)}, u32[]{:S(2)}, u32[]{:S(2)}) collective-permute-start(bf16[7,64,128]{2,1,0:T(8,128)(2,1)S(1)} %get-tuple-element.76.refs_7_), channel_id=1, source_target_pairs={{0,4},{2,10},{8,0},{10,18},{16,8},{18,26},{24,16},{26,30},{28,24},... | collective-permute-start | bytes 344072 | tf_op jit(solution)/shard_map/ppermute | solution.py:595
  7.0 0.1 collective-permute-start.36
  7.1 3.0 %collective-permute-done.40.refs_6_ = bf16[7,64,128]{2,1,0:T(8,128)(2,1)S(1)} collective-permute-done((bf16[7,64,128]{2,1,0:T(8,128)(2,1)S(1)}, bf16[7,64,128]{2,1,0:T(8,128)(2,1)S(1)}, u32[]{:S(2)}, u32[]{:S(2)}) %collective-permute-start.40) | collective-permute-done | bytes 114720 | tf_op jit(solution)/shard_map/ppermute | solution.py:595
  10.2 2.1 %collective-permute-start.41 = (bf16[7,64,128]{2,1,0:T(8,128)(2,1)S(1)}, bf16[7,64,128]{2,1,0:T(8,128)(2,1)S(1)}, u32[]{:S(2)}, u32[]{:S(2)}) collective-permute-start(bf16[7,64,128]{2,1,0:T(8,128)(2,1)S(1)} %collective-permute-done.40.refs_6_), channel_id=1, source_target_pairs={{0,4},{2,10},{8,0},{10,18},{16,8},{18,26},{24,16},{26,30},{28,24},... | collective-permute-start | bytes 344072 | tf_op jit(solution)/shard_map/ppermute | solution.py:595
  12.3 0.0 collective-permute-done.36.refs_5_
  12.3 0.4 collective-permute-start.37
  12.7 0.5 collective-permute-start.49
  13.2 3.1 %collective-permute-done.41.refs_4_ = bf16[7,64,128]{2,1,0:T(8,128)(2,1)S(1)} collective-permute-done((bf16[7,64,128]{2,1,0:T(8,128)(2,1)S(1)}, bf16[7,64,128]{2,1,0:T(8,128)(2,1)S(1)}, u32[]{:S(2)}, u32[]{:S(2)}) %collective-permute-start.41) | collective-permute-done | bytes 114720 | tf_op jit(solution)/shard_map/ppermute | solution.py:595
  16.3 0.8 %collective-permute-start.42 = (bf16[7,64,128]{2,1,0:T(8,128)(2,1)S(1)}, bf16[7,64,128]{2,1,0:T(8,128)(2,1)S(1)}, u32[]{:S(2)}, u32[]{:S(2)}) collective-permute-start(bf16[7,64,128]{2,1,0:T(8,128)(2,1)S(1)} %collective-permute-done.41.refs_4_), channel_id=1, source_target_pairs={{0,4},{2,10},{8,0},{10,18},{16,8},{18,26},{24,16},{26,30},{28,24},... | collective-permute-start | bytes 344072 | tf_op jit(solution)/shard_map/ppermute | solution.py:595
  17.1 1.2 %collective-permute-done.37.refs_3_ = bf16[7,64,128]{2,1,0:T(8,128)(2,1)S(1)} collective-permute-done((bf16[7,64,128]{2,1,0:T(8,128)(2,1)S(1)}, bf16[7,64,128]{2,1,0:T(8,128)(2,1)S(1)}, u32[]{:S(2)}, u32[]{:S(2)}) %collective-permute-start.37) | collective-permute-done | bytes 114720 | tf_op jit(solution)/shard_map/ppermute | solution.py:595
  18.3 0.1 collective-permute-start.38
  18.3 0.5 collective-permute-start.47
  18.9 0.0 collective-permute-done.49.refs_14_
  18.9 0.1 collective-permute-start.46
  18.9 2.2 %collective-permute-done.42.refs_2_ = bf16[7,64,128]{2,1,0:T(8,128)(2,1)S(1)} collective-permute-done((bf16[7,64,128]{2,1,0:T(8,128)(2,1)S(1)}, bf16[7,64,128]{2,1,0:T(8,128)(2,1)S(1)}, u32[]{:S(2)}, u32[]{:S(2)}) %collective-permute-start.42) | collective-permute-done | bytes 114720 | tf_op jit(solution)/shard_map/ppermute | solution.py:595
  21.2 0.0 collective-permute-start.45
  21.2 1.9 %collective-permute-done.38.refs_1_ = bf16[7,64,128]{2,1,0:T(8,128)(2,1)S(1)} collective-permute-done((bf16[7,64,128]{2,1,0:T(8,128)(2,1)S(1)}, bf16[7,64,128]{2,1,0:T(8,128)(2,1)S(1)}, u32[]{:S(2)}, u32[]{:S(2)}) %collective-permute-start.38) | collective-permute-done | bytes 114720 | tf_op jit(solution)/shard_map/ppermute | solution.py:595
  23.1 0.0 collective-permute-start.44
  23.1 0.2 collective-permute-start.43
  23.3 1.7 %collective-permute-start.39 = (bf16[7,64,128]{2,1,0:T(8,128)(2,1)S(1)}, bf16[7,64,128]{2,1,0:T(8,128)(2,1)S(1)}, u32[]{:S(2)}, u32[]{:S(2)}) collective-permute-start(bf16[7,64,128]{2,1,0:T(8,128)(2,1)S(1)} %collective-permute-done.38.refs_1_), channel_id=1, source_target_pairs={{0,8},{2,6},{8,16},{10,2},{16,24},{18,10},{24,28},{26,18},{28,20},... | collective-permute-start | bytes 344072 | tf_op jit(solution)/shard_map/ppermute | solution.py:598
  24.9 0.0 collective-permute-done.46.refs_11_
  24.9 0.0 collective-permute-done.45.refs_10_
  24.9 2.4 %collective-permute-done.43.refs_8_ = bf16[7,64,128]{2,1,0:T(8,128)(2,1)S(1)} collective-permute-done((bf16[7,64,128]{2,1,0:T(8,128)(2,1)S(1)}, bf16[7,64,128]{2,1,0:T(8,128)(2,1)S(1)}, u32[]{:S(2)}, u32[]{:S(2)}) %collective-permute-start.43) | collective-permute-done | bytes 114720 | tf_op jit(solution)/shard_map/ppermute | solution.py:599
  27.3 1.9 %collective-permute-done.39.refs_0_ = bf16[7,64,128]{2,1,0:T(8,128)(2,1)S(1)} collective-permute-done((bf16[7,64,128]{2,1,0:T(8,128)(2,1)S(1)}, bf16[7,64,128]{2,1,0:T(8,128)(2,1)S(1)}, u32[]{:S(2)}, u32[]{:S(2)}) %collective-permute-start.39) | collective-permute-done | bytes 114720 | tf_op jit(solution)/shard_map/ppermute | solution.py:598
  29.2 6.2 %compute.3 = (bf16[56,64,128]{2,1,0:T(8,128)(2,1)S(1)}, bf16[14,64,128]{2,1,0:T(8,128)(2,1)S(1)}, bf16[42,64,128]{2,1,0:T(8,128)(2,1)S(1)}, bf16[18,128,128]{2,1,0:T(8,128)(2,1)S(1)}, bf16[18,128,128]{2,1,0:T(8,128)(2,1)S(1)}) custom-call(s32[32,128]{1,0:T(8,128)S(1)} %get-tuple-element.74.plan, bf16[128,8192]{1,0:T(8,128)(2,1)} %tokens.1, ...), custom_call_target="tpu_custom_call" | custom-call | flops 1000000000 | bytes 20000000 | tf_op jit(solution)/shard_map/compute/pallas_call | solution.py:541
  35.4 0.1 collective-permute-start.52
  35.5 1.5 %collective-permute-done.52.__1_ = bf16[14,64,128]{2,1,0:T(8,128)(2,1)S(1)} collective-permute-done((bf16[14,64,128]{2,1,0:T(8,128)(2,1)S(1)}, bf16[14,64,128]{2,1,0:T(8,128)(2,1)S(1)}, u32[]{:S(2)}, u32[]{:S(2)}) %collective-permute-start.52) | collective-permute-done | bytes 229408 | tf_op jit(solution)/shard_map/ppermute | solution.py:606
  36.9 0.1 collective-permute-start.53
  37.1 0.1 add_convert_fusion.13
  37.1 0.6 collective-permute-start.54
  37.7 1.5 %collective-permute-start.55 = (bf16[7,64,128]{2,1,0:T(8,128)(2,1)S(1)}, bf16[7,64,128]{2,1,0:T(8,128)(2,1)S(1)}, u32[]{:S(2)}, u32[]{:S(2)}) collective-permute-start(bf16[7,64,128]{2,1,0:T(8,128)(2,1)S(1)} %get-tuple-element.82), channel_id=1, source_target_pairs={{0,4},{2,10},{8,0},{10,18},{16,8},{18,26},{24,16},{26,30},{28,24},... | collective-permute-start | bytes 344072 | tf_op jit(solution)/shard_map/ppermute | solution.py:620
  39.2 0.0 collective-permute-start.35
  39.2 2.0 %collective-permute-start.51 = (bf16[18,128,128]{2,1,0:T(8,128)(2,1)S(1)}, bf16[18,128,128]{2,1,0:T(8,128)(2,1)S(1)}, u32[]{:S(2)}, u32[]{:S(2)}) collective-permute-start(bf16[18,128,128]{2,1,0:T(8,128)(2,1)S(1)} %get-tuple-element.77), channel_id=1, source_target_pairs={{0,1},{1,0},{2,3},{3,2},{4,5},{5,4},{6,7},{7,6},{8,9},{9,8},{10,11... | collective-permute-start | bytes 1769480 | tf_op jit(solution)/shard_map/ppermute | solution.py:649
  41.3 1.5 %collective-permute-done.35.__2_.note.refs_0_ = s32[1,128]{1,0:T(1,128)S(1)} collective-permute-done((s32[1,128]{1,0:T(1,128)S(1)}, s32[1,128]{1,0:T(1,128)S(1)}, u32[]{:S(2)}, u32[]{:S(2)}) %collective-permute-start.35) | collective-permute-done | bytes 544 | tf_op jit(solution)/shard_map/ppermute | solution.py:649
  42.8 0.0 collective-permute-done.53
  42.8 0.1 add_convert_fusion.12.__1_
  42.9 1.6 %collective-permute-start.56 = (bf16[7,64,128]{2,1,0:T(8,128)(2,1)S(1)}, bf16[7,64,128]{2,1,0:T(8,128)(2,1)S(1)}, u32[]{:S(2)}, u32[]{:S(2)}) collective-permute-start(bf16[7,64,128]{2,1,0:T(8,128)(2,1)S(1)} %add_convert_fusion.12.__1_), channel_id=1, source_target_pairs={{0,8},{2,6},{8,16},{10,2},{16,24},{18,10},{24,28},{26,18},{28,20},... | collective-permute-start | bytes 344072 | tf_op jit(solution)/shard_map/ppermute | solution.py:620
  44.5 0.1 add_convert_fusion.11.__1_
  44.6 0.5 collective-permute-start.58
  45.0 2.9 %collective-permute-done.56.__0_ = bf16[7,64,128]{2,1,0:T(8,128)(2,1)S(1)} collective-permute-done((bf16[7,64,128]{2,1,0:T(8,128)(2,1)S(1)}, bf16[7,64,128]{2,1,0:T(8,128)(2,1)S(1)}, u32[]{:S(2)}, u32[]{:S(2)}) %collective-permute-start.56) | collective-permute-done | bytes 114720 | tf_op jit(solution)/shard_map/ppermute | solution.py:620
  47.9 0.1 add_convert_fusion.10.__1_
  48.0 2.5 %collective-permute-start.57 = (bf16[7,64,128]{2,1,0:T(8,128)(2,1)S(1)}, bf16[7,64,128]{2,1,0:T(8,128)(2,1)S(1)}, u32[]{:S(2)}, u32[]{:S(2)}) collective-permute-start(bf16[7,64,128]{2,1,0:T(8,128)(2,1)S(1)} %add_convert_fusion.10.__1_), channel_id=1, source_target_pairs={{0,8},{2,6},{8,16},{10,2},{16,24},{18,10},{24,28},{26,18},{28,20},... | collective-permute-start | bytes 344072 | tf_op jit(solution)/shard_map/ppermute | solution.py:620
  50.5 0.0 collective-permute-done.58.__0_
  50.5 0.1 add_convert_fusion.9.__1_
  50.5 0.1 collective-permute-start.63
  50.6 1.3 %collective-permute-start.60 = (bf16[7,64,128]{2,1,0:T(8,128)(2,1)S(1)}, bf16[7,64,128]{2,1,0:T(8,128)(2,1)S(1)}, u32[]{:S(2)}, u32[]{:S(2)}) collective-permute-start(bf16[7,64,128]{2,1,0:T(8,128)(2,1)S(1)} %add_convert_fusion.9.__1_), channel_id=1, source_target_pairs={{0,4},{2,10},{8,0},{10,18},{16,8},{18,26},{24,16},{26,30},{28,24},... | collective-permute-start | bytes 344072 | tf_op jit(solution)/shard_map/ppermute | solution.py:620
  52.0 0.9 %collective-permute-done.57.__0_ = bf16[7,64,128]{2,1,0:T(8,128)(2,1)S(1)} collective-permute-done((bf16[7,64,128]{2,1,0:T(8,128)(2,1)S(1)}, bf16[7,64,128]{2,1,0:T(8,128)(2,1)S(1)}, u32[]{:S(2)}, u32[]{:S(2)}) %collective-permute-start.57) | collective-permute-done | bytes 114720 | tf_op jit(solution)/shard_map/ppermute | solution.py:620
  52.8 0.1 add_convert_fusion.8
  52.9 1.0 %collective-permute-start.62 = (bf16[7,64,128]{2,1,0:T(8,128)(2,1)S(1)}, bf16[7,64,128]{2,1,0:T(8,128)(2,1)S(1)}, u32[]{:S(2)}, u32[]{:S(2)}) collective-permute-start(bf16[7,64,128]{2,1,0:T(8,128)(2,1)S(1)} %get-tuple-element.109), channel_id=1, source_target_pairs={{0,10},{2,4},{8,18},{10,0},{16,26},{18,8},{24,30},{26,16},{28,22},... | collective-permute-start | bytes 344072 | tf_op jit(solution)/shard_map/ppermute | solution.py:636
  54.0 1.7 %collective-permute-start.59 = (bf16[7,64,128]{2,1,0:T(8,128)(2,1)S(1)}, bf16[7,64,128]{2,1,0:T(8,128)(2,1)S(1)}, u32[]{:S(2)}, u32[]{:S(2)}) collective-permute-start(bf16[7,64,128]{2,1,0:T(8,128)(2,1)S(1)} %get-tuple-element.109), channel_id=1, source_target_pairs={{0,8},{2,6},{8,16},{10,2},{16,24},{18,10},{24,28},{26,18},{28,20},... | collective-permute-start | bytes 344072 | tf_op jit(solution)/shard_map/ppermute | solution.py:633
  55.7 2.2 %collective-permute-start.61 = (bf16[7,64,128]{2,1,0:T(8,128)(2,1)S(1)}, bf16[7,64,128]{2,1,0:T(8,128)(2,1)S(1)}, u32[]{:S(2)}, u32[]{:S(2)}) collective-permute-start(bf16[7,64,128]{2,1,0:T(8,128)(2,1)S(1)} %get-tuple-element.110.refs_2_), channel_id=1, source_target_pairs={{0,2},{2,0},{8,10},{10,8},{16,18},{18,16},{24,26},{26,24},{28,30},... | collective-permute-start | bytes 344072 | tf_op jit(solution)/shard_map/ppermute | solution.py:635
  57.8 2.5 %prepare.3 = (bf16[128,4096]{1,0:T(8,128)(2,1)}, bf16[128,4096]{1,0:T(8,128)(2,1)}, bf16[18,128,128]{2,1,0:T(8,128)(2,1)S(1)}) custom-call(s32[32,128]{1,0:T(8,128)S(1)} %get-tuple-element.74.plan, s32[1,128]{1,0:T(1,128)S(1)} %collective-permute-done.35.__2_.note.refs_0_, bf16[18,128,128]{2,1,0:T(8,128)(2,1)S(1)} %get-tuple-element.85.first), custom_call_target="tpu_custom_call" | custom-call | flops 1000000 | bytes 6000000 | tf_op jit(solution)/shard_map/prepare/pallas_call | solution.py:558
  60.4 0.0 copy-start
  60.4 0.0 copy-start.1
  60.4 0.0 copy-start.2
  60.4 2.5 %last.3 = (bf16[128,4096]{1,0:T(8,128)(2,1)}, bf16[128,4096]{1,0:T(8,128)(2,1)}, bf16[1,2,128,128]{3,2,1,0:T(8,128)(2,1)}, bf16[1,2,128,128]{3,2,1,0:T(8,128)(2,...) custom-call(s32[32,128]{1,0:T(8,128)S(1)} %get-tuple-element.74.plan, ...), custom_call_target="tpu_custom_call", output_to_operand_aliasing={{0}: (10, {}), {1}: (11, {})} | custom-call | flops 1000000 | bytes 3000000 | tf_op jit(solution)/shard_map/last/pallas_call | solution.py:572
  (25 shorter events, 0.1 us)
Async XLA Ops:
  0.6 1.8 %collective-permute-start.32 = (bf16[1,2,128,128]{3,2,1,0:T(8,128)(2,1)}, bf16[1,2,128,128]{3,2,1,0:T(8,128)(2,1)S(1)}, u32[]{:S(2)}, u32[]{:S(2)}) collective-permute-start(bf16[1,2,128,128]{3,2,1,0:T(8,128)(2,1)} %refs_0_.1), channel_id=1, source_target_pairs={{0,2},{2,0},{8,10},{10,8},{16,18},{18,16},{24,26},{26,24},{28,30},... | collective-permute-start | bytes 196616 | tf_op jit(solution)/shard_map/ppermute | solution.py:645
  1.2 1.5 %collective-permute-start.33 = (bf16[1,2,128,128]{3,2,1,0:T(8,128)(2,1)}, bf16[1,2,128,128]{3,2,1,0:T(8,128)(2,1)S(1)}, u32[]{:S(2)}, u32[]{:S(2)}) collective-permute-start(bf16[1,2,128,128]{3,2,1,0:T(8,128)(2,1)} %refs_1_.1), channel_id=1, source_target_pairs={{0,2},{2,0},{8,10},{10,8},{16,18},{18,16},{24,26},{26,24},{28,30},... | collective-permute-start | bytes 196616 | tf_op jit(solution)/shard_map/ppermute | solution.py:645
  1.2 1.5 %collective-permute-start.34 = (bf16[1,2,128,128]{3,2,1,0:T(8,128)(2,1)}, bf16[1,2,128,128]{3,2,1,0:T(8,128)(2,1)S(1)}, u32[]{:S(2)}, u32[]{:S(2)}) collective-permute-start(bf16[1,2,128,128]{3,2,1,0:T(8,128)(2,1)} %refs_2_.1), channel_id=1, source_target_pairs={{0,2},{2,0},{8,10},{10,8},{16,18},{18,16},{24,26},{26,24},{28,30},... | collective-permute-start | bytes 196616 | tf_op jit(solution)/shard_map/ppermute | solution.py:645
  4.1 6.1 %collective-permute-start.40 = (bf16[7,64,128]{2,1,0:T(8,128)(2,1)S(1)}, bf16[7,64,128]{2,1,0:T(8,128)(2,1)S(1)}, u32[]{:S(2)}, u32[]{:S(2)}) collective-permute-start(bf16[7,64,128]{2,1,0:T(8,128)(2,1)S(1)} %get-tuple-element.76.refs_7_), channel_id=1, source_target_pairs={{0,4},{2,10},{8,0},{10,18},{16,8},{18,26},{24,16},{26,30},{28,24},... | collective-permute-start | bytes 344072 | tf_op jit(solution)/shard_map/ppermute | solution.py:595
  7.0 5.3 %collective-permute-start.36 = (bf16[7,64,128]{2,1,0:T(8,128)(2,1)S(1)}, bf16[7,64,128]{2,1,0:T(8,128)(2,1)S(1)}, u32[]{:S(2)}, u32[]{:S(2)}) collective-permute-start(bf16[7,64,128]{2,1,0:T(8,128)(2,1)S(1)} %get-tuple-element.76.refs_7_), channel_id=1, source_target_pairs={{0,8},{2,6},{8,16},{10,2},{16,24},{18,10},{24,28},{26,18},{28,20},... | collective-permute-start | bytes 344072 | tf_op jit(solution)/shard_map/ppermute | solution.py:595
  10.2 6.1 %collective-permute-start.41 = (bf16[7,64,128]{2,1,0:T(8,128)(2,1)S(1)}, bf16[7,64,128]{2,1,0:T(8,128)(2,1)S(1)}, u32[]{:S(2)}, u32[]{:S(2)}) collective-permute-start(bf16[7,64,128]{2,1,0:T(8,128)(2,1)S(1)} %collective-permute-done.40.refs_6_), channel_id=1, source_target_pairs={{0,4},{2,10},{8,0},{10,18},{16,8},{18,26},{24,16},{26,30},{28,24},... | collective-permute-start | bytes 344072 | tf_op jit(solution)/shard_map/ppermute | solution.py:595
  12.3 6.0 %collective-permute-start.37 = (bf16[7,64,128]{2,1,0:T(8,128)(2,1)S(1)}, bf16[7,64,128]{2,1,0:T(8,128)(2,1)S(1)}, u32[]{:S(2)}, u32[]{:S(2)}) collective-permute-start(bf16[7,64,128]{2,1,0:T(8,128)(2,1)S(1)} %collective-permute-done.36.refs_5_), channel_id=1, source_target_pairs={{0,8},{2,6},{8,16},{10,2},{16,24},{18,10},{24,28},{26,18},{28,20},... | collective-permute-start | bytes 344072 | tf_op jit(solution)/shard_map/ppermute | solution.py:595
  12.7 5.6 %collective-permute-start.50 = (bf16[7,64,128]{2,1,0:T(8,128)(2,1)S(1)}, bf16[7,64,128]{2,1,0:T(8,128)(2,1)S(1)}, u32[]{:S(2)}, u32[]{:S(2)}) collective-permute-start(bf16[7,64,128]{2,1,0:T(8,128)(2,1)S(1)} %get-tuple-element.76.refs_7_), channel_id=1, source_target_pairs={{0,2},{2,0},{8,10},{10,8},{16,18},{18,16},{24,26},{26,24},{28,30},... | collective-permute-start | bytes 344072 | tf_op jit(solution)/shard_map/ppermute | solution.py:597
  12.7 6.1 %collective-permute-start.49 = (bf16[7,64,128]{2,1,0:T(8,128)(2,1)S(1)}, bf16[7,64,128]{2,1,0:T(8,128)(2,1)S(1)}, u32[]{:S(2)}, u32[]{:S(2)}) collective-permute-start(bf16[7,64,128]{2,1,0:T(8,128)(2,1)S(1)} %collective-permute-done.40.refs_6_), channel_id=1, source_target_pairs={{0,2},{2,0},{8,10},{10,8},{16,18},{18,16},{24,26},{26,24},{28,30},... | collective-permute-start | bytes 344072 | tf_op jit(solution)/shard_map/ppermute | solution.py:597
  16.3 4.9 %collective-permute-start.42 = (bf16[7,64,128]{2,1,0:T(8,128)(2,1)S(1)}, bf16[7,64,128]{2,1,0:T(8,128)(2,1)S(1)}, u32[]{:S(2)}, u32[]{:S(2)}) collective-permute-start(bf16[7,64,128]{2,1,0:T(8,128)(2,1)S(1)} %collective-permute-done.41.refs_4_), channel_id=1, source_target_pairs={{0,4},{2,10},{8,0},{10,18},{16,8},{18,26},{24,16},{26,30},{28,24},... | collective-permute-start | bytes 344072 | tf_op jit(solution)/shard_map/ppermute | solution.py:595
  18.3 4.8 %collective-permute-start.38 = (bf16[7,64,128]{2,1,0:T(8,128)(2,1)S(1)}, bf16[7,64,128]{2,1,0:T(8,128)(2,1)S(1)}, u32[]{:S(2)}, u32[]{:S(2)}) collective-permute-start(bf16[7,64,128]{2,1,0:T(8,128)(2,1)S(1)} %collective-permute-done.37.refs_3_), channel_id=1, source_target_pairs={{0,8},{2,6},{8,16},{10,2},{16,24},{18,10},{24,28},{26,18},{28,20},... | collective-permute-start | bytes 344072 | tf_op jit(solution)/shard_map/ppermute | solution.py:595
  18.3 4.7 %collective-permute-start.48 = (bf16[7,64,128]{2,1,0:T(8,128)(2,1)S(1)}, bf16[7,64,128]{2,1,0:T(8,128)(2,1)S(1)}, u32[]{:S(2)}, u32[]{:S(2)}) collective-permute-start(bf16[7,64,128]{2,1,0:T(8,128)(2,1)S(1)} %collective-permute-done.36.refs_5_), channel_id=1, source_target_pairs={{0,2},{2,0},{8,10},{10,8},{16,18},{18,16},{24,26},{26,24},{28,30},... | collective-permute-start | bytes 344072 | tf_op jit(solution)/shard_map/ppermute | solution.py:597
  18.3 4.9 %collective-permute-start.47 = (bf16[7,64,128]{2,1,0:T(8,128)(2,1)S(1)}, bf16[7,64,128]{2,1,0:T(8,128)(2,1)S(1)}, u32[]{:S(2)}, u32[]{:S(2)}) collective-permute-start(bf16[7,64,128]{2,1,0:T(8,128)(2,1)S(1)} %collective-permute-done.41.refs_4_), channel_id=1, source_target_pairs={{0,2},{2,0},{8,10},{10,8},{16,18},{18,16},{24,26},{26,24},{28,30},... | collective-permute-start | bytes 344072 | tf_op jit(solution)/shard_map/ppermute | solution.py:597
  18.9 6.1 %collective-permute-start.46 = (bf16[7,64,128]{2,1,0:T(8,128)(2,1)S(1)}, bf16[7,64,128]{2,1,0:T(8,128)(2,1)S(1)}, u32[]{:S(2)}, u32[]{:S(2)}) collective-permute-start(bf16[7,64,128]{2,1,0:T(8,128)(2,1)S(1)} %collective-permute-done.37.refs_3_), channel_id=1, source_target_pairs={{0,2},{2,0},{8,10},{10,8},{16,18},{18,16},{24,26},{26,24},{28,30},... | collective-permute-start | bytes 344072 | tf_op jit(solution)/shard_map/ppermute | solution.py:597
  21.2 3.7 %collective-permute-start.45 = (bf16[7,64,128]{2,1,0:T(8,128)(2,1)S(1)}, bf16[7,64,128]{2,1,0:T(8,128)(2,1)S(1)}, u32[]{:S(2)}, u32[]{:S(2)}) collective-permute-start(bf16[7,64,128]{2,1,0:T(8,128)(2,1)S(1)} %collective-permute-done.42.refs_2_), channel_id=1, source_target_pairs={{0,2},{2,0},{8,10},{10,8},{16,18},{18,16},{24,26},{26,24},{28,30},... | collective-permute-start | bytes 344072 | tf_op jit(solution)/shard_map/ppermute | solution.py:597
  23.1 1.9 %collective-permute-start.44 = (bf16[7,64,128]{2,1,0:T(8,128)(2,1)S(1)}, bf16[7,64,128]{2,1,0:T(8,128)(2,1)S(1)}, u32[]{:S(2)}, u32[]{:S(2)}) collective-permute-start(bf16[7,64,128]{2,1,0:T(8,128)(2,1)S(1)} %collective-permute-done.38.refs_1_), channel_id=1, source_target_pairs={{0,2},{2,0},{8,10},{10,8},{16,18},{18,16},{24,26},{26,24},{28,30},... | collective-permute-start | bytes 344072 | tf_op jit(solution)/shard_map/ppermute | solution.py:597
  23.1 4.2 %collective-permute-start.43 = (bf16[7,64,128]{2,1,0:T(8,128)(2,1)S(1)}, bf16[7,64,128]{2,1,0:T(8,128)(2,1)S(1)}, u32[]{:S(2)}, u32[]{:S(2)}) collective-permute-start(bf16[7,64,128]{2,1,0:T(8,128)(2,1)S(1)} %collective-permute-done.38.refs_1_), channel_id=1, source_target_pairs={{0,10},{2,4},{8,18},{10,0},{16,26},{18,8},{24,30},{26,16},{28,22},... | collective-permute-start | bytes 344072 | tf_op jit(solution)/shard_map/ppermute | solution.py:599
  23.3 6.0 %collective-permute-start.39 = (bf16[7,64,128]{2,1,0:T(8,128)(2,1)S(1)}, bf16[7,64,128]{2,1,0:T(8,128)(2,1)S(1)}, u32[]{:S(2)}, u32[]{:S(2)}) collective-permute-start(bf16[7,64,128]{2,1,0:T(8,128)(2,1)S(1)} %collective-permute-done.38.refs_1_), channel_id=1, source_target_pairs={{0,8},{2,6},{8,16},{10,2},{16,24},{18,10},{24,28},{26,18},{28,20},... | collective-permute-start | bytes 344072 | tf_op jit(solution)/shard_map/ppermute | solution.py:598
  35.4 1.6 %collective-permute-start.52 = (bf16[14,64,128]{2,1,0:T(8,128)(2,1)S(1)}, bf16[14,64,128]{2,1,0:T(8,128)(2,1)S(1)}, u32[]{:S(2)}, u32[]{:S(2)}) collective-permute-start(bf16[14,64,128]{2,1,0:T(8,128)(2,1)S(1)} %get-tuple-element.80), channel_id=1, source_target_pairs={{0,2},{2,0},{8,10},{10,8},{16,18},{18,16},{24,26},{26,24},{28,30},... | collective-permute-start | bytes 688136 | tf_op jit(solution)/shard_map/ppermute | solution.py:606
  36.9 5.9 %collective-permute-start.53 = (bf16[42,64,128]{2,1,0:T(8,128)(2,1)S(1)}, bf16[42,64,128]{2,1,0:T(8,128)(2,1)S(1)}, u32[]{:S(2)}, u32[]{:S(2)}) collective-permute-start(bf16[42,64,128]{2,1,0:T(8,128)(2,1)S(1)} %turn.18), channel_id=1, source_target_pairs={{0,2},{2,0},{8,10},{10,8},{16,18},{18,16},{24,26},{26,24},{28,30},... | collective-permute-start | bytes 2064392 | tf_op jit(solution)/shard_map/ppermute | solution.py:607
  37.1 5.6 %collective-permute-start.54 = (bf16[7,64,128]{2,1,0:T(8,128)(2,1)S(1)}, bf16[7,64,128]{2,1,0:T(8,128)(2,1)S(1)}, u32[]{:S(2)}, u32[]{:S(2)}) collective-permute-start(bf16[7,64,128]{2,1,0:T(8,128)(2,1)S(1)} %get-tuple-element.81), channel_id=1, source_target_pairs={{0,8},{2,6},{8,16},{10,2},{16,24},{18,10},{24,28},{26,18},{28,20},... | collective-permute-start | bytes 344072 | tf_op jit(solution)/shard_map/ppermute | solution.py:620
  37.7 5.1 %collective-permute-start.55 = (bf16[7,64,128]{2,1,0:T(8,128)(2,1)S(1)}, bf16[7,64,128]{2,1,0:T(8,128)(2,1)S(1)}, u32[]{:S(2)}, u32[]{:S(2)}) collective-permute-start(bf16[7,64,128]{2,1,0:T(8,128)(2,1)S(1)} %get-tuple-element.82), channel_id=1, source_target_pairs={{0,4},{2,10},{8,0},{10,18},{16,8},{18,26},{24,16},{26,30},{28,24},... | collective-permute-start | bytes 344072 | tf_op jit(solution)/shard_map/ppermute | solution.py:620
  39.2 3.6 %collective-permute-start.35 = (s32[1,128]{1,0:T(1,128)S(1)}, s32[1,128]{1,0:T(1,128)S(1)}, u32[]{:S(2)}, u32[]{:S(2)}) collective-permute-start(s32[1,128]{1,0:T(1,128)S(1)} %get-tuple-element.75), channel_id=1, source_target_pairs={{0,1},{1,0},{2,3},{3,2},{4,5},{5,4},{6,7},{7,6},{8,9},{9,8},{10,11... | collective-permute-start | bytes 1544 | tf_op jit(solution)/shard_map/ppermute | solution.py:649
  39.2 16.5 %collective-permute-start.51 = (bf16[18,128,128]{2,1,0:T(8,128)(2,1)S(1)}, bf16[18,128,128]{2,1,0:T(8,128)(2,1)S(1)}, u32[]{:S(2)}, u32[]{:S(2)}) collective-permute-start(bf16[18,128,128]{2,1,0:T(8,128)(2,1)S(1)} %get-tuple-element.77), channel_id=1, source_target_pairs={{0,1},{1,0},{2,3},{3,2},{4,5},{5,4},{6,7},{7,6},{8,9},{9,8},{10,11... | collective-permute-start | bytes 1769480 | tf_op jit(solution)/shard_map/ppermute | solution.py:649
  42.9 5.1 %collective-permute-start.56 = (bf16[7,64,128]{2,1,0:T(8,128)(2,1)S(1)}, bf16[7,64,128]{2,1,0:T(8,128)(2,1)S(1)}, u32[]{:S(2)}, u32[]{:S(2)}) collective-permute-start(bf16[7,64,128]{2,1,0:T(8,128)(2,1)S(1)} %add_convert_fusion.12.__1_), channel_id=1, source_target_pairs={{0,8},{2,6},{8,16},{10,2},{16,24},{18,10},{24,28},{26,18},{28,20},... | collective-permute-start | bytes 344072 | tf_op jit(solution)/shard_map/ppermute | solution.py:620
  44.6 5.9 %collective-permute-start.58 = (bf16[7,64,128]{2,1,0:T(8,128)(2,1)S(1)}, bf16[7,64,128]{2,1,0:T(8,128)(2,1)S(1)}, u32[]{:S(2)}, u32[]{:S(2)}) collective-permute-start(bf16[7,64,128]{2,1,0:T(8,128)(2,1)S(1)} %add_convert_fusion.11.__1_), channel_id=1, source_target_pairs={{0,4},{2,10},{8,0},{10,18},{16,8},{18,26},{24,16},{26,30},{28,24},... | collective-permute-start | bytes 344072 | tf_op jit(solution)/shard_map/ppermute | solution.py:620
  48.0 4.9 %collective-permute-start.57 = (bf16[7,64,128]{2,1,0:T(8,128)(2,1)S(1)}, bf16[7,64,128]{2,1,0:T(8,128)(2,1)S(1)}, u32[]{:S(2)}, u32[]{:S(2)}) collective-permute-start(bf16[7,64,128]{2,1,0:T(8,128)(2,1)S(1)} %add_convert_fusion.10.__1_), channel_id=1, source_target_pairs={{0,8},{2,6},{8,16},{10,2},{16,24},{18,10},{24,28},{26,18},{28,20},... | collective-permute-start | bytes 344072 | tf_op jit(solution)/shard_map/ppermute | solution.py:620
  50.5 9.8 %collective-permute-start.63 = (bf16[7,64,128]{2,1,0:T(8,128)(2,1)S(1)}, bf16[7,64,128]{2,1,0:T(8,128)(2,1)S(1)}, u32[]{:S(2)}, u32[]{:S(2)}) collective-permute-start(bf16[7,64,128]{2,1,0:T(8,128)(2,1)S(1)} %add_convert_fusion.9.__1_), channel_id=1, source_target_pairs={{0,6},{2,8},{8,2},{10,16},{16,10},{18,24},{24,18},{26,28},{28,26},... | collective-permute-start | bytes 344072 | tf_op jit(solution)/shard_map/ppermute | solution.py:637
  50.6 9.8 %collective-permute-start.60 = (bf16[7,64,128]{2,1,0:T(8,128)(2,1)S(1)}, bf16[7,64,128]{2,1,0:T(8,128)(2,1)S(1)}, u32[]{:S(2)}, u32[]{:S(2)}) collective-permute-start(bf16[7,64,128]{2,1,0:T(8,128)(2,1)S(1)} %add_convert_fusion.9.__1_), channel_id=1, source_target_pairs={{0,4},{2,10},{8,0},{10,18},{16,8},{18,26},{24,16},{26,30},{28,24},... | collective-permute-start | bytes 344072 | tf_op jit(solution)/shard_map/ppermute | solution.py:620
  52.9 7.4 %collective-permute-start.62 = (bf16[7,64,128]{2,1,0:T(8,128)(2,1)S(1)}, bf16[7,64,128]{2,1,0:T(8,128)(2,1)S(1)}, u32[]{:S(2)}, u32[]{:S(2)}) collective-permute-start(bf16[7,64,128]{2,1,0:T(8,128)(2,1)S(1)} %get-tuple-element.109), channel_id=1, source_target_pairs={{0,10},{2,4},{8,18},{10,0},{16,26},{18,8},{24,30},{26,16},{28,22},... | collective-permute-start | bytes 344072 | tf_op jit(solution)/shard_map/ppermute | solution.py:636
  54.0 6.4 %collective-permute-start.59 = (bf16[7,64,128]{2,1,0:T(8,128)(2,1)S(1)}, bf16[7,64,128]{2,1,0:T(8,128)(2,1)S(1)}, u32[]{:S(2)}, u32[]{:S(2)}) collective-permute-start(bf16[7,64,128]{2,1,0:T(8,128)(2,1)S(1)} %get-tuple-element.109), channel_id=1, source_target_pairs={{0,8},{2,6},{8,16},{10,2},{16,24},{18,10},{24,28},{26,18},{28,20},... | collective-permute-start | bytes 344072 | tf_op jit(solution)/shard_map/ppermute | solution.py:633
  55.7 4.7 %collective-permute-start.61 = (bf16[7,64,128]{2,1,0:T(8,128)(2,1)S(1)}, bf16[7,64,128]{2,1,0:T(8,128)(2,1)S(1)}, u32[]{:S(2)}, u32[]{:S(2)}) collective-permute-start(bf16[7,64,128]{2,1,0:T(8,128)(2,1)S(1)} %get-tuple-element.110.refs_2_), channel_id=1, source_target_pairs={{0,2},{2,0},{8,10},{10,8},{16,18},{18,16},{24,26},{26,24},{28,30},... | collective-permute-start | bytes 344072 | tf_op jit(solution)/shard_map/ppermute | solution.py:635
  60.4 3.1 %copy-start = (bf16[1,2,128,128]{3,2,1,0:T(8,128)(2,1)S(1)}, bf16[1,2,128,128]{3,2,1,0:T(8,128)(2,1)}, u32[]{:S(2)}) copy-start(bf16[1,2,128,128]{3,2,1,0:T(8,128)(2,1)} %refs_0_.1) | copy-start | bytes 196612
  60.4 3.1 %copy-start.1 = (bf16[1,2,128,128]{3,2,1,0:T(8,128)(2,1)S(1)}, bf16[1,2,128,128]{3,2,1,0:T(8,128)(2,1)}, u32[]{:S(2)}) copy-start(bf16[1,2,128,128]{3,2,1,0:T(8,128)(2,1)} %refs_1_.1) | copy-start | bytes 196612
  60.4 3.1 %copy-start.2 = (bf16[1,2,128,128]{3,2,1,0:T(8,128)(2,1)S(1)}, bf16[1,2,128,128]{3,2,1,0:T(8,128)(2,1)}, u32[]{:S(2)}) copy-start(bf16[1,2,128,128]{3,2,1,0:T(8,128)(2,1)} %refs_2_.1) | copy-start | bytes 196612

commit v3 on v2

--- a/solution.py
+++ b/solution.py
@@ -587,6 +587,10 @@
     )(plan, *notes, *firsts, *terms, strips, *partial)
 
 
+def across(pairs):
+    return [(i, j ^ 1) for i, j in pairs]
+
+
 def gather_chunks(sz, chunk):
     ahead, behind, swap = permutations(sz)
     same = {0: chunk}
@@ -596,11 +600,11 @@
         same[sz.ring - s], same[s] = a, b
     other = {d: lax.ppermute(same[d], "fsdp", swap) for d in same}
     same[sz.top] = lax.ppermute(a, "fsdp", ahead)
-    other[sz.top] = lax.ppermute(a, "fsdp", [(i, j ^ 1) for i, j in ahead])
+    other[sz.top] = lax.ppermute(a, "fsdp", across(ahead))
     return [side[d] for side in (same, other) for d in sz.order]
 
 
-def reduce_parts(sz, same, far, near, notes):
+def reduce_parts(sz, same, far, near, notes, prepare):
     ahead, behind, swap = permutations(sz)
     keep = sz.keep
     far = lax.ppermute(far, "fsdp", swap)
@@ -615,28 +619,26 @@
         return out.astype(jnp.bfloat16)
 
     a, b = lax.optimization_barrier((term(sz.top), term(sz.top + 1)))
+    here = term(0)
+    here_across = lax.ppermute(here, "fsdp", swap)
+    prepared = prepare(here_across)
     for s in range(1, sz.top):
         last_b = b
         a, b = lax.ppermute(a, "fsdp", ahead), lax.ppermute(b, "fsdp", behind)
         if s == 1:
             a, b = call_turn([a, b], notes)
         else:
-            a = call_turn([a], [last_b])[0]
+            a = call_turn([a], [last_b] + (list(prepared[2:]) if s == 2 else []))[0]
         a = term(sz.top - s, a)
         if s + 1 < sz.top:
             b = term(sz.top + 1 + s, call_turn([b], [a])[0])
-    here = term(0)
-
-    def across(pairs):
-        return [(i, j ^ 1) for i, j in pairs]
-
     mine = [here, lax.ppermute(a, "fsdp", ahead), b]
     theirs = [
-        lax.ppermute(here, "fsdp", swap),
+        here_across,
         lax.ppermute(a, "fsdp", across(ahead)),
         lax.ppermute(last_b, "fsdp", across(behind)),
     ]
-    return mine + theirs
+    return mine + theirs, prepared
 
 
 def program(sz, own, tokens, cotangent, mine):
@@ -651,10 +653,13 @@
     notes = [exchange(note, s) for s, note in enumerate(notes, 1)]
     chunks = gather_chunks(sz, chunk)
     same, far, near, *firsts = call_compute(sz, plan, tokens, cotangent, chunks)
-    *partial, strips = call_prepare(sz, plan, notes[0], firsts[0])
-    firsts = [exchange(firsts[s], s) for s in range(1, T)]
-    terms = reduce_parts(sz, same, far, near, notes)
-    *outs, flag = call_last(sz, plan, notes, firsts, terms, strips, partial)
+
+    def prepare(after):
+        return call_prepare(sz, plan, notes[0], call_turn([firsts[0]], [after])[0])
+
+    sent = [exchange(firsts[s], s) for s in range(1, T)]
+    terms, (*partial, strips) = reduce_parts(sz, same, far, near, notes, prepare)
+    *outs, flag = call_last(sz, plan, notes, sent, terms, strips, partial)
     return tuple(outs), flag
 
 

time: 63.6 us -> 62.4 us (0.981); the launches traced: 63.5 us -> 61.5 us
  starting transfers between devices: 25.6 us -> 23.5 us
  waiting for transfers between devices: 22.9 us -> 24.4 us
  Pallas kernels: 12.4 us -> 11.1 us
    ppermute x2, waiting for transfers between devices: 1.53 us -> 5.14 us  [exchange(): return lax.ppermute(array, 'tensor', [(i, (i + s) % T) for i in range(T)])]
    ppermute x2, waiting for transfers between devices: 2.37 us -> 0.01 us  [the longest x1 0.01 us: reduce_parts(): here_across = lax.ppermute(here, 'fsdp', swap)]
    ppermute x2, starting transfers between devices: 2.33 us -> 0.17 us  [the longest x1 0.17 us: reduce_parts(): here_across = lax.ppermute(here, 'fsdp', swap)]
    ppermute x2, starting transfers between devices: 2.03 us -> 3.7 us  [exchange(): return lax.ppermute(array, 'tensor', [(i, (i + s) % T) for i in range(T)])]
    ppermute x1, starting transfers between devices: 1.66 us -> 0.17 us  [gather_chunks(): same[sz.top] = lax.ppermute(a, 'fsdp', ahead)]
    pallas_call x1, Pallas kernels: 6.16 us -> 4.84 us  [call_compute(): pl.pallas_call(functools.partial(compute_kernel, sz), out_shape=out_shape...]
    ppermute x1, starting transfers between devices: 1.04 us -> 0.01 us  [reduce_parts(): lax.ppermute(a, 'fsdp', across(ahead))]
    ppermute x1, starting transfers between devices: 0.07 us -> 1.09 us  [reduce_parts(): far = lax.ppermute(far, 'fsdp', swap)]
  transfers between devices with their start and end apart: 32 -> 32, of which waited for: 13 -> 14; matrix products, arithmetic and copies ran while one was open for 2% -> 2% of each run, Pallas kernels for 4% -> 4%
where the time goes in v3:
time: 62.4 us; the launch traced here: 61.5 us
  waiting for transfers between devices  24.4 us (39%)
  starting transfers between devices  23.5 us (38%)
  Pallas kernels  11.1 us (18%)
  between operations  1.34 us (2%)
  local copies, waits for them, and re-layouts  0.8 us (1%)
    ppermute x6, waiting for transfers between devices, gather_chunks(): a, b = (lax.ppermute(a, 'fsdp', ahead), lax.ppermute(b, 'fsdp', behind))  11.9 us
    ppermute x6, starting transfers between devices, reduce_parts(): a, b = (lax.ppermute(a, 'fsdp', ahead), lax.ppermute(b, 'fsdp', behind))  7.27 us
    ppermute x6, starting transfers between devices, gather_chunks(): a, b = (lax.ppermute(a, 'fsdp', ahead), lax.ppermute(b, 'fsdp', behind))  6.3 us
    ppermute x2, waiting for transfers between devices, exchange(): return lax.ppermute(array, 'tensor', [(i, (i + s) % T) for i in range(T)])  5.14 us
    pallas_call x1, Pallas kernels, call_compute(): pl.pallas_call(functools.partial(compute_kernel, sz), out_shape=out_shape...  4.84 us
    ppermute x2, starting transfers between devices, exchange(): return lax.ppermute(array, 'tensor', [(i, (i + s) % T) for i in range(T)])  3.7 us
    ppermute x6, waiting for transfers between devices, reduce_parts(): a, b = (lax.ppermute(a, 'fsdp', ahead), lax.ppermute(b, 'fsdp', behind))  3.22 us
    pallas_call x1, Pallas kernels, call_last(): pl.pallas_call(functools.partial(last_kernel, sz), out_shape=[jax.ShapeDt...  2.49 us
  transfers between devices with their start and end apart: 32, of which 14 were waited for; matrix products, arithmetic and copies ran while one was open for 2% of the time, Pallas kernels for 4%

profile of v3, /device:TPU:0, one launch (start us, length us, event | category | flops | bytes accessed | tf_op | source)
XLA Modules:
  0.0 61.5 jit_solution(5585231040267173733)
XLA Ops:
  0.6 0.5 collective-permute-start.32
  1.2 0.1 collective-permute-start.33
  1.2 0.4 collective-permute-start.34
  1.7 0.8 %concatenate.3 = s32[101]{0:T(128)S(1)} concatenate(s32[32]{0:T(128)} %bitcast.9, s32[32]{0:T(128)} %bitcast.10, s32[32]{0:T(128)} %bitcast.11, s32[3]{0:T(128)} %bitcast.12, s32[1]{0:T(128)} %bitcast.4, s32[1]{0:T(128)} %bitcast.5), dimensions={0} | concatenate | bytes 808 | tf_op jit(solution)/shard_map/concatenate | solution.py:681
  2.4 0.0 collective-permute-done.32.refs_3_
  2.5 0.2 collective-permute-done.33.refs_4_
  2.6 0.2 collective-permute-done.34.refs_5_
  2.8 1.3 %plan.3 = (s32[32,128]{1,0:T(8,128)S(1)}, bf16[7,64,128]{2,1,0:T(8,128)(2,1)S(1)}, s32[1,128]{1,0:T(1,128)S(1)}) custom-call(s32[1,128]{1,0:T(1,128)S(1)} %pad_bitcast_fusion.own, bf16[1,2,128,128]{3,2,1,0:T(8,128)(2,1)} %refs_0_.1, bf16[1,2,128,128]{3,2,1,0:T(8,128)(2,1)} %refs_1_.1, bf16[1,2,128,128]{3,2,1,0:T(8,128)(2,1)} %refs_2_.1, ...), custom_call_target="tpu_custom_call" | custom-call | flops 1000000 | bytes 4000000 | tf_op jit(solution)/shard_map/plan/pallas_call | solution.py:485
  4.1 3.0 %collective-permute-start.36 = (bf16[7,64,128]{2,1,0:T(8,128)(2,1)S(1)}, bf16[7,64,128]{2,1,0:T(8,128)(2,1)S(1)}, u32[]{:S(2)}, u32[]{:S(2)}) collective-permute-start(bf16[7,64,128]{2,1,0:T(8,128)(2,1)S(1)} %get-tuple-element.76.refs_7_), channel_id=1, source_target_pairs={{0,8},{2,6},{8,16},{10,2},{16,24},{18,10},{24,28},{26,18},{28,20},... | collective-permute-start | bytes 344072 | tf_op jit(solution)/shard_map/ppermute | solution.py:599
  7.0 0.0 collective-permute-start.40
  7.1 3.2 %collective-permute-done.36.refs_5_ = bf16[7,64,128]{2,1,0:T(8,128)(2,1)S(1)} collective-permute-done((bf16[7,64,128]{2,1,0:T(8,128)(2,1)S(1)}, bf16[7,64,128]{2,1,0:T(8,128)(2,1)S(1)}, u32[]{:S(2)}, u32[]{:S(2)}) %collective-permute-start.36) | collective-permute-done | bytes 114720 | tf_op jit(solution)/shard_map/ppermute | solution.py:599
  10.3 2.1 %collective-permute-start.37 = (bf16[7,64,128]{2,1,0:T(8,128)(2,1)S(1)}, bf16[7,64,128]{2,1,0:T(8,128)(2,1)S(1)}, u32[]{:S(2)}, u32[]{:S(2)}) collective-permute-start(bf16[7,64,128]{2,1,0:T(8,128)(2,1)S(1)} %collective-permute-done.36.refs_5_), channel_id=1, source_target_pairs={{0,8},{2,6},{8,16},{10,2},{16,24},{18,10},{24,28},{26,18},{28,20},... | collective-permute-start | bytes 344072 | tf_op jit(solution)/shard_map/ppermute | solution.py:599
  12.4 0.3 collective-permute-start.41
  12.6 0.0 collective-permute-start.50
  12.6 0.5 collective-permute-start.48
  13.1 3.0 %collective-permute-done.37.refs_3_ = bf16[7,64,128]{2,1,0:T(8,128)(2,1)S(1)} collective-permute-done((bf16[7,64,128]{2,1,0:T(8,128)(2,1)S(1)}, bf16[7,64,128]{2,1,0:T(8,128)(2,1)S(1)}, u32[]{:S(2)}, u32[]{:S(2)}) %collective-permute-start.37) | collective-permute-done | bytes 114720 | tf_op jit(solution)/shard_map/ppermute | solution.py:599
  16.2 1.0 %collective-permute-start.38 = (bf16[7,64,128]{2,1,0:T(8,128)(2,1)S(1)}, bf16[7,64,128]{2,1,0:T(8,128)(2,1)S(1)}, u32[]{:S(2)}, u32[]{:S(2)}) collective-permute-start(bf16[7,64,128]{2,1,0:T(8,128)(2,1)S(1)} %collective-permute-done.37.refs_3_), channel_id=1, source_target_pairs={{0,8},{2,6},{8,16},{10,2},{16,24},{18,10},{24,28},{26,18},{28,20},... | collective-permute-start | bytes 344072 | tf_op jit(solution)/shard_map/ppermute | solution.py:599
  17.1 0.0 collective-permute-start.49
  17.1 1.1 %collective-permute-done.41.refs_4_ = bf16[7,64,128]{2,1,0:T(8,128)(2,1)S(1)} collective-permute-done((bf16[7,64,128]{2,1,0:T(8,128)(2,1)S(1)}, bf16[7,64,128]{2,1,0:T(8,128)(2,1)S(1)}, u32[]{:S(2)}, u32[]{:S(2)}) %collective-permute-start.41) | collective-permute-done | bytes 114720 | tf_op jit(solution)/shard_map/ppermute | solution.py:599
  18.2 0.0 collective-permute-start.42
  18.2 0.0 collective-permute-done.50.refs_15_
  18.2 0.8 %collective-permute-start.46 = (bf16[7,64,128]{2,1,0:T(8,128)(2,1)S(1)}, bf16[7,64,128]{2,1,0:T(8,128)(2,1)S(1)}, u32[]{:S(2)}, u32[]{:S(2)}) collective-permute-start(bf16[7,64,128]{2,1,0:T(8,128)(2,1)S(1)} %collective-permute-done.37.refs_3_), channel_id=1, source_target_pairs={{0,2},{2,0},{8,10},{10,8},{16,18},{18,16},{24,26},{26,24},{28,30},... | collective-permute-start | bytes 344072 | tf_op jit(solution)/shard_map/ppermute | solution.py:601
  19.1 0.0 collective-permute-done.48.refs_13_
  19.1 0.1 collective-permute-start.47
  19.1 2.6 %collective-permute-done.38.refs_1_ = bf16[7,64,128]{2,1,0:T(8,128)(2,1)S(1)} collective-permute-done((bf16[7,64,128]{2,1,0:T(8,128)(2,1)S(1)}, bf16[7,64,128]{2,1,0:T(8,128)(2,1)S(1)}, u32[]{:S(2)}, u32[]{:S(2)}) %collective-permute-start.38) | collective-permute-done | bytes 114720 | tf_op jit(solution)/shard_map/ppermute | solution.py:599
  21.8 0.2 collective-permute-start.39
  21.9 0.0 collective-permute-done.49.refs_14_
  21.9 2.0 %collective-permute-done.42.refs_2_ = bf16[7,64,128]{2,1,0:T(8,128)(2,1)S(1)} collective-permute-done((bf16[7,64,128]{2,1,0:T(8,128)(2,1)S(1)}, bf16[7,64,128]{2,1,0:T(8,128)(2,1)S(1)}, u32[]{:S(2)}, u32[]{:S(2)}) %collective-permute-start.42) | collective-permute-done | bytes 114720 | tf_op jit(solution)/shard_map/ppermute | solution.py:599
  23.9 0.0 collective-permute-start.44
  23.9 0.0 collective-permute-done.46.refs_11_
  23.9 0.5 collective-permute-start.45
  24.4 0.0 collective-permute-done.47.refs_12_
  24.4 2.1 %collective-permute-done.39.refs_0_ = bf16[7,64,128]{2,1,0:T(8,128)(2,1)S(1)} collective-permute-done((bf16[7,64,128]{2,1,0:T(8,128)(2,1)S(1)}, bf16[7,64,128]{2,1,0:T(8,128)(2,1)S(1)}, u32[]{:S(2)}, u32[]{:S(2)}) %collective-permute-start.39) | collective-permute-done | bytes 114720 | tf_op jit(solution)/shard_map/ppermute | solution.py:602
  26.6 0.0 collective-permute-done.45.refs_10_
  26.6 4.8 %compute.3 = (bf16[56,64,128]{2,1,0:T(8,128)(2,1)S(1)}, bf16[14,64,128]{2,1,0:T(8,128)(2,1)S(1)}, bf16[42,64,128]{2,1,0:T(8,128)(2,1)S(1)}, bf16[18,128,128]{2,1,0:T(8,128)(2,1)S(1)}, bf16[18,128,128]{2,1,0:T(8,128)(2,1)S(1)}) custom-call(s32[32,128]{1,0:T(8,128)S(1)} %get-tuple-element.74.plan, bf16[128,8192]{1,0:T(8,128)(2,1)} %tokens.1, ...), custom_call_target="tpu_custom_call" | custom-call | flops 1000000000 | bytes 20000000 | tf_op jit(solution)/shard_map/compute/pallas_call | solution.py:541
  31.4 1.1 %collective-permute-start.52 = (bf16[14,64,128]{2,1,0:T(8,128)(2,1)S(1)}, bf16[14,64,128]{2,1,0:T(8,128)(2,1)S(1)}, u32[]{:S(2)}, u32[]{:S(2)}) collective-permute-start(bf16[14,64,128]{2,1,0:T(8,128)(2,1)S(1)} %get-tuple-element.80), channel_id=1, source_target_pairs={{0,2},{2,0},{8,10},{10,8},{16,18},{18,16},{24,26},{26,24},{28,30},... | collective-permute-start | bytes 688136 | tf_op jit(solution)/shard_map/ppermute | solution.py:610
  32.5 1.1 %collective-permute-done.52.__1_ = bf16[14,64,128]{2,1,0:T(8,128)(2,1)S(1)} collective-permute-done((bf16[14,64,128]{2,1,0:T(8,128)(2,1)S(1)}, bf16[14,64,128]{2,1,0:T(8,128)(2,1)S(1)}, u32[]{:S(2)}, u32[]{:S(2)}) %collective-permute-start.52) | collective-permute-done | bytes 229408 | tf_op jit(solution)/shard_map/ppermute | solution.py:610
  33.6 0.4 collective-permute-start.53
  34.0 0.1 add_convert_fusion.13
  34.1 0.5 collective-permute-start.54
  34.6 1.6 %collective-permute-start.55 = (bf16[7,64,128]{2,1,0:T(8,128)(2,1)S(1)}, bf16[7,64,128]{2,1,0:T(8,128)(2,1)S(1)}, u32[]{:S(2)}, u32[]{:S(2)}) collective-permute-start(bf16[7,64,128]{2,1,0:T(8,128)(2,1)S(1)} %get-tuple-element.82), channel_id=1, source_target_pairs={{0,4},{2,10},{8,0},{10,18},{16,8},{18,26},{24,16},{26,30},{28,24},... | collective-permute-start | bytes 344072 | tf_op jit(solution)/shard_map/ppermute | solution.py:627
  36.2 2.2 %collective-permute-start.35 = (s32[1,128]{1,0:T(1,128)S(1)}, s32[1,128]{1,0:T(1,128)S(1)}, u32[]{:S(2)}, u32[]{:S(2)}) collective-permute-start(s32[1,128]{1,0:T(1,128)S(1)} %get-tuple-element.75), channel_id=1, source_target_pairs={{0,1},{1,0},{2,3},{3,2},{4,5},{5,4},{6,7},{7,6},{8,9},{9,8},{10,11... | collective-permute-start | bytes 1544 | tf_op jit(solution)/shard_map/ppermute | solution.py:651
  38.4 1.5 %collective-permute-done.35.__2_.note.refs_0_ = s32[1,128]{1,0:T(1,128)S(1)} collective-permute-done((s32[1,128]{1,0:T(1,128)S(1)}, s32[1,128]{1,0:T(1,128)S(1)}, u32[]{:S(2)}, u32[]{:S(2)}) %collective-permute-start.35) | collective-permute-done | bytes 544 | tf_op jit(solution)/shard_map/ppermute | solution.py:651
  39.9 0.0 collective-permute-done.54.__0_
  39.9 0.0 collective-permute-done.55.__1_
  40.0 0.1 add_convert_fusion.12.__1_
  40.0 0.1 add_convert_fusion.11
  40.1 0.2 collective-permute-start.57
  40.3 1.8 %collective-permute-start.56 = (bf16[7,64,128]{2,1,0:T(8,128)(2,1)S(1)}, bf16[7,64,128]{2,1,0:T(8,128)(2,1)S(1)}, u32[]{:S(2)}, u32[]{:S(2)}) collective-permute-start(bf16[7,64,128]{2,1,0:T(8,128)(2,1)S(1)} %add_convert_fusion.12.__1_), channel_id=1, source_target_pairs={{0,8},{2,6},{8,16},{10,2},{16,24},{18,10},{24,28},{26,18},{28,20},... | collective-permute-start | bytes 344072 | tf_op jit(solution)/shard_map/ppermute | solution.py:627
  42.1 1.5 %collective-permute-start.51 = (bf16[18,128,128]{2,1,0:T(8,128)(2,1)S(1)}, bf16[18,128,128]{2,1,0:T(8,128)(2,1)S(1)}, u32[]{:S(2)}, u32[]{:S(2)}) collective-permute-start(bf16[18,128,128]{2,1,0:T(8,128)(2,1)S(1)} %get-tuple-element.77), channel_id=1, source_target_pairs={{0,1},{1,0},{2,3},{3,2},{4,5},{5,4},{6,7},{7,6},{8,9},{9,8},{10,11... | collective-permute-start | bytes 1769480 | tf_op jit(solution)/shard_map/ppermute | solution.py:651
  43.6 1.2 %collective-permute-start.59 = (bf16[7,64,128]{2,1,0:T(8,128)(2,1)S(1)}, bf16[7,64,128]{2,1,0:T(8,128)(2,1)S(1)}, u32[]{:S(2)}, u32[]{:S(2)}) collective-permute-start(bf16[7,64,128]{2,1,0:T(8,128)(2,1)S(1)} %get-tuple-element.109.__1_), channel_id=1, source_target_pairs={{0,4},{2,10},{8,0},{10,18},{16,8},{18,26},{24,16},{26,30},{28,24},... | collective-permute-start | bytes 344072 | tf_op jit(solution)/shard_map/ppermute | solution.py:627
  44.8 0.0 collective-permute-done.57.__1_.refs_5_
  44.8 2.5 %prepare.3 = (bf16[128,4096]{1,0:T(8,128)(2,1)}, bf16[128,4096]{1,0:T(8,128)(2,1)}, bf16[18,128,128]{2,1,0:T(8,128)(2,1)S(1)}) custom-call(s32[32,128]{1,0:T(8,128)S(1)} %get-tuple-element.74.plan, s32[1,128]{1,0:T(1,128)S(1)} %collective-permute-done.35.__2_.note.refs_0_, bf16[18,128,128]{2,1,0:T(8,128)(2,1)S(1)} %turn.24.first), custom_call_target="tpu_custom_call" | custom-call | flops 1000000 | bytes 6000000 | tf_op jit(solution)/shard_map/prepare/pallas_call | solution.py:558
  47.2 0.1 add_convert_fusion.10.__1_
  47.3 0.9 %collective-permute-start.58 = (bf16[7,64,128]{2,1,0:T(8,128)(2,1)S(1)}, bf16[7,64,128]{2,1,0:T(8,128)(2,1)S(1)}, u32[]{:S(2)}, u32[]{:S(2)}) collective-permute-start(bf16[7,64,128]{2,1,0:T(8,128)(2,1)S(1)} %add_convert_fusion.10.__1_), channel_id=1, source_target_pairs={{0,8},{2,6},{8,16},{10,2},{16,24},{18,10},{24,28},{26,18},{28,20},... | collective-permute-start | bytes 344072 | tf_op jit(solution)/shard_map/ppermute | solution.py:627
  48.2 0.2 collective-permute-done.59.__0_
  48.4 0.1 add_convert_fusion.9.__1_
  48.4 1.2 %collective-permute-start.61 = (bf16[7,64,128]{2,1,0:T(8,128)(2,1)S(1)}, bf16[7,64,128]{2,1,0:T(8,128)(2,1)S(1)}, u32[]{:S(2)}, u32[]{:S(2)}) collective-permute-start(bf16[7,64,128]{2,1,0:T(8,128)(2,1)S(1)} %add_convert_fusion.9.__1_), channel_id=1, source_target_pairs={{0,4},{2,10},{8,0},{10,18},{16,8},{18,26},{24,16},{26,30},{28,24},... | collective-permute-start | bytes 344072 | tf_op jit(solution)/shard_map/ppermute | solution.py:627
  49.7 3.0 %collective-permute-done.58.__0_ = bf16[7,64,128]{2,1,0:T(8,128)(2,1)S(1)} collective-permute-done((bf16[7,64,128]{2,1,0:T(8,128)(2,1)S(1)}, bf16[7,64,128]{2,1,0:T(8,128)(2,1)S(1)}, u32[]{:S(2)}, u32[]{:S(2)}) %collective-permute-start.58) | collective-permute-done | bytes 114720 | tf_op jit(solution)/shard_map/ppermute | solution.py:627
  52.7 0.1 add_convert_fusion.8
  52.8 1.4 %collective-permute-start.60 = (bf16[7,64,128]{2,1,0:T(8,128)(2,1)S(1)}, bf16[7,64,128]{2,1,0:T(8,128)(2,1)S(1)}, u32[]{:S(2)}, u32[]{:S(2)}) collective-permute-start(bf16[7,64,128]{2,1,0:T(8,128)(2,1)S(1)} %add_convert_fusion.8), channel_id=1, source_target_pairs={{0,8},{2,6},{8,16},{10,2},{16,24},{18,10},{24,28},{26,18},{28,20},... | collective-permute-start | bytes 344072 | tf_op jit(solution)/shard_map/ppermute | solution.py:635
  54.2 3.6 %collective-permute-done.51.refs_1_ = bf16[18,128,128]{2,1,0:T(8,128)(2,1)S(1)} collective-permute-done((bf16[18,128,128]{2,1,0:T(8,128)(2,1)S(1)}, bf16[18,128,128]{2,1,0:T(8,128)(2,1)S(1)}, u32[]{:S(2)}, u32[]{:S(2)}) %collective-permute-start.51) | collective-permute-done | bytes 589856 | tf_op jit(solution)/shard_map/ppermute | solution.py:651
  57.8 0.6 collective-permute-done.62.refs_6_
  58.4 2.5 %last.3 = (bf16[128,4096]{1,0:T(8,128)(2,1)}, bf16[128,4096]{1,0:T(8,128)(2,1)}, bf16[1,2,128,128]{3,2,1,0:T(8,128)(2,1)}, bf16[1,2,128,128]{3,2,1,0:T(8,128)(2,...) custom-call(s32[32,128]{1,0:T(8,128)S(1)} %get-tuple-element.74.plan, ...), custom_call_target="tpu_custom_call", output_to_operand_aliasing={{0}: (10, {}), {1}: (11, {})} | custom-call | flops 1000000 | bytes 3000000 | tf_op jit(solution)/shard_map/last/pallas_call | solution.py:572
  (26 shorter events, 0.1 us)
Async XLA Ops:
  0.6 1.8 %collective-permute-start.32 = (bf16[1,2,128,128]{3,2,1,0:T(8,128)(2,1)}, bf16[1,2,128,128]{3,2,1,0:T(8,128)(2,1)S(1)}, u32[]{:S(2)}, u32[]{:S(2)}) collective-permute-start(bf16[1,2,128,128]{3,2,1,0:T(8,128)(2,1)} %refs_0_.1), channel_id=1, source_target_pairs={{0,2},{2,0},{8,10},{10,8},{16,18},{18,16},{24,26},{26,24},{28,30},... | collective-permute-start | bytes 196616 | tf_op jit(solution)/shard_map/ppermute | solution.py:647
  1.2 1.5 %collective-permute-start.33 = (bf16[1,2,128,128]{3,2,1,0:T(8,128)(2,1)}, bf16[1,2,128,128]{3,2,1,0:T(8,128)(2,1)S(1)}, u32[]{:S(2)}, u32[]{:S(2)}) collective-permute-start(bf16[1,2,128,128]{3,2,1,0:T(8,128)(2,1)} %refs_1_.1), channel_id=1, source_target_pairs={{0,2},{2,0},{8,10},{10,8},{16,18},{18,16},{24,26},{26,24},{28,30},... | collective-permute-start | bytes 196616 | tf_op jit(solution)/shard_map/ppermute | solution.py:647
  1.2 1.5 %collective-permute-start.34 = (bf16[1,2,128,128]{3,2,1,0:T(8,128)(2,1)}, bf16[1,2,128,128]{3,2,1,0:T(8,128)(2,1)S(1)}, u32[]{:S(2)}, u32[]{:S(2)}) collective-permute-start(bf16[1,2,128,128]{3,2,1,0:T(8,128)(2,1)} %refs_2_.1), channel_id=1, source_target_pairs={{0,2},{2,0},{8,10},{10,8},{16,18},{18,16},{24,26},{26,24},{28,30},... | collective-permute-start | bytes 196616 | tf_op jit(solution)/shard_map/ppermute | solution.py:647
  4.1 6.2 %collective-permute-start.36 = (bf16[7,64,128]{2,1,0:T(8,128)(2,1)S(1)}, bf16[7,64,128]{2,1,0:T(8,128)(2,1)S(1)}, u32[]{:S(2)}, u32[]{:S(2)}) collective-permute-start(bf16[7,64,128]{2,1,0:T(8,128)(2,1)S(1)} %get-tuple-element.76.refs_7_), channel_id=1, source_target_pairs={{0,8},{2,6},{8,16},{10,2},{16,24},{18,10},{24,28},{26,18},{28,20},... | collective-permute-start | bytes 344072 | tf_op jit(solution)/shard_map/ppermute | solution.py:599
  7.0 5.3 %collective-permute-start.40 = (bf16[7,64,128]{2,1,0:T(8,128)(2,1)S(1)}, bf16[7,64,128]{2,1,0:T(8,128)(2,1)S(1)}, u32[]{:S(2)}, u32[]{:S(2)}) collective-permute-start(bf16[7,64,128]{2,1,0:T(8,128)(2,1)S(1)} %get-tuple-element.76.refs_7_), channel_id=1, source_target_pairs={{0,4},{2,10},{8,0},{10,18},{16,8},{18,26},{24,16},{26,30},{28,24},... | collective-permute-start | bytes 344072 | tf_op jit(solution)/shard_map/ppermute | solution.py:599
  10.3 5.9 %collective-permute-start.37 = (bf16[7,64,128]{2,1,0:T(8,128)(2,1)S(1)}, bf16[7,64,128]{2,1,0:T(8,128)(2,1)S(1)}, u32[]{:S(2)}, u32[]{:S(2)}) collective-permute-start(bf16[7,64,128]{2,1,0:T(8,128)(2,1)S(1)} %collective-permute-done.36.refs_5_), channel_id=1, source_target_pairs={{0,8},{2,6},{8,16},{10,2},{16,24},{18,10},{24,28},{26,18},{28,20},... | collective-permute-start | bytes 344072 | tf_op jit(solution)/shard_map/ppermute | solution.py:599
  12.4 5.9 %collective-permute-start.41 = (bf16[7,64,128]{2,1,0:T(8,128)(2,1)S(1)}, bf16[7,64,128]{2,1,0:T(8,128)(2,1)S(1)}, u32[]{:S(2)}, u32[]{:S(2)}) collective-permute-start(bf16[7,64,128]{2,1,0:T(8,128)(2,1)S(1)} %collective-permute-done.40.refs_6_), channel_id=1, source_target_pairs={{0,4},{2,10},{8,0},{10,18},{16,8},{18,26},{24,16},{26,30},{28,24},... | collective-permute-start | bytes 344072 | tf_op jit(solution)/shard_map/ppermute | solution.py:599
  12.6 5.6 %collective-permute-start.50 = (bf16[7,64,128]{2,1,0:T(8,128)(2,1)S(1)}, bf16[7,64,128]{2,1,0:T(8,128)(2,1)S(1)}, u32[]{:S(2)}, u32[]{:S(2)}) collective-permute-start(bf16[7,64,128]{2,1,0:T(8,128)(2,1)S(1)} %get-tuple-element.76.refs_7_), channel_id=1, source_target_pairs={{0,2},{2,0},{8,10},{10,8},{16,18},{18,16},{24,26},{26,24},{28,30},... | collective-permute-start | bytes 344072 | tf_op jit(solution)/shard_map/ppermute | solution.py:601
  12.6 6.4 %collective-permute-start.48 = (bf16[7,64,128]{2,1,0:T(8,128)(2,1)S(1)}, bf16[7,64,128]{2,1,0:T(8,128)(2,1)S(1)}, u32[]{:S(2)}, u32[]{:S(2)}) collective-permute-start(bf16[7,64,128]{2,1,0:T(8,128)(2,1)S(1)} %collective-permute-done.36.refs_5_), channel_id=1, source_target_pairs={{0,2},{2,0},{8,10},{10,8},{16,18},{18,16},{24,26},{26,24},{28,30},... | collective-permute-start | bytes 344072 | tf_op jit(solution)/shard_map/ppermute | solution.py:601
  16.2 5.6 %collective-permute-start.38 = (bf16[7,64,128]{2,1,0:T(8,128)(2,1)S(1)}, bf16[7,64,128]{2,1,0:T(8,128)(2,1)S(1)}, u32[]{:S(2)}, u32[]{:S(2)}) collective-permute-start(bf16[7,64,128]{2,1,0:T(8,128)(2,1)S(1)} %collective-permute-done.37.refs_3_), channel_id=1, source_target_pairs={{0,8},{2,6},{8,16},{10,2},{16,24},{18,10},{24,28},{26,18},{28,20},... | collective-permute-start | bytes 344072 | tf_op jit(solution)/shard_map/ppermute | solution.py:599
  17.1 4.8 %collective-permute-start.49 = (bf16[7,64,128]{2,1,0:T(8,128)(2,1)S(1)}, bf16[7,64,128]{2,1,0:T(8,128)(2,1)S(1)}, u32[]{:S(2)}, u32[]{:S(2)}) collective-permute-start(bf16[7,64,128]{2,1,0:T(8,128)(2,1)S(1)} %collective-permute-done.40.refs_6_), channel_id=1, source_target_pairs={{0,2},{2,0},{8,10},{10,8},{16,18},{18,16},{24,26},{26,24},{28,30},... | collective-permute-start | bytes 344072 | tf_op jit(solution)/shard_map/ppermute | solution.py:601
  18.2 5.7 %collective-permute-start.42 = (bf16[7,64,128]{2,1,0:T(8,128)(2,1)S(1)}, bf16[7,64,128]{2,1,0:T(8,128)(2,1)S(1)}, u32[]{:S(2)}, u32[]{:S(2)}) collective-permute-start(bf16[7,64,128]{2,1,0:T(8,128)(2,1)S(1)} %collective-permute-done.41.refs_4_), channel_id=1, source_target_pairs={{0,4},{2,10},{8,0},{10,18},{16,8},{18,26},{24,16},{26,30},{28,24},... | collective-permute-start | bytes 344072 | tf_op jit(solution)/shard_map/ppermute | solution.py:599
  18.2 5.7 %collective-permute-start.46 = (bf16[7,64,128]{2,1,0:T(8,128)(2,1)S(1)}, bf16[7,64,128]{2,1,0:T(8,128)(2,1)S(1)}, u32[]{:S(2)}, u32[]{:S(2)}) collective-permute-start(bf16[7,64,128]{2,1,0:T(8,128)(2,1)S(1)} %collective-permute-done.37.refs_3_), channel_id=1, source_target_pairs={{0,2},{2,0},{8,10},{10,8},{16,18},{18,16},{24,26},{26,24},{28,30},... | collective-permute-start | bytes 344072 | tf_op jit(solution)/shard_map/ppermute | solution.py:601
  19.1 5.4 %collective-permute-start.47 = (bf16[7,64,128]{2,1,0:T(8,128)(2,1)S(1)}, bf16[7,64,128]{2,1,0:T(8,128)(2,1)S(1)}, u32[]{:S(2)}, u32[]{:S(2)}) collective-permute-start(bf16[7,64,128]{2,1,0:T(8,128)(2,1)S(1)} %collective-permute-done.41.refs_4_), channel_id=1, source_target_pairs={{0,2},{2,0},{8,10},{10,8},{16,18},{18,16},{24,26},{26,24},{28,30},... | collective-permute-start | bytes 344072 | tf_op jit(solution)/shard_map/ppermute | solution.py:601
  21.8 4.8 %collective-permute-start.39 = (bf16[7,64,128]{2,1,0:T(8,128)(2,1)S(1)}, bf16[7,64,128]{2,1,0:T(8,128)(2,1)S(1)}, u32[]{:S(2)}, u32[]{:S(2)}) collective-permute-start(bf16[7,64,128]{2,1,0:T(8,128)(2,1)S(1)} %collective-permute-done.38.refs_1_), channel_id=1, source_target_pairs={{0,8},{2,6},{8,16},{10,2},{16,24},{18,10},{24,28},{26,18},{28,20},... | collective-permute-start | bytes 344072 | tf_op jit(solution)/shard_map/ppermute | solution.py:602
  21.9 4.6 %collective-permute-start.43 = (bf16[7,64,128]{2,1,0:T(8,128)(2,1)S(1)}, bf16[7,64,128]{2,1,0:T(8,128)(2,1)S(1)}, u32[]{:S(2)}, u32[]{:S(2)}) collective-permute-start(bf16[7,64,128]{2,1,0:T(8,128)(2,1)S(1)} %collective-permute-done.38.refs_1_), channel_id=1, source_target_pairs={{0,10},{2,4},{8,18},{10,0},{16,26},{18,8},{24,30},{26,16},{28,22},... | collective-permute-start | bytes 344072 | tf_op jit(solution)/shard_map/ppermute | solution.py:603
  23.9 2.6 %collective-permute-start.44 = (bf16[7,64,128]{2,1,0:T(8,128)(2,1)S(1)}, bf16[7,64,128]{2,1,0:T(8,128)(2,1)S(1)}, u32[]{:S(2)}, u32[]{:S(2)}) collective-permute-start(bf16[7,64,128]{2,1,0:T(8,128)(2,1)S(1)} %collective-permute-done.38.refs_1_), channel_id=1, source_target_pairs={{0,2},{2,0},{8,10},{10,8},{16,18},{18,16},{24,26},{26,24},{28,30},... | collective-permute-start | bytes 344072 | tf_op jit(solution)/shard_map/ppermute | solution.py:601
  23.9 2.6 %collective-permute-start.45 = (bf16[7,64,128]{2,1,0:T(8,128)(2,1)S(1)}, bf16[7,64,128]{2,1,0:T(8,128)(2,1)S(1)}, u32[]{:S(2)}, u32[]{:S(2)}) collective-permute-start(bf16[7,64,128]{2,1,0:T(8,128)(2,1)S(1)} %collective-permute-done.42.refs_2_), channel_id=1, source_target_pairs={{0,2},{2,0},{8,10},{10,8},{16,18},{18,16},{24,26},{26,24},{28,30},... | collective-permute-start | bytes 344072 | tf_op jit(solution)/shard_map/ppermute | solution.py:601
  31.4 2.2 %collective-permute-start.52 = (bf16[14,64,128]{2,1,0:T(8,128)(2,1)S(1)}, bf16[14,64,128]{2,1,0:T(8,128)(2,1)S(1)}, u32[]{:S(2)}, u32[]{:S(2)}) collective-permute-start(bf16[14,64,128]{2,1,0:T(8,128)(2,1)S(1)} %get-tuple-element.80), channel_id=1, source_target_pairs={{0,2},{2,0},{8,10},{10,8},{16,18},{18,16},{24,26},{26,24},{28,30},... | collective-permute-start | bytes 688136 | tf_op jit(solution)/shard_map/ppermute | solution.py:610
  33.6 6.3 %collective-permute-start.53 = (bf16[42,64,128]{2,1,0:T(8,128)(2,1)S(1)}, bf16[42,64,128]{2,1,0:T(8,128)(2,1)S(1)}, u32[]{:S(2)}, u32[]{:S(2)}) collective-permute-start(bf16[42,64,128]{2,1,0:T(8,128)(2,1)S(1)} %turn.21), channel_id=1, source_target_pairs={{0,2},{2,0},{8,10},{10,8},{16,18},{18,16},{24,26},{26,24},{28,30},... | collective-permute-start | bytes 2064392 | tf_op jit(solution)/shard_map/ppermute | solution.py:611
  34.1 5.9 %collective-permute-start.54 = (bf16[7,64,128]{2,1,0:T(8,128)(2,1)S(1)}, bf16[7,64,128]{2,1,0:T(8,128)(2,1)S(1)}, u32[]{:S(2)}, u32[]{:S(2)}) collective-permute-start(bf16[7,64,128]{2,1,0:T(8,128)(2,1)S(1)} %get-tuple-element.81), channel_id=1, source_target_pairs={{0,8},{2,6},{8,16},{10,2},{16,24},{18,10},{24,28},{26,18},{28,20},... | collective-permute-start | bytes 344072 | tf_op jit(solution)/shard_map/ppermute | solution.py:627
  34.6 5.4 %collective-permute-start.55 = (bf16[7,64,128]{2,1,0:T(8,128)(2,1)S(1)}, bf16[7,64,128]{2,1,0:T(8,128)(2,1)S(1)}, u32[]{:S(2)}, u32[]{:S(2)}) collective-permute-start(bf16[7,64,128]{2,1,0:T(8,128)(2,1)S(1)} %get-tuple-element.82), channel_id=1, source_target_pairs={{0,4},{2,10},{8,0},{10,18},{16,8},{18,26},{24,16},{26,30},{28,24},... | collective-permute-start | bytes 344072 | tf_op jit(solution)/shard_map/ppermute | solution.py:627
  36.2 3.8 %collective-permute-start.35 = (s32[1,128]{1,0:T(1,128)S(1)}, s32[1,128]{1,0:T(1,128)S(1)}, u32[]{:S(2)}, u32[]{:S(2)}) collective-permute-start(s32[1,128]{1,0:T(1,128)S(1)} %get-tuple-element.75), channel_id=1, source_target_pairs={{0,1},{1,0},{2,3},{3,2},{4,5},{5,4},{6,7},{7,6},{8,9},{9,8},{10,11... | collective-permute-start | bytes 1544 | tf_op jit(solution)/shard_map/ppermute | solution.py:651
  40.1 4.6 %collective-permute-start.57 = (bf16[7,64,128]{2,1,0:T(8,128)(2,1)S(1)}, bf16[7,64,128]{2,1,0:T(8,128)(2,1)S(1)}, u32[]{:S(2)}, u32[]{:S(2)}) collective-permute-start(bf16[7,64,128]{2,1,0:T(8,128)(2,1)S(1)} %get-tuple-element.110.refs_2_), channel_id=1, source_target_pairs={{0,2},{2,0},{8,10},{10,8},{16,18},{18,16},{24,26},{26,24},{28,30},... | collective-permute-start | bytes 344072 | tf_op jit(solution)/shard_map/ppermute | solution.py:623
  40.3 7.0 %collective-permute-start.56 = (bf16[7,64,128]{2,1,0:T(8,128)(2,1)S(1)}, bf16[7,64,128]{2,1,0:T(8,128)(2,1)S(1)}, u32[]{:S(2)}, u32[]{:S(2)}) collective-permute-start(bf16[7,64,128]{2,1,0:T(8,128)(2,1)S(1)} %add_convert_fusion.12.__1_), channel_id=1, source_target_pairs={{0,8},{2,6},{8,16},{10,2},{16,24},{18,10},{24,28},{26,18},{28,20},... | collective-permute-start | bytes 344072 | tf_op jit(solution)/shard_map/ppermute | solution.py:627
  42.1 15.7 %collective-permute-start.51 = (bf16[18,128,128]{2,1,0:T(8,128)(2,1)S(1)}, bf16[18,128,128]{2,1,0:T(8,128)(2,1)S(1)}, u32[]{:S(2)}, u32[]{:S(2)}) collective-permute-start(bf16[18,128,128]{2,1,0:T(8,128)(2,1)S(1)} %get-tuple-element.77), channel_id=1, source_target_pairs={{0,1},{1,0},{2,3},{3,2},{4,5},{5,4},{6,7},{7,6},{8,9},{9,8},{10,11... | collective-permute-start | bytes 1769480 | tf_op jit(solution)/shard_map/ppermute | solution.py:651
  43.6 4.8 %collective-permute-start.59 = (bf16[7,64,128]{2,1,0:T(8,128)(2,1)S(1)}, bf16[7,64,128]{2,1,0:T(8,128)(2,1)S(1)}, u32[]{:S(2)}, u32[]{:S(2)}) collective-permute-start(bf16[7,64,128]{2,1,0:T(8,128)(2,1)S(1)} %get-tuple-element.109.__1_), channel_id=1, source_target_pairs={{0,4},{2,10},{8,0},{10,18},{16,8},{18,26},{24,16},{26,30},{28,24},... | collective-permute-start | bytes 344072 | tf_op jit(solution)/shard_map/ppermute | solution.py:627
  47.3 5.4 %collective-permute-start.58 = (bf16[7,64,128]{2,1,0:T(8,128)(2,1)S(1)}, bf16[7,64,128]{2,1,0:T(8,128)(2,1)S(1)}, u32[]{:S(2)}, u32[]{:S(2)}) collective-permute-start(bf16[7,64,128]{2,1,0:T(8,128)(2,1)S(1)} %add_convert_fusion.10.__1_), channel_id=1, source_target_pairs={{0,8},{2,6},{8,16},{10,2},{16,24},{18,10},{24,28},{26,18},{28,20},... | collective-permute-start | bytes 344072 | tf_op jit(solution)/shard_map/ppermute | solution.py:627
  48.4 9.4 %collective-permute-start.61 = (bf16[7,64,128]{2,1,0:T(8,128)(2,1)S(1)}, bf16[7,64,128]{2,1,0:T(8,128)(2,1)S(1)}, u32[]{:S(2)}, u32[]{:S(2)}) collective-permute-start(bf16[7,64,128]{2,1,0:T(8,128)(2,1)S(1)} %add_convert_fusion.9.__1_), channel_id=1, source_target_pairs={{0,4},{2,10},{8,0},{10,18},{16,8},{18,26},{24,16},{26,30},{28,24},... | collective-permute-start | bytes 344072 | tf_op jit(solution)/shard_map/ppermute | solution.py:627
  49.7 8.1 %collective-permute-start.63 = (bf16[7,64,128]{2,1,0:T(8,128)(2,1)S(1)}, bf16[7,64,128]{2,1,0:T(8,128)(2,1)S(1)}, u32[]{:S(2)}, u32[]{:S(2)}) collective-permute-start(bf16[7,64,128]{2,1,0:T(8,128)(2,1)S(1)} %add_convert_fusion.9.__1_), channel_id=1, source_target_pairs={{0,6},{2,8},{8,2},{10,16},{16,10},{18,24},{24,18},{26,28},{28,26},... | collective-permute-start | bytes 344072 | tf_op jit(solution)/shard_map/ppermute | solution.py:639
  52.8 5.1 %collective-permute-start.60 = (bf16[7,64,128]{2,1,0:T(8,128)(2,1)S(1)}, bf16[7,64,128]{2,1,0:T(8,128)(2,1)S(1)}, u32[]{:S(2)}, u32[]{:S(2)}) collective-permute-start(bf16[7,64,128]{2,1,0:T(8,128)(2,1)S(1)} %add_convert_fusion.8), channel_id=1, source_target_pairs={{0,8},{2,6},{8,16},{10,2},{16,24},{18,10},{24,28},{26,18},{28,20},... | collective-permute-start | bytes 344072 | tf_op jit(solution)/shard_map/ppermute | solution.py:635
  54.2 4.2 %collective-permute-start.62 = (bf16[7,64,128]{2,1,0:T(8,128)(2,1)S(1)}, bf16[7,64,128]{2,1,0:T(8,128)(2,1)S(1)}, u32[]{:S(2)}, u32[]{:S(2)}) collective-permute-start(bf16[7,64,128]{2,1,0:T(8,128)(2,1)S(1)} %add_convert_fusion.8), channel_id=1, source_target_pairs={{0,10},{2,4},{8,18},{10,0},{16,26},{18,8},{24,30},{26,16},{28,22},... | collective-permute-start | bytes 344072 | tf_op jit(solution)/shard_map/ppermute | solution.py:638
  58.4 3.1 %copy-start = (bf16[1,2,128,128]{3,2,1,0:T(8,128)(2,1)S(1)}, bf16[1,2,128,128]{3,2,1,0:T(8,128)(2,1)}, u32[]{:S(2)}) copy-start(bf16[1,2,128,128]{3,2,1,0:T(8,128)(2,1)} %refs_0_.1) | copy-start | bytes 196612
  58.4 3.1 %copy-start.1 = (bf16[1,2,128,128]{3,2,1,0:T(8,128)(2,1)S(1)}, bf16[1,2,128,128]{3,2,1,0:T(8,128)(2,1)}, u32[]{:S(2)}) copy-start(bf16[1,2,128,128]{3,2,1,0:T(8,128)(2,1)} %refs_1_.1) | copy-start | bytes 196612
  58.4 3.1 %copy-start.2 = (bf16[1,2,128,128]{3,2,1,0:T(8,128)(2,1)S(1)}, bf16[1,2,128,128]{3,2,1,0:T(8,128)(2,1)}, u32[]{:S(2)}) copy-start(bf16[1,2,128,128]{3,2,1,0:T(8,128)(2,1)} %refs_2_.1) | copy-start | bytes 196612

commit v4 on v3

--- a/solution.py
+++ b/solution.py
@@ -13,6 +13,7 @@
 FIRST_SEND = 18
 LEAN_SLOTS = 7
 ROWS = BLK // 2
+PIECE = 3
 SMALL = 4 * 1024 * 1024
 PART, STRIP, CIDX, CWAS, OIDX, OWAS = range(6)
 FIELDS = 6
@@ -346,7 +347,8 @@
         ref, at = (far, j) if j < sz.far else (near, j - sz.far)
         outs.append(pltpu.make_async_copy(
             parts.at[pl.ds(sz.place_across(d), sz.keep), sides[1]], ref.at[pl.ds(at * sz.keep, sz.keep)], sems.at[j]))
-    outs.append(pltpu.make_async_copy(parts.at[pl.ds(0, sz.blocks), sides[0]], same, sems.at[sz.ring]))
+        mine = pl.ds(j * sz.keep, sz.keep)
+        outs.append(pltpu.make_async_copy(parts.at[mine, sides[0]], same.at[mine], sems.at[sz.ring + j]))
     for c in outs:
         c.start()
 
@@ -364,9 +366,12 @@
             stage[s * sz.first + i] = out_acc[plan[LISTS_ROW + 2 * s, i]].astype(jnp.bfloat16)
 
         lax.fori_loop(0, jnp.minimum(plan[HEAD_ROW, HEAD_LISTS + s], sz.first), staged, None)
-        copy = pltpu.make_async_copy(stage.at[pl.ds(s * sz.first, sz.first)], firsts[s], sems.at[sz.ring + 1 + s])
-        copy.start()
-        outs.append(copy)
+        for lo in range(0, sz.first, PIECE):
+            n = min(PIECE, sz.first - lo)
+            piece = stage.at[pl.ds(s * sz.first + lo, n)]
+            copy = pltpu.make_async_copy(piece, firsts[s].at[pl.ds(lo, n)], sems.at[len(outs)])
+            copy.start()
+            outs.append(copy)
     for c in outs:
         c.wait()
 
@@ -413,7 +418,7 @@
     firsts, refs = refs[:T - 1], refs[T - 1:]
     mine, theirs, held_strips, refs = refs[:3], refs[3:6], refs[6], refs[9:]
     outputs, input_grads, grads, flag = refs[0], refs[1], refs[2:5], refs[5]
-    strips, read_sems, write_sems = refs[6:]
+    strips, arrived, read_sems, write_sems, arrive_sems = refs[6:]
     over = plan[HEAD_ROW, HEAD_OVER]
     for note in notes:
         over = jnp.maximum(over, note[0, sz.note_over])
@@ -433,13 +438,20 @@
     def loop(s, body):
         lax.fori_loop(0, jnp.minimum(notes[s][0, sz.note_n], sz.first), lambda i, _: body(i), None)
 
+    def fetch(s, i, act):
+        act(pltpu.make_async_copy(firsts[s].at[i], arrived.at[i], arrive_sems.at[i]))
+        if s:
+            move(s, i, False, act)
+        else:
+            act(pltpu.make_async_copy(held_strips.at[i], strips.at[i], read_sems.at[i]))
+
     def begin(s):
-        loop(s, lambda i: move(s, i, False, lambda c: c.start()))
+        loop(s, lambda i: fetch(s, i, lambda c: c.start()))
 
     def add(s):
         def step(i):
-            move(s, i, False, lambda c: c.wait())
-            value = strips[i].astype(jnp.float32) + firsts[s][i].astype(jnp.float32)
+            fetch(s, i, lambda c: c.wait())
+            value = strips[i].astype(jnp.float32) + arrived[i].astype(jnp.float32)
             strips[i] = value.astype(jnp.bfloat16)
             move(s, i, True, lambda c: c.start())
 
@@ -448,12 +460,7 @@
     def end(s):
         loop(s, lambda i: move(s, i, True, lambda c: c.wait()))
 
-    def first_add(i):
-        value = held_strips[i].astype(jnp.float32) + firsts[0][i].astype(jnp.float32)
-        strips[i] = value.astype(jnp.bfloat16)
-        move(0, i, True, lambda c: c.start())
-
-    loop(0, first_add)
+    begin(0)
     core = plan[HEAD_ROW, HEAD_CORE]
     for k in range(3):
         for a in range(sz.nb):
@@ -463,6 +470,7 @@
                 value = sum(t[p].astype(jnp.float32) for t in terms)
                 rows = pl.ds(pl.multiple_of(c * ROWS, ROWS), ROWS)
                 grads[k][0, a, rows] = jnp.where(at > 0, value, 0.0).astype(jnp.bfloat16)
+    add(0)
     end(0)
     for s in range(1, T - 1):
         begin(s)
@@ -545,7 +553,7 @@
         out_specs=[spec(ANY)] * len(out_shape),
         scratch_shapes=[pltpu.VMEM(s, t) for s, t in scratch] + [
             pltpu.SemaphoreType.DMA((3 * sz.room,)),
-            pltpu.SemaphoreType.DMA((max(len(chunks), sz.ring + 1 + T),)),
+            pltpu.SemaphoreType.DMA((2 * sz.ring + T * -(-sz.first // PIECE),)),
         ],
         compiler_params=pltpu.CompilerParams(vmem_limit_bytes=held(scratch)),
         cost_estimate=cost(1_000_000_000, 20_000_000),
@@ -573,11 +581,13 @@
         functools.partial(last_kernel, sz),
         out_shape=[jax.ShapeDtypeStruct(p.shape, p.dtype) for p in partial] + [out] * 3 + [
             jax.ShapeDtypeStruct((1,), jnp.int32)],
-        in_specs=[spec(SMEM)] * (1 + len(notes)) + [spec(VMEM)] * (len(firsts) + len(terms) + 1) + [spec(ANY)] * 2,
+        in_specs=[spec(SMEM)] * (1 + len(notes)) + [spec(ANY)] * len(firsts) + [spec(VMEM)] * len(terms) + [spec(ANY)] * 3,
         out_specs=[spec(ANY)] * 2 + [spec(VMEM)] * 3 + [spec(SMEM)],
         input_output_aliases={n: 0, n + 1: 1},
         scratch_shapes=[
             pltpu.VMEM((sz.first, sz.tok, BLK), jnp.bfloat16),
+            pltpu.VMEM((sz.first, sz.tok, BLK), jnp.bfloat16),
+            pltpu.SemaphoreType.DMA((sz.first,)),
             pltpu.SemaphoreType.DMA((sz.first,)),
             pltpu.SemaphoreType.DMA((sz.first,)),
         ],

time: 62.4 us -> 66.2 us (1.061)
  Pallas kernels: 11.1 us -> 14.4 us
  starting transfers between devices: 23.5 us -> 26.4 us
  waiting for transfers between devices: 24.4 us -> 22.4 us
    ppermute x2, starting transfers between devices: 3.7 us -> 6.47 us  [exchange(): return lax.ppermute(array, 'tensor', [(i, (i + s) % T) for i in range(T)])]
    ppermute x6, waiting for transfers between devices: 11.9 us -> 9.91 us  [gather_chunks(): a, b = (lax.ppermute(a, 'fsdp', ahead), lax.ppermute(b, 'fsdp', behind))]
    pallas_call x1, Pallas kernels: 4.84 us -> 6.67 us  [call_compute(): pl.pallas_call(functools.partial(compute_kernel, sz), out_shape=out_shape...]
    pallas_call x1, Pallas kernels: 2.49 us -> 3.75 us  [call_last(): pl.pallas_call(functools.partial(last_kernel, sz), out_shape=[jax.ShapeDt...]
    ppermute x6, starting transfers between devices: 7.27 us -> 6.07 us  [reduce_parts(): a, b = (lax.ppermute(a, 'fsdp', ahead), lax.ppermute(b, 'fsdp', behind))]
    ppermute x1, starting transfers between devices: 0.17 us -> 1.17 us  [gather_chunks(): same[sz.top] = lax.ppermute(a, 'fsdp', ahead)]
    ppermute x1, waiting for transfers between devices: 0.01 us -> 0.68 us  [reduce_parts(): mine = [here, lax.ppermute(a, 'fsdp', ahead), b]]
where the time goes in v4:
time: 66.2 us; the launch traced here: 65.7 us
  starting transfers between devices  26.4 us (40%)
  waiting for transfers between devices  22.4 us (34%)
  Pallas kernels  14.4 us (22%)
  between operations  1.35 us (2%)
  local copies, waits for them, and re-layouts  0.8 us (1%)
    ppermute x6, waiting for transfers between devices, gather_chunks(): a, b = (lax.ppermute(a, 'fsdp', ahead), lax.ppermute(b, 'fsdp', behind))  9.91 us
    ppermute x6, starting transfers between devices, gather_chunks(): a, b = (lax.ppermute(a, 'fsdp', ahead), lax.ppermute(b, 'fsdp', behind))  6.89 us
    pallas_call x1, Pallas kernels, call_compute(): pl.pallas_call(functools.partial(compute_kernel, sz), out_shape=out_shape...  6.67 us
    ppermute x2, starting transfers between devices, exchange(): return lax.ppermute(array, 'tensor', [(i, (i + s) % T) for i in range(T)])  6.47 us
    ppermute x6, starting transfers between devices, reduce_parts(): a, b = (lax.ppermute(a, 'fsdp', ahead), lax.ppermute(b, 'fsdp', behind))  6.07 us
    ppermute x2, waiting for transfers between devices, exchange(): return lax.ppermute(array, 'tensor', [(i, (i + s) % T) for i in range(T)])  4.59 us
    pallas_call x1, Pallas kernels, call_last(): pl.pallas_call(functools.partial(last_kernel, sz), out_shape=[jax.ShapeDt...  3.75 us
    ppermute x6, waiting for transfers between devices, reduce_parts(): a, b = (lax.ppermute(a, 'fsdp', ahead), lax.ppermute(b, 'fsdp', behind))  3.41 us
  transfers between devices with their start and end apart: 32, of which 14 were waited for; matrix products, arithmetic and copies ran while one was open for 2% of the time, Pallas kernels for 4%

profile of v4, /device:TPU:0, one launch (start us, length us, event | category | flops | bytes accessed | tf_op | source)
XLA Modules:
  0.0 65.7 jit_solution(2685274166082646240)
XLA Ops:
  0.6 0.5 collective-permute-start.32
  1.2 0.1 collective-permute-start.33
  1.2 0.4 collective-permute-start.34
  1.7 0.8 %concatenate.3 = s32[101]{0:T(128)S(1)} concatenate(s32[32]{0:T(128)} %bitcast.9, s32[32]{0:T(128)} %bitcast.10, s32[32]{0:T(128)} %bitcast.11, s32[3]{0:T(128)} %bitcast.12, s32[1]{0:T(128)} %bitcast.4, s32[1]{0:T(128)} %bitcast.5), dimensions={0} | concatenate | bytes 808 | tf_op jit(solution)/shard_map/concatenate | solution.py:691
  2.5 0.2 collective-permute-done.33.refs_4_
  2.6 0.2 collective-permute-done.34.refs_5_
  2.8 1.3 %plan.3 = (s32[32,128]{1,0:T(8,128)S(1)}, bf16[7,64,128]{2,1,0:T(8,128)(2,1)S(1)}, s32[1,128]{1,0:T(1,128)S(1)}) custom-call(s32[1,128]{1,0:T(1,128)S(1)} %pad_bitcast_fusion.own, bf16[1,2,128,128]{3,2,1,0:T(8,128)(2,1)} %refs_0_.1, bf16[1,2,128,128]{3,2,1,0:T(8,128)(2,1)} %refs_1_.1, bf16[1,2,128,128]{3,2,1,0:T(8,128)(2,1)} %refs_2_.1, ...), custom_call_target="tpu_custom_call" | custom-call | flops 1000000 | bytes 4000000 | tf_op jit(solution)/shard_map/plan/pallas_call | solution.py:493
  4.1 3.0 %collective-permute-start.36 = (bf16[7,64,128]{2,1,0:T(8,128)(2,1)S(1)}, bf16[7,64,128]{2,1,0:T(8,128)(2,1)S(1)}, u32[]{:S(2)}, u32[]{:S(2)}) collective-permute-start(bf16[7,64,128]{2,1,0:T(8,128)(2,1)S(1)} %get-tuple-element.76.refs_7_), channel_id=1, source_target_pairs={{0,8},{2,6},{8,16},{10,2},{16,24},{18,10},{24,28},{26,18},{28,20},... | collective-permute-start | bytes 344072 | tf_op jit(solution)/shard_map/ppermute | solution.py:609
  7.1 0.0 collective-permute-start.40
  7.1 2.8 %collective-permute-done.36.refs_5_ = bf16[7,64,128]{2,1,0:T(8,128)(2,1)S(1)} collective-permute-done((bf16[7,64,128]{2,1,0:T(8,128)(2,1)S(1)}, bf16[7,64,128]{2,1,0:T(8,128)(2,1)S(1)}, u32[]{:S(2)}, u32[]{:S(2)}) %collective-permute-start.36) | collective-permute-done | bytes 114720 | tf_op jit(solution)/shard_map/ppermute | solution.py:609
  9.9 2.5 %collective-permute-start.37 = (bf16[7,64,128]{2,1,0:T(8,128)(2,1)S(1)}, bf16[7,64,128]{2,1,0:T(8,128)(2,1)S(1)}, u32[]{:S(2)}, u32[]{:S(2)}) collective-permute-start(bf16[7,64,128]{2,1,0:T(8,128)(2,1)S(1)} %collective-permute-done.36.refs_5_), channel_id=1, source_target_pairs={{0,8},{2,6},{8,16},{10,2},{16,24},{18,10},{24,28},{26,18},{28,20},... | collective-permute-start | bytes 344072 | tf_op jit(solution)/shard_map/ppermute | solution.py:609
  12.3 0.0 collective-permute-done.40.refs_6_
  12.3 0.0 collective-permute-start.41
  12.3 0.0 collective-permute-start.50
  12.4 0.5 collective-permute-start.48
  12.9 2.8 %collective-permute-done.37.refs_3_ = bf16[7,64,128]{2,1,0:T(8,128)(2,1)S(1)} collective-permute-done((bf16[7,64,128]{2,1,0:T(8,128)(2,1)S(1)}, bf16[7,64,128]{2,1,0:T(8,128)(2,1)S(1)}, u32[]{:S(2)}, u32[]{:S(2)}) %collective-permute-start.37) | collective-permute-done | bytes 114720 | tf_op jit(solution)/shard_map/ppermute | solution.py:609
  15.7 1.4 %collective-permute-start.38 = (bf16[7,64,128]{2,1,0:T(8,128)(2,1)S(1)}, bf16[7,64,128]{2,1,0:T(8,128)(2,1)S(1)}, u32[]{:S(2)}, u32[]{:S(2)}) collective-permute-start(bf16[7,64,128]{2,1,0:T(8,128)(2,1)S(1)} %collective-permute-done.37.refs_3_), channel_id=1, source_target_pairs={{0,8},{2,6},{8,16},{10,2},{16,24},{18,10},{24,28},{26,18},{28,20},... | collective-permute-start | bytes 344072 | tf_op jit(solution)/shard_map/ppermute | solution.py:609
  17.1 1.1 %collective-permute-done.41.refs_4_ = bf16[7,64,128]{2,1,0:T(8,128)(2,1)S(1)} collective-permute-done((bf16[7,64,128]{2,1,0:T(8,128)(2,1)S(1)}, bf16[7,64,128]{2,1,0:T(8,128)(2,1)S(1)}, u32[]{:S(2)}, u32[]{:S(2)}) %collective-permute-start.41) | collective-permute-done | bytes 114720 | tf_op jit(solution)/shard_map/ppermute | solution.py:609
  18.2 0.0 collective-permute-start.42
  18.2 0.0 collective-permute-done.50.refs_15_
  18.2 1.0 %collective-permute-start.46 = (bf16[7,64,128]{2,1,0:T(8,128)(2,1)S(1)}, bf16[7,64,128]{2,1,0:T(8,128)(2,1)S(1)}, u32[]{:S(2)}, u32[]{:S(2)}) collective-permute-start(bf16[7,64,128]{2,1,0:T(8,128)(2,1)S(1)} %collective-permute-done.37.refs_3_), channel_id=1, source_target_pairs={{0,2},{2,0},{8,10},{10,8},{16,18},{18,16},{24,26},{26,24},{28,30},... | collective-permute-start | bytes 344072 | tf_op jit(solution)/shard_map/ppermute | solution.py:611
  19.2 0.1 collective-permute-start.47
  19.3 1.4 %collective-permute-done.38.refs_1_ = bf16[7,64,128]{2,1,0:T(8,128)(2,1)S(1)} collective-permute-done((bf16[7,64,128]{2,1,0:T(8,128)(2,1)S(1)}, bf16[7,64,128]{2,1,0:T(8,128)(2,1)S(1)}, u32[]{:S(2)}, u32[]{:S(2)}) %collective-permute-start.38) | collective-permute-done | bytes 114720 | tf_op jit(solution)/shard_map/ppermute | solution.py:609
  20.8 1.2 %collective-permute-start.39 = (bf16[7,64,128]{2,1,0:T(8,128)(2,1)S(1)}, bf16[7,64,128]{2,1,0:T(8,128)(2,1)S(1)}, u32[]{:S(2)}, u32[]{:S(2)}) collective-permute-start(bf16[7,64,128]{2,1,0:T(8,128)(2,1)S(1)} %collective-permute-done.38.refs_1_), channel_id=1, source_target_pairs={{0,8},{2,6},{8,16},{10,2},{16,24},{18,10},{24,28},{26,18},{28,20},... | collective-permute-start | bytes 344072 | tf_op jit(solution)/shard_map/ppermute | solution.py:612
  21.9 0.0 collective-permute-done.49.refs_14_
  21.9 0.0 collective-permute-start.43
  21.9 1.8 %collective-permute-done.42.refs_2_ = bf16[7,64,128]{2,1,0:T(8,128)(2,1)S(1)} collective-permute-done((bf16[7,64,128]{2,1,0:T(8,128)(2,1)S(1)}, bf16[7,64,128]{2,1,0:T(8,128)(2,1)S(1)}, u32[]{:S(2)}, u32[]{:S(2)}) %collective-permute-start.42) | collective-permute-done | bytes 114720 | tf_op jit(solution)/shard_map/ppermute | solution.py:609
  23.7 0.0 collective-permute-start.44
  23.7 0.0 collective-permute-done.46.refs_11_
  23.7 0.5 collective-permute-start.45
  24.2 0.0 collective-permute-done.47.refs_12_
  24.2 1.9 %collective-permute-done.39.refs_0_ = bf16[7,64,128]{2,1,0:T(8,128)(2,1)S(1)} collective-permute-done((bf16[7,64,128]{2,1,0:T(8,128)(2,1)S(1)}, bf16[7,64,128]{2,1,0:T(8,128)(2,1)S(1)}, u32[]{:S(2)}, u32[]{:S(2)}) %collective-permute-start.39) | collective-permute-done | bytes 114720 | tf_op jit(solution)/shard_map/ppermute | solution.py:612
  26.1 0.0 collective-permute-done.43.refs_8_
  26.1 0.0 collective-permute-done.44.refs_9_
  26.2 0.0 collective-permute-done.45.refs_10_
  26.2 6.7 %compute.3 = (bf16[56,64,128]{2,1,0:T(8,128)(2,1)S(1)}, bf16[14,64,128]{2,1,0:T(8,128)(2,1)S(1)}, bf16[42,64,128]{2,1,0:T(8,128)(2,1)S(1)}, bf16[18,128,128]{2,1,0:T(8,128)(2,1)S(1)}, bf16[18,128,128]{2,1,0:T(8,128)(2,1)S(1)}) custom-call(s32[32,128]{1,0:T(8,128)S(1)} %get-tuple-element.74.plan, bf16[128,8192]{1,0:T(8,128)(2,1)} %tokens.1, ...), custom_call_target="tpu_custom_call" | custom-call | flops 1000000000 | bytes 20000000 | tf_op jit(solution)/shard_map/compute/pallas_call | solution.py:549
  32.8 1.1 %collective-permute-start.52 = (bf16[14,64,128]{2,1,0:T(8,128)(2,1)S(1)}, bf16[14,64,128]{2,1,0:T(8,128)(2,1)S(1)}, u32[]{:S(2)}, u32[]{:S(2)}) collective-permute-start(bf16[14,64,128]{2,1,0:T(8,128)(2,1)S(1)} %get-tuple-element.80), channel_id=1, source_target_pairs={{0,2},{2,0},{8,10},{10,8},{16,18},{18,16},{24,26},{26,24},{28,30},... | collective-permute-start | bytes 688136 | tf_op jit(solution)/shard_map/ppermute | solution.py:620
  33.9 1.1 %collective-permute-done.52.__1_ = bf16[14,64,128]{2,1,0:T(8,128)(2,1)S(1)} collective-permute-done((bf16[14,64,128]{2,1,0:T(8,128)(2,1)S(1)}, bf16[14,64,128]{2,1,0:T(8,128)(2,1)S(1)}, u32[]{:S(2)}, u32[]{:S(2)}) %collective-permute-start.52) | collective-permute-done | bytes 229408 | tf_op jit(solution)/shard_map/ppermute | solution.py:620
  35.0 0.4 collective-permute-start.53
  35.4 0.1 add_convert_fusion.13
  35.5 1.5 %collective-permute-start.54 = (bf16[7,64,128]{2,1,0:T(8,128)(2,1)S(1)}, bf16[7,64,128]{2,1,0:T(8,128)(2,1)S(1)}, u32[]{:S(2)}, u32[]{:S(2)}) collective-permute-start(bf16[7,64,128]{2,1,0:T(8,128)(2,1)S(1)} %get-tuple-element.81), channel_id=1, source_target_pairs={{0,8},{2,6},{8,16},{10,2},{16,24},{18,10},{24,28},{26,18},{28,20},... | collective-permute-start | bytes 344072 | tf_op jit(solution)/shard_map/ppermute | solution.py:637
  36.9 0.7 %collective-permute-start.55 = (bf16[7,64,128]{2,1,0:T(8,128)(2,1)S(1)}, bf16[7,64,128]{2,1,0:T(8,128)(2,1)S(1)}, u32[]{:S(2)}, u32[]{:S(2)}) collective-permute-start(bf16[7,64,128]{2,1,0:T(8,128)(2,1)S(1)} %get-tuple-element.82), channel_id=1, source_target_pairs={{0,4},{2,10},{8,0},{10,18},{16,8},{18,26},{24,16},{26,30},{28,24},... | collective-permute-start | bytes 344072 | tf_op jit(solution)/shard_map/ppermute | solution.py:637
  37.6 3.8 %collective-permute-start.35 = (s32[1,128]{1,0:T(1,128)S(1)}, s32[1,128]{1,0:T(1,128)S(1)}, u32[]{:S(2)}, u32[]{:S(2)}) collective-permute-start(s32[1,128]{1,0:T(1,128)S(1)} %get-tuple-element.75), channel_id=1, source_target_pairs={{0,1},{1,0},{2,3},{3,2},{4,5},{5,4},{6,7},{7,6},{8,9},{9,8},{10,11... | collective-permute-start | bytes 1544 | tf_op jit(solution)/shard_map/ppermute | solution.py:661
  41.4 1.5 %collective-permute-done.35.__2_.note.refs_0_ = s32[1,128]{1,0:T(1,128)S(1)} collective-permute-done((s32[1,128]{1,0:T(1,128)S(1)}, s32[1,128]{1,0:T(1,128)S(1)}, u32[]{:S(2)}, u32[]{:S(2)}) %collective-permute-start.35) | collective-permute-done | bytes 544 | tf_op jit(solution)/shard_map/ppermute | solution.py:661
  42.9 0.0 collective-permute-done.54.__0_
  42.9 0.1 add_convert_fusion.12.__1_
  43.0 0.1 add_convert_fusion.11
  43.1 0.1 collective-permute-start.57
  43.2 0.3 collective-permute-start.56
  43.5 2.7 %collective-permute-start.51 = (bf16[18,128,128]{2,1,0:T(8,128)(2,1)S(1)}, bf16[18,128,128]{2,1,0:T(8,128)(2,1)S(1)}, u32[]{:S(2)}, u32[]{:S(2)}) collective-permute-start(bf16[18,128,128]{2,1,0:T(8,128)(2,1)S(1)} %get-tuple-element.77), channel_id=1, source_target_pairs={{0,1},{1,0},{2,3},{3,2},{4,5},{5,4},{6,7},{7,6},{8,9},{9,8},{10,11... | collective-permute-start | bytes 1769480 | tf_op jit(solution)/shard_map/ppermute | solution.py:661
  46.2 1.5 %collective-permute-start.59 = (bf16[7,64,128]{2,1,0:T(8,128)(2,1)S(1)}, bf16[7,64,128]{2,1,0:T(8,128)(2,1)S(1)}, u32[]{:S(2)}, u32[]{:S(2)}) collective-permute-start(bf16[7,64,128]{2,1,0:T(8,128)(2,1)S(1)} %get-tuple-element.109.__1_), channel_id=1, source_target_pairs={{0,4},{2,10},{8,0},{10,18},{16,8},{18,26},{24,16},{26,30},{28,24},... | collective-permute-start | bytes 344072 | tf_op jit(solution)/shard_map/ppermute | solution.py:637
  47.7 2.6 %prepare.3 = (bf16[128,4096]{1,0:T(8,128)(2,1)}, bf16[128,4096]{1,0:T(8,128)(2,1)}, bf16[18,128,128]{2,1,0:T(8,128)(2,1)S(1)}) custom-call(s32[32,128]{1,0:T(8,128)S(1)} %get-tuple-element.74.plan, s32[1,128]{1,0:T(1,128)S(1)} %collective-permute-done.35.__2_.note.refs_0_, bf16[18,128,128]{2,1,0:T(8,128)(2,1)S(1)} %turn.24.first), custom_call_target="tpu_custom_call" | custom-call | flops 1000000 | bytes 6000000 | tf_op jit(solution)/shard_map/prepare/pallas_call | solution.py:566
  50.3 0.1 add_convert_fusion.10.__1_
  50.4 0.6 collective-permute-start.58
  51.0 0.0 collective-permute-done.59.__0_
  51.0 0.1 add_convert_fusion.9.__1_
  51.0 1.5 %collective-permute-start.61 = (bf16[7,64,128]{2,1,0:T(8,128)(2,1)S(1)}, bf16[7,64,128]{2,1,0:T(8,128)(2,1)S(1)}, u32[]{:S(2)}, u32[]{:S(2)}) collective-permute-start(bf16[7,64,128]{2,1,0:T(8,128)(2,1)S(1)} %add_convert_fusion.9.__1_), channel_id=1, source_target_pairs={{0,4},{2,10},{8,0},{10,18},{16,8},{18,26},{24,16},{26,30},{28,24},... | collective-permute-start | bytes 344072 | tf_op jit(solution)/shard_map/ppermute | solution.py:637
  52.6 3.4 %collective-permute-done.58.__0_ = bf16[7,64,128]{2,1,0:T(8,128)(2,1)S(1)} collective-permute-done((bf16[7,64,128]{2,1,0:T(8,128)(2,1)S(1)}, bf16[7,64,128]{2,1,0:T(8,128)(2,1)S(1)}, u32[]{:S(2)}, u32[]{:S(2)}) %collective-permute-start.58) | collective-permute-done | bytes 114720 | tf_op jit(solution)/shard_map/ppermute | solution.py:637
  55.9 0.1 add_convert_fusion.8
  56.0 1.1 %collective-permute-start.60 = (bf16[7,64,128]{2,1,0:T(8,128)(2,1)S(1)}, bf16[7,64,128]{2,1,0:T(8,128)(2,1)S(1)}, u32[]{:S(2)}, u32[]{:S(2)}) collective-permute-start(bf16[7,64,128]{2,1,0:T(8,128)(2,1)S(1)} %add_convert_fusion.8), channel_id=1, source_target_pairs={{0,8},{2,6},{8,16},{10,2},{16,24},{18,10},{24,28},{26,18},{28,20},... | collective-permute-start | bytes 344072 | tf_op jit(solution)/shard_map/ppermute | solution.py:645
  57.1 3.1 %collective-permute-done.51.refs_1_ = bf16[18,128,128]{2,1,0:T(8,128)(2,1)S(1)} collective-permute-done((bf16[18,128,128]{2,1,0:T(8,128)(2,1)S(1)}, bf16[18,128,128]{2,1,0:T(8,128)(2,1)S(1)}, u32[]{:S(2)}, u32[]{:S(2)}) %collective-permute-start.51) | collective-permute-done | bytes 589856 | tf_op jit(solution)/shard_map/ppermute | solution.py:661
  60.2 0.7 %collective-permute-done.60.refs_3_ = bf16[7,64,128]{2,1,0:T(8,128)(2,1)S(1)} collective-permute-done((bf16[7,64,128]{2,1,0:T(8,128)(2,1)S(1)}, bf16[7,64,128]{2,1,0:T(8,128)(2,1)S(1)}, u32[]{:S(2)}, u32[]{:S(2)}) %collective-permute-start.60) | collective-permute-done | bytes 114720 | tf_op jit(solution)/shard_map/ppermute | solution.py:645
  60.8 0.4 collective-permute-done.62.refs_6_
  61.3 3.7 %last.3 = (bf16[128,4096]{1,0:T(8,128)(2,1)}, bf16[128,4096]{1,0:T(8,128)(2,1)}, bf16[1,2,128,128]{3,2,1,0:T(8,128)(2,1)}, bf16[1,2,128,128]{3,2,1,0:T(8,128)(2,...) custom-call(s32[32,128]{1,0:T(8,128)S(1)} %get-tuple-element.74.plan, ...), custom_call_target="tpu_custom_call", output_to_operand_aliasing={{0}: (10, {}), {1}: (11, {})} | custom-call | flops 1000000 | bytes 3000000 | tf_op jit(solution)/shard_map/last/pallas_call | solution.py:580
  (26 shorter events, 0.1 us)
Async XLA Ops:
  0.6 1.8 %collective-permute-start.32 = (bf16[1,2,128,128]{3,2,1,0:T(8,128)(2,1)}, bf16[1,2,128,128]{3,2,1,0:T(8,128)(2,1)S(1)}, u32[]{:S(2)}, u32[]{:S(2)}) collective-permute-start(bf16[1,2,128,128]{3,2,1,0:T(8,128)(2,1)} %refs_0_.1), channel_id=1, source_target_pairs={{0,2},{2,0},{8,10},{10,8},{16,18},{18,16},{24,26},{26,24},{28,30},... | collective-permute-start | bytes 196616 | tf_op jit(solution)/shard_map/ppermute | solution.py:657
  1.2 1.5 %collective-permute-start.33 = (bf16[1,2,128,128]{3,2,1,0:T(8,128)(2,1)}, bf16[1,2,128,128]{3,2,1,0:T(8,128)(2,1)S(1)}, u32[]{:S(2)}, u32[]{:S(2)}) collective-permute-start(bf16[1,2,128,128]{3,2,1,0:T(8,128)(2,1)} %refs_1_.1), channel_id=1, source_target_pairs={{0,2},{2,0},{8,10},{10,8},{16,18},{18,16},{24,26},{26,24},{28,30},... | collective-permute-start | bytes 196616 | tf_op jit(solution)/shard_map/ppermute | solution.py:657
  1.2 1.5 %collective-permute-start.34 = (bf16[1,2,128,128]{3,2,1,0:T(8,128)(2,1)}, bf16[1,2,128,128]{3,2,1,0:T(8,128)(2,1)S(1)}, u32[]{:S(2)}, u32[]{:S(2)}) collective-permute-start(bf16[1,2,128,128]{3,2,1,0:T(8,128)(2,1)} %refs_2_.1), channel_id=1, source_target_pairs={{0,2},{2,0},{8,10},{10,8},{16,18},{18,16},{24,26},{26,24},{28,30},... | collective-permute-start | bytes 196616 | tf_op jit(solution)/shard_map/ppermute | solution.py:657
  4.1 5.8 %collective-permute-start.36 = (bf16[7,64,128]{2,1,0:T(8,128)(2,1)S(1)}, bf16[7,64,128]{2,1,0:T(8,128)(2,1)S(1)}, u32[]{:S(2)}, u32[]{:S(2)}) collective-permute-start(bf16[7,64,128]{2,1,0:T(8,128)(2,1)S(1)} %get-tuple-element.76.refs_7_), channel_id=1, source_target_pairs={{0,8},{2,6},{8,16},{10,2},{16,24},{18,10},{24,28},{26,18},{28,20},... | collective-permute-start | bytes 344072 | tf_op jit(solution)/shard_map/ppermute | solution.py:609
  7.1 5.3 %collective-permute-start.40 = (bf16[7,64,128]{2,1,0:T(8,128)(2,1)S(1)}, bf16[7,64,128]{2,1,0:T(8,128)(2,1)S(1)}, u32[]{:S(2)}, u32[]{:S(2)}) collective-permute-start(bf16[7,64,128]{2,1,0:T(8,128)(2,1)S(1)} %get-tuple-element.76.refs_7_), channel_id=1, source_target_pairs={{0,4},{2,10},{8,0},{10,18},{16,8},{18,26},{24,16},{26,30},{28,24},... | collective-permute-start | bytes 344072 | tf_op jit(solution)/shard_map/ppermute | solution.py:609
  9.9 5.8 %collective-permute-start.37 = (bf16[7,64,128]{2,1,0:T(8,128)(2,1)S(1)}, bf16[7,64,128]{2,1,0:T(8,128)(2,1)S(1)}, u32[]{:S(2)}, u32[]{:S(2)}) collective-permute-start(bf16[7,64,128]{2,1,0:T(8,128)(2,1)S(1)} %collective-permute-done.36.refs_5_), channel_id=1, source_target_pairs={{0,8},{2,6},{8,16},{10,2},{16,24},{18,10},{24,28},{26,18},{28,20},... | collective-permute-start | bytes 344072 | tf_op jit(solution)/shard_map/ppermute | solution.py:609
  12.3 5.9 %collective-permute-start.41 = (bf16[7,64,128]{2,1,0:T(8,128)(2,1)S(1)}, bf16[7,64,128]{2,1,0:T(8,128)(2,1)S(1)}, u32[]{:S(2)}, u32[]{:S(2)}) collective-permute-start(bf16[7,64,128]{2,1,0:T(8,128)(2,1)S(1)} %collective-permute-done.40.refs_6_), channel_id=1, source_target_pairs={{0,4},{2,10},{8,0},{10,18},{16,8},{18,26},{24,16},{26,30},{28,24},... | collective-permute-start | bytes 344072 | tf_op jit(solution)/shard_map/ppermute | solution.py:609
  12.3 5.9 %collective-permute-start.50 = (bf16[7,64,128]{2,1,0:T(8,128)(2,1)S(1)}, bf16[7,64,128]{2,1,0:T(8,128)(2,1)S(1)}, u32[]{:S(2)}, u32[]{:S(2)}) collective-permute-start(bf16[7,64,128]{2,1,0:T(8,128)(2,1)S(1)} %get-tuple-element.76.refs_7_), channel_id=1, source_target_pairs={{0,2},{2,0},{8,10},{10,8},{16,18},{18,16},{24,26},{26,24},{28,30},... | collective-permute-start | bytes 344072 | tf_op jit(solution)/shard_map/ppermute | solution.py:611
  12.4 6.9 %collective-permute-start.48 = (bf16[7,64,128]{2,1,0:T(8,128)(2,1)S(1)}, bf16[7,64,128]{2,1,0:T(8,128)(2,1)S(1)}, u32[]{:S(2)}, u32[]{:S(2)}) collective-permute-start(bf16[7,64,128]{2,1,0:T(8,128)(2,1)S(1)} %collective-permute-done.36.refs_5_), channel_id=1, source_target_pairs={{0,2},{2,0},{8,10},{10,8},{16,18},{18,16},{24,26},{26,24},{28,30},... | collective-permute-start | bytes 344072 | tf_op jit(solution)/shard_map/ppermute | solution.py:611
  15.7 5.0 %collective-permute-start.38 = (bf16[7,64,128]{2,1,0:T(8,128)(2,1)S(1)}, bf16[7,64,128]{2,1,0:T(8,128)(2,1)S(1)}, u32[]{:S(2)}, u32[]{:S(2)}) collective-permute-start(bf16[7,64,128]{2,1,0:T(8,128)(2,1)S(1)} %collective-permute-done.37.refs_3_), channel_id=1, source_target_pairs={{0,8},{2,6},{8,16},{10,2},{16,24},{18,10},{24,28},{26,18},{28,20},... | collective-permute-start | bytes 344072 | tf_op jit(solution)/shard_map/ppermute | solution.py:609
  17.1 4.8 %collective-permute-start.49 = (bf16[7,64,128]{2,1,0:T(8,128)(2,1)S(1)}, bf16[7,64,128]{2,1,0:T(8,128)(2,1)S(1)}, u32[]{:S(2)}, u32[]{:S(2)}) collective-permute-start(bf16[7,64,128]{2,1,0:T(8,128)(2,1)S(1)} %collective-permute-done.40.refs_6_), channel_id=1, source_target_pairs={{0,2},{2,0},{8,10},{10,8},{16,18},{18,16},{24,26},{26,24},{28,30},... | collective-permute-start | bytes 344072 | tf_op jit(solution)/shard_map/ppermute | solution.py:611
  18.2 5.5 %collective-permute-start.42 = (bf16[7,64,128]{2,1,0:T(8,128)(2,1)S(1)}, bf16[7,64,128]{2,1,0:T(8,128)(2,1)S(1)}, u32[]{:S(2)}, u32[]{:S(2)}) collective-permute-start(bf16[7,64,128]{2,1,0:T(8,128)(2,1)S(1)} %collective-permute-done.41.refs_4_), channel_id=1, source_target_pairs={{0,4},{2,10},{8,0},{10,18},{16,8},{18,26},{24,16},{26,30},{28,24},... | collective-permute-start | bytes 344072 | tf_op jit(solution)/shard_map/ppermute | solution.py:609
  18.2 5.5 %collective-permute-start.46 = (bf16[7,64,128]{2,1,0:T(8,128)(2,1)S(1)}, bf16[7,64,128]{2,1,0:T(8,128)(2,1)S(1)}, u32[]{:S(2)}, u32[]{:S(2)}) collective-permute-start(bf16[7,64,128]{2,1,0:T(8,128)(2,1)S(1)} %collective-permute-done.37.refs_3_), channel_id=1, source_target_pairs={{0,2},{2,0},{8,10},{10,8},{16,18},{18,16},{24,26},{26,24},{28,30},... | collective-permute-start | bytes 344072 | tf_op jit(solution)/shard_map/ppermute | solution.py:611
  19.2 5.0 %collective-permute-start.47 = (bf16[7,64,128]{2,1,0:T(8,128)(2,1)S(1)}, bf16[7,64,128]{2,1,0:T(8,128)(2,1)S(1)}, u32[]{:S(2)}, u32[]{:S(2)}) collective-permute-start(bf16[7,64,128]{2,1,0:T(8,128)(2,1)S(1)} %collective-permute-done.41.refs_4_), channel_id=1, source_target_pairs={{0,2},{2,0},{8,10},{10,8},{16,18},{18,16},{24,26},{26,24},{28,30},... | collective-permute-start | bytes 344072 | tf_op jit(solution)/shard_map/ppermute | solution.py:611
  20.8 5.4 %collective-permute-start.39 = (bf16[7,64,128]{2,1,0:T(8,128)(2,1)S(1)}, bf16[7,64,128]{2,1,0:T(8,128)(2,1)S(1)}, u32[]{:S(2)}, u32[]{:S(2)}) collective-permute-start(bf16[7,64,128]{2,1,0:T(8,128)(2,1)S(1)} %collective-permute-done.38.refs_1_), channel_id=1, source_target_pairs={{0,8},{2,6},{8,16},{10,2},{16,24},{18,10},{24,28},{26,18},{28,20},... | collective-permute-start | bytes 344072 | tf_op jit(solution)/shard_map/ppermute | solution.py:612
  21.9 4.2 %collective-permute-start.43 = (bf16[7,64,128]{2,1,0:T(8,128)(2,1)S(1)}, bf16[7,64,128]{2,1,0:T(8,128)(2,1)S(1)}, u32[]{:S(2)}, u32[]{:S(2)}) collective-permute-start(bf16[7,64,128]{2,1,0:T(8,128)(2,1)S(1)} %collective-permute-done.38.refs_1_), channel_id=1, source_target_pairs={{0,10},{2,4},{8,18},{10,0},{16,26},{18,8},{24,30},{26,16},{28,22},... | collective-permute-start | bytes 344072 | tf_op jit(solution)/shard_map/ppermute | solution.py:613
  23.7 2.5 %collective-permute-start.44 = (bf16[7,64,128]{2,1,0:T(8,128)(2,1)S(1)}, bf16[7,64,128]{2,1,0:T(8,128)(2,1)S(1)}, u32[]{:S(2)}, u32[]{:S(2)}) collective-permute-start(bf16[7,64,128]{2,1,0:T(8,128)(2,1)S(1)} %collective-permute-done.38.refs_1_), channel_id=1, source_target_pairs={{0,2},{2,0},{8,10},{10,8},{16,18},{18,16},{24,26},{26,24},{28,30},... | collective-permute-start | bytes 344072 | tf_op jit(solution)/shard_map/ppermute | solution.py:611
  23.7 2.5 %collective-permute-start.45 = (bf16[7,64,128]{2,1,0:T(8,128)(2,1)S(1)}, bf16[7,64,128]{2,1,0:T(8,128)(2,1)S(1)}, u32[]{:S(2)}, u32[]{:S(2)}) collective-permute-start(bf16[7,64,128]{2,1,0:T(8,128)(2,1)S(1)} %collective-permute-done.42.refs_2_), channel_id=1, source_target_pairs={{0,2},{2,0},{8,10},{10,8},{16,18},{18,16},{24,26},{26,24},{28,30},... | collective-permute-start | bytes 344072 | tf_op jit(solution)/shard_map/ppermute | solution.py:611
  32.8 2.2 %collective-permute-start.52 = (bf16[14,64,128]{2,1,0:T(8,128)(2,1)S(1)}, bf16[14,64,128]{2,1,0:T(8,128)(2,1)S(1)}, u32[]{:S(2)}, u32[]{:S(2)}) collective-permute-start(bf16[14,64,128]{2,1,0:T(8,128)(2,1)S(1)} %get-tuple-element.80), channel_id=1, source_target_pairs={{0,2},{2,0},{8,10},{10,8},{16,18},{18,16},{24,26},{26,24},{28,30},... | collective-permute-start | bytes 688136 | tf_op jit(solution)/shard_map/ppermute | solution.py:620
  35.0 7.9 %collective-permute-start.53 = (bf16[42,64,128]{2,1,0:T(8,128)(2,1)S(1)}, bf16[42,64,128]{2,1,0:T(8,128)(2,1)S(1)}, u32[]{:S(2)}, u32[]{:S(2)}) collective-permute-start(bf16[42,64,128]{2,1,0:T(8,128)(2,1)S(1)} %turn.21), channel_id=1, source_target_pairs={{0,2},{2,0},{8,10},{10,8},{16,18},{18,16},{24,26},{26,24},{28,30},... | collective-permute-start | bytes 2064392 | tf_op jit(solution)/shard_map/ppermute | solution.py:621
  35.5 7.4 %collective-permute-start.54 = (bf16[7,64,128]{2,1,0:T(8,128)(2,1)S(1)}, bf16[7,64,128]{2,1,0:T(8,128)(2,1)S(1)}, u32[]{:S(2)}, u32[]{:S(2)}) collective-permute-start(bf16[7,64,128]{2,1,0:T(8,128)(2,1)S(1)} %get-tuple-element.81), channel_id=1, source_target_pairs={{0,8},{2,6},{8,16},{10,2},{16,24},{18,10},{24,28},{26,18},{28,20},... | collective-permute-start | bytes 344072 | tf_op jit(solution)/shard_map/ppermute | solution.py:637
  36.9 6.0 %collective-permute-start.55 = (bf16[7,64,128]{2,1,0:T(8,128)(2,1)S(1)}, bf16[7,64,128]{2,1,0:T(8,128)(2,1)S(1)}, u32[]{:S(2)}, u32[]{:S(2)}) collective-permute-start(bf16[7,64,128]{2,1,0:T(8,128)(2,1)S(1)} %get-tuple-element.82), channel_id=1, source_target_pairs={{0,4},{2,10},{8,0},{10,18},{16,8},{18,26},{24,16},{26,30},{28,24},... | collective-permute-start | bytes 344072 | tf_op jit(solution)/shard_map/ppermute | solution.py:637
  37.6 5.3 %collective-permute-start.35 = (s32[1,128]{1,0:T(1,128)S(1)}, s32[1,128]{1,0:T(1,128)S(1)}, u32[]{:S(2)}, u32[]{:S(2)}) collective-permute-start(s32[1,128]{1,0:T(1,128)S(1)} %get-tuple-element.75), channel_id=1, source_target_pairs={{0,1},{1,0},{2,3},{3,2},{4,5},{5,4},{6,7},{7,6},{8,9},{9,8},{10,11... | collective-permute-start | bytes 1544 | tf_op jit(solution)/shard_map/ppermute | solution.py:661
  43.1 4.6 %collective-permute-start.57 = (bf16[7,64,128]{2,1,0:T(8,128)(2,1)S(1)}, bf16[7,64,128]{2,1,0:T(8,128)(2,1)S(1)}, u32[]{:S(2)}, u32[]{:S(2)}) collective-permute-start(bf16[7,64,128]{2,1,0:T(8,128)(2,1)S(1)} %get-tuple-element.110.refs_2_), channel_id=1, source_target_pairs={{0,2},{2,0},{8,10},{10,8},{16,18},{18,16},{24,26},{26,24},{28,30},... | collective-permute-start | bytes 344072 | tf_op jit(solution)/shard_map/ppermute | solution.py:633
  43.2 7.1 %collective-permute-start.56 = (bf16[7,64,128]{2,1,0:T(8,128)(2,1)S(1)}, bf16[7,64,128]{2,1,0:T(8,128)(2,1)S(1)}, u32[]{:S(2)}, u32[]{:S(2)}) collective-permute-start(bf16[7,64,128]{2,1,0:T(8,128)(2,1)S(1)} %add_convert_fusion.12.__1_), channel_id=1, source_target_pairs={{0,8},{2,6},{8,16},{10,2},{16,24},{18,10},{24,28},{26,18},{28,20},... | collective-permute-start | bytes 344072 | tf_op jit(solution)/shard_map/ppermute | solution.py:637
  43.5 16.7 %collective-permute-start.51 = (bf16[18,128,128]{2,1,0:T(8,128)(2,1)S(1)}, bf16[18,128,128]{2,1,0:T(8,128)(2,1)S(1)}, u32[]{:S(2)}, u32[]{:S(2)}) collective-permute-start(bf16[18,128,128]{2,1,0:T(8,128)(2,1)S(1)} %get-tuple-element.77), channel_id=1, source_target_pairs={{0,1},{1,0},{2,3},{3,2},{4,5},{5,4},{6,7},{7,6},{8,9},{9,8},{10,11... | collective-permute-start | bytes 1769480 | tf_op jit(solution)/shard_map/ppermute | solution.py:661
  46.2 4.8 %collective-permute-start.59 = (bf16[7,64,128]{2,1,0:T(8,128)(2,1)S(1)}, bf16[7,64,128]{2,1,0:T(8,128)(2,1)S(1)}, u32[]{:S(2)}, u32[]{:S(2)}) collective-permute-start(bf16[7,64,128]{2,1,0:T(8,128)(2,1)S(1)} %get-tuple-element.109.__1_), channel_id=1, source_target_pairs={{0,4},{2,10},{8,0},{10,18},{16,8},{18,26},{24,16},{26,30},{28,24},... | collective-permute-start | bytes 344072 | tf_op jit(solution)/shard_map/ppermute | solution.py:637
  50.4 5.6 %collective-permute-start.58 = (bf16[7,64,128]{2,1,0:T(8,128)(2,1)S(1)}, bf16[7,64,128]{2,1,0:T(8,128)(2,1)S(1)}, u32[]{:S(2)}, u32[]{:S(2)}) collective-permute-start(bf16[7,64,128]{2,1,0:T(8,128)(2,1)S(1)} %add_convert_fusion.10.__1_), channel_id=1, source_target_pairs={{0,8},{2,6},{8,16},{10,2},{16,24},{18,10},{24,28},{26,18},{28,20},... | collective-permute-start | bytes 344072 | tf_op jit(solution)/shard_map/ppermute | solution.py:637
  51.0 9.1 %collective-permute-start.61 = (bf16[7,64,128]{2,1,0:T(8,128)(2,1)S(1)}, bf16[7,64,128]{2,1,0:T(8,128)(2,1)S(1)}, u32[]{:S(2)}, u32[]{:S(2)}) collective-permute-start(bf16[7,64,128]{2,1,0:T(8,128)(2,1)S(1)} %add_convert_fusion.9.__1_), channel_id=1, source_target_pairs={{0,4},{2,10},{8,0},{10,18},{16,8},{18,26},{24,16},{26,30},{28,24},... | collective-permute-start | bytes 344072 | tf_op jit(solution)/shard_map/ppermute | solution.py:637
  52.6 7.6 %collective-permute-start.63 = (bf16[7,64,128]{2,1,0:T(8,128)(2,1)S(1)}, bf16[7,64,128]{2,1,0:T(8,128)(2,1)S(1)}, u32[]{:S(2)}, u32[]{:S(2)}) collective-permute-start(bf16[7,64,128]{2,1,0:T(8,128)(2,1)S(1)} %add_convert_fusion.9.__1_), channel_id=1, source_target_pairs={{0,6},{2,8},{8,2},{10,16},{16,10},{18,24},{24,18},{26,28},{28,26},... | collective-permute-start | bytes 344072 | tf_op jit(solution)/shard_map/ppermute | solution.py:649
  56.0 4.8 %collective-permute-start.60 = (bf16[7,64,128]{2,1,0:T(8,128)(2,1)S(1)}, bf16[7,64,128]{2,1,0:T(8,128)(2,1)S(1)}, u32[]{:S(2)}, u32[]{:S(2)}) collective-permute-start(bf16[7,64,128]{2,1,0:T(8,128)(2,1)S(1)} %add_convert_fusion.8), channel_id=1, source_target_pairs={{0,8},{2,6},{8,16},{10,2},{16,24},{18,10},{24,28},{26,18},{28,20},... | collective-permute-start | bytes 344072 | tf_op jit(solution)/shard_map/ppermute | solution.py:645
  57.1 4.2 %collective-permute-start.62 = (bf16[7,64,128]{2,1,0:T(8,128)(2,1)S(1)}, bf16[7,64,128]{2,1,0:T(8,128)(2,1)S(1)}, u32[]{:S(2)}, u32[]{:S(2)}) collective-permute-start(bf16[7,64,128]{2,1,0:T(8,128)(2,1)S(1)} %add_convert_fusion.8), channel_id=1, source_target_pairs={{0,10},{2,4},{8,18},{10,0},{16,26},{18,8},{24,30},{26,16},{28,22},... | collective-permute-start | bytes 344072 | tf_op jit(solution)/shard_map/ppermute | solution.py:648
  61.3 4.3 %copy-start = (bf16[1,2,128,128]{3,2,1,0:T(8,128)(2,1)S(1)}, bf16[1,2,128,128]{3,2,1,0:T(8,128)(2,1)}, u32[]{:S(2)}) copy-start(bf16[1,2,128,128]{3,2,1,0:T(8,128)(2,1)} %refs_0_.1) | copy-start | bytes 196612
  61.3 4.3 %copy-start.1 = (bf16[1,2,128,128]{3,2,1,0:T(8,128)(2,1)S(1)}, bf16[1,2,128,128]{3,2,1,0:T(8,128)(2,1)}, u32[]{:S(2)}) copy-start(bf16[1,2,128,128]{3,2,1,0:T(8,128)(2,1)} %refs_1_.1) | copy-start | bytes 196612
  61.3 4.4 %copy-start.2 = (bf16[1,2,128,128]{3,2,1,0:T(8,128)(2,1)S(1)}, bf16[1,2,128,128]{3,2,1,0:T(8,128)(2,1)}, u32[]{:S(2)}) copy-start(bf16[1,2,128,128]{3,2,1,0:T(8,128)(2,1)} %refs_2_.1) | copy-start | bytes 196612

commit v5 on v3

--- a/solution.py
+++ b/solution.py
@@ -9,7 +9,8 @@
 
 FF = 14336
 BLK = 128
-GROUP = 4
+GROUP = 8
+COLUMNS = 4
 FIRST_SEND = 18
 LEAN_SLOTS = 7
 ROWS = BLK // 2
@@ -322,8 +323,8 @@
     walk(plan, forward)
 
     def columns(i, _):
-        for j in range(GROUP):
-            c = plan[COLS_ROW, i * GROUP + j]
+        for j in range(COLUMNS):
+            c = plan[COLS_ROW, i * COLUMNS + j]
             g, u, h = gate_acc[c], up_acc[c], hg_acc[c]
             s = lax.logistic(g)
             silu = g * s
@@ -331,7 +332,7 @@
             acts[A + c] = (h * silu).astype(jnp.bfloat16)
             acts[2 * A + c] = (silu * u).astype(jnp.bfloat16)
 
-    lax.fori_loop(0, (plan[HEAD_ROW, HEAD_COLS] + (GROUP - 1)) // GROUP, columns, None)
+    lax.fori_loop(0, (plan[HEAD_ROW, HEAD_COLS] + (COLUMNS - 1)) // COLUMNS, columns, None)
 
     def gradients(e0):
         for k, u in group:

time: 62.4 us -> 63 us (level); the launches traced: 61.5 us -> 63.6 us
  starting transfers between devices: 23.5 us -> 19.8 us
  Pallas kernels: 11.1 us -> 14.2 us
  waiting for transfers between devices: 24.4 us -> 27.1 us
    ppermute x2, starting transfers between devices: 3.7 us -> 0.01 us  [exchange(): return lax.ppermute(array, 'tensor', [(i, (i + s) % T) for i in range(T)])]
    ppermute x2, waiting for transfers between devices: 5.14 us -> 8.05 us  [exchange(): return lax.ppermute(array, 'tensor', [(i, (i + s) % T) for i in range(T)])]
    pallas_call x1, Pallas kernels: 4.84 us -> 7.62 us  [call_compute(): pl.pallas_call(functools.partial(compute_kernel, sz), out_shape=out_shape...]
where the time goes in v5:
time: 63 us; the launch traced here: 63.6 us
  waiting for transfers between devices  27.1 us (43%)
  starting transfers between devices  19.8 us (31%)
  Pallas kernels  14.2 us (23%)
  between operations  1.37 us (2%)
  local copies, waits for them, and re-layouts  0.8 us (1%)
    ppermute x6, waiting for transfers between devices, gather_chunks(): a, b = (lax.ppermute(a, 'fsdp', ahead), lax.ppermute(b, 'fsdp', behind))  11.4 us
    ppermute x2, waiting for transfers between devices, exchange(): return lax.ppermute(array, 'tensor', [(i, (i + s) % T) for i in range(T)])  8.05 us
    pallas_call x1, Pallas kernels, call_compute(): pl.pallas_call(functools.partial(compute_kernel, sz), out_shape=out_shape...  7.62 us
    ppermute x6, starting transfers between devices, reduce_parts(): a, b = (lax.ppermute(a, 'fsdp', ahead), lax.ppermute(b, 'fsdp', behind))  7.07 us
    ppermute x6, starting transfers between devices, gather_chunks(): a, b = (lax.ppermute(a, 'fsdp', ahead), lax.ppermute(b, 'fsdp', behind))  6.47 us
    ppermute x6, waiting for transfers between devices, reduce_parts(): a, b = (lax.ppermute(a, 'fsdp', ahead), lax.ppermute(b, 'fsdp', behind))  3.84 us
    pallas_call x1, Pallas kernels, call_prepare(): pl.pallas_call(functools.partial(prepare_kernel, sz), out_shape=[half, ha...  2.71 us
    pallas_call x1, Pallas kernels, call_last(): pl.pallas_call(functools.partial(last_kernel, sz), out_shape=[jax.ShapeDt...  2.5 us
  transfers between devices with their start and end apart: 32, of which 14 were waited for; matrix products, arithmetic and copies ran while one was open for 2% of the time, Pallas kernels for 4%

profile of v5, /device:TPU:0, one launch (start us, length us, event | category | flops | bytes accessed | tf_op | source)
XLA Modules:
  0.0 63.6 jit_solution(15466475922284430502)
XLA Ops:
  0.6 0.5 collective-permute-start.32
  1.2 0.1 collective-permute-start.33
  1.2 0.4 collective-permute-start.34
  1.7 0.8 %concatenate.3 = s32[101]{0:T(128)S(1)} concatenate(s32[32]{0:T(128)} %bitcast.9, s32[32]{0:T(128)} %bitcast.10, s32[32]{0:T(128)} %bitcast.11, s32[3]{0:T(128)} %bitcast.12, s32[1]{0:T(128)} %bitcast.4, s32[1]{0:T(128)} %bitcast.5), dimensions={0} | concatenate | bytes 808 | tf_op jit(solution)/shard_map/concatenate | solution.py:682
  2.4 0.0 collective-permute-done.32.refs_3_
  2.5 0.2 collective-permute-done.33.refs_4_
  2.6 0.2 collective-permute-done.34.refs_5_
  2.8 1.3 %plan.3 = (s32[32,128]{1,0:T(8,128)S(1)}, bf16[7,64,128]{2,1,0:T(8,128)(2,1)S(1)}, s32[1,128]{1,0:T(1,128)S(1)}) custom-call(s32[1,128]{1,0:T(1,128)S(1)} %pad_bitcast_fusion.own, bf16[1,2,128,128]{3,2,1,0:T(8,128)(2,1)} %refs_0_.1, bf16[1,2,128,128]{3,2,1,0:T(8,128)(2,1)} %refs_1_.1, bf16[1,2,128,128]{3,2,1,0:T(8,128)(2,1)} %refs_2_.1, ...), custom_call_target="tpu_custom_call" | custom-call | flops 1000000 | bytes 4000000 | tf_op jit(solution)/shard_map/plan/pallas_call | solution.py:486
  4.1 3.0 %collective-permute-start.36 = (bf16[7,64,128]{2,1,0:T(8,128)(2,1)S(1)}, bf16[7,64,128]{2,1,0:T(8,128)(2,1)S(1)}, u32[]{:S(2)}, u32[]{:S(2)}) collective-permute-start(bf16[7,64,128]{2,1,0:T(8,128)(2,1)S(1)} %get-tuple-element.76.refs_7_), channel_id=1, source_target_pairs={{0,8},{2,6},{8,16},{10,2},{16,24},{18,10},{24,28},{26,18},{28,20},... | collective-permute-start | bytes 344072 | tf_op jit(solution)/shard_map/ppermute | solution.py:600
  7.1 0.0 collective-permute-start.40
  7.1 3.1 %collective-permute-done.36.refs_5_ = bf16[7,64,128]{2,1,0:T(8,128)(2,1)S(1)} collective-permute-done((bf16[7,64,128]{2,1,0:T(8,128)(2,1)S(1)}, bf16[7,64,128]{2,1,0:T(8,128)(2,1)S(1)}, u32[]{:S(2)}, u32[]{:S(2)}) %collective-permute-start.36) | collective-permute-done | bytes 114720 | tf_op jit(solution)/shard_map/ppermute | solution.py:600
  10.2 2.2 %collective-permute-start.37 = (bf16[7,64,128]{2,1,0:T(8,128)(2,1)S(1)}, bf16[7,64,128]{2,1,0:T(8,128)(2,1)S(1)}, u32[]{:S(2)}, u32[]{:S(2)}) collective-permute-start(bf16[7,64,128]{2,1,0:T(8,128)(2,1)S(1)} %collective-permute-done.36.refs_5_), channel_id=1, source_target_pairs={{0,8},{2,6},{8,16},{10,2},{16,24},{18,10},{24,28},{26,18},{28,20},... | collective-permute-start | bytes 344072 | tf_op jit(solution)/shard_map/ppermute | solution.py:600
  12.4 0.0 collective-permute-done.40.refs_6_
  12.4 0.3 collective-permute-start.41
  12.7 0.0 collective-permute-start.50
  12.7 0.5 collective-permute-start.48
  13.2 3.0 %collective-permute-done.37.refs_3_ = bf16[7,64,128]{2,1,0:T(8,128)(2,1)S(1)} collective-permute-done((bf16[7,64,128]{2,1,0:T(8,128)(2,1)S(1)}, bf16[7,64,128]{2,1,0:T(8,128)(2,1)S(1)}, u32[]{:S(2)}, u32[]{:S(2)}) %collective-permute-start.37) | collective-permute-done | bytes 114720 | tf_op jit(solution)/shard_map/ppermute | solution.py:600
  16.2 0.9 %collective-permute-start.38 = (bf16[7,64,128]{2,1,0:T(8,128)(2,1)S(1)}, bf16[7,64,128]{2,1,0:T(8,128)(2,1)S(1)}, u32[]{:S(2)}, u32[]{:S(2)}) collective-permute-start(bf16[7,64,128]{2,1,0:T(8,128)(2,1)S(1)} %collective-permute-done.37.refs_3_), channel_id=1, source_target_pairs={{0,8},{2,6},{8,16},{10,2},{16,24},{18,10},{24,28},{26,18},{28,20},... | collective-permute-start | bytes 344072 | tf_op jit(solution)/shard_map/ppermute | solution.py:600
  17.2 1.1 %collective-permute-done.41.refs_4_ = bf16[7,64,128]{2,1,0:T(8,128)(2,1)S(1)} collective-permute-done((bf16[7,64,128]{2,1,0:T(8,128)(2,1)S(1)}, bf16[7,64,128]{2,1,0:T(8,128)(2,1)S(1)}, u32[]{:S(2)}, u32[]{:S(2)}) %collective-permute-start.41) | collective-permute-done | bytes 114720 | tf_op jit(solution)/shard_map/ppermute | solution.py:600
  18.3 0.0 collective-permute-start.42
  18.3 1.0 %collective-permute-start.46 = (bf16[7,64,128]{2,1,0:T(8,128)(2,1)S(1)}, bf16[7,64,128]{2,1,0:T(8,128)(2,1)S(1)}, u32[]{:S(2)}, u32[]{:S(2)}) collective-permute-start(bf16[7,64,128]{2,1,0:T(8,128)(2,1)S(1)} %collective-permute-done.37.refs_3_), channel_id=1, source_target_pairs={{0,2},{2,0},{8,10},{10,8},{16,18},{18,16},{24,26},{26,24},{28,30},... | collective-permute-start | bytes 344072 | tf_op jit(solution)/shard_map/ppermute | solution.py:602
  19.3 0.0 collective-permute-done.48.refs_13_
  19.3 0.1 collective-permute-start.47
  19.4 2.4 %collective-permute-done.38.refs_1_ = bf16[7,64,128]{2,1,0:T(8,128)(2,1)S(1)} collective-permute-done((bf16[7,64,128]{2,1,0:T(8,128)(2,1)S(1)}, bf16[7,64,128]{2,1,0:T(8,128)(2,1)S(1)}, u32[]{:S(2)}, u32[]{:S(2)}) %collective-permute-start.38) | collective-permute-done | bytes 114720 | tf_op jit(solution)/shard_map/ppermute | solution.py:600
  21.8 0.1 collective-permute-start.39
  22.0 0.0 collective-permute-done.49.refs_14_
  22.0 0.0 collective-permute-start.43
  22.0 1.8 %collective-permute-done.42.refs_2_ = bf16[7,64,128]{2,1,0:T(8,128)(2,1)S(1)} collective-permute-done((bf16[7,64,128]{2,1,0:T(8,128)(2,1)S(1)}, bf16[7,64,128]{2,1,0:T(8,128)(2,1)S(1)}, u32[]{:S(2)}, u32[]{:S(2)}) %collective-permute-start.42) | collective-permute-done | bytes 114720 | tf_op jit(solution)/shard_map/ppermute | solution.py:600
  23.8 0.2 collective-permute-start.44
  24.0 0.3 collective-permute-start.45
  24.3 0.0 collective-permute-done.47.refs_12_
  24.3 2.3 %collective-permute-done.39.refs_0_ = bf16[7,64,128]{2,1,0:T(8,128)(2,1)S(1)} collective-permute-done((bf16[7,64,128]{2,1,0:T(8,128)(2,1)S(1)}, bf16[7,64,128]{2,1,0:T(8,128)(2,1)S(1)}, u32[]{:S(2)}, u32[]{:S(2)}) %collective-permute-start.39) | collective-permute-done | bytes 114720 | tf_op jit(solution)/shard_map/ppermute | solution.py:603
  26.6 0.0 collective-permute-done.43.refs_8_
  26.6 0.0 collective-permute-done.44.refs_9_
  26.6 7.6 %compute.3 = (bf16[56,64,128]{2,1,0:T(8,128)(2,1)S(1)}, bf16[14,64,128]{2,1,0:T(8,128)(2,1)S(1)}, bf16[42,64,128]{2,1,0:T(8,128)(2,1)S(1)}, bf16[18,128,128]{2,1,0:T(8,128)(2,1)S(1)}, bf16[18,128,128]{2,1,0:T(8,128)(2,1)S(1)}) custom-call(s32[32,128]{1,0:T(8,128)S(1)} %get-tuple-element.74.plan, bf16[128,8192]{1,0:T(8,128)(2,1)} %tokens.1, ...), custom_call_target="tpu_custom_call" | custom-call | flops 1000000000 | bytes 20000000 | tf_op jit(solution)/shard_map/compute/pallas_call | solution.py:542
  34.2 1.1 %collective-permute-start.52 = (bf16[14,64,128]{2,1,0:T(8,128)(2,1)S(1)}, bf16[14,64,128]{2,1,0:T(8,128)(2,1)S(1)}, u32[]{:S(2)}, u32[]{:S(2)}) collective-permute-start(bf16[14,64,128]{2,1,0:T(8,128)(2,1)S(1)} %get-tuple-element.80), channel_id=1, source_target_pairs={{0,2},{2,0},{8,10},{10,8},{16,18},{18,16},{24,26},{26,24},{28,30},... | collective-permute-start | bytes 688136 | tf_op jit(solution)/shard_map/ppermute | solution.py:611
  35.3 1.1 %collective-permute-done.52.__1_ = bf16[14,64,128]{2,1,0:T(8,128)(2,1)S(1)} collective-permute-done((bf16[14,64,128]{2,1,0:T(8,128)(2,1)S(1)}, bf16[14,64,128]{2,1,0:T(8,128)(2,1)S(1)}, u32[]{:S(2)}, u32[]{:S(2)}) %collective-permute-start.52) | collective-permute-done | bytes 229408 | tf_op jit(solution)/shard_map/ppermute | solution.py:611
  36.5 0.4 collective-permute-start.53
  36.8 0.1 add_convert_fusion.13
  36.9 1.0 %collective-permute-start.54 = (bf16[7,64,128]{2,1,0:T(8,128)(2,1)S(1)}, bf16[7,64,128]{2,1,0:T(8,128)(2,1)S(1)}, u32[]{:S(2)}, u32[]{:S(2)}) collective-permute-start(bf16[7,64,128]{2,1,0:T(8,128)(2,1)S(1)} %get-tuple-element.81), channel_id=1, source_target_pairs={{0,8},{2,6},{8,16},{10,2},{16,24},{18,10},{24,28},{26,18},{28,20},... | collective-permute-start | bytes 344072 | tf_op jit(solution)/shard_map/ppermute | solution.py:628
  38.0 1.1 %collective-permute-start.55 = (bf16[7,64,128]{2,1,0:T(8,128)(2,1)S(1)}, bf16[7,64,128]{2,1,0:T(8,128)(2,1)S(1)}, u32[]{:S(2)}, u32[]{:S(2)}) collective-permute-start(bf16[7,64,128]{2,1,0:T(8,128)(2,1)S(1)} %get-tuple-element.82), channel_id=1, source_target_pairs={{0,4},{2,10},{8,0},{10,18},{16,8},{18,26},{24,16},{26,30},{28,24},... | collective-permute-start | bytes 344072 | tf_op jit(solution)/shard_map/ppermute | solution.py:628
  39.0 3.5 %collective-permute-done.35.__2_.note.refs_0_ = s32[1,128]{1,0:T(1,128)S(1)} collective-permute-done((s32[1,128]{1,0:T(1,128)S(1)}, s32[1,128]{1,0:T(1,128)S(1)}, u32[]{:S(2)}, u32[]{:S(2)}) %collective-permute-start.35) | collective-permute-done | bytes 544 | tf_op jit(solution)/shard_map/ppermute | solution.py:652
  42.5 0.0 collective-permute-done.54.__0_
  42.6 0.2 collective-permute-done.55.__1_
  42.7 0.1 add_convert_fusion.12.__1_
  42.8 0.1 add_convert_fusion.11
  42.9 0.2 collective-permute-start.57
  43.1 1.4 %collective-permute-start.56 = (bf16[7,64,128]{2,1,0:T(8,128)(2,1)S(1)}, bf16[7,64,128]{2,1,0:T(8,128)(2,1)S(1)}, u32[]{:S(2)}, u32[]{:S(2)}) collective-permute-start(bf16[7,64,128]{2,1,0:T(8,128)(2,1)S(1)} %add_convert_fusion.12.__1_), channel_id=1, source_target_pairs={{0,8},{2,6},{8,16},{10,2},{16,24},{18,10},{24,28},{26,18},{28,20},... | collective-permute-start | bytes 344072 | tf_op jit(solution)/shard_map/ppermute | solution.py:628
  44.5 0.7 %collective-permute-start.59 = (bf16[7,64,128]{2,1,0:T(8,128)(2,1)S(1)}, bf16[7,64,128]{2,1,0:T(8,128)(2,1)S(1)}, u32[]{:S(2)}, u32[]{:S(2)}) collective-permute-start(bf16[7,64,128]{2,1,0:T(8,128)(2,1)S(1)} %get-tuple-element.109.__1_), channel_id=1, source_target_pairs={{0,4},{2,10},{8,0},{10,18},{16,8},{18,26},{24,16},{26,30},{28,24},... | collective-permute-start | bytes 344072 | tf_op jit(solution)/shard_map/ppermute | solution.py:628
  45.2 2.7 %prepare.3 = (bf16[128,4096]{1,0:T(8,128)(2,1)}, bf16[128,4096]{1,0:T(8,128)(2,1)}, bf16[18,128,128]{2,1,0:T(8,128)(2,1)S(1)}) custom-call(s32[32,128]{1,0:T(8,128)S(1)} %get-tuple-element.74.plan, s32[1,128]{1,0:T(1,128)S(1)} %collective-permute-done.35.__2_.note.refs_0_, bf16[18,128,128]{2,1,0:T(8,128)(2,1)S(1)} %turn.24.first), custom_call_target="tpu_custom_call" | custom-call | flops 1000000 | bytes 6000000 | tf_op jit(solution)/shard_map/prepare/pallas_call | solution.py:559
  47.9 0.2 collective-permute-done.56.__0_
  48.0 0.1 add_convert_fusion.10.__1_
  48.1 2.5 %collective-permute-start.58 = (bf16[7,64,128]{2,1,0:T(8,128)(2,1)S(1)}, bf16[7,64,128]{2,1,0:T(8,128)(2,1)S(1)}, u32[]{:S(2)}, u32[]{:S(2)}) collective-permute-start(bf16[7,64,128]{2,1,0:T(8,128)(2,1)S(1)} %add_convert_fusion.10.__1_), channel_id=1, source_target_pairs={{0,8},{2,6},{8,16},{10,2},{16,24},{18,10},{24,28},{26,18},{28,20},... | collective-permute-start | bytes 344072 | tf_op jit(solution)/shard_map/ppermute | solution.py:628
  50.6 0.1 add_convert_fusion.9.__1_
  50.7 0.3 collective-permute-start.61
  51.0 0.3 collective-permute-start.63
  51.3 3.5 %collective-permute-done.58.__0_ = bf16[7,64,128]{2,1,0:T(8,128)(2,1)S(1)} collective-permute-done((bf16[7,64,128]{2,1,0:T(8,128)(2,1)S(1)}, bf16[7,64,128]{2,1,0:T(8,128)(2,1)S(1)}, u32[]{:S(2)}, u32[]{:S(2)}) %collective-permute-start.58) | collective-permute-done | bytes 114720 | tf_op jit(solution)/shard_map/ppermute | solution.py:628
  54.8 0.1 add_convert_fusion.8
  54.8 1.1 %collective-permute-start.60 = (bf16[7,64,128]{2,1,0:T(8,128)(2,1)S(1)}, bf16[7,64,128]{2,1,0:T(8,128)(2,1)S(1)}, u32[]{:S(2)}, u32[]{:S(2)}) collective-permute-start(bf16[7,64,128]{2,1,0:T(8,128)(2,1)S(1)} %add_convert_fusion.8), channel_id=1, source_target_pairs={{0,8},{2,6},{8,16},{10,2},{16,24},{18,10},{24,28},{26,18},{28,20},... | collective-permute-start | bytes 344072 | tf_op jit(solution)/shard_map/ppermute | solution.py:636
  55.9 4.5 %collective-permute-done.51.refs_1_ = bf16[18,128,128]{2,1,0:T(8,128)(2,1)S(1)} collective-permute-done((bf16[18,128,128]{2,1,0:T(8,128)(2,1)S(1)}, bf16[18,128,128]{2,1,0:T(8,128)(2,1)S(1)}, u32[]{:S(2)}, u32[]{:S(2)}) %collective-permute-start.51) | collective-permute-done | bytes 589856 | tf_op jit(solution)/shard_map/ppermute | solution.py:652
  60.5 0.0 copy-start
  60.5 0.0 copy-start.1
  60.5 0.0 copy-start.2
  60.5 2.5 %last.3 = (bf16[128,4096]{1,0:T(8,128)(2,1)}, bf16[128,4096]{1,0:T(8,128)(2,1)}, bf16[1,2,128,128]{3,2,1,0:T(8,128)(2,1)}, bf16[1,2,128,128]{3,2,1,0:T(8,128)(2,...) custom-call(s32[32,128]{1,0:T(8,128)S(1)} %get-tuple-element.74.plan, ...), custom_call_target="tpu_custom_call", output_to_operand_aliasing={{0}: (10, {}), {1}: (11, {})} | custom-call | flops 1000000 | bytes 3000000 | tf_op jit(solution)/shard_map/last/pallas_call | solution.py:573
  (26 shorter events, 0.1 us)
Async XLA Ops:
  0.6 1.8 %collective-permute-start.32 = (bf16[1,2,128,128]{3,2,1,0:T(8,128)(2,1)}, bf16[1,2,128,128]{3,2,1,0:T(8,128)(2,1)S(1)}, u32[]{:S(2)}, u32[]{:S(2)}) collective-permute-start(bf16[1,2,128,128]{3,2,1,0:T(8,128)(2,1)} %refs_0_.1), channel_id=1, source_target_pairs={{0,2},{2,0},{8,10},{10,8},{16,18},{18,16},{24,26},{26,24},{28,30},... | collective-permute-start | bytes 196616 | tf_op jit(solution)/shard_map/ppermute | solution.py:648
  1.2 1.5 %collective-permute-start.33 = (bf16[1,2,128,128]{3,2,1,0:T(8,128)(2,1)}, bf16[1,2,128,128]{3,2,1,0:T(8,128)(2,1)S(1)}, u32[]{:S(2)}, u32[]{:S(2)}) collective-permute-start(bf16[1,2,128,128]{3,2,1,0:T(8,128)(2,1)} %refs_1_.1), channel_id=1, source_target_pairs={{0,2},{2,0},{8,10},{10,8},{16,18},{18,16},{24,26},{26,24},{28,30},... | collective-permute-start | bytes 196616 | tf_op jit(solution)/shard_map/ppermute | solution.py:648
  1.2 1.5 %collective-permute-start.34 = (bf16[1,2,128,128]{3,2,1,0:T(8,128)(2,1)}, bf16[1,2,128,128]{3,2,1,0:T(8,128)(2,1)S(1)}, u32[]{:S(2)}, u32[]{:S(2)}) collective-permute-start(bf16[1,2,128,128]{3,2,1,0:T(8,128)(2,1)} %refs_2_.1), channel_id=1, source_target_pairs={{0,2},{2,0},{8,10},{10,8},{16,18},{18,16},{24,26},{26,24},{28,30},... | collective-permute-start | bytes 196616 | tf_op jit(solution)/shard_map/ppermute | solution.py:648
  4.1 6.0 %collective-permute-start.36 = (bf16[7,64,128]{2,1,0:T(8,128)(2,1)S(1)}, bf16[7,64,128]{2,1,0:T(8,128)(2,1)S(1)}, u32[]{:S(2)}, u32[]{:S(2)}) collective-permute-start(bf16[7,64,128]{2,1,0:T(8,128)(2,1)S(1)} %get-tuple-element.76.refs_7_), channel_id=1, source_target_pairs={{0,8},{2,6},{8,16},{10,2},{16,24},{18,10},{24,28},{26,18},{28,20},... | collective-permute-start | bytes 344072 | tf_op jit(solution)/shard_map/ppermute | solution.py:600
  7.1 5.3 %collective-permute-start.40 = (bf16[7,64,128]{2,1,0:T(8,128)(2,1)S(1)}, bf16[7,64,128]{2,1,0:T(8,128)(2,1)S(1)}, u32[]{:S(2)}, u32[]{:S(2)}) collective-permute-start(bf16[7,64,128]{2,1,0:T(8,128)(2,1)S(1)} %get-tuple-element.76.refs_7_), channel_id=1, source_target_pairs={{0,4},{2,10},{8,0},{10,18},{16,8},{18,26},{24,16},{26,30},{28,24},... | collective-permute-start | bytes 344072 | tf_op jit(solution)/shard_map/ppermute | solution.py:600
  10.2 6.1 %collective-permute-start.37 = (bf16[7,64,128]{2,1,0:T(8,128)(2,1)S(1)}, bf16[7,64,128]{2,1,0:T(8,128)(2,1)S(1)}, u32[]{:S(2)}, u32[]{:S(2)}) collective-permute-start(bf16[7,64,128]{2,1,0:T(8,128)(2,1)S(1)} %collective-permute-done.36.refs_5_), channel_id=1, source_target_pairs={{0,8},{2,6},{8,16},{10,2},{16,24},{18,10},{24,28},{26,18},{28,20},... | collective-permute-start | bytes 344072 | tf_op jit(solution)/shard_map/ppermute | solution.py:600
  12.4 5.9 %collective-permute-start.41 = (bf16[7,64,128]{2,1,0:T(8,128)(2,1)S(1)}, bf16[7,64,128]{2,1,0:T(8,128)(2,1)S(1)}, u32[]{:S(2)}, u32[]{:S(2)}) collective-permute-start(bf16[7,64,128]{2,1,0:T(8,128)(2,1)S(1)} %collective-permute-done.40.refs_6_), channel_id=1, source_target_pairs={{0,4},{2,10},{8,0},{10,18},{16,8},{18,26},{24,16},{26,30},{28,24},... | collective-permute-start | bytes 344072 | tf_op jit(solution)/shard_map/ppermute | solution.py:600
  12.7 5.6 %collective-permute-start.50 = (bf16[7,64,128]{2,1,0:T(8,128)(2,1)S(1)}, bf16[7,64,128]{2,1,0:T(8,128)(2,1)S(1)}, u32[]{:S(2)}, u32[]{:S(2)}) collective-permute-start(bf16[7,64,128]{2,1,0:T(8,128)(2,1)S(1)} %get-tuple-element.76.refs_7_), channel_id=1, source_target_pairs={{0,2},{2,0},{8,10},{10,8},{16,18},{18,16},{24,26},{26,24},{28,30},... | collective-permute-start | bytes 344072 | tf_op jit(solution)/shard_map/ppermute | solution.py:602
  12.7 6.6 %collective-permute-start.48 = (bf16[7,64,128]{2,1,0:T(8,128)(2,1)S(1)}, bf16[7,64,128]{2,1,0:T(8,128)(2,1)S(1)}, u32[]{:S(2)}, u32[]{:S(2)}) collective-permute-start(bf16[7,64,128]{2,1,0:T(8,128)(2,1)S(1)} %collective-permute-done.36.refs_5_), channel_id=1, source_target_pairs={{0,2},{2,0},{8,10},{10,8},{16,18},{18,16},{24,26},{26,24},{28,30},... | collective-permute-start | bytes 344072 | tf_op jit(solution)/shard_map/ppermute | solution.py:602
  16.2 5.6 %collective-permute-start.38 = (bf16[7,64,128]{2,1,0:T(8,128)(2,1)S(1)}, bf16[7,64,128]{2,1,0:T(8,128)(2,1)S(1)}, u32[]{:S(2)}, u32[]{:S(2)}) collective-permute-start(bf16[7,64,128]{2,1,0:T(8,128)(2,1)S(1)} %collective-permute-done.37.refs_3_), channel_id=1, source_target_pairs={{0,8},{2,6},{8,16},{10,2},{16,24},{18,10},{24,28},{26,18},{28,20},... | collective-permute-start | bytes 344072 | tf_op jit(solution)/shard_map/ppermute | solution.py:600
  17.2 4.8 %collective-permute-start.49 = (bf16[7,64,128]{2,1,0:T(8,128)(2,1)S(1)}, bf16[7,64,128]{2,1,0:T(8,128)(2,1)S(1)}, u32[]{:S(2)}, u32[]{:S(2)}) collective-permute-start(bf16[7,64,128]{2,1,0:T(8,128)(2,1)S(1)} %collective-permute-done.40.refs_6_), channel_id=1, source_target_pairs={{0,2},{2,0},{8,10},{10,8},{16,18},{18,16},{24,26},{26,24},{28,30},... | collective-permute-start | bytes 344072 | tf_op jit(solution)/shard_map/ppermute | solution.py:602
  18.3 5.5 %collective-permute-start.42 = (bf16[7,64,128]{2,1,0:T(8,128)(2,1)S(1)}, bf16[7,64,128]{2,1,0:T(8,128)(2,1)S(1)}, u32[]{:S(2)}, u32[]{:S(2)}) collective-permute-start(bf16[7,64,128]{2,1,0:T(8,128)(2,1)S(1)} %collective-permute-done.41.refs_4_), channel_id=1, source_target_pairs={{0,4},{2,10},{8,0},{10,18},{16,8},{18,26},{24,16},{26,30},{28,24},... | collective-permute-start | bytes 344072 | tf_op jit(solution)/shard_map/ppermute | solution.py:600
  18.3 5.7 %collective-permute-start.46 = (bf16[7,64,128]{2,1,0:T(8,128)(2,1)S(1)}, bf16[7,64,128]{2,1,0:T(8,128)(2,1)S(1)}, u32[]{:S(2)}, u32[]{:S(2)}) collective-permute-start(bf16[7,64,128]{2,1,0:T(8,128)(2,1)S(1)} %collective-permute-done.37.refs_3_), channel_id=1, source_target_pairs={{0,2},{2,0},{8,10},{10,8},{16,18},{18,16},{24,26},{26,24},{28,30},... | collective-permute-start | bytes 344072 | tf_op jit(solution)/shard_map/ppermute | solution.py:602
  19.3 5.0 %collective-permute-start.47 = (bf16[7,64,128]{2,1,0:T(8,128)(2,1)S(1)}, bf16[7,64,128]{2,1,0:T(8,128)(2,1)S(1)}, u32[]{:S(2)}, u32[]{:S(2)}) collective-permute-start(bf16[7,64,128]{2,1,0:T(8,128)(2,1)S(1)} %collective-permute-done.41.refs_4_), channel_id=1, source_target_pairs={{0,2},{2,0},{8,10},{10,8},{16,18},{18,16},{24,26},{26,24},{28,30},... | collective-permute-start | bytes 344072 | tf_op jit(solution)/shard_map/ppermute | solution.py:602
  21.8 4.8 %collective-permute-start.39 = (bf16[7,64,128]{2,1,0:T(8,128)(2,1)S(1)}, bf16[7,64,128]{2,1,0:T(8,128)(2,1)S(1)}, u32[]{:S(2)}, u32[]{:S(2)}) collective-permute-start(bf16[7,64,128]{2,1,0:T(8,128)(2,1)S(1)} %collective-permute-done.38.refs_1_), channel_id=1, source_target_pairs={{0,8},{2,6},{8,16},{10,2},{16,24},{18,10},{24,28},{26,18},{28,20},... | collective-permute-start | bytes 344072 | tf_op jit(solution)/shard_map/ppermute | solution.py:603
  22.0 4.6 %collective-permute-start.43 = (bf16[7,64,128]{2,1,0:T(8,128)(2,1)S(1)}, bf16[7,64,128]{2,1,0:T(8,128)(2,1)S(1)}, u32[]{:S(2)}, u32[]{:S(2)}) collective-permute-start(bf16[7,64,128]{2,1,0:T(8,128)(2,1)S(1)} %collective-permute-done.38.refs_1_), channel_id=1, source_target_pairs={{0,10},{2,4},{8,18},{10,0},{16,26},{18,8},{24,30},{26,16},{28,22},... | collective-permute-start | bytes 344072 | tf_op jit(solution)/shard_map/ppermute | solution.py:604
  23.8 2.9 %collective-permute-start.44 = (bf16[7,64,128]{2,1,0:T(8,128)(2,1)S(1)}, bf16[7,64,128]{2,1,0:T(8,128)(2,1)S(1)}, u32[]{:S(2)}, u32[]{:S(2)}) collective-permute-start(bf16[7,64,128]{2,1,0:T(8,128)(2,1)S(1)} %collective-permute-done.38.refs_1_), channel_id=1, source_target_pairs={{0,2},{2,0},{8,10},{10,8},{16,18},{18,16},{24,26},{26,24},{28,30},... | collective-permute-start | bytes 344072 | tf_op jit(solution)/shard_map/ppermute | solution.py:602
  24.0 2.6 %collective-permute-start.45 = (bf16[7,64,128]{2,1,0:T(8,128)(2,1)S(1)}, bf16[7,64,128]{2,1,0:T(8,128)(2,1)S(1)}, u32[]{:S(2)}, u32[]{:S(2)}) collective-permute-start(bf16[7,64,128]{2,1,0:T(8,128)(2,1)S(1)} %collective-permute-done.42.refs_2_), channel_id=1, source_target_pairs={{0,2},{2,0},{8,10},{10,8},{16,18},{18,16},{24,26},{26,24},{28,30},... | collective-permute-start | bytes 344072 | tf_op jit(solution)/shard_map/ppermute | solution.py:602
  34.2 2.2 %collective-permute-start.52 = (bf16[14,64,128]{2,1,0:T(8,128)(2,1)S(1)}, bf16[14,64,128]{2,1,0:T(8,128)(2,1)S(1)}, u32[]{:S(2)}, u32[]{:S(2)}) collective-permute-start(bf16[14,64,128]{2,1,0:T(8,128)(2,1)S(1)} %get-tuple-element.80), channel_id=1, source_target_pairs={{0,2},{2,0},{8,10},{10,8},{16,18},{18,16},{24,26},{26,24},{28,30},... | collective-permute-start | bytes 688136 | tf_op jit(solution)/shard_map/ppermute | solution.py:611
  36.5 6.3 %collective-permute-start.53 = (bf16[42,64,128]{2,1,0:T(8,128)(2,1)S(1)}, bf16[42,64,128]{2,1,0:T(8,128)(2,1)S(1)}, u32[]{:S(2)}, u32[]{:S(2)}) collective-permute-start(bf16[42,64,128]{2,1,0:T(8,128)(2,1)S(1)} %turn.21), channel_id=1, source_target_pairs={{0,2},{2,0},{8,10},{10,8},{16,18},{18,16},{24,26},{26,24},{28,30},... | collective-permute-start | bytes 2064392 | tf_op jit(solution)/shard_map/ppermute | solution.py:612
  36.9 5.6 %collective-permute-start.54 = (bf16[7,64,128]{2,1,0:T(8,128)(2,1)S(1)}, bf16[7,64,128]{2,1,0:T(8,128)(2,1)S(1)}, u32[]{:S(2)}, u32[]{:S(2)}) collective-permute-start(bf16[7,64,128]{2,1,0:T(8,128)(2,1)S(1)} %get-tuple-element.81), channel_id=1, source_target_pairs={{0,8},{2,6},{8,16},{10,2},{16,24},{18,10},{24,28},{26,18},{28,20},... | collective-permute-start | bytes 344072 | tf_op jit(solution)/shard_map/ppermute | solution.py:628
  38.0 4.8 %collective-permute-start.55 = (bf16[7,64,128]{2,1,0:T(8,128)(2,1)S(1)}, bf16[7,64,128]{2,1,0:T(8,128)(2,1)S(1)}, u32[]{:S(2)}, u32[]{:S(2)}) collective-permute-start(bf16[7,64,128]{2,1,0:T(8,128)(2,1)S(1)} %get-tuple-element.82), channel_id=1, source_target_pairs={{0,4},{2,10},{8,0},{10,18},{16,8},{18,26},{24,16},{26,30},{28,24},... | collective-permute-start | bytes 344072 | tf_op jit(solution)/shard_map/ppermute | solution.py:628
  39.0 3.5 %collective-permute-start.35 = (s32[1,128]{1,0:T(1,128)S(1)}, s32[1,128]{1,0:T(1,128)S(1)}, u32[]{:S(2)}, u32[]{:S(2)}) collective-permute-start(s32[1,128]{1,0:T(1,128)S(1)} %get-tuple-element.75), channel_id=1, source_target_pairs={{0,1},{1,0},{2,3},{3,2},{4,5},{5,4},{6,7},{7,6},{8,9},{9,8},{10,11... | collective-permute-start | bytes 1544 | tf_op jit(solution)/shard_map/ppermute | solution.py:652
  42.9 2.3 %collective-permute-start.57 = (bf16[7,64,128]{2,1,0:T(8,128)(2,1)S(1)}, bf16[7,64,128]{2,1,0:T(8,128)(2,1)S(1)}, u32[]{:S(2)}, u32[]{:S(2)}) collective-permute-start(bf16[7,64,128]{2,1,0:T(8,128)(2,1)S(1)} %get-tuple-element.110.refs_2_), channel_id=1, source_target_pairs={{0,2},{2,0},{8,10},{10,8},{16,18},{18,16},{24,26},{26,24},{28,30},... | collective-permute-start | bytes 344072 | tf_op jit(solution)/shard_map/ppermute | solution.py:624
  43.1 5.0 %collective-permute-start.56 = (bf16[7,64,128]{2,1,0:T(8,128)(2,1)S(1)}, bf16[7,64,128]{2,1,0:T(8,128)(2,1)S(1)}, u32[]{:S(2)}, u32[]{:S(2)}) collective-permute-start(bf16[7,64,128]{2,1,0:T(8,128)(2,1)S(1)} %add_convert_fusion.12.__1_), channel_id=1, source_target_pairs={{0,8},{2,6},{8,16},{10,2},{16,24},{18,10},{24,28},{26,18},{28,20},... | collective-permute-start | bytes 344072 | tf_op jit(solution)/shard_map/ppermute | solution.py:628
  44.5 15.9 %collective-permute-start.51 = (bf16[18,128,128]{2,1,0:T(8,128)(2,1)S(1)}, bf16[18,128,128]{2,1,0:T(8,128)(2,1)S(1)}, u32[]{:S(2)}, u32[]{:S(2)}) collective-permute-start(bf16[18,128,128]{2,1,0:T(8,128)(2,1)S(1)} %get-tuple-element.77), channel_id=1, source_target_pairs={{0,1},{1,0},{2,3},{3,2},{4,5},{5,4},{6,7},{7,6},{8,9},{9,8},{10,11... | collective-permute-start | bytes 1769480 | tf_op jit(solution)/shard_map/ppermute | solution.py:652
  44.5 6.1 %collective-permute-start.59 = (bf16[7,64,128]{2,1,0:T(8,128)(2,1)S(1)}, bf16[7,64,128]{2,1,0:T(8,128)(2,1)S(1)}, u32[]{:S(2)}, u32[]{:S(2)}) collective-permute-start(bf16[7,64,128]{2,1,0:T(8,128)(2,1)S(1)} %get-tuple-element.109.__1_), channel_id=1, source_target_pairs={{0,4},{2,10},{8,0},{10,18},{16,8},{18,26},{24,16},{26,30},{28,24},... | collective-permute-start | bytes 344072 | tf_op jit(solution)/shard_map/ppermute | solution.py:628
  48.1 6.7 %collective-permute-start.58 = (bf16[7,64,128]{2,1,0:T(8,128)(2,1)S(1)}, bf16[7,64,128]{2,1,0:T(8,128)(2,1)S(1)}, u32[]{:S(2)}, u32[]{:S(2)}) collective-permute-start(bf16[7,64,128]{2,1,0:T(8,128)(2,1)S(1)} %add_convert_fusion.10.__1_), channel_id=1, source_target_pairs={{0,8},{2,6},{8,16},{10,2},{16,24},{18,10},{24,28},{26,18},{28,20},... | collective-permute-start | bytes 344072 | tf_op jit(solution)/shard_map/ppermute | solution.py:628
  50.7 9.7 %collective-permute-start.61 = (bf16[7,64,128]{2,1,0:T(8,128)(2,1)S(1)}, bf16[7,64,128]{2,1,0:T(8,128)(2,1)S(1)}, u32[]{:S(2)}, u32[]{:S(2)}) collective-permute-start(bf16[7,64,128]{2,1,0:T(8,128)(2,1)S(1)} %add_convert_fusion.9.__1_), channel_id=1, source_target_pairs={{0,4},{2,10},{8,0},{10,18},{16,8},{18,26},{24,16},{26,30},{28,24},... | collective-permute-start | bytes 344072 | tf_op jit(solution)/shard_map/ppermute | solution.py:628
  51.0 9.4 %collective-permute-start.63 = (bf16[7,64,128]{2,1,0:T(8,128)(2,1)S(1)}, bf16[7,64,128]{2,1,0:T(8,128)(2,1)S(1)}, u32[]{:S(2)}, u32[]{:S(2)}) collective-permute-start(bf16[7,64,128]{2,1,0:T(8,128)(2,1)S(1)} %add_convert_fusion.9.__1_), channel_id=1, source_target_pairs={{0,6},{2,8},{8,2},{10,16},{16,10},{18,24},{24,18},{26,28},{28,26},... | collective-permute-start | bytes 344072 | tf_op jit(solution)/shard_map/ppermute | solution.py:640
  54.8 5.6 %collective-permute-start.60 = (bf16[7,64,128]{2,1,0:T(8,128)(2,1)S(1)}, bf16[7,64,128]{2,1,0:T(8,128)(2,1)S(1)}, u32[]{:S(2)}, u32[]{:S(2)}) collective-permute-start(bf16[7,64,128]{2,1,0:T(8,128)(2,1)S(1)} %add_convert_fusion.8), channel_id=1, source_target_pairs={{0,8},{2,6},{8,16},{10,2},{16,24},{18,10},{24,28},{26,18},{28,20},... | collective-permute-start | bytes 344072 | tf_op jit(solution)/shard_map/ppermute | solution.py:636
  55.9 4.5 %collective-permute-start.62 = (bf16[7,64,128]{2,1,0:T(8,128)(2,1)S(1)}, bf16[7,64,128]{2,1,0:T(8,128)(2,1)S(1)}, u32[]{:S(2)}, u32[]{:S(2)}) collective-permute-start(bf16[7,64,128]{2,1,0:T(8,128)(2,1)S(1)} %add_convert_fusion.8), channel_id=1, source_target_pairs={{0,10},{2,4},{8,18},{10,0},{16,26},{18,8},{24,30},{26,16},{28,22},... | collective-permute-start | bytes 344072 | tf_op jit(solution)/shard_map/ppermute | solution.py:639
  60.5 3.1 %copy-start = (bf16[1,2,128,128]{3,2,1,0:T(8,128)(2,1)S(1)}, bf16[1,2,128,128]{3,2,1,0:T(8,128)(2,1)}, u32[]{:S(2)}) copy-start(bf16[1,2,128,128]{3,2,1,0:T(8,128)(2,1)} %refs_0_.1) | copy-start | bytes 196612
  60.5 3.1 %copy-start.1 = (bf16[1,2,128,128]{3,2,1,0:T(8,128)(2,1)S(1)}, bf16[1,2,128,128]{3,2,1,0:T(8,128)(2,1)}, u32[]{:S(2)}) copy-start(bf16[1,2,128,128]{3,2,1,0:T(8,128)(2,1)} %refs_1_.1) | copy-start | bytes 196612
  60.5 3.1 %copy-start.2 = (bf16[1,2,128,128]{3,2,1,0:T(8,128)(2,1)S(1)}, bf16[1,2,128,128]{3,2,1,0:T(8,128)(2,1)}, u32[]{:S(2)}) copy-start(bf16[1,2,128,128]{3,2,1,0:T(8,128)(2,1)} %refs_2_.1) | copy-start | bytes 196612

commit v6 on v5

--- a/solution.py
+++ b/solution.py
@@ -408,13 +408,11 @@
     lax.fori_loop(0, jnp.minimum(note[0, sz.note_n], sz.first), pick, None)
 
 
-def last_kernel(sz, plan, *refs):
+def add_kernel(sz, plan, *refs):
     T = sz.n_tensor
     notes, refs = refs[:T - 1], refs[T - 1:]
-    firsts, refs = refs[:T - 1], refs[T - 1:]
-    mine, theirs, held_strips, refs = refs[:3], refs[3:6], refs[6], refs[9:]
-    outputs, input_grads, grads, flag = refs[0], refs[1], refs[2:5], refs[5]
-    strips, read_sems, write_sems = refs[6:]
+    firsts, held_strips, refs = refs[:T - 1], refs[T - 1], refs[T + 2:]
+    outputs, input_grads, flag, strips, read_sems, write_sems = refs
     over = plan[HEAD_ROW, HEAD_OVER]
     for note in notes:
         over = jnp.maximum(over, note[0, sz.note_over])
@@ -434,27 +432,24 @@
     def loop(s, body):
         lax.fori_loop(0, jnp.minimum(notes[s][0, sz.note_n], sz.first), lambda i, _: body(i), None)
 
-    def begin(s):
-        loop(s, lambda i: move(s, i, False, lambda c: c.start()))
-
-    def add(s):
+    for s in range(T - 1):
+        if s:
+            loop(s, lambda i: move(s, i, False, lambda c: c.start()))
+
         def step(i):
-            move(s, i, False, lambda c: c.wait())
-            value = strips[i].astype(jnp.float32) + firsts[s][i].astype(jnp.float32)
+            if s:
+                move(s, i, False, lambda c: c.wait())
+            held = strips[i] if s else held_strips[i]
+            value = held.astype(jnp.float32) + firsts[s][i].astype(jnp.float32)
             strips[i] = value.astype(jnp.bfloat16)
             move(s, i, True, lambda c: c.start())
 
         loop(s, step)
-
-    def end(s):
         loop(s, lambda i: move(s, i, True, lambda c: c.wait()))
 
-    def first_add(i):
-        value = held_strips[i].astype(jnp.float32) + firsts[0][i].astype(jnp.float32)
-        strips[i] = value.astype(jnp.bfloat16)
-        move(0, i, True, lambda c: c.start())
-
-    loop(0, first_add)
+
+def last_kernel(sz, plan, *refs):
+    mine, theirs, grads = refs[:3], refs[3:6], refs[6:]
     core = plan[HEAD_ROW, HEAD_CORE]
     for k in range(3):
         for a in range(sz.nb):
@@ -464,11 +459,6 @@
                 value = sum(t[p].astype(jnp.float32) for t in terms)
                 rows = pl.ds(pl.multiple_of(c * ROWS, ROWS), ROWS)
                 grads[k][0, a, rows] = jnp.where(at > 0, value, 0.0).astype(jnp.bfloat16)
-    end(0)
-    for s in range(1, T - 1):
-        begin(s)
-        add(s)
-        end(s)
 
 
 def spec(space):
@@ -567,15 +557,13 @@
     )(plan, note, first)
 
 
-def call_last(sz, plan, notes, firsts, terms, strips, partial):
-    n = 2 + len(notes) + len(firsts) + len(terms)
-    out = jax.ShapeDtypeStruct((1, sz.nb, BLK, BLK), jnp.bfloat16)
+def call_add(sz, plan, notes, firsts, strips, partial):
+    n = 2 + len(notes) + len(firsts)
     return pl.pallas_call(
-        functools.partial(last_kernel, sz),
-        out_shape=[jax.ShapeDtypeStruct(p.shape, p.dtype) for p in partial] + [out] * 3 + [
-            jax.ShapeDtypeStruct((1,), jnp.int32)],
-        in_specs=[spec(SMEM)] * (1 + len(notes)) + [spec(VMEM)] * (len(firsts) + len(terms) + 1) + [spec(ANY)] * 2,
-        out_specs=[spec(ANY)] * 2 + [spec(VMEM)] * 3 + [spec(SMEM)],
+        functools.partial(add_kernel, sz),
+        out_shape=[jax.ShapeDtypeStruct(p.shape, p.dtype) for p in partial] + [jax.ShapeDtypeStruct((1,), jnp.int32)],
+        in_specs=[spec(SMEM)] * (1 + len(notes)) + [spec(VMEM)] * (len(firsts) + 1) + [spec(ANY)] * 2,
+        out_specs=[spec(ANY)] * 2 + [spec(SMEM)],
         input_output_aliases={n: 0, n + 1: 1},
         scratch_shapes=[
             pltpu.VMEM((sz.first, sz.tok, BLK), jnp.bfloat16),
@@ -584,8 +572,21 @@
         ],
         compiler_params=pltpu.CompilerParams(vmem_limit_bytes=12 * 1024 * 1024),
         cost_estimate=cost(1_000_000, 3_000_000),
+        name="add",
+    )(plan, *notes, *firsts, strips, *partial)
+
+
+def call_last(sz, plan, terms):
+    out = jax.ShapeDtypeStruct((1, sz.nb, BLK, BLK), jnp.bfloat16)
+    return pl.pallas_call(
+        functools.partial(last_kernel, sz),
+        out_shape=[out] * 3,
+        in_specs=[spec(SMEM)] + [spec(VMEM)] * len(terms),
+        out_specs=[spec(VMEM)] * 3,
+        compiler_params=pltpu.CompilerParams(vmem_limit_bytes=SMALL),
+        cost_estimate=cost(1_000_000, 1_000_000),
         name="last",
-    )(plan, *notes, *firsts, *terms, strips, *partial)
+    )(plan, *terms)
 
 
 def across(pairs):
@@ -605,7 +606,7 @@
     return [side[d] for side in (same, other) for d in sz.order]
 
 
-def reduce_parts(sz, same, far, near, notes, prepare):
+def reduce_parts(sz, same, far, near, notes, prepare, sent):
     ahead, behind, swap = permutations(sz)
     keep = sz.keep
     far = lax.ppermute(far, "fsdp", swap)
@@ -629,7 +630,7 @@
         if s == 1:
             a, b = call_turn([a, b], notes)
         else:
-            a = call_turn([a], [last_b] + (list(prepared[2:]) if s == 2 else []))[0]
+            a = call_turn([a], [last_b] + (list(prepared[2:]) if s == 2 else sent))[0]
         a = term(sz.top - s, a)
         if s + 1 < sz.top:
             b = term(sz.top + 1 + s, call_turn([b], [a])[0])
@@ -659,9 +660,10 @@
         return call_prepare(sz, plan, notes[0], call_turn([firsts[0]], [after])[0])
 
     sent = [exchange(firsts[s], s) for s in range(1, T)]
-    terms, (*partial, strips) = reduce_parts(sz, same, far, near, notes, prepare)
-    *outs, flag = call_last(sz, plan, notes, sent, terms, strips, partial)
-    return tuple(outs), flag
+    terms, (*partial, strips) = reduce_parts(sz, same, far, near, notes, prepare, sent)
+    sent = call_turn(sent, [terms[2], terms[5]])
+    outputs, input_grads, flag = call_add(sz, plan, notes, sent, strips, partial)
+    return (outputs, input_grads, *call_last(sz, plan, terms)), flag
 
 
 def shards(

time: 63 us -> 60.8 us (0.965); the launches traced: 63.6 us -> 60.3 us
  waiting for transfers between devices: 27.1 us -> 22.2 us
  starting transfers between devices: 19.8 us -> 22.2 us
  Pallas kernels: 14.2 us -> 13.4 us
    ppermute x6, waiting for transfers between devices: 3.84 us -> 0.02 us  [reduce_parts(): a, b = (lax.ppermute(a, 'fsdp', ahead), lax.ppermute(b, 'fsdp', behind))]
    ppermute x2, waiting for transfers between devices: 8.05 us -> 5.5 us  [exchange(): return lax.ppermute(array, 'tensor', [(i, (i + s) % T) for i in range(T)])]
    ppermute x2, starting transfers between devices: 0.01 us -> 2.03 us  [exchange(): return lax.ppermute(array, 'tensor', [(i, (i + s) % T) for i in range(T)])]
    pallas_call x1, Pallas kernels: 7.62 us -> 5.61 us  [call_compute(): pl.pallas_call(functools.partial(compute_kernel, sz), out_shape=out_shape...]
    pallas_call x1 -> x2, Pallas kernels: 2.5 us -> 3.87 us  [the longest x1 2.32 us: call_add(): pl.pallas_call(functools.partial(add_kernel, sz), out_shape=[jax.ShapeDty...]
    ppermute x1, waiting for transfers between devices: 0.01 us -> 0.85 us  [reduce_parts(): mine = [here, lax.ppermute(a, 'fsdp', ahead), b]]
    ppermute x6, starting transfers between devices: 7.07 us -> 7.78 us  [reduce_parts(): a, b = (lax.ppermute(a, 'fsdp', ahead), lax.ppermute(b, 'fsdp', behind))]
  transfers between devices with their start and end apart: 32 -> 32, of which waited for: 14 -> 13; matrix products, arithmetic and copies ran while one was open for 2% -> 2% of each run, Pallas kernels for 4% -> 8%
where the time goes in v6:
time: 60.8 us; the launch traced here: 60.3 us
  starting transfers between devices  22.2 us (37%)
  waiting for transfers between devices  22.2 us (37%)
  Pallas kernels  13.4 us (22%)
  between operations  1.42 us (2%)
  local copies, waits for them, and re-layouts  0.8 us (1%)
    ppermute x6, waiting for transfers between devices, gather_chunks(): a, b = (lax.ppermute(a, 'fsdp', ahead), lax.ppermute(b, 'fsdp', behind))  11.9 us
    ppermute x6, starting transfers between devices, reduce_parts(): a, b = (lax.ppermute(a, 'fsdp', ahead), lax.ppermute(b, 'fsdp', behind))  7.78 us
    ppermute x6, starting transfers between devices, gather_chunks(): a, b = (lax.ppermute(a, 'fsdp', ahead), lax.ppermute(b, 'fsdp', behind))  6.51 us
    pallas_call x1, Pallas kernels, call_compute(): pl.pallas_call(functools.partial(compute_kernel, sz), out_shape=out_shape...  5.61 us
    ppermute x2, waiting for transfers between devices, exchange(): return lax.ppermute(array, 'tensor', [(i, (i + s) % T) for i in range(T)])  5.5 us
    pallas_call x1, Pallas kernels, call_prepare(): pl.pallas_call(functools.partial(prepare_kernel, sz), out_shape=[half, ha...  2.54 us
    pallas_call x1, Pallas kernels, call_add(): pl.pallas_call(functools.partial(add_kernel, sz), out_shape=[jax.ShapeDty...  2.32 us
    ppermute x1, waiting for transfers between devices, gather_chunks(): same[sz.top] = lax.ppermute(a, 'fsdp', ahead)  2.11 us
  transfers between devices with their start and end apart: 32, of which 13 were waited for; matrix products, arithmetic and copies ran while one was open for 2% of the time, Pallas kernels for 8%

profile of v6, /device:TPU:0, one launch (start us, length us, event | category | flops | bytes accessed | tf_op | source)
XLA Modules:
  0.0 60.3 jit_solution(12694155068244355089)
XLA Ops:
  0.6 0.5 collective-permute-start.32
  1.2 0.1 collective-permute-start.33
  1.2 0.4 collective-permute-start.34
  1.7 0.8 %concatenate.3 = s32[101]{0:T(128)S(1)} concatenate(s32[32]{0:T(128)} %bitcast.9, s32[32]{0:T(128)} %bitcast.10, s32[32]{0:T(128)} %bitcast.11, s32[3]{0:T(128)} %bitcast.12, s32[1]{0:T(128)} %bitcast.4, s32[1]{0:T(128)} %bitcast.5), dimensions={0} | concatenate | bytes 808 | tf_op jit(solution)/shard_map/concatenate | solution.py:684
  2.4 0.0 collective-permute-done.32.refs_3_
  2.5 0.2 collective-permute-done.33.refs_4_
  2.6 0.2 collective-permute-done.34.refs_5_
  2.8 1.3 %plan.3 = (s32[32,128]{1,0:T(8,128)S(1)}, bf16[7,64,128]{2,1,0:T(8,128)(2,1)S(1)}, s32[1,128]{1,0:T(1,128)S(1)}) custom-call(s32[1,128]{1,0:T(1,128)S(1)} %pad_bitcast_fusion.own, bf16[1,2,128,128]{3,2,1,0:T(8,128)(2,1)} %refs_0_.1, bf16[1,2,128,128]{3,2,1,0:T(8,128)(2,1)} %refs_1_.1, bf16[1,2,128,128]{3,2,1,0:T(8,128)(2,1)} %refs_2_.1, ...), custom_call_target="tpu_custom_call" | custom-call | flops 1000000 | bytes 4000000 | tf_op jit(solution)/shard_map/plan/pallas_call | solution.py:476
  4.1 2.9 %collective-permute-start.36 = (bf16[7,64,128]{2,1,0:T(8,128)(2,1)S(1)}, bf16[7,64,128]{2,1,0:T(8,128)(2,1)S(1)}, u32[]{:S(2)}, u32[]{:S(2)}) collective-permute-start(bf16[7,64,128]{2,1,0:T(8,128)(2,1)S(1)} %get-tuple-element.76.refs_7_), channel_id=1, source_target_pairs={{0,8},{2,6},{8,16},{10,2},{16,24},{18,10},{24,28},{26,18},{28,20},... | collective-permute-start | bytes 344072 | tf_op jit(solution)/shard_map/ppermute | solution.py:601
  7.0 0.0 collective-permute-start.40
  7.1 3.0 %collective-permute-done.36.refs_5_ = bf16[7,64,128]{2,1,0:T(8,128)(2,1)S(1)} collective-permute-done((bf16[7,64,128]{2,1,0:T(8,128)(2,1)S(1)}, bf16[7,64,128]{2,1,0:T(8,128)(2,1)S(1)}, u32[]{:S(2)}, u32[]{:S(2)}) %collective-permute-start.36) | collective-permute-done | bytes 114720 | tf_op jit(solution)/shard_map/ppermute | solution.py:601
  10.1 2.2 %collective-permute-start.37 = (bf16[7,64,128]{2,1,0:T(8,128)(2,1)S(1)}, bf16[7,64,128]{2,1,0:T(8,128)(2,1)S(1)}, u32[]{:S(2)}, u32[]{:S(2)}) collective-permute-start(bf16[7,64,128]{2,1,0:T(8,128)(2,1)S(1)} %collective-permute-done.36.refs_5_), channel_id=1, source_target_pairs={{0,8},{2,6},{8,16},{10,2},{16,24},{18,10},{24,28},{26,18},{28,20},... | collective-permute-start | bytes 344072 | tf_op jit(solution)/shard_map/ppermute | solution.py:601
  12.4 0.4 collective-permute-start.41
  12.7 0.0 collective-permute-start.50
  12.7 0.5 collective-permute-start.48
  13.2 3.0 %collective-permute-done.37.refs_3_ = bf16[7,64,128]{2,1,0:T(8,128)(2,1)S(1)} collective-permute-done((bf16[7,64,128]{2,1,0:T(8,128)(2,1)S(1)}, bf16[7,64,128]{2,1,0:T(8,128)(2,1)S(1)}, u32[]{:S(2)}, u32[]{:S(2)}) %collective-permute-start.37) | collective-permute-done | bytes 114720 | tf_op jit(solution)/shard_map/ppermute | solution.py:601
  16.2 0.9 %collective-permute-start.38 = (bf16[7,64,128]{2,1,0:T(8,128)(2,1)S(1)}, bf16[7,64,128]{2,1,0:T(8,128)(2,1)S(1)}, u32[]{:S(2)}, u32[]{:S(2)}) collective-permute-start(bf16[7,64,128]{2,1,0:T(8,128)(2,1)S(1)} %collective-permute-done.37.refs_3_), channel_id=1, source_target_pairs={{0,8},{2,6},{8,16},{10,2},{16,24},{18,10},{24,28},{26,18},{28,20},... | collective-permute-start | bytes 344072 | tf_op jit(solution)/shard_map/ppermute | solution.py:601
  17.1 0.0 collective-permute-start.49
  17.1 1.1 %collective-permute-done.41.refs_4_ = bf16[7,64,128]{2,1,0:T(8,128)(2,1)S(1)} collective-permute-done((bf16[7,64,128]{2,1,0:T(8,128)(2,1)S(1)}, bf16[7,64,128]{2,1,0:T(8,128)(2,1)S(1)}, u32[]{:S(2)}, u32[]{:S(2)}) %collective-permute-start.41) | collective-permute-done | bytes 114720 | tf_op jit(solution)/shard_map/ppermute | solution.py:601
  18.3 0.0 collective-permute-start.42
  18.3 0.0 collective-permute-done.50.refs_15_
  18.3 0.8 %collective-permute-start.46 = (bf16[7,64,128]{2,1,0:T(8,128)(2,1)S(1)}, bf16[7,64,128]{2,1,0:T(8,128)(2,1)S(1)}, u32[]{:S(2)}, u32[]{:S(2)}) collective-permute-start(bf16[7,64,128]{2,1,0:T(8,128)(2,1)S(1)} %collective-permute-done.37.refs_3_), channel_id=1, source_target_pairs={{0,2},{2,0},{8,10},{10,8},{16,18},{18,16},{24,26},{26,24},{28,30},... | collective-permute-start | bytes 344072 | tf_op jit(solution)/shard_map/ppermute | solution.py:603
  19.1 0.1 collective-permute-start.47
  19.1 2.7 %collective-permute-done.38.refs_1_ = bf16[7,64,128]{2,1,0:T(8,128)(2,1)S(1)} collective-permute-done((bf16[7,64,128]{2,1,0:T(8,128)(2,1)S(1)}, bf16[7,64,128]{2,1,0:T(8,128)(2,1)S(1)}, u32[]{:S(2)}, u32[]{:S(2)}) %collective-permute-start.38) | collective-permute-done | bytes 114720 | tf_op jit(solution)/shard_map/ppermute | solution.py:601
  21.8 0.1 collective-permute-start.39
  21.9 2.0 %collective-permute-done.42.refs_2_ = bf16[7,64,128]{2,1,0:T(8,128)(2,1)S(1)} collective-permute-done((bf16[7,64,128]{2,1,0:T(8,128)(2,1)S(1)}, bf16[7,64,128]{2,1,0:T(8,128)(2,1)S(1)}, u32[]{:S(2)}, u32[]{:S(2)}) %collective-permute-start.42) | collective-permute-done | bytes 114720 | tf_op jit(solution)/shard_map/ppermute | solution.py:601
  24.0 0.5 collective-permute-start.45
  24.5 2.1 %collective-permute-done.39.refs_0_ = bf16[7,64,128]{2,1,0:T(8,128)(2,1)S(1)} collective-permute-done((bf16[7,64,128]{2,1,0:T(8,128)(2,1)S(1)}, bf16[7,64,128]{2,1,0:T(8,128)(2,1)S(1)}, u32[]{:S(2)}, u32[]{:S(2)}) %collective-permute-start.39) | collective-permute-done | bytes 114720 | tf_op jit(solution)/shard_map/ppermute | solution.py:604
  26.6 0.0 collective-permute-done.43.refs_8_
  26.6 0.0 collective-permute-done.44.refs_9_
  26.6 0.0 collective-permute-done.45.refs_10_
  26.6 5.6 %compute.3 = (bf16[56,64,128]{2,1,0:T(8,128)(2,1)S(1)}, bf16[14,64,128]{2,1,0:T(8,128)(2,1)S(1)}, bf16[42,64,128]{2,1,0:T(8,128)(2,1)S(1)}, bf16[18,128,128]{2,1,0:T(8,128)(2,1)S(1)}, bf16[18,128,128]{2,1,0:T(8,128)(2,1)S(1)}) custom-call(s32[32,128]{1,0:T(8,128)S(1)} %get-tuple-element.74.plan, bf16[128,8192]{1,0:T(8,128)(2,1)} %tokens.1, ...), custom_call_target="tpu_custom_call" | custom-call | flops 1000000000 | bytes 20000000 | tf_op jit(solution)/shard_map/compute/pallas_call | solution.py:532
  32.2 1.1 %collective-permute-start.52 = (bf16[14,64,128]{2,1,0:T(8,128)(2,1)S(1)}, bf16[14,64,128]{2,1,0:T(8,128)(2,1)S(1)}, u32[]{:S(2)}, u32[]{:S(2)}) collective-permute-start(bf16[14,64,128]{2,1,0:T(8,128)(2,1)S(1)} %get-tuple-element.80), channel_id=1, source_target_pairs={{0,2},{2,0},{8,10},{10,8},{16,18},{18,16},{24,26},{26,24},{28,30},... | collective-permute-start | bytes 688136 | tf_op jit(solution)/shard_map/ppermute | solution.py:612
  33.3 1.1 %collective-permute-done.52.__1_ = bf16[14,64,128]{2,1,0:T(8,128)(2,1)S(1)} collective-permute-done((bf16[14,64,128]{2,1,0:T(8,128)(2,1)S(1)}, bf16[14,64,128]{2,1,0:T(8,128)(2,1)S(1)}, u32[]{:S(2)}, u32[]{:S(2)}) %collective-permute-start.52) | collective-permute-done | bytes 229408 | tf_op jit(solution)/shard_map/ppermute | solution.py:612
  34.5 0.4 collective-permute-start.53
  34.8 0.1 add_convert_fusion.14
  34.9 0.5 collective-permute-start.54
  35.4 1.6 %collective-permute-start.55 = (bf16[7,64,128]{2,1,0:T(8,128)(2,1)S(1)}, bf16[7,64,128]{2,1,0:T(8,128)(2,1)S(1)}, u32[]{:S(2)}, u32[]{:S(2)}) collective-permute-start(bf16[7,64,128]{2,1,0:T(8,128)(2,1)S(1)} %get-tuple-element.82), channel_id=1, source_target_pairs={{0,4},{2,10},{8,0},{10,18},{16,8},{18,26},{24,16},{26,30},{28,24},... | collective-permute-start | bytes 344072 | tf_op jit(solution)/shard_map/ppermute | solution.py:629
  37.0 1.9 %collective-permute-start.35 = (s32[1,128]{1,0:T(1,128)S(1)}, s32[1,128]{1,0:T(1,128)S(1)}, u32[]{:S(2)}, u32[]{:S(2)}) collective-permute-start(s32[1,128]{1,0:T(1,128)S(1)} %get-tuple-element.75), channel_id=1, source_target_pairs={{0,1},{1,0},{2,3},{3,2},{4,5},{5,4},{6,7},{7,6},{8,9},{9,8},{10,11... | collective-permute-start | bytes 1544 | tf_op jit(solution)/shard_map/ppermute | solution.py:653
  38.9 0.1 collective-permute-start.51
  39.0 1.5 %collective-permute-done.35.__2_.note.refs_0_ = s32[1,128]{1,0:T(1,128)S(1)} collective-permute-done((s32[1,128]{1,0:T(1,128)S(1)}, s32[1,128]{1,0:T(1,128)S(1)}, u32[]{:S(2)}, u32[]{:S(2)}) %collective-permute-start.35) | collective-permute-done | bytes 544 | tf_op jit(solution)/shard_map/ppermute | solution.py:653
  40.6 0.0 collective-permute-done.55.__1_
  40.6 0.0 collective-permute-done.53
  40.6 0.1 add_convert_fusion.11
  40.7 1.7 %collective-permute-start.57 = (bf16[7,64,128]{2,1,0:T(8,128)(2,1)S(1)}, bf16[7,64,128]{2,1,0:T(8,128)(2,1)S(1)}, u32[]{:S(2)}, u32[]{:S(2)}) collective-permute-start(bf16[7,64,128]{2,1,0:T(8,128)(2,1)S(1)} %get-tuple-element.110.__1_), channel_id=1, source_target_pairs={{0,8},{2,6},{8,16},{10,2},{16,24},{18,10},{24,28},{26,18},{28,20},... | collective-permute-start | bytes 344072 | tf_op jit(solution)/shard_map/ppermute | solution.py:629
  42.4 0.3 collective-permute-start.58
  42.6 0.1 add_convert_fusion.12.__1_
  42.7 1.7 %collective-permute-start.56 = (bf16[7,64,128]{2,1,0:T(8,128)(2,1)S(1)}, bf16[7,64,128]{2,1,0:T(8,128)(2,1)S(1)}, u32[]{:S(2)}, u32[]{:S(2)}) collective-permute-start(bf16[7,64,128]{2,1,0:T(8,128)(2,1)S(1)} %add_convert_fusion.12.__1_), channel_id=1, source_target_pairs={{0,4},{2,10},{8,0},{10,18},{16,8},{18,26},{24,16},{26,30},{28,24},... | collective-permute-start | bytes 344072 | tf_op jit(solution)/shard_map/ppermute | solution.py:629
  44.4 2.5 %prepare.3 = (bf16[128,4096]{1,0:T(8,128)(2,1)}, bf16[128,4096]{1,0:T(8,128)(2,1)}, bf16[18,128,128]{2,1,0:T(8,128)(2,1)S(1)}) custom-call(s32[32,128]{1,0:T(8,128)S(1)} %get-tuple-element.74.plan, s32[1,128]{1,0:T(1,128)S(1)} %collective-permute-done.35.__2_.note.refs_0_, bf16[18,128,128]{2,1,0:T(8,128)(2,1)S(1)} %turn.27.first), custom_call_target="tpu_custom_call" | custom-call | flops 1000000 | bytes 6000000 | tf_op jit(solution)/shard_map/prepare/pallas_call | solution.py:549
  47.0 0.1 add_convert_fusion.10.__1_
  47.0 1.3 %collective-permute-start.61 = (bf16[7,64,128]{2,1,0:T(8,128)(2,1)S(1)}, bf16[7,64,128]{2,1,0:T(8,128)(2,1)S(1)}, u32[]{:S(2)}, u32[]{:S(2)}) collective-permute-start(bf16[7,64,128]{2,1,0:T(8,128)(2,1)S(1)} %add_convert_fusion.10.__1_), channel_id=1, source_target_pairs={{0,8},{2,6},{8,16},{10,2},{16,24},{18,10},{24,28},{26,18},{28,20},... | collective-permute-start | bytes 344072 | tf_op jit(solution)/shard_map/ppermute | solution.py:629
  48.4 0.1 add_convert_fusion.9.__1_
  48.4 0.9 %collective-permute-start.59 = (bf16[7,64,128]{2,1,0:T(8,128)(2,1)S(1)}, bf16[7,64,128]{2,1,0:T(8,128)(2,1)S(1)}, u32[]{:S(2)}, u32[]{:S(2)}) collective-permute-start(bf16[7,64,128]{2,1,0:T(8,128)(2,1)S(1)} %add_convert_fusion.9.__1_), channel_id=1, source_target_pairs={{0,4},{2,10},{8,0},{10,18},{16,8},{18,26},{24,16},{26,30},{28,24},... | collective-permute-start | bytes 344072 | tf_op jit(solution)/shard_map/ppermute | solution.py:629
  49.3 0.2 collective-permute-start.60
  49.5 4.0 %collective-permute-done.51.__0_.__2_ = bf16[18,128,128]{2,1,0:T(8,128)(2,1)S(1)} collective-permute-done((bf16[18,128,128]{2,1,0:T(8,128)(2,1)S(1)}, bf16[18,128,128]{2,1,0:T(8,128)(2,1)S(1)}, u32[]{:S(2)}, u32[]{:S(2)}) %collective-permute-start.51) | collective-permute-done | bytes 589856 | tf_op jit(solution)/shard_map/ppermute | solution.py:653
  53.5 0.1 add_convert_fusion.8
  53.5 1.0 %collective-permute-start.62 = (bf16[7,64,128]{2,1,0:T(8,128)(2,1)S(1)}, bf16[7,64,128]{2,1,0:T(8,128)(2,1)S(1)}, u32[]{:S(2)}, u32[]{:S(2)}) collective-permute-start(bf16[7,64,128]{2,1,0:T(8,128)(2,1)S(1)} %add_convert_fusion.8), channel_id=1, source_target_pairs={{0,8},{2,6},{8,16},{10,2},{16,24},{18,10},{24,28},{26,18},{28,20},... | collective-permute-start | bytes 344072 | tf_op jit(solution)/shard_map/ppermute | solution.py:637
  54.5 0.0 copy-start
  54.5 0.0 copy-start.1
  54.5 0.0 copy-start.2
  54.6 2.3 %add.122 = (bf16[128,4096]{1,0:T(8,128)(2,1)}, bf16[128,4096]{1,0:T(8,128)(2,1)}, s32[1]{0:T(128)}) custom-call(s32[32,128]{1,0:T(8,128)S(1)} %get-tuple-element.74.plan, s32[1,128]{1,0:T(1,128)S(1)} %collective-permute-done.35.__2_.note.refs_0_, bf16[18,128,128]{2,1,0:T(8,128)(2,1)S(1)} %turn.30.refs_1_, ...), custom_call_target="tpu_custom_call", output_to_operand_aliasing={{0}: (4, {}), {1}: (5, {})} | custom-call | flops 1000000 | bytes 3000000 | tf_op jit(solution)/shard_map/add/pallas_call | solution.py:562
  57.5 0.8 %collective-permute-done.62.refs_1_ = bf16[7,64,128]{2,1,0:T(8,128)(2,1)S(1)} collective-permute-done((bf16[7,64,128]{2,1,0:T(8,128)(2,1)S(1)}, bf16[7,64,128]{2,1,0:T(8,128)(2,1)S(1)}, u32[]{:S(2)}, u32[]{:S(2)}) %collective-permute-start.62) | collective-permute-done | bytes 114720 | tf_op jit(solution)/shard_map/ppermute | solution.py:637
  58.4 0.3 collective-permute-done.63.refs_4_
  58.7 1.6 %last.3 = (bf16[1,2,128,128]{3,2,1,0:T(8,128)(2,1)}, bf16[1,2,128,128]{3,2,1,0:T(8,128)(2,1)}, bf16[1,2,128,128]{3,2,1,0:T(8,128)(2,1)}) custom-call(s32[32,128]{1,0:T(8,128)S(1)} %get-tuple-element.74.plan, bf16[7,64,128]{2,1,0:T(8,128)(2,1)S(1)} %get-tuple-element.109.refs_0_, bf16[7,64,128]{2,1,0:T(8,128)(2,1)S(1)} %collective-permute-done.62.refs_1_, ...), custom_call_target="tpu_custom_call" | custom-call | flops 1000000 | bytes 1000000 | tf_op jit(solution)/shard_map/last/pallas_call | solution.py:581
  (28 shorter events, 0.1 us)
Async XLA Ops:
  0.6 1.8 %collective-permute-start.32 = (bf16[1,2,128,128]{3,2,1,0:T(8,128)(2,1)}, bf16[1,2,128,128]{3,2,1,0:T(8,128)(2,1)S(1)}, u32[]{:S(2)}, u32[]{:S(2)}) collective-permute-start(bf16[1,2,128,128]{3,2,1,0:T(8,128)(2,1)} %refs_0_.1), channel_id=1, source_target_pairs={{0,2},{2,0},{8,10},{10,8},{16,18},{18,16},{24,26},{26,24},{28,30},... | collective-permute-start | bytes 196616 | tf_op jit(solution)/shard_map/ppermute | solution.py:649
  1.2 1.5 %collective-permute-start.33 = (bf16[1,2,128,128]{3,2,1,0:T(8,128)(2,1)}, bf16[1,2,128,128]{3,2,1,0:T(8,128)(2,1)S(1)}, u32[]{:S(2)}, u32[]{:S(2)}) collective-permute-start(bf16[1,2,128,128]{3,2,1,0:T(8,128)(2,1)} %refs_1_.1), channel_id=1, source_target_pairs={{0,2},{2,0},{8,10},{10,8},{16,18},{18,16},{24,26},{26,24},{28,30},... | collective-permute-start | bytes 196616 | tf_op jit(solution)/shard_map/ppermute | solution.py:649
  1.2 1.5 %collective-permute-start.34 = (bf16[1,2,128,128]{3,2,1,0:T(8,128)(2,1)}, bf16[1,2,128,128]{3,2,1,0:T(8,128)(2,1)S(1)}, u32[]{:S(2)}, u32[]{:S(2)}) collective-permute-start(bf16[1,2,128,128]{3,2,1,0:T(8,128)(2,1)} %refs_2_.1), channel_id=1, source_target_pairs={{0,2},{2,0},{8,10},{10,8},{16,18},{18,16},{24,26},{26,24},{28,30},... | collective-permute-start | bytes 196616 | tf_op jit(solution)/shard_map/ppermute | solution.py:649
  4.1 6.0 %collective-permute-start.36 = (bf16[7,64,128]{2,1,0:T(8,128)(2,1)S(1)}, bf16[7,64,128]{2,1,0:T(8,128)(2,1)S(1)}, u32[]{:S(2)}, u32[]{:S(2)}) collective-permute-start(bf16[7,64,128]{2,1,0:T(8,128)(2,1)S(1)} %get-tuple-element.76.refs_7_), channel_id=1, source_target_pairs={{0,8},{2,6},{8,16},{10,2},{16,24},{18,10},{24,28},{26,18},{28,20},... | collective-permute-start | bytes 344072 | tf_op jit(solution)/shard_map/ppermute | solution.py:601
  7.0 5.3 %collective-permute-start.40 = (bf16[7,64,128]{2,1,0:T(8,128)(2,1)S(1)}, bf16[7,64,128]{2,1,0:T(8,128)(2,1)S(1)}, u32[]{:S(2)}, u32[]{:S(2)}) collective-permute-start(bf16[7,64,128]{2,1,0:T(8,128)(2,1)S(1)} %get-tuple-element.76.refs_7_), channel_id=1, source_target_pairs={{0,4},{2,10},{8,0},{10,18},{16,8},{18,26},{24,16},{26,30},{28,24},... | collective-permute-start | bytes 344072 | tf_op jit(solution)/shard_map/ppermute | solution.py:601
  10.1 6.1 %collective-permute-start.37 = (bf16[7,64,128]{2,1,0:T(8,128)(2,1)S(1)}, bf16[7,64,128]{2,1,0:T(8,128)(2,1)S(1)}, u32[]{:S(2)}, u32[]{:S(2)}) collective-permute-start(bf16[7,64,128]{2,1,0:T(8,128)(2,1)S(1)} %collective-permute-done.36.refs_5_), channel_id=1, source_target_pairs={{0,8},{2,6},{8,16},{10,2},{16,24},{18,10},{24,28},{26,18},{28,20},... | collective-permute-start | bytes 344072 | tf_op jit(solution)/shard_map/ppermute | solution.py:601
  12.4 5.9 %collective-permute-start.41 = (bf16[7,64,128]{2,1,0:T(8,128)(2,1)S(1)}, bf16[7,64,128]{2,1,0:T(8,128)(2,1)S(1)}, u32[]{:S(2)}, u32[]{:S(2)}) collective-permute-start(bf16[7,64,128]{2,1,0:T(8,128)(2,1)S(1)} %collective-permute-done.40.refs_6_), channel_id=1, source_target_pairs={{0,4},{2,10},{8,0},{10,18},{16,8},{18,26},{24,16},{26,30},{28,24},... | collective-permute-start | bytes 344072 | tf_op jit(solution)/shard_map/ppermute | solution.py:601
  12.7 5.6 %collective-permute-start.50 = (bf16[7,64,128]{2,1,0:T(8,128)(2,1)S(1)}, bf16[7,64,128]{2,1,0:T(8,128)(2,1)S(1)}, u32[]{:S(2)}, u32[]{:S(2)}) collective-permute-start(bf16[7,64,128]{2,1,0:T(8,128)(2,1)S(1)} %get-tuple-element.76.refs_7_), channel_id=1, source_target_pairs={{0,2},{2,0},{8,10},{10,8},{16,18},{18,16},{24,26},{26,24},{28,30},... | collective-permute-start | bytes 344072 | tf_op jit(solution)/shard_map/ppermute | solution.py:603
  12.7 6.3 %collective-permute-start.48 = (bf16[7,64,128]{2,1,0:T(8,128)(2,1)S(1)}, bf16[7,64,128]{2,1,0:T(8,128)(2,1)S(1)}, u32[]{:S(2)}, u32[]{:S(2)}) collective-permute-start(bf16[7,64,128]{2,1,0:T(8,128)(2,1)S(1)} %collective-permute-done.36.refs_5_), channel_id=1, source_target_pairs={{0,2},{2,0},{8,10},{10,8},{16,18},{18,16},{24,26},{26,24},{28,30},... | collective-permute-start | bytes 344072 | tf_op jit(solution)/shard_map/ppermute | solution.py:603
  16.2 5.6 %collective-permute-start.38 = (bf16[7,64,128]{2,1,0:T(8,128)(2,1)S(1)}, bf16[7,64,128]{2,1,0:T(8,128)(2,1)S(1)}, u32[]{:S(2)}, u32[]{:S(2)}) collective-permute-start(bf16[7,64,128]{2,1,0:T(8,128)(2,1)S(1)} %collective-permute-done.37.refs_3_), channel_id=1, source_target_pairs={{0,8},{2,6},{8,16},{10,2},{16,24},{18,10},{24,28},{26,18},{28,20},... | collective-permute-start | bytes 344072 | tf_op jit(solution)/shard_map/ppermute | solution.py:601
  17.1 4.8 %collective-permute-start.49 = (bf16[7,64,128]{2,1,0:T(8,128)(2,1)S(1)}, bf16[7,64,128]{2,1,0:T(8,128)(2,1)S(1)}, u32[]{:S(2)}, u32[]{:S(2)}) collective-permute-start(bf16[7,64,128]{2,1,0:T(8,128)(2,1)S(1)} %collective-permute-done.40.refs_6_), channel_id=1, source_target_pairs={{0,2},{2,0},{8,10},{10,8},{16,18},{18,16},{24,26},{26,24},{28,30},... | collective-permute-start | bytes 344072 | tf_op jit(solution)/shard_map/ppermute | solution.py:603
  18.3 5.7 %collective-permute-start.42 = (bf16[7,64,128]{2,1,0:T(8,128)(2,1)S(1)}, bf16[7,64,128]{2,1,0:T(8,128)(2,1)S(1)}, u32[]{:S(2)}, u32[]{:S(2)}) collective-permute-start(bf16[7,64,128]{2,1,0:T(8,128)(2,1)S(1)} %collective-permute-done.41.refs_4_), channel_id=1, source_target_pairs={{0,4},{2,10},{8,0},{10,18},{16,8},{18,26},{24,16},{26,30},{28,24},... | collective-permute-start | bytes 344072 | tf_op jit(solution)/shard_map/ppermute | solution.py:601
  18.3 5.7 %collective-permute-start.46 = (bf16[7,64,128]{2,1,0:T(8,128)(2,1)S(1)}, bf16[7,64,128]{2,1,0:T(8,128)(2,1)S(1)}, u32[]{:S(2)}, u32[]{:S(2)}) collective-permute-start(bf16[7,64,128]{2,1,0:T(8,128)(2,1)S(1)} %collective-permute-done.37.refs_3_), channel_id=1, source_target_pairs={{0,2},{2,0},{8,10},{10,8},{16,18},{18,16},{24,26},{26,24},{28,30},... | collective-permute-start | bytes 344072 | tf_op jit(solution)/shard_map/ppermute | solution.py:603
  19.1 5.4 %collective-permute-start.47 = (bf16[7,64,128]{2,1,0:T(8,128)(2,1)S(1)}, bf16[7,64,128]{2,1,0:T(8,128)(2,1)S(1)}, u32[]{:S(2)}, u32[]{:S(2)}) collective-permute-start(bf16[7,64,128]{2,1,0:T(8,128)(2,1)S(1)} %collective-permute-done.41.refs_4_), channel_id=1, source_target_pairs={{0,2},{2,0},{8,10},{10,8},{16,18},{18,16},{24,26},{26,24},{28,30},... | collective-permute-start | bytes 344072 | tf_op jit(solution)/shard_map/ppermute | solution.py:603
  21.8 4.8 %collective-permute-start.39 = (bf16[7,64,128]{2,1,0:T(8,128)(2,1)S(1)}, bf16[7,64,128]{2,1,0:T(8,128)(2,1)S(1)}, u32[]{:S(2)}, u32[]{:S(2)}) collective-permute-start(bf16[7,64,128]{2,1,0:T(8,128)(2,1)S(1)} %collective-permute-done.38.refs_1_), channel_id=1, source_target_pairs={{0,8},{2,6},{8,16},{10,2},{16,24},{18,10},{24,28},{26,18},{28,20},... | collective-permute-start | bytes 344072 | tf_op jit(solution)/shard_map/ppermute | solution.py:604
  21.9 4.7 %collective-permute-start.43 = (bf16[7,64,128]{2,1,0:T(8,128)(2,1)S(1)}, bf16[7,64,128]{2,1,0:T(8,128)(2,1)S(1)}, u32[]{:S(2)}, u32[]{:S(2)}) collective-permute-start(bf16[7,64,128]{2,1,0:T(8,128)(2,1)S(1)} %collective-permute-done.38.refs_1_), channel_id=1, source_target_pairs={{0,10},{2,4},{8,18},{10,0},{16,26},{18,8},{24,30},{26,16},{28,22},... | collective-permute-start | bytes 344072 | tf_op jit(solution)/shard_map/ppermute | solution.py:605
  24.0 2.6 %collective-permute-start.44 = (bf16[7,64,128]{2,1,0:T(8,128)(2,1)S(1)}, bf16[7,64,128]{2,1,0:T(8,128)(2,1)S(1)}, u32[]{:S(2)}, u32[]{:S(2)}) collective-permute-start(bf16[7,64,128]{2,1,0:T(8,128)(2,1)S(1)} %collective-permute-done.38.refs_1_), channel_id=1, source_target_pairs={{0,2},{2,0},{8,10},{10,8},{16,18},{18,16},{24,26},{26,24},{28,30},... | collective-permute-start | bytes 344072 | tf_op jit(solution)/shard_map/ppermute | solution.py:603
  24.0 2.6 %collective-permute-start.45 = (bf16[7,64,128]{2,1,0:T(8,128)(2,1)S(1)}, bf16[7,64,128]{2,1,0:T(8,128)(2,1)S(1)}, u32[]{:S(2)}, u32[]{:S(2)}) collective-permute-start(bf16[7,64,128]{2,1,0:T(8,128)(2,1)S(1)} %collective-permute-done.42.refs_2_), channel_id=1, source_target_pairs={{0,2},{2,0},{8,10},{10,8},{16,18},{18,16},{24,26},{26,24},{28,30},... | collective-permute-start | bytes 344072 | tf_op jit(solution)/shard_map/ppermute | solution.py:603
  32.2 2.2 %collective-permute-start.52 = (bf16[14,64,128]{2,1,0:T(8,128)(2,1)S(1)}, bf16[14,64,128]{2,1,0:T(8,128)(2,1)S(1)}, u32[]{:S(2)}, u32[]{:S(2)}) collective-permute-start(bf16[14,64,128]{2,1,0:T(8,128)(2,1)S(1)} %get-tuple-element.80), channel_id=1, source_target_pairs={{0,2},{2,0},{8,10},{10,8},{16,18},{18,16},{24,26},{26,24},{28,30},... | collective-permute-start | bytes 688136 | tf_op jit(solution)/shard_map/ppermute | solution.py:612
  34.5 6.1 %collective-permute-start.53 = (bf16[42,64,128]{2,1,0:T(8,128)(2,1)S(1)}, bf16[42,64,128]{2,1,0:T(8,128)(2,1)S(1)}, u32[]{:S(2)}, u32[]{:S(2)}) collective-permute-start(bf16[42,64,128]{2,1,0:T(8,128)(2,1)S(1)} %turn.24), channel_id=1, source_target_pairs={{0,2},{2,0},{8,10},{10,8},{16,18},{18,16},{24,26},{26,24},{28,30},... | collective-permute-start | bytes 2064392 | tf_op jit(solution)/shard_map/ppermute | solution.py:613
  34.9 5.7 %collective-permute-start.54 = (bf16[7,64,128]{2,1,0:T(8,128)(2,1)S(1)}, bf16[7,64,128]{2,1,0:T(8,128)(2,1)S(1)}, u32[]{:S(2)}, u32[]{:S(2)}) collective-permute-start(bf16[7,64,128]{2,1,0:T(8,128)(2,1)S(1)} %get-tuple-element.81), channel_id=1, source_target_pairs={{0,8},{2,6},{8,16},{10,2},{16,24},{18,10},{24,28},{26,18},{28,20},... | collective-permute-start | bytes 344072 | tf_op jit(solution)/shard_map/ppermute | solution.py:629
  35.4 5.1 %collective-permute-start.55 = (bf16[7,64,128]{2,1,0:T(8,128)(2,1)S(1)}, bf16[7,64,128]{2,1,0:T(8,128)(2,1)S(1)}, u32[]{:S(2)}, u32[]{:S(2)}) collective-permute-start(bf16[7,64,128]{2,1,0:T(8,128)(2,1)S(1)} %get-tuple-element.82), channel_id=1, source_target_pairs={{0,4},{2,10},{8,0},{10,18},{16,8},{18,26},{24,16},{26,30},{28,24},... | collective-permute-start | bytes 344072 | tf_op jit(solution)/shard_map/ppermute | solution.py:629
  37.0 3.5 %collective-permute-start.35 = (s32[1,128]{1,0:T(1,128)S(1)}, s32[1,128]{1,0:T(1,128)S(1)}, u32[]{:S(2)}, u32[]{:S(2)}) collective-permute-start(s32[1,128]{1,0:T(1,128)S(1)} %get-tuple-element.75), channel_id=1, source_target_pairs={{0,1},{1,0},{2,3},{3,2},{4,5},{5,4},{6,7},{7,6},{8,9},{9,8},{10,11... | collective-permute-start | bytes 1544 | tf_op jit(solution)/shard_map/ppermute | solution.py:653
  38.9 14.5 %collective-permute-start.51 = (bf16[18,128,128]{2,1,0:T(8,128)(2,1)S(1)}, bf16[18,128,128]{2,1,0:T(8,128)(2,1)S(1)}, u32[]{:S(2)}, u32[]{:S(2)}) collective-permute-start(bf16[18,128,128]{2,1,0:T(8,128)(2,1)S(1)} %get-tuple-element.77), channel_id=1, source_target_pairs={{0,1},{1,0},{2,3},{3,2},{4,5},{5,4},{6,7},{7,6},{8,9},{9,8},{10,11... | collective-permute-start | bytes 1769480 | tf_op jit(solution)/shard_map/ppermute | solution.py:653
  40.7 6.3 %collective-permute-start.57 = (bf16[7,64,128]{2,1,0:T(8,128)(2,1)S(1)}, bf16[7,64,128]{2,1,0:T(8,128)(2,1)S(1)}, u32[]{:S(2)}, u32[]{:S(2)}) collective-permute-start(bf16[7,64,128]{2,1,0:T(8,128)(2,1)S(1)} %get-tuple-element.110.__1_), channel_id=1, source_target_pairs={{0,8},{2,6},{8,16},{10,2},{16,24},{18,10},{24,28},{26,18},{28,20},... | collective-permute-start | bytes 344072 | tf_op jit(solution)/shard_map/ppermute | solution.py:629
  42.4 2.1 %collective-permute-start.58 = (bf16[7,64,128]{2,1,0:T(8,128)(2,1)S(1)}, bf16[7,64,128]{2,1,0:T(8,128)(2,1)S(1)}, u32[]{:S(2)}, u32[]{:S(2)}) collective-permute-start(bf16[7,64,128]{2,1,0:T(8,128)(2,1)S(1)} %get-tuple-element.109.refs_0_), channel_id=1, source_target_pairs={{0,2},{2,0},{8,10},{10,8},{16,18},{18,16},{24,26},{26,24},{28,30},... | collective-permute-start | bytes 344072 | tf_op jit(solution)/shard_map/ppermute | solution.py:625
  42.7 5.7 %collective-permute-start.56 = (bf16[7,64,128]{2,1,0:T(8,128)(2,1)S(1)}, bf16[7,64,128]{2,1,0:T(8,128)(2,1)S(1)}, u32[]{:S(2)}, u32[]{:S(2)}) collective-permute-start(bf16[7,64,128]{2,1,0:T(8,128)(2,1)S(1)} %add_convert_fusion.12.__1_), channel_id=1, source_target_pairs={{0,4},{2,10},{8,0},{10,18},{16,8},{18,26},{24,16},{26,30},{28,24},... | collective-permute-start | bytes 344072 | tf_op jit(solution)/shard_map/ppermute | solution.py:629
  47.0 6.4 %collective-permute-start.61 = (bf16[7,64,128]{2,1,0:T(8,128)(2,1)S(1)}, bf16[7,64,128]{2,1,0:T(8,128)(2,1)S(1)}, u32[]{:S(2)}, u32[]{:S(2)}) collective-permute-start(bf16[7,64,128]{2,1,0:T(8,128)(2,1)S(1)} %add_convert_fusion.10.__1_), channel_id=1, source_target_pairs={{0,8},{2,6},{8,16},{10,2},{16,24},{18,10},{24,28},{26,18},{28,20},... | collective-permute-start | bytes 344072 | tf_op jit(solution)/shard_map/ppermute | solution.py:629
  48.4 6.1 %collective-permute-start.59 = (bf16[7,64,128]{2,1,0:T(8,128)(2,1)S(1)}, bf16[7,64,128]{2,1,0:T(8,128)(2,1)S(1)}, u32[]{:S(2)}, u32[]{:S(2)}) collective-permute-start(bf16[7,64,128]{2,1,0:T(8,128)(2,1)S(1)} %add_convert_fusion.9.__1_), channel_id=1, source_target_pairs={{0,4},{2,10},{8,0},{10,18},{16,8},{18,26},{24,16},{26,30},{28,24},... | collective-permute-start | bytes 344072 | tf_op jit(solution)/shard_map/ppermute | solution.py:629
  49.3 5.2 %collective-permute-start.60 = (bf16[7,64,128]{2,1,0:T(8,128)(2,1)S(1)}, bf16[7,64,128]{2,1,0:T(8,128)(2,1)S(1)}, u32[]{:S(2)}, u32[]{:S(2)}) collective-permute-start(bf16[7,64,128]{2,1,0:T(8,128)(2,1)S(1)} %add_convert_fusion.9.__1_), channel_id=1, source_target_pairs={{0,6},{2,8},{8,2},{10,16},{16,10},{18,24},{24,18},{26,28},{28,26},... | collective-permute-start | bytes 344072 | tf_op jit(solution)/shard_map/ppermute | solution.py:641
  53.5 4.8 %collective-permute-start.62 = (bf16[7,64,128]{2,1,0:T(8,128)(2,1)S(1)}, bf16[7,64,128]{2,1,0:T(8,128)(2,1)S(1)}, u32[]{:S(2)}, u32[]{:S(2)}) collective-permute-start(bf16[7,64,128]{2,1,0:T(8,128)(2,1)S(1)} %add_convert_fusion.8), channel_id=1, source_target_pairs={{0,8},{2,6},{8,16},{10,2},{16,24},{18,10},{24,28},{26,18},{28,20},... | collective-permute-start | bytes 344072 | tf_op jit(solution)/shard_map/ppermute | solution.py:637
  54.5 4.2 %collective-permute-start.63 = (bf16[7,64,128]{2,1,0:T(8,128)(2,1)S(1)}, bf16[7,64,128]{2,1,0:T(8,128)(2,1)S(1)}, u32[]{:S(2)}, u32[]{:S(2)}) collective-permute-start(bf16[7,64,128]{2,1,0:T(8,128)(2,1)S(1)} %add_convert_fusion.8), channel_id=1, source_target_pairs={{0,10},{2,4},{8,18},{10,0},{16,26},{18,8},{24,30},{26,16},{28,22},... | collective-permute-start | bytes 344072 | tf_op jit(solution)/shard_map/ppermute | solution.py:640
  54.5 5.8 %copy-start = (bf16[1,2,128,128]{3,2,1,0:T(8,128)(2,1)S(1)}, bf16[1,2,128,128]{3,2,1,0:T(8,128)(2,1)}, u32[]{:S(2)}) copy-start(bf16[1,2,128,128]{3,2,1,0:T(8,128)(2,1)} %refs_0_.1) | copy-start | bytes 196612
  54.5 5.7 %copy-start.1 = (bf16[1,2,128,128]{3,2,1,0:T(8,128)(2,1)S(1)}, bf16[1,2,128,128]{3,2,1,0:T(8,128)(2,1)}, u32[]{:S(2)}) copy-start(bf16[1,2,128,128]{3,2,1,0:T(8,128)(2,1)} %refs_1_.1) | copy-start | bytes 196612
  54.5 5.7 %copy-start.2 = (bf16[1,2,128,128]{3,2,1,0:T(8,128)(2,1)S(1)}, bf16[1,2,128,128]{3,2,1,0:T(8,128)(2,1)}, u32[]{:S(2)}) copy-start(bf16[1,2,128,128]{3,2,1,0:T(8,128)(2,1)} %refs_2_.1) | copy-start | bytes 196612

commit v7 on v6

--- a/solution.py
+++ b/solution.py
@@ -606,7 +606,7 @@
     return [side[d] for side in (same, other) for d in sz.order]
 
 
-def reduce_parts(sz, same, far, near, notes, prepare, sent):
+def reduce_parts(sz, same, far, near, exchange_notes, prepare, sent):
     ahead, behind, swap = permutations(sz)
     keep = sz.keep
     far = lax.ppermute(far, "fsdp", swap)
@@ -623,24 +623,26 @@
     a, b = lax.optimization_barrier((term(sz.top), term(sz.top + 1)))
     here = term(0)
     here_across = lax.ppermute(here, "fsdp", swap)
-    prepared = prepare(here_across)
     for s in range(1, sz.top):
         last_b = b
         a, b = lax.ppermute(a, "fsdp", ahead), lax.ppermute(b, "fsdp", behind)
         if s == 1:
-            a, b = call_turn([a, b], notes)
+            a, b = call_turn([a, b], [])
         else:
-            a = call_turn([a], [last_b] + (list(prepared[2:]) if s == 2 else sent))[0]
+            a = call_turn([a], [last_b] + (notes if s == 2 else sent + list(prepared[2:])))[0]
         a = term(sz.top - s, a)
         if s + 1 < sz.top:
             b = term(sz.top + 1 + s, call_turn([b], [a])[0])
+        if s == 1:
+            notes = exchange_notes(b)
+            prepared = prepare(here_across, notes)
     mine = [here, lax.ppermute(a, "fsdp", ahead), b]
     theirs = [
         here_across,
         lax.ppermute(a, "fsdp", across(ahead)),
         lax.ppermute(last_b, "fsdp", across(behind)),
     ]
-    return mine + theirs, prepared
+    return mine + theirs, notes, prepared
 
 
 def program(sz, own, tokens, cotangent, mine):
@@ -652,15 +654,17 @@
     def exchange(array, s):
         return lax.ppermute(array, "tensor", [(i, (i + s) % T) for i in range(T)])
 
-    notes = [exchange(note, s) for s, note in enumerate(notes, 1)]
     chunks = gather_chunks(sz, chunk)
     same, far, near, *firsts = call_compute(sz, plan, tokens, cotangent, chunks)
 
-    def prepare(after):
+    def exchange_notes(after):
+        return [exchange(note, s) for s, note in enumerate(call_turn(notes, [after]), 1)]
+
+    def prepare(after, notes):
         return call_prepare(sz, plan, notes[0], call_turn([firsts[0]], [after])[0])
 
     sent = [exchange(firsts[s], s) for s in range(1, T)]
-    terms, (*partial, strips) = reduce_parts(sz, same, far, near, notes, prepare, sent)
+    terms, notes, (*partial, strips) = reduce_parts(sz, same, far, near, exchange_notes, prepare, sent)
     sent = call_turn(sent, [terms[2], terms[5]])
     outputs, input_grads, flag = call_add(sz, plan, notes, sent, strips, partial)
     return (outputs, input_grads, *call_last(sz, plan, terms)), flag

time: 60.8 us -> 65.7 us (1.081)
  waiting for transfers between devices: 22.2 us -> 26.4 us
  starting transfers between devices: 22.2 us -> 23.1 us
    ppermute x6, waiting for transfers between devices: 0.02 us -> 2.58 us  [reduce_parts(): a, b = (lax.ppermute(a, 'fsdp', ahead), lax.ppermute(b, 'fsdp', behind))]
    ppermute x2, waiting for transfers between devices: 5.5 us -> 7.05 us  [exchange(): return lax.ppermute(array, 'tensor', [(i, (i + s) % T) for i in range(T)])]
    ppermute x2, starting transfers between devices: 2.03 us -> 2.78 us  [exchange(): return lax.ppermute(array, 'tensor', [(i, (i + s) % T) for i in range(T)])]
  transfers between devices with their start and end apart: 32 -> 32, of which waited for: 13 -> 14; matrix products, arithmetic and copies ran while one was open for 2% -> 2% of each run, Pallas kernels for 8% -> 7%
where the time goes in v7:
time: 65.7 us; the launch traced here: 65.6 us
  waiting for transfers between devices  26.4 us (40%)
  starting transfers between devices  23.1 us (35%)
  Pallas kernels  13.5 us (21%)
  between operations  1.42 us (2%)
  local copies, waits for them, and re-layouts  0.8 us (1%)
    ppermute x6, waiting for transfers between devices, gather_chunks(): a, b = (lax.ppermute(a, 'fsdp', ahead), lax.ppermute(b, 'fsdp', behind))  11.9 us
    ppermute x6, starting transfers between devices, reduce_parts(): a, b = (lax.ppermute(a, 'fsdp', ahead), lax.ppermute(b, 'fsdp', behind))  7.93 us
    ppermute x2, waiting for transfers between devices, exchange(): return lax.ppermute(array, 'tensor', [(i, (i + s) % T) for i in range(T)])  7.05 us
    ppermute x6, starting transfers between devices, gather_chunks(): a, b = (lax.ppermute(a, 'fsdp', ahead), lax.ppermute(b, 'fsdp', behind))  6.52 us
    pallas_call x1, Pallas kernels, call_compute(): pl.pallas_call(functools.partial(compute_kernel, sz), out_shape=out_shape...  5.83 us
    ppermute x2, starting transfers between devices, exchange(): return lax.ppermute(array, 'tensor', [(i, (i + s) % T) for i in range(T)])  2.78 us
    ppermute x6, waiting for transfers between devices, reduce_parts(): a, b = (lax.ppermute(a, 'fsdp', ahead), lax.ppermute(b, 'fsdp', behind))  2.58 us
    pallas_call x1, Pallas kernels, call_prepare(): pl.pallas_call(functools.partial(prepare_kernel, sz), out_shape=[half, ha...  2.5 us
  transfers between devices with their start and end apart: 32, of which 14 were waited for; matrix products, arithmetic and copies ran while one was open for 2% of the time, Pallas kernels for 7%

profile of v7, /device:TPU:0, one launch (start us, length us, event | category | flops | bytes accessed | tf_op | source)
XLA Modules:
  0.0 65.6 jit_solution(4752384601404792023)
XLA Ops:
  0.6 0.5 collective-permute-start.32
  1.2 0.1 collective-permute-start.33
  1.2 0.4 collective-permute-start.34
  1.7 0.8 %concatenate.3 = s32[101]{0:T(128)S(1)} concatenate(s32[32]{0:T(128)} %bitcast.9, s32[32]{0:T(128)} %bitcast.10, s32[32]{0:T(128)} %bitcast.11, s32[3]{0:T(128)} %bitcast.12, s32[1]{0:T(128)} %bitcast.4, s32[1]{0:T(128)} %bitcast.5), dimensions={0} | concatenate | bytes 808 | tf_op jit(solution)/shard_map/concatenate | solution.py:688
  2.4 0.0 collective-permute-done.32.refs_3_
  2.5 0.2 collective-permute-done.33.refs_4_
  2.6 0.2 collective-permute-done.34.refs_5_
  2.8 1.3 %plan.3 = (s32[32,128]{1,0:T(8,128)S(1)}, bf16[7,64,128]{2,1,0:T(8,128)(2,1)S(1)}, s32[1,128]{1,0:T(1,128)S(1)}) custom-call(s32[1,128]{1,0:T(1,128)S(1)} %pad_bitcast_fusion.own, bf16[1,2,128,128]{3,2,1,0:T(8,128)(2,1)} %refs_0_.1, bf16[1,2,128,128]{3,2,1,0:T(8,128)(2,1)} %refs_1_.1, bf16[1,2,128,128]{3,2,1,0:T(8,128)(2,1)} %refs_2_.1, ...), custom_call_target="tpu_custom_call" | custom-call | flops 1000000 | bytes 4000000 | tf_op jit(solution)/shard_map/plan/pallas_call | solution.py:476
  4.1 2.6 %collective-permute-start.35 = (bf16[7,64,128]{2,1,0:T(8,128)(2,1)S(1)}, bf16[7,64,128]{2,1,0:T(8,128)(2,1)S(1)}, u32[]{:S(2)}, u32[]{:S(2)}) collective-permute-start(bf16[7,64,128]{2,1,0:T(8,128)(2,1)S(1)} %get-tuple-element.76.refs_7_), channel_id=1, source_target_pairs={{0,8},{2,6},{8,16},{10,2},{16,24},{18,10},{24,28},{26,18},{28,20},... | collective-permute-start | bytes 344072 | tf_op jit(solution)/shard_map/ppermute | solution.py:601
  6.7 0.4 collective-permute-start.39
  7.1 3.0 %collective-permute-done.35.refs_5_ = bf16[7,64,128]{2,1,0:T(8,128)(2,1)S(1)} collective-permute-done((bf16[7,64,128]{2,1,0:T(8,128)(2,1)S(1)}, bf16[7,64,128]{2,1,0:T(8,128)(2,1)S(1)}, u32[]{:S(2)}, u32[]{:S(2)}) %collective-permute-start.35) | collective-permute-done | bytes 114720 | tf_op jit(solution)/shard_map/ppermute | solution.py:601
  10.1 2.3 %collective-permute-start.36 = (bf16[7,64,128]{2,1,0:T(8,128)(2,1)S(1)}, bf16[7,64,128]{2,1,0:T(8,128)(2,1)S(1)}, u32[]{:S(2)}, u32[]{:S(2)}) collective-permute-start(bf16[7,64,128]{2,1,0:T(8,128)(2,1)S(1)} %collective-permute-done.35.refs_5_), channel_id=1, source_target_pairs={{0,8},{2,6},{8,16},{10,2},{16,24},{18,10},{24,28},{26,18},{28,20},... | collective-permute-start | bytes 344072 | tf_op jit(solution)/shard_map/ppermute | solution.py:601
  12.3 0.3 collective-permute-start.40
  12.6 0.5 collective-permute-start.47
  13.2 3.1 %collective-permute-done.36.refs_3_ = bf16[7,64,128]{2,1,0:T(8,128)(2,1)S(1)} collective-permute-done((bf16[7,64,128]{2,1,0:T(8,128)(2,1)S(1)}, bf16[7,64,128]{2,1,0:T(8,128)(2,1)S(1)}, u32[]{:S(2)}, u32[]{:S(2)}) %collective-permute-start.36) | collective-permute-done | bytes 114720 | tf_op jit(solution)/shard_map/ppermute | solution.py:601
  16.3 0.9 %collective-permute-start.37 = (bf16[7,64,128]{2,1,0:T(8,128)(2,1)S(1)}, bf16[7,64,128]{2,1,0:T(8,128)(2,1)S(1)}, u32[]{:S(2)}, u32[]{:S(2)}) collective-permute-start(bf16[7,64,128]{2,1,0:T(8,128)(2,1)S(1)} %collective-permute-done.36.refs_3_), channel_id=1, source_target_pairs={{0,8},{2,6},{8,16},{10,2},{16,24},{18,10},{24,28},{26,18},{28,20},... | collective-permute-start | bytes 344072 | tf_op jit(solution)/shard_map/ppermute | solution.py:601
  17.2 1.0 %collective-permute-done.40.refs_4_ = bf16[7,64,128]{2,1,0:T(8,128)(2,1)S(1)} collective-permute-done((bf16[7,64,128]{2,1,0:T(8,128)(2,1)S(1)}, bf16[7,64,128]{2,1,0:T(8,128)(2,1)S(1)}, u32[]{:S(2)}, u32[]{:S(2)}) %collective-permute-start.40) | collective-permute-done | bytes 114720 | tf_op jit(solution)/shard_map/ppermute | solution.py:601
  18.2 0.1 collective-permute-start.41
  18.3 0.0 collective-permute-done.49.refs_15_
  18.3 0.8 %collective-permute-start.45 = (bf16[7,64,128]{2,1,0:T(8,128)(2,1)S(1)}, bf16[7,64,128]{2,1,0:T(8,128)(2,1)S(1)}, u32[]{:S(2)}, u32[]{:S(2)}) collective-permute-start(bf16[7,64,128]{2,1,0:T(8,128)(2,1)S(1)} %collective-permute-done.36.refs_3_), channel_id=1, source_target_pairs={{0,2},{2,0},{8,10},{10,8},{16,18},{18,16},{24,26},{26,24},{28,30},... | collective-permute-start | bytes 344072 | tf_op jit(solution)/shard_map/ppermute | solution.py:603
  19.1 0.0 collective-permute-done.47.refs_13_
  19.1 0.1 collective-permute-start.46
  19.1 2.8 %collective-permute-done.37.refs_1_ = bf16[7,64,128]{2,1,0:T(8,128)(2,1)S(1)} collective-permute-done((bf16[7,64,128]{2,1,0:T(8,128)(2,1)S(1)}, bf16[7,64,128]{2,1,0:T(8,128)(2,1)S(1)}, u32[]{:S(2)}, u32[]{:S(2)}) %collective-permute-start.37) | collective-permute-done | bytes 114720 | tf_op jit(solution)/shard_map/ppermute | solution.py:601
  21.9 0.1 collective-permute-start.38
  22.0 0.0 collective-permute-done.48.refs_14_
  22.0 2.0 %collective-permute-done.41.refs_2_ = bf16[7,64,128]{2,1,0:T(8,128)(2,1)S(1)} collective-permute-done((bf16[7,64,128]{2,1,0:T(8,128)(2,1)S(1)}, bf16[7,64,128]{2,1,0:T(8,128)(2,1)S(1)}, u32[]{:S(2)}, u32[]{:S(2)}) %collective-permute-start.41) | collective-permute-done | bytes 114720 | tf_op jit(solution)/shard_map/ppermute | solution.py:601
  23.9 0.1 collective-permute-start.43
  24.1 0.4 collective-permute-start.44
  24.4 0.0 collective-permute-done.46.refs_12_
  24.4 2.2 %collective-permute-done.38.refs_0_ = bf16[7,64,128]{2,1,0:T(8,128)(2,1)S(1)} collective-permute-done((bf16[7,64,128]{2,1,0:T(8,128)(2,1)S(1)}, bf16[7,64,128]{2,1,0:T(8,128)(2,1)S(1)}, u32[]{:S(2)}, u32[]{:S(2)}) %collective-permute-start.38) | collective-permute-done | bytes 114720 | tf_op jit(solution)/shard_map/ppermute | solution.py:604
  26.7 0.0 collective-permute-done.42.refs_8_
  26.7 0.0 collective-permute-done.43.refs_9_
  26.7 0.0 collective-permute-done.44.refs_10_
  26.7 5.8 %compute.3 = (bf16[56,64,128]{2,1,0:T(8,128)(2,1)S(1)}, bf16[14,64,128]{2,1,0:T(8,128)(2,1)S(1)}, bf16[42,64,128]{2,1,0:T(8,128)(2,1)S(1)}, bf16[18,128,128]{2,1,0:T(8,128)(2,1)S(1)}, bf16[18,128,128]{2,1,0:T(8,128)(2,1)S(1)}) custom-call(s32[32,128]{1,0:T(8,128)S(1)} %get-tuple-element.74.plan, bf16[128,8192]{1,0:T(8,128)(2,1)} %tokens.1, ...), custom_call_target="tpu_custom_call" | custom-call | flops 1000000000 | bytes 20000000 | tf_op jit(solution)/shard_map/compute/pallas_call | solution.py:532
  32.5 1.1 %collective-permute-start.50 = (bf16[14,64,128]{2,1,0:T(8,128)(2,1)S(1)}, bf16[14,64,128]{2,1,0:T(8,128)(2,1)S(1)}, u32[]{:S(2)}, u32[]{:S(2)}) collective-permute-start(bf16[14,64,128]{2,1,0:T(8,128)(2,1)S(1)} %get-tuple-element.79), channel_id=1, source_target_pairs={{0,2},{2,0},{8,10},{10,8},{16,18},{18,16},{24,26},{26,24},{28,30},... | collective-permute-start | bytes 688136 | tf_op jit(solution)/shard_map/ppermute | solution.py:612
  33.6 1.1 %collective-permute-done.50.__1_ = bf16[14,64,128]{2,1,0:T(8,128)(2,1)S(1)} collective-permute-done((bf16[14,64,128]{2,1,0:T(8,128)(2,1)S(1)}, bf16[14,64,128]{2,1,0:T(8,128)(2,1)S(1)}, u32[]{:S(2)}, u32[]{:S(2)}) %collective-permute-start.50) | collective-permute-done | bytes 229408 | tf_op jit(solution)/shard_map/ppermute | solution.py:612
  34.8 0.4 collective-permute-start.51
  35.1 0.1 add_convert_fusion.14
  35.2 0.4 collective-permute-start.52
  35.6 1.7 %collective-permute-start.53 = (bf16[7,64,128]{2,1,0:T(8,128)(2,1)S(1)}, bf16[7,64,128]{2,1,0:T(8,128)(2,1)S(1)}, u32[]{:S(2)}, u32[]{:S(2)}) collective-permute-start(bf16[7,64,128]{2,1,0:T(8,128)(2,1)S(1)} %get-tuple-element.81), channel_id=1, source_target_pairs={{0,4},{2,10},{8,0},{10,18},{16,8},{18,26},{24,16},{26,30},{28,24},... | collective-permute-start | bytes 344072 | tf_op jit(solution)/shard_map/ppermute | solution.py:628
  37.3 1.8 %collective-permute-start.55 = (bf16[18,128,128]{2,1,0:T(8,128)(2,1)S(1)}, bf16[18,128,128]{2,1,0:T(8,128)(2,1)S(1)}, u32[]{:S(2)}, u32[]{:S(2)}) collective-permute-start(bf16[18,128,128]{2,1,0:T(8,128)(2,1)S(1)} %get-tuple-element.84), channel_id=1, source_target_pairs={{0,1},{1,0},{2,3},{3,2},{4,5},{5,4},{6,7},{7,6},{8,9},{9,8},{10,11... | collective-permute-start | bytes 1769480 | tf_op jit(solution)/shard_map/ppermute | solution.py:655
  39.1 1.4 %collective-permute-done.52.__0_ = bf16[7,64,128]{2,1,0:T(8,128)(2,1)S(1)} collective-permute-done((bf16[7,64,128]{2,1,0:T(8,128)(2,1)S(1)}, bf16[7,64,128]{2,1,0:T(8,128)(2,1)S(1)}, u32[]{:S(2)}, u32[]{:S(2)}) %collective-permute-start.52) | collective-permute-done | bytes 114720 | tf_op jit(solution)/shard_map/ppermute | solution.py:628
  40.5 0.1 add_convert_fusion.13.__1_
  40.5 2.0 %collective-permute-start.57 = (bf16[7,64,128]{2,1,0:T(8,128)(2,1)S(1)}, bf16[7,64,128]{2,1,0:T(8,128)(2,1)S(1)}, u32[]{:S(2)}, u32[]{:S(2)}) collective-permute-start(bf16[7,64,128]{2,1,0:T(8,128)(2,1)S(1)} %add_convert_fusion.13.__1_), channel_id=1, source_target_pairs={{0,8},{2,6},{8,16},{10,2},{16,24},{18,10},{24,28},{26,18},{28,20},... | collective-permute-start | bytes 344072 | tf_op jit(solution)/shard_map/ppermute | solution.py:628
  42.5 0.1 add_convert_fusion.12.__1_
  42.5 1.0 %collective-permute-start.54 = (s32[1,128]{1,0:T(1,128)S(1)}, s32[1,128]{1,0:T(1,128)S(1)}, u32[]{:S(2)}, u32[]{:S(2)}) collective-permute-start(s32[1,128]{1,0:T(1,128)S(1)} %turn.30), channel_id=1, source_target_pairs={{0,1},{1,0},{2,3},{3,2},{4,5},{5,4},{6,7},{7,6},{8,9},{9,8},{10,11... | collective-permute-start | bytes 1544 | tf_op jit(solution)/shard_map/ppermute | solution.py:655
  43.5 1.8 %collective-permute-start.56 = (bf16[7,64,128]{2,1,0:T(8,128)(2,1)S(1)}, bf16[7,64,128]{2,1,0:T(8,128)(2,1)S(1)}, u32[]{:S(2)}, u32[]{:S(2)}) collective-permute-start(bf16[7,64,128]{2,1,0:T(8,128)(2,1)S(1)} %add_convert_fusion.12.__1_), channel_id=1, source_target_pairs={{0,4},{2,10},{8,0},{10,18},{16,8},{18,26},{24,16},{26,30},{28,24},... | collective-permute-start | bytes 344072 | tf_op jit(solution)/shard_map/ppermute | solution.py:628
  45.3 7.0 %collective-permute-done.54.__2_.note.refs_0_ = s32[1,128]{1,0:T(1,128)S(1)} collective-permute-done((s32[1,128]{1,0:T(1,128)S(1)}, s32[1,128]{1,0:T(1,128)S(1)}, u32[]{:S(2)}, u32[]{:S(2)}) %collective-permute-start.54) | collective-permute-done | bytes 544 | tf_op jit(solution)/shard_map/ppermute | solution.py:655
  52.4 0.1 add_convert_fusion.9
  52.4 0.4 collective-permute-start.61
  52.9 0.1 add_convert_fusion.10.__1_
  52.9 1.7 %collective-permute-start.58 = (bf16[7,64,128]{2,1,0:T(8,128)(2,1)S(1)}, bf16[7,64,128]{2,1,0:T(8,128)(2,1)S(1)}, u32[]{:S(2)}, u32[]{:S(2)}) collective-permute-start(bf16[7,64,128]{2,1,0:T(8,128)(2,1)S(1)} %add_convert_fusion.10.__1_), channel_id=1, source_target_pairs={{0,4},{2,10},{8,0},{10,18},{16,8},{18,26},{24,16},{26,30},{28,24},... | collective-permute-start | bytes 344072 | tf_op jit(solution)/shard_map/ppermute | solution.py:628
  54.6 0.2 collective-permute-start.59
  54.8 2.5 %prepare.3 = (bf16[128,4096]{1,0:T(8,128)(2,1)}, bf16[128,4096]{1,0:T(8,128)(2,1)}, bf16[18,128,128]{2,1,0:T(8,128)(2,1)S(1)}) custom-call(s32[32,128]{1,0:T(8,128)S(1)} %get-tuple-element.74.plan, s32[1,128]{1,0:T(1,128)S(1)} %collective-permute-done.54.__2_.note.refs_0_, bf16[18,128,128]{2,1,0:T(8,128)(2,1)S(1)} %turn.34.first), custom_call_target="tpu_custom_call" | custom-call | flops 1000000 | bytes 6000000 | tf_op jit(solution)/shard_map/prepare/pallas_call | solution.py:549
  57.3 1.2 %collective-permute-done.61.__0_ = bf16[7,64,128]{2,1,0:T(8,128)(2,1)S(1)} collective-permute-done((bf16[7,64,128]{2,1,0:T(8,128)(2,1)S(1)}, bf16[7,64,128]{2,1,0:T(8,128)(2,1)S(1)}, u32[]{:S(2)}, u32[]{:S(2)}) %collective-permute-start.61) | collective-permute-done | bytes 114720 | tf_op jit(solution)/shard_map/ppermute | solution.py:628
  58.5 0.1 add_convert_fusion.8
  58.6 1.3 %collective-permute-start.62 = (bf16[7,64,128]{2,1,0:T(8,128)(2,1)S(1)}, bf16[7,64,128]{2,1,0:T(8,128)(2,1)S(1)}, u32[]{:S(2)}, u32[]{:S(2)}) collective-permute-start(bf16[7,64,128]{2,1,0:T(8,128)(2,1)S(1)} %add_convert_fusion.8), channel_id=1, source_target_pairs={{0,8},{2,6},{8,16},{10,2},{16,24},{18,10},{24,28},{26,18},{28,20},... | collective-permute-start | bytes 344072 | tf_op jit(solution)/shard_map/ppermute | solution.py:639
  59.8 0.0 copy-start
  59.9 0.0 copy-start.1
  59.9 0.0 copy-start.2
  59.9 2.3 %add.122 = (bf16[128,4096]{1,0:T(8,128)(2,1)}, bf16[128,4096]{1,0:T(8,128)(2,1)}, s32[1]{0:T(128)}) custom-call(s32[32,128]{1,0:T(8,128)S(1)} %get-tuple-element.74.plan, s32[1,128]{1,0:T(1,128)S(1)} %collective-permute-done.54.__2_.note.refs_0_, bf16[18,128,128]{2,1,0:T(8,128)(2,1)S(1)} %turn.33.refs_1_, ...), custom_call_target="tpu_custom_call", output_to_operand_aliasing={{0}: (4, {}), {1}: (5, {})} | custom-call | flops 1000000 | bytes 3000000 | tf_op jit(solution)/shard_map/add/pallas_call | solution.py:562
  62.9 0.6 collective-permute-done.62.refs_1_
  63.4 0.6 collective-permute-done.63.refs_4_
  64.0 1.6 %last.3 = (bf16[1,2,128,128]{3,2,1,0:T(8,128)(2,1)}, bf16[1,2,128,128]{3,2,1,0:T(8,128)(2,1)}, bf16[1,2,128,128]{3,2,1,0:T(8,128)(2,1)}) custom-call(s32[32,128]{1,0:T(8,128)S(1)} %get-tuple-element.74.plan, bf16[7,64,128]{2,1,0:T(8,128)(2,1)S(1)} %get-tuple-element.109.refs_0_, bf16[7,64,128]{2,1,0:T(8,128)(2,1)S(1)} %collective-permute-done.62.refs_1_, ...), custom_call_target="tpu_custom_call" | custom-call | flops 1000000 | bytes 1000000 | tf_op jit(solution)/shard_map/last/pallas_call | solution.py:581
  (29 shorter events, 0.1 us)
Async XLA Ops:
  0.6 1.8 %collective-permute-start.32 = (bf16[1,2,128,128]{3,2,1,0:T(8,128)(2,1)}, bf16[1,2,128,128]{3,2,1,0:T(8,128)(2,1)S(1)}, u32[]{:S(2)}, u32[]{:S(2)}) collective-permute-start(bf16[1,2,128,128]{3,2,1,0:T(8,128)(2,1)} %refs_0_.1), channel_id=1, source_target_pairs={{0,2},{2,0},{8,10},{10,8},{16,18},{18,16},{24,26},{26,24},{28,30},... | collective-permute-start | bytes 196616 | tf_op jit(solution)/shard_map/ppermute | solution.py:651
  1.2 1.5 %collective-permute-start.33 = (bf16[1,2,128,128]{3,2,1,0:T(8,128)(2,1)}, bf16[1,2,128,128]{3,2,1,0:T(8,128)(2,1)S(1)}, u32[]{:S(2)}, u32[]{:S(2)}) collective-permute-start(bf16[1,2,128,128]{3,2,1,0:T(8,128)(2,1)} %refs_1_.1), channel_id=1, source_target_pairs={{0,2},{2,0},{8,10},{10,8},{16,18},{18,16},{24,26},{26,24},{28,30},... | collective-permute-start | bytes 196616 | tf_op jit(solution)/shard_map/ppermute | solution.py:651
  1.2 1.5 %collective-permute-start.34 = (bf16[1,2,128,128]{3,2,1,0:T(8,128)(2,1)}, bf16[1,2,128,128]{3,2,1,0:T(8,128)(2,1)S(1)}, u32[]{:S(2)}, u32[]{:S(2)}) collective-permute-start(bf16[1,2,128,128]{3,2,1,0:T(8,128)(2,1)} %refs_2_.1), channel_id=1, source_target_pairs={{0,2},{2,0},{8,10},{10,8},{16,18},{18,16},{24,26},{26,24},{28,30},... | collective-permute-start | bytes 196616 | tf_op jit(solution)/shard_map/ppermute | solution.py:651
  4.1 6.0 %collective-permute-start.35 = (bf16[7,64,128]{2,1,0:T(8,128)(2,1)S(1)}, bf16[7,64,128]{2,1,0:T(8,128)(2,1)S(1)}, u32[]{:S(2)}, u32[]{:S(2)}) collective-permute-start(bf16[7,64,128]{2,1,0:T(8,128)(2,1)S(1)} %get-tuple-element.76.refs_7_), channel_id=1, source_target_pairs={{0,8},{2,6},{8,16},{10,2},{16,24},{18,10},{24,28},{26,18},{28,20},... | collective-permute-start | bytes 344072 | tf_op jit(solution)/shard_map/ppermute | solution.py:601
  6.7 5.7 %collective-permute-start.39 = (bf16[7,64,128]{2,1,0:T(8,128)(2,1)S(1)}, bf16[7,64,128]{2,1,0:T(8,128)(2,1)S(1)}, u32[]{:S(2)}, u32[]{:S(2)}) collective-permute-start(bf16[7,64,128]{2,1,0:T(8,128)(2,1)S(1)} %get-tuple-element.76.refs_7_), channel_id=1, source_target_pairs={{0,4},{2,10},{8,0},{10,18},{16,8},{18,26},{24,16},{26,30},{28,24},... | collective-permute-start | bytes 344072 | tf_op jit(solution)/shard_map/ppermute | solution.py:601
  10.1 6.2 %collective-permute-start.36 = (bf16[7,64,128]{2,1,0:T(8,128)(2,1)S(1)}, bf16[7,64,128]{2,1,0:T(8,128)(2,1)S(1)}, u32[]{:S(2)}, u32[]{:S(2)}) collective-permute-start(bf16[7,64,128]{2,1,0:T(8,128)(2,1)S(1)} %collective-permute-done.35.refs_5_), channel_id=1, source_target_pairs={{0,8},{2,6},{8,16},{10,2},{16,24},{18,10},{24,28},{26,18},{28,20},... | collective-permute-start | bytes 344072 | tf_op jit(solution)/shard_map/ppermute | solution.py:601
  12.3 5.9 %collective-permute-start.40 = (bf16[7,64,128]{2,1,0:T(8,128)(2,1)S(1)}, bf16[7,64,128]{2,1,0:T(8,128)(2,1)S(1)}, u32[]{:S(2)}, u32[]{:S(2)}) collective-permute-start(bf16[7,64,128]{2,1,0:T(8,128)(2,1)S(1)} %collective-permute-done.39.refs_6_), channel_id=1, source_target_pairs={{0,4},{2,10},{8,0},{10,18},{16,8},{18,26},{24,16},{26,30},{28,24},... | collective-permute-start | bytes 344072 | tf_op jit(solution)/shard_map/ppermute | solution.py:601
  12.6 5.7 %collective-permute-start.49 = (bf16[7,64,128]{2,1,0:T(8,128)(2,1)S(1)}, bf16[7,64,128]{2,1,0:T(8,128)(2,1)S(1)}, u32[]{:S(2)}, u32[]{:S(2)}) collective-permute-start(bf16[7,64,128]{2,1,0:T(8,128)(2,1)S(1)} %get-tuple-element.76.refs_7_), channel_id=1, source_target_pairs={{0,2},{2,0},{8,10},{10,8},{16,18},{18,16},{24,26},{26,24},{28,30},... | collective-permute-start | bytes 344072 | tf_op jit(solution)/shard_map/ppermute | solution.py:603
  12.6 6.4 %collective-permute-start.47 = (bf16[7,64,128]{2,1,0:T(8,128)(2,1)S(1)}, bf16[7,64,128]{2,1,0:T(8,128)(2,1)S(1)}, u32[]{:S(2)}, u32[]{:S(2)}) collective-permute-start(bf16[7,64,128]{2,1,0:T(8,128)(2,1)S(1)} %collective-permute-done.35.refs_5_), channel_id=1, source_target_pairs={{0,2},{2,0},{8,10},{10,8},{16,18},{18,16},{24,26},{26,24},{28,30},... | collective-permute-start | bytes 344072 | tf_op jit(solution)/shard_map/ppermute | solution.py:603
  16.3 5.6 %collective-permute-start.37 = (bf16[7,64,128]{2,1,0:T(8,128)(2,1)S(1)}, bf16[7,64,128]{2,1,0:T(8,128)(2,1)S(1)}, u32[]{:S(2)}, u32[]{:S(2)}) collective-permute-start(bf16[7,64,128]{2,1,0:T(8,128)(2,1)S(1)} %collective-permute-done.36.refs_3_), channel_id=1, source_target_pairs={{0,8},{2,6},{8,16},{10,2},{16,24},{18,10},{24,28},{26,18},{28,20},... | collective-permute-start | bytes 344072 | tf_op jit(solution)/shard_map/ppermute | solution.py:601
  17.2 4.8 %collective-permute-start.48 = (bf16[7,64,128]{2,1,0:T(8,128)(2,1)S(1)}, bf16[7,64,128]{2,1,0:T(8,128)(2,1)S(1)}, u32[]{:S(2)}, u32[]{:S(2)}) collective-permute-start(bf16[7,64,128]{2,1,0:T(8,128)(2,1)S(1)} %collective-permute-done.39.refs_6_), channel_id=1, source_target_pairs={{0,2},{2,0},{8,10},{10,8},{16,18},{18,16},{24,26},{26,24},{28,30},... | collective-permute-start | bytes 344072 | tf_op jit(solution)/shard_map/ppermute | solution.py:603
  18.2 5.7 %collective-permute-start.41 = (bf16[7,64,128]{2,1,0:T(8,128)(2,1)S(1)}, bf16[7,64,128]{2,1,0:T(8,128)(2,1)S(1)}, u32[]{:S(2)}, u32[]{:S(2)}) collective-permute-start(bf16[7,64,128]{2,1,0:T(8,128)(2,1)S(1)} %collective-permute-done.40.refs_4_), channel_id=1, source_target_pairs={{0,4},{2,10},{8,0},{10,18},{16,8},{18,26},{24,16},{26,30},{28,24},... | collective-permute-start | bytes 344072 | tf_op jit(solution)/shard_map/ppermute | solution.py:601
  18.3 5.8 %collective-permute-start.45 = (bf16[7,64,128]{2,1,0:T(8,128)(2,1)S(1)}, bf16[7,64,128]{2,1,0:T(8,128)(2,1)S(1)}, u32[]{:S(2)}, u32[]{:S(2)}) collective-permute-start(bf16[7,64,128]{2,1,0:T(8,128)(2,1)S(1)} %collective-permute-done.36.refs_3_), channel_id=1, source_target_pairs={{0,2},{2,0},{8,10},{10,8},{16,18},{18,16},{24,26},{26,24},{28,30},... | collective-permute-start | bytes 344072 | tf_op jit(solution)/shard_map/ppermute | solution.py:603
  19.1 5.4 %collective-permute-start.46 = (bf16[7,64,128]{2,1,0:T(8,128)(2,1)S(1)}, bf16[7,64,128]{2,1,0:T(8,128)(2,1)S(1)}, u32[]{:S(2)}, u32[]{:S(2)}) collective-permute-start(bf16[7,64,128]{2,1,0:T(8,128)(2,1)S(1)} %collective-permute-done.40.refs_4_), channel_id=1, source_target_pairs={{0,2},{2,0},{8,10},{10,8},{16,18},{18,16},{24,26},{26,24},{28,30},... | collective-permute-start | bytes 344072 | tf_op jit(solution)/shard_map/ppermute | solution.py:603
  21.9 4.8 %collective-permute-start.38 = (bf16[7,64,128]{2,1,0:T(8,128)(2,1)S(1)}, bf16[7,64,128]{2,1,0:T(8,128)(2,1)S(1)}, u32[]{:S(2)}, u32[]{:S(2)}) collective-permute-start(bf16[7,64,128]{2,1,0:T(8,128)(2,1)S(1)} %collective-permute-done.37.refs_1_), channel_id=1, source_target_pairs={{0,8},{2,6},{8,16},{10,2},{16,24},{18,10},{24,28},{26,18},{28,20},... | collective-permute-start | bytes 344072 | tf_op jit(solution)/shard_map/ppermute | solution.py:604
  22.0 4.7 %collective-permute-start.42 = (bf16[7,64,128]{2,1,0:T(8,128)(2,1)S(1)}, bf16[7,64,128]{2,1,0:T(8,128)(2,1)S(1)}, u32[]{:S(2)}, u32[]{:S(2)}) collective-permute-start(bf16[7,64,128]{2,1,0:T(8,128)(2,1)S(1)} %collective-permute-done.37.refs_1_), channel_id=1, source_target_pairs={{0,10},{2,4},{8,18},{10,0},{16,26},{18,8},{24,30},{26,16},{28,22},... | collective-permute-start | bytes 344072 | tf_op jit(solution)/shard_map/ppermute | solution.py:605
  23.9 2.8 %collective-permute-start.43 = (bf16[7,64,128]{2,1,0:T(8,128)(2,1)S(1)}, bf16[7,64,128]{2,1,0:T(8,128)(2,1)S(1)}, u32[]{:S(2)}, u32[]{:S(2)}) collective-permute-start(bf16[7,64,128]{2,1,0:T(8,128)(2,1)S(1)} %collective-permute-done.37.refs_1_), channel_id=1, source_target_pairs={{0,2},{2,0},{8,10},{10,8},{16,18},{18,16},{24,26},{26,24},{28,30},... | collective-permute-start | bytes 344072 | tf_op jit(solution)/shard_map/ppermute | solution.py:603
  24.1 2.6 %collective-permute-start.44 = (bf16[7,64,128]{2,1,0:T(8,128)(2,1)S(1)}, bf16[7,64,128]{2,1,0:T(8,128)(2,1)S(1)}, u32[]{:S(2)}, u32[]{:S(2)}) collective-permute-start(bf16[7,64,128]{2,1,0:T(8,128)(2,1)S(1)} %collective-permute-done.41.refs_2_), channel_id=1, source_target_pairs={{0,2},{2,0},{8,10},{10,8},{16,18},{18,16},{24,26},{26,24},{28,30},... | collective-permute-start | bytes 344072 | tf_op jit(solution)/shard_map/ppermute | solution.py:603
  32.5 2.2 %collective-permute-start.50 = (bf16[14,64,128]{2,1,0:T(8,128)(2,1)S(1)}, bf16[14,64,128]{2,1,0:T(8,128)(2,1)S(1)}, u32[]{:S(2)}, u32[]{:S(2)}) collective-permute-start(bf16[14,64,128]{2,1,0:T(8,128)(2,1)S(1)} %get-tuple-element.79), channel_id=1, source_target_pairs={{0,2},{2,0},{8,10},{10,8},{16,18},{18,16},{24,26},{26,24},{28,30},... | collective-permute-start | bytes 688136 | tf_op jit(solution)/shard_map/ppermute | solution.py:612
  34.8 5.7 %collective-permute-start.51 = (bf16[42,64,128]{2,1,0:T(8,128)(2,1)S(1)}, bf16[42,64,128]{2,1,0:T(8,128)(2,1)S(1)}, u32[]{:S(2)}, u32[]{:S(2)}) collective-permute-start(bf16[42,64,128]{2,1,0:T(8,128)(2,1)S(1)} %turn.27), channel_id=1, source_target_pairs={{0,2},{2,0},{8,10},{10,8},{16,18},{18,16},{24,26},{26,24},{28,30},... | collective-permute-start | bytes 2064392 | tf_op jit(solution)/shard_map/ppermute | solution.py:613
  35.2 5.3 %collective-permute-start.52 = (bf16[7,64,128]{2,1,0:T(8,128)(2,1)S(1)}, bf16[7,64,128]{2,1,0:T(8,128)(2,1)S(1)}, u32[]{:S(2)}, u32[]{:S(2)}) collective-permute-start(bf16[7,64,128]{2,1,0:T(8,128)(2,1)S(1)} %get-tuple-element.80), channel_id=1, source_target_pairs={{0,8},{2,6},{8,16},{10,2},{16,24},{18,10},{24,28},{26,18},{28,20},... | collective-permute-start | bytes 344072 | tf_op jit(solution)/shard_map/ppermute | solution.py:628
  35.6 4.9 %collective-permute-start.53 = (bf16[7,64,128]{2,1,0:T(8,128)(2,1)S(1)}, bf16[7,64,128]{2,1,0:T(8,128)(2,1)S(1)}, u32[]{:S(2)}, u32[]{:S(2)}) collective-permute-start(bf16[7,64,128]{2,1,0:T(8,128)(2,1)S(1)} %get-tuple-element.81), channel_id=1, source_target_pairs={{0,4},{2,10},{8,0},{10,18},{16,8},{18,26},{24,16},{26,30},{28,24},... | collective-permute-start | bytes 344072 | tf_op jit(solution)/shard_map/ppermute | solution.py:628
  37.3 20.1 %collective-permute-start.55 = (bf16[18,128,128]{2,1,0:T(8,128)(2,1)S(1)}, bf16[18,128,128]{2,1,0:T(8,128)(2,1)S(1)}, u32[]{:S(2)}, u32[]{:S(2)}) collective-permute-start(bf16[18,128,128]{2,1,0:T(8,128)(2,1)S(1)} %get-tuple-element.84), channel_id=1, source_target_pairs={{0,1},{1,0},{2,3},{3,2},{4,5},{5,4},{6,7},{7,6},{8,9},{9,8},{10,11... | collective-permute-start | bytes 1769480 | tf_op jit(solution)/shard_map/ppermute | solution.py:655
  40.5 11.8 %collective-permute-start.57 = (bf16[7,64,128]{2,1,0:T(8,128)(2,1)S(1)}, bf16[7,64,128]{2,1,0:T(8,128)(2,1)S(1)}, u32[]{:S(2)}, u32[]{:S(2)}) collective-permute-start(bf16[7,64,128]{2,1,0:T(8,128)(2,1)S(1)} %add_convert_fusion.13.__1_), channel_id=1, source_target_pairs={{0,8},{2,6},{8,16},{10,2},{16,24},{18,10},{24,28},{26,18},{28,20},... | collective-permute-start | bytes 344072 | tf_op jit(solution)/shard_map/ppermute | solution.py:628
  42.5 9.8 %collective-permute-start.54 = (s32[1,128]{1,0:T(1,128)S(1)}, s32[1,128]{1,0:T(1,128)S(1)}, u32[]{:S(2)}, u32[]{:S(2)}) collective-permute-start(s32[1,128]{1,0:T(1,128)S(1)} %turn.30), channel_id=1, source_target_pairs={{0,1},{1,0},{2,3},{3,2},{4,5},{5,4},{6,7},{7,6},{8,9},{9,8},{10,11... | collective-permute-start | bytes 1544 | tf_op jit(solution)/shard_map/ppermute | solution.py:655
  43.5 9.3 %collective-permute-start.56 = (bf16[7,64,128]{2,1,0:T(8,128)(2,1)S(1)}, bf16[7,64,128]{2,1,0:T(8,128)(2,1)S(1)}, u32[]{:S(2)}, u32[]{:S(2)}) collective-permute-start(bf16[7,64,128]{2,1,0:T(8,128)(2,1)S(1)} %add_convert_fusion.12.__1_), channel_id=1, source_target_pairs={{0,4},{2,10},{8,0},{10,18},{16,8},{18,26},{24,16},{26,30},{28,24},... | collective-permute-start | bytes 344072 | tf_op jit(solution)/shard_map/ppermute | solution.py:628
  52.4 6.1 %collective-permute-start.61 = (bf16[7,64,128]{2,1,0:T(8,128)(2,1)S(1)}, bf16[7,64,128]{2,1,0:T(8,128)(2,1)S(1)}, u32[]{:S(2)}, u32[]{:S(2)}) collective-permute-start(bf16[7,64,128]{2,1,0:T(8,128)(2,1)S(1)} %get-tuple-element.110.__1_), channel_id=1, source_target_pairs={{0,8},{2,6},{8,16},{10,2},{16,24},{18,10},{24,28},{26,18},{28,20},... | collective-permute-start | bytes 344072 | tf_op jit(solution)/shard_map/ppermute | solution.py:628
  52.9 2.0 %collective-permute-start.60 = (bf16[7,64,128]{2,1,0:T(8,128)(2,1)S(1)}, bf16[7,64,128]{2,1,0:T(8,128)(2,1)S(1)}, u32[]{:S(2)}, u32[]{:S(2)}) collective-permute-start(bf16[7,64,128]{2,1,0:T(8,128)(2,1)S(1)} %get-tuple-element.109.refs_0_), channel_id=1, source_target_pairs={{0,2},{2,0},{8,10},{10,8},{16,18},{18,16},{24,26},{26,24},{28,30},... | collective-permute-start | bytes 344072 | tf_op jit(solution)/shard_map/ppermute | solution.py:625
  52.9 6.9 %collective-permute-start.58 = (bf16[7,64,128]{2,1,0:T(8,128)(2,1)S(1)}, bf16[7,64,128]{2,1,0:T(8,128)(2,1)S(1)}, u32[]{:S(2)}, u32[]{:S(2)}) collective-permute-start(bf16[7,64,128]{2,1,0:T(8,128)(2,1)S(1)} %add_convert_fusion.10.__1_), channel_id=1, source_target_pairs={{0,4},{2,10},{8,0},{10,18},{16,8},{18,26},{24,16},{26,30},{28,24},... | collective-permute-start | bytes 344072 | tf_op jit(solution)/shard_map/ppermute | solution.py:628
  54.6 5.2 %collective-permute-start.59 = (bf16[7,64,128]{2,1,0:T(8,128)(2,1)S(1)}, bf16[7,64,128]{2,1,0:T(8,128)(2,1)S(1)}, u32[]{:S(2)}, u32[]{:S(2)}) collective-permute-start(bf16[7,64,128]{2,1,0:T(8,128)(2,1)S(1)} %add_convert_fusion.10.__1_), channel_id=1, source_target_pairs={{0,6},{2,8},{8,2},{10,16},{16,10},{18,24},{24,18},{26,28},{28,26},... | collective-permute-start | bytes 344072 | tf_op jit(solution)/shard_map/ppermute | solution.py:643
  58.6 4.8 %collective-permute-start.62 = (bf16[7,64,128]{2,1,0:T(8,128)(2,1)S(1)}, bf16[7,64,128]{2,1,0:T(8,128)(2,1)S(1)}, u32[]{:S(2)}, u32[]{:S(2)}) collective-permute-start(bf16[7,64,128]{2,1,0:T(8,128)(2,1)S(1)} %add_convert_fusion.8), channel_id=1, source_target_pairs={{0,8},{2,6},{8,16},{10,2},{16,24},{18,10},{24,28},{26,18},{28,20},... | collective-permute-start | bytes 344072 | tf_op jit(solution)/shard_map/ppermute | solution.py:639
  59.8 4.2 %collective-permute-start.63 = (bf16[7,64,128]{2,1,0:T(8,128)(2,1)S(1)}, bf16[7,64,128]{2,1,0:T(8,128)(2,1)S(1)}, u32[]{:S(2)}, u32[]{:S(2)}) collective-permute-start(bf16[7,64,128]{2,1,0:T(8,128)(2,1)S(1)} %add_convert_fusion.8), channel_id=1, source_target_pairs={{0,10},{2,4},{8,18},{10,0},{16,26},{18,8},{24,30},{26,16},{28,22},... | collective-permute-start | bytes 344072 | tf_op jit(solution)/shard_map/ppermute | solution.py:642
  59.8 5.7 %copy-start = (bf16[1,2,128,128]{3,2,1,0:T(8,128)(2,1)S(1)}, bf16[1,2,128,128]{3,2,1,0:T(8,128)(2,1)}, u32[]{:S(2)}) copy-start(bf16[1,2,128,128]{3,2,1,0:T(8,128)(2,1)} %refs_0_.1) | copy-start | bytes 196612
  59.9 5.7 %copy-start.1 = (bf16[1,2,128,128]{3,2,1,0:T(8,128)(2,1)S(1)}, bf16[1,2,128,128]{3,2,1,0:T(8,128)(2,1)}, u32[]{:S(2)}) copy-start(bf16[1,2,128,128]{3,2,1,0:T(8,128)(2,1)} %refs_1_.1) | copy-start | bytes 196612
  59.9 5.7 %copy-start.2 = (bf16[1,2,128,128]{3,2,1,0:T(8,128)(2,1)S(1)}, bf16[1,2,128,128]{3,2,1,0:T(8,128)(2,1)}, u32[]{:S(2)}) copy-start(bf16[1,2,128,128]{3,2,1,0:T(8,128)(2,1)} %refs_2_.1) | copy-start | bytes 196612

commit v8 on v6

--- a/solution.py
+++ b/solution.py
@@ -11,7 +11,7 @@
 BLK = 128
 GROUP = 8
 COLUMNS = 4
-FIRST_SEND = 18
+FIRST_SEND = 17
 LEAN_SLOTS = 7
 ROWS = BLK // 2
 SMALL = 4 * 1024 * 1024
@@ -628,9 +628,9 @@
         last_b = b
         a, b = lax.ppermute(a, "fsdp", ahead), lax.ppermute(b, "fsdp", behind)
         if s == 1:
-            a, b = call_turn([a, b], notes)
+            a, b = call_turn([a, b], [])
         else:
-            a = call_turn([a], [last_b] + (list(prepared[2:]) if s == 2 else sent))[0]
+            a = call_turn([a], [last_b] + (notes if s == 2 else sent + list(prepared[2:])))[0]
         a = term(sz.top - s, a)
         if s + 1 < sz.top:
             b = term(sz.top + 1 + s, call_turn([b], [a])[0])

time: 60.8 us -> 61.8 us (1.016)
  waiting for transfers between devices: 22.2 us -> 20.1 us
  Pallas kernels: 13.4 us -> 15.3 us
  starting transfers between devices: 22.2 us -> 23.5 us
    ppermute x2, waiting for transfers between devices: 5.5 us -> 0.01 us  [exchange(): return lax.ppermute(array, 'tensor', [(i, (i + s) % T) for i in range(T)])]
    ppermute x6, waiting for transfers between devices: 0.02 us -> 3.83 us  [reduce_parts(): a, b = (lax.ppermute(a, 'fsdp', ahead), lax.ppermute(b, 'fsdp', behind))]
    pallas_call x1, Pallas kernels: 5.61 us -> 7.53 us  [call_compute(): pl.pallas_call(functools.partial(compute_kernel, sz), out_shape=out_shape...]
    ppermute x1, waiting for transfers between devices: 0.85 us -> 0.01 us  [reduce_parts(): mine = [here, lax.ppermute(a, 'fsdp', ahead), b]]
    ppermute x1, starting transfers between devices: 0.01 us -> 0.82 us  [reduce_parts(): lax.ppermute(a, 'fsdp', across(ahead))]
    ppermute x1, starting transfers between devices: 0.16 us -> 0.89 us  [reduce_parts(): lax.ppermute(last_b, 'fsdp', across(behind))]
  transfers between devices with their start and end apart: 32 -> 32, of which waited for: 13 -> 12; matrix products, arithmetic and copies ran while one was open for 2% -> 2% of each run, Pallas kernels for 8% -> 8%
where the time goes in v8:
time: 61.8 us; the launch traced here: 61.5 us
  starting transfers between devices  23.5 us (38%)
  waiting for transfers between devices  20.1 us (33%)
  Pallas kernels  15.3 us (25%)
  between operations  1.41 us (2%)
  local copies, waits for them, and re-layouts  0.8 us (1%)
    ppermute x6, waiting for transfers between devices, gather_chunks(): a, b = (lax.ppermute(a, 'fsdp', ahead), lax.ppermute(b, 'fsdp', behind))  12.1 us
    ppermute x6, starting transfers between devices, reduce_parts(): a, b = (lax.ppermute(a, 'fsdp', ahead), lax.ppermute(b, 'fsdp', behind))  7.58 us
    pallas_call x1, Pallas kernels, call_compute(): pl.pallas_call(functools.partial(compute_kernel, sz), out_shape=out_shape...  7.53 us
    ppermute x6, starting transfers between devices, gather_chunks(): a, b = (lax.ppermute(a, 'fsdp', ahead), lax.ppermute(b, 'fsdp', behind))  6.52 us
    ppermute x6, waiting for transfers between devices, reduce_parts(): a, b = (lax.ppermute(a, 'fsdp', ahead), lax.ppermute(b, 'fsdp', behind))  3.83 us
    pallas_call x1, Pallas kernels, call_prepare(): pl.pallas_call(functools.partial(prepare_kernel, sz), out_shape=[half, ha...  2.61 us
    pallas_call x1, Pallas kernels, call_add(): pl.pallas_call(functools.partial(add_kernel, sz), out_shape=[jax.ShapeDty...  2.3 us
    ppermute x1, waiting for transfers between devices, gather_chunks(): same[sz.top] = lax.ppermute(a, 'fsdp', ahead)  2.12 us
  transfers between devices with their start and end apart: 32, of which 12 were waited for; matrix products, arithmetic and copies ran while one was open for 2% of the time, Pallas kernels for 8%

profile of v8, /device:TPU:0, one launch (start us, length us, event | category | flops | bytes accessed | tf_op | source)
XLA Modules:
  0.0 61.5 jit_solution(9875611972589357531)
XLA Ops:
  0.6 0.5 collective-permute-start.32
  1.2 0.1 collective-permute-start.33
  1.2 0.4 collective-permute-start.34
  1.7 0.8 %concatenate.3 = s32[101]{0:T(128)S(1)} concatenate(s32[32]{0:T(128)} %bitcast.9, s32[32]{0:T(128)} %bitcast.10, s32[32]{0:T(128)} %bitcast.11, s32[3]{0:T(128)} %bitcast.12, s32[1]{0:T(128)} %bitcast.4, s32[1]{0:T(128)} %bitcast.5), dimensions={0} | concatenate | bytes 808 | tf_op jit(solution)/shard_map/concatenate | solution.py:684
  2.5 0.2 collective-permute-done.33.refs_4_
  2.6 0.2 collective-permute-done.34.refs_5_
  2.8 1.3 %plan.3 = (s32[32,128]{1,0:T(8,128)S(1)}, bf16[7,64,128]{2,1,0:T(8,128)(2,1)S(1)}, s32[1,128]{1,0:T(1,128)S(1)}) custom-call(s32[1,128]{1,0:T(1,128)S(1)} %pad_bitcast_fusion.own, bf16[1,2,128,128]{3,2,1,0:T(8,128)(2,1)} %refs_0_.1, bf16[1,2,128,128]{3,2,1,0:T(8,128)(2,1)} %refs_1_.1, bf16[1,2,128,128]{3,2,1,0:T(8,128)(2,1)} %refs_2_.1, ...), custom_call_target="tpu_custom_call" | custom-call | flops 1000000 | bytes 4000000 | tf_op jit(solution)/shard_map/plan/pallas_call | solution.py:476
  4.1 3.0 %collective-permute-start.36 = (bf16[7,64,128]{2,1,0:T(8,128)(2,1)S(1)}, bf16[7,64,128]{2,1,0:T(8,128)(2,1)S(1)}, u32[]{:S(2)}, u32[]{:S(2)}) collective-permute-start(bf16[7,64,128]{2,1,0:T(8,128)(2,1)S(1)} %get-tuple-element.76.refs_7_), channel_id=1, source_target_pairs={{0,8},{2,6},{8,16},{10,2},{16,24},{18,10},{24,28},{26,18},{28,20},... | collective-permute-start | bytes 344072 | tf_op jit(solution)/shard_map/ppermute | solution.py:601
  7.1 0.0 collective-permute-start.40
  7.1 3.0 %collective-permute-done.36.refs_5_ = bf16[7,64,128]{2,1,0:T(8,128)(2,1)S(1)} collective-permute-done((bf16[7,64,128]{2,1,0:T(8,128)(2,1)S(1)}, bf16[7,64,128]{2,1,0:T(8,128)(2,1)S(1)}, u32[]{:S(2)}, u32[]{:S(2)}) %collective-permute-start.36) | collective-permute-done | bytes 114720 | tf_op jit(solution)/shard_map/ppermute | solution.py:601
  10.1 2.2 %collective-permute-start.37 = (bf16[7,64,128]{2,1,0:T(8,128)(2,1)S(1)}, bf16[7,64,128]{2,1,0:T(8,128)(2,1)S(1)}, u32[]{:S(2)}, u32[]{:S(2)}) collective-permute-start(bf16[7,64,128]{2,1,0:T(8,128)(2,1)S(1)} %collective-permute-done.36.refs_5_), channel_id=1, source_target_pairs={{0,8},{2,6},{8,16},{10,2},{16,24},{18,10},{24,28},{26,18},{28,20},... | collective-permute-start | bytes 344072 | tf_op jit(solution)/shard_map/ppermute | solution.py:601
  12.3 0.4 collective-permute-start.41
  12.7 0.0 collective-permute-start.50
  12.7 0.5 collective-permute-start.48
  13.3 3.0 %collective-permute-done.37.refs_3_ = bf16[7,64,128]{2,1,0:T(8,128)(2,1)S(1)} collective-permute-done((bf16[7,64,128]{2,1,0:T(8,128)(2,1)S(1)}, bf16[7,64,128]{2,1,0:T(8,128)(2,1)S(1)}, u32[]{:S(2)}, u32[]{:S(2)}) %collective-permute-start.37) | collective-permute-done | bytes 114720 | tf_op jit(solution)/shard_map/ppermute | solution.py:601
  16.2 0.9 %collective-permute-start.38 = (bf16[7,64,128]{2,1,0:T(8,128)(2,1)S(1)}, bf16[7,64,128]{2,1,0:T(8,128)(2,1)S(1)}, u32[]{:S(2)}, u32[]{:S(2)}) collective-permute-start(bf16[7,64,128]{2,1,0:T(8,128)(2,1)S(1)} %collective-permute-done.37.refs_3_), channel_id=1, source_target_pairs={{0,8},{2,6},{8,16},{10,2},{16,24},{18,10},{24,28},{26,18},{28,20},... | collective-permute-start | bytes 344072 | tf_op jit(solution)/shard_map/ppermute | solution.py:601
  17.1 0.0 collective-permute-start.49
  17.1 1.2 %collective-permute-done.41.refs_4_ = bf16[7,64,128]{2,1,0:T(8,128)(2,1)S(1)} collective-permute-done((bf16[7,64,128]{2,1,0:T(8,128)(2,1)S(1)}, bf16[7,64,128]{2,1,0:T(8,128)(2,1)S(1)}, u32[]{:S(2)}, u32[]{:S(2)}) %collective-permute-start.41) | collective-permute-done | bytes 114720 | tf_op jit(solution)/shard_map/ppermute | solution.py:601
  18.3 0.7 %collective-permute-start.46 = (bf16[7,64,128]{2,1,0:T(8,128)(2,1)S(1)}, bf16[7,64,128]{2,1,0:T(8,128)(2,1)S(1)}, u32[]{:S(2)}, u32[]{:S(2)}) collective-permute-start(bf16[7,64,128]{2,1,0:T(8,128)(2,1)S(1)} %collective-permute-done.37.refs_3_), channel_id=1, source_target_pairs={{0,2},{2,0},{8,10},{10,8},{16,18},{18,16},{24,26},{26,24},{28,30},... | collective-permute-start | bytes 344072 | tf_op jit(solution)/shard_map/ppermute | solution.py:603
  19.1 0.0 collective-permute-done.48.refs_13_
  19.1 0.1 collective-permute-start.47
  19.1 2.8 %collective-permute-done.38.refs_1_ = bf16[7,64,128]{2,1,0:T(8,128)(2,1)S(1)} collective-permute-done((bf16[7,64,128]{2,1,0:T(8,128)(2,1)S(1)}, bf16[7,64,128]{2,1,0:T(8,128)(2,1)S(1)}, u32[]{:S(2)}, u32[]{:S(2)}) %collective-permute-start.38) | collective-permute-done | bytes 114720 | tf_op jit(solution)/shard_map/ppermute | solution.py:601
  21.9 0.0 collective-permute-start.39
  21.9 2.1 %collective-permute-done.42.refs_2_ = bf16[7,64,128]{2,1,0:T(8,128)(2,1)S(1)} collective-permute-done((bf16[7,64,128]{2,1,0:T(8,128)(2,1)S(1)}, bf16[7,64,128]{2,1,0:T(8,128)(2,1)S(1)}, u32[]{:S(2)}, u32[]{:S(2)}) %collective-permute-start.42) | collective-permute-done | bytes 114720 | tf_op jit(solution)/shard_map/ppermute | solution.py:601
  24.0 0.0 collective-permute-done.46.refs_11_
  24.1 0.5 collective-permute-start.45
  24.6 0.0 collective-permute-done.47.refs_12_
  24.6 2.1 %collective-permute-done.39.refs_0_ = bf16[7,64,128]{2,1,0:T(8,128)(2,1)S(1)} collective-permute-done((bf16[7,64,128]{2,1,0:T(8,128)(2,1)S(1)}, bf16[7,64,128]{2,1,0:T(8,128)(2,1)S(1)}, u32[]{:S(2)}, u32[]{:S(2)}) %collective-permute-start.39) | collective-permute-done | bytes 114720 | tf_op jit(solution)/shard_map/ppermute | solution.py:604
  26.7 0.0 collective-permute-done.43.refs_8_
  26.7 0.0 collective-permute-done.44.refs_9_
  26.7 0.0 collective-permute-done.45.refs_10_
  26.7 7.5 %compute.3 = (bf16[56,64,128]{2,1,0:T(8,128)(2,1)S(1)}, bf16[14,64,128]{2,1,0:T(8,128)(2,1)S(1)}, bf16[42,64,128]{2,1,0:T(8,128)(2,1)S(1)}, bf16[17,128,128]{2,1,0:T(8,128)(2,1)S(1)}, bf16[17,128,128]{2,1,0:T(8,128)(2,1)S(1)}) custom-call(s32[32,128]{1,0:T(8,128)S(1)} %get-tuple-element.74.plan, bf16[128,8192]{1,0:T(8,128)(2,1)} %tokens.1, ...), custom_call_target="tpu_custom_call" | custom-call | flops 1000000000 | bytes 20000000 | tf_op jit(solution)/shard_map/compute/pallas_call | solution.py:532
  34.2 1.1 %collective-permute-start.52 = (bf16[14,64,128]{2,1,0:T(8,128)(2,1)S(1)}, bf16[14,64,128]{2,1,0:T(8,128)(2,1)S(1)}, u32[]{:S(2)}, u32[]{:S(2)}) collective-permute-start(bf16[14,64,128]{2,1,0:T(8,128)(2,1)S(1)} %get-tuple-element.80), channel_id=1, source_target_pairs={{0,2},{2,0},{8,10},{10,8},{16,18},{18,16},{24,26},{26,24},{28,30},... | collective-permute-start | bytes 688136 | tf_op jit(solution)/shard_map/ppermute | solution.py:612
  35.3 1.1 %collective-permute-done.52.__1_ = bf16[14,64,128]{2,1,0:T(8,128)(2,1)S(1)} collective-permute-done((bf16[14,64,128]{2,1,0:T(8,128)(2,1)S(1)}, bf16[14,64,128]{2,1,0:T(8,128)(2,1)S(1)}, u32[]{:S(2)}, u32[]{:S(2)}) %collective-permute-start.52) | collective-permute-done | bytes 229408 | tf_op jit(solution)/shard_map/ppermute | solution.py:612
  36.4 0.4 collective-permute-start.53
  36.8 0.1 add_convert_fusion.14
  36.9 0.3 collective-permute-start.54
  37.2 1.7 %collective-permute-start.55 = (bf16[7,64,128]{2,1,0:T(8,128)(2,1)S(1)}, bf16[7,64,128]{2,1,0:T(8,128)(2,1)S(1)}, u32[]{:S(2)}, u32[]{:S(2)}) collective-permute-start(bf16[7,64,128]{2,1,0:T(8,128)(2,1)S(1)} %get-tuple-element.82), channel_id=1, source_target_pairs={{0,4},{2,10},{8,0},{10,18},{16,8},{18,26},{24,16},{26,30},{28,24},... | collective-permute-start | bytes 344072 | tf_op jit(solution)/shard_map/ppermute | solution.py:629
  39.0 0.6 collective-permute-start.35
  39.5 1.5 %collective-permute-start.51 = (bf16[17,128,128]{2,1,0:T(8,128)(2,1)S(1)}, bf16[17,128,128]{2,1,0:T(8,128)(2,1)S(1)}, u32[]{:S(2)}, u32[]{:S(2)}) collective-permute-start(bf16[17,128,128]{2,1,0:T(8,128)(2,1)S(1)} %get-tuple-element.77), channel_id=1, source_target_pairs={{0,1},{1,0},{2,3},{3,2},{4,5},{5,4},{6,7},{7,6},{8,9},{9,8},{10,11... | collective-permute-start | bytes 1671176 | tf_op jit(solution)/shard_map/ppermute | solution.py:653
  41.0 1.2 %collective-permute-done.54.__0_ = bf16[7,64,128]{2,1,0:T(8,128)(2,1)S(1)} collective-permute-done((bf16[7,64,128]{2,1,0:T(8,128)(2,1)S(1)}, bf16[7,64,128]{2,1,0:T(8,128)(2,1)S(1)}, u32[]{:S(2)}, u32[]{:S(2)}) %collective-permute-start.54) | collective-permute-done | bytes 114720 | tf_op jit(solution)/shard_map/ppermute | solution.py:629
  42.2 0.0 collective-permute-done.53
  42.2 0.1 add_convert_fusion.13.__1_
  42.2 1.5 %collective-permute-start.57 = (bf16[7,64,128]{2,1,0:T(8,128)(2,1)S(1)}, bf16[7,64,128]{2,1,0:T(8,128)(2,1)S(1)}, u32[]{:S(2)}, u32[]{:S(2)}) collective-permute-start(bf16[7,64,128]{2,1,0:T(8,128)(2,1)S(1)} %add_convert_fusion.13.__1_), channel_id=1, source_target_pairs={{0,8},{2,6},{8,16},{10,2},{16,24},{18,10},{24,28},{26,18},{28,20},... | collective-permute-start | bytes 344072 | tf_op jit(solution)/shard_map/ppermute | solution.py:629
  43.8 0.1 add_convert_fusion.12.__1_
  43.8 1.0 %collective-permute-start.56 = (bf16[7,64,128]{2,1,0:T(8,128)(2,1)S(1)}, bf16[7,64,128]{2,1,0:T(8,128)(2,1)S(1)}, u32[]{:S(2)}, u32[]{:S(2)}) collective-permute-start(bf16[7,64,128]{2,1,0:T(8,128)(2,1)S(1)} %add_convert_fusion.12.__1_), channel_id=1, source_target_pairs={{0,4},{2,10},{8,0},{10,18},{16,8},{18,26},{24,16},{26,30},{28,24},... | collective-permute-start | bytes 344072 | tf_op jit(solution)/shard_map/ppermute | solution.py:629
  44.8 0.0 collective-permute-done.35.__2_.note.refs_0_
  44.8 2.6 %collective-permute-done.57.__0_ = bf16[7,64,128]{2,1,0:T(8,128)(2,1)S(1)} collective-permute-done((bf16[7,64,128]{2,1,0:T(8,128)(2,1)S(1)}, bf16[7,64,128]{2,1,0:T(8,128)(2,1)S(1)}, u32[]{:S(2)}, u32[]{:S(2)}) %collective-permute-start.57) | collective-permute-done | bytes 114720 | tf_op jit(solution)/shard_map/ppermute | solution.py:629
  47.4 0.1 add_convert_fusion.9
  47.5 2.0 %collective-permute-start.61 = (bf16[7,64,128]{2,1,0:T(8,128)(2,1)S(1)}, bf16[7,64,128]{2,1,0:T(8,128)(2,1)S(1)}, u32[]{:S(2)}, u32[]{:S(2)}) collective-permute-start(bf16[7,64,128]{2,1,0:T(8,128)(2,1)S(1)} %get-tuple-element.110.__1_), channel_id=1, source_target_pairs={{0,8},{2,6},{8,16},{10,2},{16,24},{18,10},{24,28},{26,18},{28,20},... | collective-permute-start | bytes 344072 | tf_op jit(solution)/shard_map/ppermute | solution.py:629
  49.5 0.0 collective-permute-done.56.__0_
  49.5 0.1 add_convert_fusion.10.__1_
  49.6 1.0 %collective-permute-start.58 = (bf16[7,64,128]{2,1,0:T(8,128)(2,1)S(1)}, bf16[7,64,128]{2,1,0:T(8,128)(2,1)S(1)}, u32[]{:S(2)}, u32[]{:S(2)}) collective-permute-start(bf16[7,64,128]{2,1,0:T(8,128)(2,1)S(1)} %add_convert_fusion.10.__1_), channel_id=1, source_target_pairs={{0,4},{2,10},{8,0},{10,18},{16,8},{18,26},{24,16},{26,30},{28,24},... | collective-permute-start | bytes 344072 | tf_op jit(solution)/shard_map/ppermute | solution.py:629
  50.6 0.9 %collective-permute-start.59 = (bf16[7,64,128]{2,1,0:T(8,128)(2,1)S(1)}, bf16[7,64,128]{2,1,0:T(8,128)(2,1)S(1)}, u32[]{:S(2)}, u32[]{:S(2)}) collective-permute-start(bf16[7,64,128]{2,1,0:T(8,128)(2,1)S(1)} %add_convert_fusion.10.__1_), channel_id=1, source_target_pairs={{0,6},{2,8},{8,2},{10,16},{16,10},{18,24},{24,18},{26,28},{28,26},... | collective-permute-start | bytes 344072 | tf_op jit(solution)/shard_map/ppermute | solution.py:641
  51.5 0.0 collective-permute-done.60.__1_.refs_3_
  51.5 2.6 %prepare.3 = (bf16[128,4096]{1,0:T(8,128)(2,1)}, bf16[128,4096]{1,0:T(8,128)(2,1)}, bf16[17,128,128]{2,1,0:T(8,128)(2,1)S(1)}) custom-call(s32[32,128]{1,0:T(8,128)S(1)} %get-tuple-element.74.plan, s32[1,128]{1,0:T(1,128)S(1)} %collective-permute-done.35.__2_.note.refs_0_, bf16[17,128,128]{2,1,0:T(8,128)(2,1)S(1)} %turn.30.first), custom_call_target="tpu_custom_call" | custom-call | flops 1000000 | bytes 6000000 | tf_op jit(solution)/shard_map/prepare/pallas_call | solution.py:549
  54.1 0.1 add_convert_fusion.8
  54.2 1.3 %collective-permute-start.62 = (bf16[7,64,128]{2,1,0:T(8,128)(2,1)S(1)}, bf16[7,64,128]{2,1,0:T(8,128)(2,1)S(1)}, u32[]{:S(2)}, u32[]{:S(2)}) collective-permute-start(bf16[7,64,128]{2,1,0:T(8,128)(2,1)S(1)} %add_convert_fusion.8), channel_id=1, source_target_pairs={{0,8},{2,6},{8,16},{10,2},{16,24},{18,10},{24,28},{26,18},{28,20},... | collective-permute-start | bytes 344072 | tf_op jit(solution)/shard_map/ppermute | solution.py:637
  55.4 0.8 %collective-permute-start.63 = (bf16[7,64,128]{2,1,0:T(8,128)(2,1)S(1)}, bf16[7,64,128]{2,1,0:T(8,128)(2,1)S(1)}, u32[]{:S(2)}, u32[]{:S(2)}) collective-permute-start(bf16[7,64,128]{2,1,0:T(8,128)(2,1)S(1)} %add_convert_fusion.8), channel_id=1, source_target_pairs={{0,10},{2,4},{8,18},{10,0},{16,26},{18,8},{24,30},{26,16},{28,22},... | collective-permute-start | bytes 344072 | tf_op jit(solution)/shard_map/ppermute | solution.py:640
  56.3 0.0 copy-start.1
  56.3 0.0 copy-start.2
  56.3 2.3 %add.122 = (bf16[128,4096]{1,0:T(8,128)(2,1)}, bf16[128,4096]{1,0:T(8,128)(2,1)}, s32[1]{0:T(128)}) custom-call(s32[32,128]{1,0:T(8,128)S(1)} %get-tuple-element.74.plan, s32[1,128]{1,0:T(1,128)S(1)} %collective-permute-done.35.__2_.note.refs_0_, bf16[17,128,128]{2,1,0:T(8,128)(2,1)S(1)} %turn.29.refs_1_, ...), custom_call_target="tpu_custom_call", output_to_operand_aliasing={{0}: (4, {}), {1}: (5, {})} | custom-call | flops 1000000 | bytes 3000000 | tf_op jit(solution)/shard_map/add/pallas_call | solution.py:562
  59.3 0.6 %collective-permute-done.63.refs_4_ = bf16[7,64,128]{2,1,0:T(8,128)(2,1)S(1)} collective-permute-done((bf16[7,64,128]{2,1,0:T(8,128)(2,1)S(1)}, bf16[7,64,128]{2,1,0:T(8,128)(2,1)S(1)}, u32[]{:S(2)}, u32[]{:S(2)}) %collective-permute-start.63) | collective-permute-done | bytes 114720 | tf_op jit(solution)/shard_map/ppermute | solution.py:640
  59.9 1.5 %last.3 = (bf16[1,2,128,128]{3,2,1,0:T(8,128)(2,1)}, bf16[1,2,128,128]{3,2,1,0:T(8,128)(2,1)}, bf16[1,2,128,128]{3,2,1,0:T(8,128)(2,1)}) custom-call(s32[32,128]{1,0:T(8,128)S(1)} %get-tuple-element.74.plan, bf16[7,64,128]{2,1,0:T(8,128)(2,1)S(1)} %get-tuple-element.109.refs_0_, bf16[7,64,128]{2,1,0:T(8,128)(2,1)S(1)} %collective-permute-done.62.refs_1_, ...), custom_call_target="tpu_custom_call" | custom-call | flops 1000000 | bytes 1000000 | tf_op jit(solution)/shard_map/last/pallas_call | solution.py:581
  (28 shorter events, 0.1 us)
Async XLA Ops:
  0.6 1.8 %collective-permute-start.32 = (bf16[1,2,128,128]{3,2,1,0:T(8,128)(2,1)}, bf16[1,2,128,128]{3,2,1,0:T(8,128)(2,1)S(1)}, u32[]{:S(2)}, u32[]{:S(2)}) collective-permute-start(bf16[1,2,128,128]{3,2,1,0:T(8,128)(2,1)} %refs_0_.1), channel_id=1, source_target_pairs={{0,2},{2,0},{8,10},{10,8},{16,18},{18,16},{24,26},{26,24},{28,30},... | collective-permute-start | bytes 196616 | tf_op jit(solution)/shard_map/ppermute | solution.py:649
  1.2 1.5 %collective-permute-start.33 = (bf16[1,2,128,128]{3,2,1,0:T(8,128)(2,1)}, bf16[1,2,128,128]{3,2,1,0:T(8,128)(2,1)S(1)}, u32[]{:S(2)}, u32[]{:S(2)}) collective-permute-start(bf16[1,2,128,128]{3,2,1,0:T(8,128)(2,1)} %refs_1_.1), channel_id=1, source_target_pairs={{0,2},{2,0},{8,10},{10,8},{16,18},{18,16},{24,26},{26,24},{28,30},... | collective-permute-start | bytes 196616 | tf_op jit(solution)/shard_map/ppermute | solution.py:649
  1.2 1.5 %collective-permute-start.34 = (bf16[1,2,128,128]{3,2,1,0:T(8,128)(2,1)}, bf16[1,2,128,128]{3,2,1,0:T(8,128)(2,1)S(1)}, u32[]{:S(2)}, u32[]{:S(2)}) collective-permute-start(bf16[1,2,128,128]{3,2,1,0:T(8,128)(2,1)} %refs_2_.1), channel_id=1, source_target_pairs={{0,2},{2,0},{8,10},{10,8},{16,18},{18,16},{24,26},{26,24},{28,30},... | collective-permute-start | bytes 196616 | tf_op jit(solution)/shard_map/ppermute | solution.py:649
  4.1 6.0 %collective-permute-start.36 = (bf16[7,64,128]{2,1,0:T(8,128)(2,1)S(1)}, bf16[7,64,128]{2,1,0:T(8,128)(2,1)S(1)}, u32[]{:S(2)}, u32[]{:S(2)}) collective-permute-start(bf16[7,64,128]{2,1,0:T(8,128)(2,1)S(1)} %get-tuple-element.76.refs_7_), channel_id=1, source_target_pairs={{0,8},{2,6},{8,16},{10,2},{16,24},{18,10},{24,28},{26,18},{28,20},... | collective-permute-start | bytes 344072 | tf_op jit(solution)/shard_map/ppermute | solution.py:601
  7.1 5.3 %collective-permute-start.40 = (bf16[7,64,128]{2,1,0:T(8,128)(2,1)S(1)}, bf16[7,64,128]{2,1,0:T(8,128)(2,1)S(1)}, u32[]{:S(2)}, u32[]{:S(2)}) collective-permute-start(bf16[7,64,128]{2,1,0:T(8,128)(2,1)S(1)} %get-tuple-element.76.refs_7_), channel_id=1, source_target_pairs={{0,4},{2,10},{8,0},{10,18},{16,8},{18,26},{24,16},{26,30},{28,24},... | collective-permute-start | bytes 344072 | tf_op jit(solution)/shard_map/ppermute | solution.py:601
  10.1 6.1 %collective-permute-start.37 = (bf16[7,64,128]{2,1,0:T(8,128)(2,1)S(1)}, bf16[7,64,128]{2,1,0:T(8,128)(2,1)S(1)}, u32[]{:S(2)}, u32[]{:S(2)}) collective-permute-start(bf16[7,64,128]{2,1,0:T(8,128)(2,1)S(1)} %collective-permute-done.36.refs_5_), channel_id=1, source_target_pairs={{0,8},{2,6},{8,16},{10,2},{16,24},{18,10},{24,28},{26,18},{28,20},... | collective-permute-start | bytes 344072 | tf_op jit(solution)/shard_map/ppermute | solution.py:601
  12.3 6.0 %collective-permute-start.41 = (bf16[7,64,128]{2,1,0:T(8,128)(2,1)S(1)}, bf16[7,64,128]{2,1,0:T(8,128)(2,1)S(1)}, u32[]{:S(2)}, u32[]{:S(2)}) collective-permute-start(bf16[7,64,128]{2,1,0:T(8,128)(2,1)S(1)} %collective-permute-done.40.refs_6_), channel_id=1, source_target_pairs={{0,4},{2,10},{8,0},{10,18},{16,8},{18,26},{24,16},{26,30},{28,24},... | collective-permute-start | bytes 344072 | tf_op jit(solution)/shard_map/ppermute | solution.py:601
  12.7 5.6 %collective-permute-start.50 = (bf16[7,64,128]{2,1,0:T(8,128)(2,1)S(1)}, bf16[7,64,128]{2,1,0:T(8,128)(2,1)S(1)}, u32[]{:S(2)}, u32[]{:S(2)}) collective-permute-start(bf16[7,64,128]{2,1,0:T(8,128)(2,1)S(1)} %get-tuple-element.76.refs_7_), channel_id=1, source_target_pairs={{0,2},{2,0},{8,10},{10,8},{16,18},{18,16},{24,26},{26,24},{28,30},... | collective-permute-start | bytes 344072 | tf_op jit(solution)/shard_map/ppermute | solution.py:603
  12.7 6.3 %collective-permute-start.48 = (bf16[7,64,128]{2,1,0:T(8,128)(2,1)S(1)}, bf16[7,64,128]{2,1,0:T(8,128)(2,1)S(1)}, u32[]{:S(2)}, u32[]{:S(2)}) collective-permute-start(bf16[7,64,128]{2,1,0:T(8,128)(2,1)S(1)} %collective-permute-done.36.refs_5_), channel_id=1, source_target_pairs={{0,2},{2,0},{8,10},{10,8},{16,18},{18,16},{24,26},{26,24},{28,30},... | collective-permute-start | bytes 344072 | tf_op jit(solution)/shard_map/ppermute | solution.py:603
  16.2 5.7 %collective-permute-start.38 = (bf16[7,64,128]{2,1,0:T(8,128)(2,1)S(1)}, bf16[7,64,128]{2,1,0:T(8,128)(2,1)S(1)}, u32[]{:S(2)}, u32[]{:S(2)}) collective-permute-start(bf16[7,64,128]{2,1,0:T(8,128)(2,1)S(1)} %collective-permute-done.37.refs_3_), channel_id=1, source_target_pairs={{0,8},{2,6},{8,16},{10,2},{16,24},{18,10},{24,28},{26,18},{28,20},... | collective-permute-start | bytes 344072 | tf_op jit(solution)/shard_map/ppermute | solution.py:601
  17.1 4.8 %collective-permute-start.49 = (bf16[7,64,128]{2,1,0:T(8,128)(2,1)S(1)}, bf16[7,64,128]{2,1,0:T(8,128)(2,1)S(1)}, u32[]{:S(2)}, u32[]{:S(2)}) collective-permute-start(bf16[7,64,128]{2,1,0:T(8,128)(2,1)S(1)} %collective-permute-done.40.refs_6_), channel_id=1, source_target_pairs={{0,2},{2,0},{8,10},{10,8},{16,18},{18,16},{24,26},{26,24},{28,30},... | collective-permute-start | bytes 344072 | tf_op jit(solution)/shard_map/ppermute | solution.py:603
  18.3 5.7 %collective-permute-start.42 = (bf16[7,64,128]{2,1,0:T(8,128)(2,1)S(1)}, bf16[7,64,128]{2,1,0:T(8,128)(2,1)S(1)}, u32[]{:S(2)}, u32[]{:S(2)}) collective-permute-start(bf16[7,64,128]{2,1,0:T(8,128)(2,1)S(1)} %collective-permute-done.41.refs_4_), channel_id=1, source_target_pairs={{0,4},{2,10},{8,0},{10,18},{16,8},{18,26},{24,16},{26,30},{28,24},... | collective-permute-start | bytes 344072 | tf_op jit(solution)/shard_map/ppermute | solution.py:601
  18.3 5.7 %collective-permute-start.46 = (bf16[7,64,128]{2,1,0:T(8,128)(2,1)S(1)}, bf16[7,64,128]{2,1,0:T(8,128)(2,1)S(1)}, u32[]{:S(2)}, u32[]{:S(2)}) collective-permute-start(bf16[7,64,128]{2,1,0:T(8,128)(2,1)S(1)} %collective-permute-done.37.refs_3_), channel_id=1, source_target_pairs={{0,2},{2,0},{8,10},{10,8},{16,18},{18,16},{24,26},{26,24},{28,30},... | collective-permute-start | bytes 344072 | tf_op jit(solution)/shard_map/ppermute | solution.py:603
  19.1 5.5 %collective-permute-start.47 = (bf16[7,64,128]{2,1,0:T(8,128)(2,1)S(1)}, bf16[7,64,128]{2,1,0:T(8,128)(2,1)S(1)}, u32[]{:S(2)}, u32[]{:S(2)}) collective-permute-start(bf16[7,64,128]{2,1,0:T(8,128)(2,1)S(1)} %collective-permute-done.41.refs_4_), channel_id=1, source_target_pairs={{0,2},{2,0},{8,10},{10,8},{16,18},{18,16},{24,26},{26,24},{28,30},... | collective-permute-start | bytes 344072 | tf_op jit(solution)/shard_map/ppermute | solution.py:603
  21.9 4.8 %collective-permute-start.39 = (bf16[7,64,128]{2,1,0:T(8,128)(2,1)S(1)}, bf16[7,64,128]{2,1,0:T(8,128)(2,1)S(1)}, u32[]{:S(2)}, u32[]{:S(2)}) collective-permute-start(bf16[7,64,128]{2,1,0:T(8,128)(2,1)S(1)} %collective-permute-done.38.refs_1_), channel_id=1, source_target_pairs={{0,8},{2,6},{8,16},{10,2},{16,24},{18,10},{24,28},{26,18},{28,20},... | collective-permute-start | bytes 344072 | tf_op jit(solution)/shard_map/ppermute | solution.py:604
  21.9 4.8 %collective-permute-start.43 = (bf16[7,64,128]{2,1,0:T(8,128)(2,1)S(1)}, bf16[7,64,128]{2,1,0:T(8,128)(2,1)S(1)}, u32[]{:S(2)}, u32[]{:S(2)}) collective-permute-start(bf16[7,64,128]{2,1,0:T(8,128)(2,1)S(1)} %collective-permute-done.38.refs_1_), channel_id=1, source_target_pairs={{0,10},{2,4},{8,18},{10,0},{16,26},{18,8},{24,30},{26,16},{28,22},... | collective-permute-start | bytes 344072 | tf_op jit(solution)/shard_map/ppermute | solution.py:605
  24.0 2.6 %collective-permute-start.44 = (bf16[7,64,128]{2,1,0:T(8,128)(2,1)S(1)}, bf16[7,64,128]{2,1,0:T(8,128)(2,1)S(1)}, u32[]{:S(2)}, u32[]{:S(2)}) collective-permute-start(bf16[7,64,128]{2,1,0:T(8,128)(2,1)S(1)} %collective-permute-done.38.refs_1_), channel_id=1, source_target_pairs={{0,2},{2,0},{8,10},{10,8},{16,18},{18,16},{24,26},{26,24},{28,30},... | collective-permute-start | bytes 344072 | tf_op jit(solution)/shard_map/ppermute | solution.py:603
  24.1 2.6 %collective-permute-start.45 = (bf16[7,64,128]{2,1,0:T(8,128)(2,1)S(1)}, bf16[7,64,128]{2,1,0:T(8,128)(2,1)S(1)}, u32[]{:S(2)}, u32[]{:S(2)}) collective-permute-start(bf16[7,64,128]{2,1,0:T(8,128)(2,1)S(1)} %collective-permute-done.42.refs_2_), channel_id=1, source_target_pairs={{0,2},{2,0},{8,10},{10,8},{16,18},{18,16},{24,26},{26,24},{28,30},... | collective-permute-start | bytes 344072 | tf_op jit(solution)/shard_map/ppermute | solution.py:603
  34.2 2.2 %collective-permute-start.52 = (bf16[14,64,128]{2,1,0:T(8,128)(2,1)S(1)}, bf16[14,64,128]{2,1,0:T(8,128)(2,1)S(1)}, u32[]{:S(2)}, u32[]{:S(2)}) collective-permute-start(bf16[14,64,128]{2,1,0:T(8,128)(2,1)S(1)} %get-tuple-element.80), channel_id=1, source_target_pairs={{0,2},{2,0},{8,10},{10,8},{16,18},{18,16},{24,26},{26,24},{28,30},... | collective-permute-start | bytes 688136 | tf_op jit(solution)/shard_map/ppermute | solution.py:612
  36.4 5.7 %collective-permute-start.53 = (bf16[42,64,128]{2,1,0:T(8,128)(2,1)S(1)}, bf16[42,64,128]{2,1,0:T(8,128)(2,1)S(1)}, u32[]{:S(2)}, u32[]{:S(2)}) collective-permute-start(bf16[42,64,128]{2,1,0:T(8,128)(2,1)S(1)} %turn.24), channel_id=1, source_target_pairs={{0,2},{2,0},{8,10},{10,8},{16,18},{18,16},{24,26},{26,24},{28,30},... | collective-permute-start | bytes 2064392 | tf_op jit(solution)/shard_map/ppermute | solution.py:613
  36.9 5.3 %collective-permute-start.54 = (bf16[7,64,128]{2,1,0:T(8,128)(2,1)S(1)}, bf16[7,64,128]{2,1,0:T(8,128)(2,1)S(1)}, u32[]{:S(2)}, u32[]{:S(2)}) collective-permute-start(bf16[7,64,128]{2,1,0:T(8,128)(2,1)S(1)} %get-tuple-element.81), channel_id=1, source_target_pairs={{0,8},{2,6},{8,16},{10,2},{16,24},{18,10},{24,28},{26,18},{28,20},... | collective-permute-start | bytes 344072 | tf_op jit(solution)/shard_map/ppermute | solution.py:629
  37.2 4.9 %collective-permute-start.55 = (bf16[7,64,128]{2,1,0:T(8,128)(2,1)S(1)}, bf16[7,64,128]{2,1,0:T(8,128)(2,1)S(1)}, u32[]{:S(2)}, u32[]{:S(2)}) collective-permute-start(bf16[7,64,128]{2,1,0:T(8,128)(2,1)S(1)} %get-tuple-element.82), channel_id=1, source_target_pairs={{0,4},{2,10},{8,0},{10,18},{16,8},{18,26},{24,16},{26,30},{28,24},... | collective-permute-start | bytes 344072 | tf_op jit(solution)/shard_map/ppermute | solution.py:629
  39.0 5.8 %collective-permute-start.35 = (s32[1,128]{1,0:T(1,128)S(1)}, s32[1,128]{1,0:T(1,128)S(1)}, u32[]{:S(2)}, u32[]{:S(2)}) collective-permute-start(s32[1,128]{1,0:T(1,128)S(1)} %get-tuple-element.75), channel_id=1, source_target_pairs={{0,1},{1,0},{2,3},{3,2},{4,5},{5,4},{6,7},{7,6},{8,9},{9,8},{10,11... | collective-permute-start | bytes 1544 | tf_op jit(solution)/shard_map/ppermute | solution.py:653
  39.5 14.6 %collective-permute-start.51 = (bf16[17,128,128]{2,1,0:T(8,128)(2,1)S(1)}, bf16[17,128,128]{2,1,0:T(8,128)(2,1)S(1)}, u32[]{:S(2)}, u32[]{:S(2)}) collective-permute-start(bf16[17,128,128]{2,1,0:T(8,128)(2,1)S(1)} %get-tuple-element.77), channel_id=1, source_target_pairs={{0,1},{1,0},{2,3},{3,2},{4,5},{5,4},{6,7},{7,6},{8,9},{9,8},{10,11... | collective-permute-start | bytes 1671176 | tf_op jit(solution)/shard_map/ppermute | solution.py:653
  42.2 5.2 %collective-permute-start.57 = (bf16[7,64,128]{2,1,0:T(8,128)(2,1)S(1)}, bf16[7,64,128]{2,1,0:T(8,128)(2,1)S(1)}, u32[]{:S(2)}, u32[]{:S(2)}) collective-permute-start(bf16[7,64,128]{2,1,0:T(8,128)(2,1)S(1)} %add_convert_fusion.13.__1_), channel_id=1, source_target_pairs={{0,8},{2,6},{8,16},{10,2},{16,24},{18,10},{24,28},{26,18},{28,20},... | collective-permute-start | bytes 344072 | tf_op jit(solution)/shard_map/ppermute | solution.py:629
  43.8 5.7 %collective-permute-start.56 = (bf16[7,64,128]{2,1,0:T(8,128)(2,1)S(1)}, bf16[7,64,128]{2,1,0:T(8,128)(2,1)S(1)}, u32[]{:S(2)}, u32[]{:S(2)}) collective-permute-start(bf16[7,64,128]{2,1,0:T(8,128)(2,1)S(1)} %add_convert_fusion.12.__1_), channel_id=1, source_target_pairs={{0,4},{2,10},{8,0},{10,18},{16,8},{18,26},{24,16},{26,30},{28,24},... | collective-permute-start | bytes 344072 | tf_op jit(solution)/shard_map/ppermute | solution.py:629
  47.5 6.6 %collective-permute-start.61 = (bf16[7,64,128]{2,1,0:T(8,128)(2,1)S(1)}, bf16[7,64,128]{2,1,0:T(8,128)(2,1)S(1)}, u32[]{:S(2)}, u32[]{:S(2)}) collective-permute-start(bf16[7,64,128]{2,1,0:T(8,128)(2,1)S(1)} %get-tuple-element.110.__1_), channel_id=1, source_target_pairs={{0,8},{2,6},{8,16},{10,2},{16,24},{18,10},{24,28},{26,18},{28,20},... | collective-permute-start | bytes 344072 | tf_op jit(solution)/shard_map/ppermute | solution.py:629
  49.5 2.0 %collective-permute-start.60 = (bf16[7,64,128]{2,1,0:T(8,128)(2,1)S(1)}, bf16[7,64,128]{2,1,0:T(8,128)(2,1)S(1)}, u32[]{:S(2)}, u32[]{:S(2)}) collective-permute-start(bf16[7,64,128]{2,1,0:T(8,128)(2,1)S(1)} %get-tuple-element.109.refs_0_), channel_id=1, source_target_pairs={{0,2},{2,0},{8,10},{10,8},{16,18},{18,16},{24,26},{26,24},{28,30},... | collective-permute-start | bytes 344072 | tf_op jit(solution)/shard_map/ppermute | solution.py:625
  49.6 6.7 %collective-permute-start.58 = (bf16[7,64,128]{2,1,0:T(8,128)(2,1)S(1)}, bf16[7,64,128]{2,1,0:T(8,128)(2,1)S(1)}, u32[]{:S(2)}, u32[]{:S(2)}) collective-permute-start(bf16[7,64,128]{2,1,0:T(8,128)(2,1)S(1)} %add_convert_fusion.10.__1_), channel_id=1, source_target_pairs={{0,4},{2,10},{8,0},{10,18},{16,8},{18,26},{24,16},{26,30},{28,24},... | collective-permute-start | bytes 344072 | tf_op jit(solution)/shard_map/ppermute | solution.py:629
  50.6 5.7 %collective-permute-start.59 = (bf16[7,64,128]{2,1,0:T(8,128)(2,1)S(1)}, bf16[7,64,128]{2,1,0:T(8,128)(2,1)S(1)}, u32[]{:S(2)}, u32[]{:S(2)}) collective-permute-start(bf16[7,64,128]{2,1,0:T(8,128)(2,1)S(1)} %add_convert_fusion.10.__1_), channel_id=1, source_target_pairs={{0,6},{2,8},{8,2},{10,16},{16,10},{18,24},{24,18},{26,28},{28,26},... | collective-permute-start | bytes 344072 | tf_op jit(solution)/shard_map/ppermute | solution.py:641
  54.2 5.1 %collective-permute-start.62 = (bf16[7,64,128]{2,1,0:T(8,128)(2,1)S(1)}, bf16[7,64,128]{2,1,0:T(8,128)(2,1)S(1)}, u32[]{:S(2)}, u32[]{:S(2)}) collective-permute-start(bf16[7,64,128]{2,1,0:T(8,128)(2,1)S(1)} %add_convert_fusion.8), channel_id=1, source_target_pairs={{0,8},{2,6},{8,16},{10,2},{16,24},{18,10},{24,28},{26,18},{28,20},... | collective-permute-start | bytes 344072 | tf_op jit(solution)/shard_map/ppermute | solution.py:637
  55.4 4.4 %collective-permute-start.63 = (bf16[7,64,128]{2,1,0:T(8,128)(2,1)S(1)}, bf16[7,64,128]{2,1,0:T(8,128)(2,1)S(1)}, u32[]{:S(2)}, u32[]{:S(2)}) collective-permute-start(bf16[7,64,128]{2,1,0:T(8,128)(2,1)S(1)} %add_convert_fusion.8), channel_id=1, source_target_pairs={{0,10},{2,4},{8,18},{10,0},{16,26},{18,8},{24,30},{26,16},{28,22},... | collective-permute-start | bytes 344072 | tf_op jit(solution)/shard_map/ppermute | solution.py:640
  56.3 5.2 %copy-start = (bf16[1,2,128,128]{3,2,1,0:T(8,128)(2,1)S(1)}, bf16[1,2,128,128]{3,2,1,0:T(8,128)(2,1)}, u32[]{:S(2)}) copy-start(bf16[1,2,128,128]{3,2,1,0:T(8,128)(2,1)} %refs_0_.1) | copy-start | bytes 196612
  56.3 5.2 %copy-start.1 = (bf16[1,2,128,128]{3,2,1,0:T(8,128)(2,1)S(1)}, bf16[1,2,128,128]{3,2,1,0:T(8,128)(2,1)}, u32[]{:S(2)}) copy-start(bf16[1,2,128,128]{3,2,1,0:T(8,128)(2,1)} %refs_1_.1) | copy-start | bytes 196612
  56.3 5.2 %copy-start.2 = (bf16[1,2,128,128]{3,2,1,0:T(8,128)(2,1)S(1)}, bf16[1,2,128,128]{3,2,1,0:T(8,128)(2,1)}, u32[]{:S(2)}) copy-start(bf16[1,2,128,128]{3,2,1,0:T(8,128)(2,1)} %refs_2_.1) | copy-start | bytes 196612

commit v9 on v8

--- a/solution.py
+++ b/solution.py
@@ -11,7 +11,7 @@
 BLK = 128
 GROUP = 8
 COLUMNS = 4
-FIRST_SEND = 17
+FIRST_SEND = 16
 LEAN_SLOTS = 7
 ROWS = BLK // 2
 SMALL = 4 * 1024 * 1024
@@ -630,7 +630,7 @@
         if s == 1:
             a, b = call_turn([a, b], [])
         else:
-            a = call_turn([a], [last_b] + (notes if s == 2 else sent + list(prepared[2:])))[0]
+            a = call_turn([a], [last_b] + (notes + list(prepared[2:]) if s == 2 else sent))[0]
         a = term(sz.top - s, a)
         if s + 1 < sz.top:
             b = term(sz.top + 1 + s, call_turn([b], [a])[0])

time: 61.8 us -> 62 us (level)
  the two profiles are of different devices: /device:TPU:0 before, /device:TPU:3 now
where the time goes in v9:
time: 62 us; the launch traced here: 61.5 us
  starting transfers between devices  32.1 us (52%)
  Pallas kernels  13.9 us (22%)
  waiting for transfers between devices  13 us (21%)
  between operations  1.42 us (2%)
  local copies, waits for them, and re-layouts  0.8 us (1%)
    pallas_call x1, Pallas kernels, call_compute(): pl.pallas_call(functools.partial(compute_kernel, sz), out_shape=out_shape...  7.29 us
    ppermute x6, starting transfers between devices, gather_chunks(): a, b = (lax.ppermute(a, 'fsdp', ahead), lax.ppermute(b, 'fsdp', behind))  5.85 us
    ppermute x7, starting transfers between devices, gather_chunks(): other = {d: lax.ppermute(same[d], 'fsdp', swap) for d in same}  5.83 us
    ppermute x6, starting transfers between devices, reduce_parts(): a, b = (lax.ppermute(a, 'fsdp', ahead), lax.ppermute(b, 'fsdp', behind))  5.62 us
    ppermute x1, starting transfers between devices, gather_chunks(): other[sz.top] = lax.ppermute(a, 'fsdp', across(ahead))  4.46 us
    ppermute x1, starting transfers between devices, reduce_parts(): lax.ppermute(a, 'fsdp', across(ahead))  3.67 us
    ppermute x6, waiting for transfers between devices, reduce_parts(): a, b = (lax.ppermute(a, 'fsdp', ahead), lax.ppermute(b, 'fsdp', behind))  3.42 us
    ppermute x6, waiting for transfers between devices, gather_chunks(): a, b = (lax.ppermute(a, 'fsdp', ahead), lax.ppermute(b, 'fsdp', behind))  3.21 us
  transfers between devices with their start and end apart: 32, of which 10 were waited for; matrix products, arithmetic and copies ran while one was open for 2% of the time, Pallas kernels for 7%

profile of v9, /device:TPU:3, one launch (start us, length us, event | category | flops | bytes accessed | tf_op | source)
XLA Modules:
  0.0 61.5 jit_solution(3178044531056527952)
XLA Ops:
  0.6 0.7 %collective-permute-start.32 = (bf16[1,2,128,128]{3,2,1,0:T(8,128)(2,1)}, bf16[1,2,128,128]{3,2,1,0:T(8,128)(2,1)S(1)}, u32[]{:S(2)}, u32[]{:S(2)}) collective-permute-start(bf16[1,2,128,128]{3,2,1,0:T(8,128)(2,1)} %refs_0_.1), channel_id=1, source_target_pairs={{0,2},{2,0},{8,10},{10,8},{16,18},{18,16},{24,26},{26,24},{28,30},... | collective-permute-start | bytes 196616 | tf_op jit(solution)/shard_map/ppermute | solution.py:649
  1.4 0.1 collective-permute-start.33
  1.5 0.4 collective-permute-start.34
  1.9 0.8 %concatenate.3 = s32[101]{0:T(128)S(1)} concatenate(s32[32]{0:T(128)} %bitcast.9, s32[32]{0:T(128)} %bitcast.10, s32[32]{0:T(128)} %bitcast.11, s32[3]{0:T(128)} %bitcast.12, s32[1]{0:T(128)} %bitcast.4, s32[1]{0:T(128)} %bitcast.5), dimensions={0} | concatenate | bytes 808 | tf_op jit(solution)/shard_map/concatenate | solution.py:684
  2.7 0.0 collective-permute-done.32.refs_3_
  2.7 0.2 collective-permute-done.33.refs_4_
  2.8 0.2 collective-permute-done.34.refs_5_
  3.0 0.9 %plan.3 = (s32[32,128]{1,0:T(8,128)S(1)}, bf16[7,64,128]{2,1,0:T(8,128)(2,1)S(1)}, s32[1,128]{1,0:T(1,128)S(1)}) custom-call(s32[1,128]{1,0:T(1,128)S(1)} %pad_bitcast_fusion.own, bf16[1,2,128,128]{3,2,1,0:T(8,128)(2,1)} %refs_0_.1, bf16[1,2,128,128]{3,2,1,0:T(8,128)(2,1)} %refs_1_.1, bf16[1,2,128,128]{3,2,1,0:T(8,128)(2,1)} %refs_2_.1, ...), custom_call_target="tpu_custom_call" | custom-call | flops 1000000 | bytes 4000000 | tf_op jit(solution)/shard_map/plan/pallas_call | solution.py:476
  3.9 1.7 %collective-permute-start.36 = (bf16[7,64,128]{2,1,0:T(8,128)(2,1)S(1)}, bf16[7,64,128]{2,1,0:T(8,128)(2,1)S(1)}, u32[]{:S(2)}, u32[]{:S(2)}) collective-permute-start(bf16[7,64,128]{2,1,0:T(8,128)(2,1)S(1)} %get-tuple-element.76.refs_7_), channel_id=1, source_target_pairs={{0,8},{2,6},{8,16},{10,2},{16,24},{18,10},{24,28},{26,18},{28,20},... | collective-permute-start | bytes 344072 | tf_op jit(solution)/shard_map/ppermute | solution.py:601
  5.6 0.1 collective-permute-start.40
  5.7 2.4 %collective-permute-done.36.refs_5_ = bf16[7,64,128]{2,1,0:T(8,128)(2,1)S(1)} collective-permute-done((bf16[7,64,128]{2,1,0:T(8,128)(2,1)S(1)}, bf16[7,64,128]{2,1,0:T(8,128)(2,1)S(1)}, u32[]{:S(2)}, u32[]{:S(2)}) %collective-permute-start.36) | collective-permute-done | bytes 114720 | tf_op jit(solution)/shard_map/ppermute | solution.py:601
  8.1 1.4 %collective-permute-start.37 = (bf16[7,64,128]{2,1,0:T(8,128)(2,1)S(1)}, bf16[7,64,128]{2,1,0:T(8,128)(2,1)S(1)}, u32[]{:S(2)}, u32[]{:S(2)}) collective-permute-start(bf16[7,64,128]{2,1,0:T(8,128)(2,1)S(1)} %collective-permute-done.36.refs_5_), channel_id=1, source_target_pairs={{0,8},{2,6},{8,16},{10,2},{16,24},{18,10},{24,28},{26,18},{28,20},... | collective-permute-start | bytes 344072 | tf_op jit(solution)/shard_map/ppermute | solution.py:601
  9.5 0.8 %collective-permute-done.40.refs_6_ = bf16[7,64,128]{2,1,0:T(8,128)(2,1)S(1)} collective-permute-done((bf16[7,64,128]{2,1,0:T(8,128)(2,1)S(1)}, bf16[7,64,128]{2,1,0:T(8,128)(2,1)S(1)}, u32[]{:S(2)}, u32[]{:S(2)}) %collective-permute-start.40) | collective-permute-done | bytes 114720 | tf_op jit(solution)/shard_map/ppermute | solution.py:601
  10.3 2.1 %collective-permute-start.50 = (bf16[7,64,128]{2,1,0:T(8,128)(2,1)S(1)}, bf16[7,64,128]{2,1,0:T(8,128)(2,1)S(1)}, u32[]{:S(2)}, u32[]{:S(2)}) collective-permute-start(bf16[7,64,128]{2,1,0:T(8,128)(2,1)S(1)} %get-tuple-element.76.refs_7_), channel_id=1, source_target_pairs={{0,2},{2,0},{8,10},{10,8},{16,18},{18,16},{24,26},{26,24},{28,30},... | collective-permute-start | bytes 344072 | tf_op jit(solution)/shard_map/ppermute | solution.py:603
  12.4 1.2 %collective-permute-start.38 = (bf16[7,64,128]{2,1,0:T(8,128)(2,1)S(1)}, bf16[7,64,128]{2,1,0:T(8,128)(2,1)S(1)}, u32[]{:S(2)}, u32[]{:S(2)}) collective-permute-start(bf16[7,64,128]{2,1,0:T(8,128)(2,1)S(1)} %collective-permute-done.37.refs_3_), channel_id=1, source_target_pairs={{0,8},{2,6},{8,16},{10,2},{16,24},{18,10},{24,28},{26,18},{28,20},... | collective-permute-start | bytes 344072 | tf_op jit(solution)/shard_map/ppermute | solution.py:601
  13.6 2.7 %collective-permute-start.49 = (bf16[7,64,128]{2,1,0:T(8,128)(2,1)S(1)}, bf16[7,64,128]{2,1,0:T(8,128)(2,1)S(1)}, u32[]{:S(2)}, u32[]{:S(2)}) collective-permute-start(bf16[7,64,128]{2,1,0:T(8,128)(2,1)S(1)} %collective-permute-done.40.refs_6_), channel_id=1, source_target_pairs={{0,2},{2,0},{8,10},{10,8},{16,18},{18,16},{24,26},{26,24},{28,30},... | collective-permute-start | bytes 344072 | tf_op jit(solution)/shard_map/ppermute | solution.py:603
  16.4 1.4 %collective-permute-start.42 = (bf16[7,64,128]{2,1,0:T(8,128)(2,1)S(1)}, bf16[7,64,128]{2,1,0:T(8,128)(2,1)S(1)}, u32[]{:S(2)}, u32[]{:S(2)}) collective-permute-start(bf16[7,64,128]{2,1,0:T(8,128)(2,1)S(1)} %collective-permute-done.41.refs_4_), channel_id=1, source_target_pairs={{0,4},{2,10},{8,0},{10,18},{16,8},{18,26},{24,16},{26,30},{28,24},... | collective-permute-start | bytes 344072 | tf_op jit(solution)/shard_map/ppermute | solution.py:601
  17.8 0.0 collective-permute-done.50.refs_15_
  17.8 0.2 collective-permute-start.46
  17.9 0.4 collective-permute-start.47
  18.3 0.8 %collective-permute-start.39 = (bf16[7,64,128]{2,1,0:T(8,128)(2,1)S(1)}, bf16[7,64,128]{2,1,0:T(8,128)(2,1)S(1)}, u32[]{:S(2)}, u32[]{:S(2)}) collective-permute-start(bf16[7,64,128]{2,1,0:T(8,128)(2,1)S(1)} %collective-permute-done.38.refs_1_), channel_id=1, source_target_pairs={{0,8},{2,6},{8,16},{10,2},{16,24},{18,10},{24,28},{26,18},{28,20},... | collective-permute-start | bytes 344072 | tf_op jit(solution)/shard_map/ppermute | solution.py:604
  19.1 0.0 collective-permute-done.49.refs_14_
  19.1 4.5 %collective-permute-start.43 = (bf16[7,64,128]{2,1,0:T(8,128)(2,1)S(1)}, bf16[7,64,128]{2,1,0:T(8,128)(2,1)S(1)}, u32[]{:S(2)}, u32[]{:S(2)}) collective-permute-start(bf16[7,64,128]{2,1,0:T(8,128)(2,1)S(1)} %collective-permute-done.38.refs_1_), channel_id=1, source_target_pairs={{0,10},{2,4},{8,18},{10,0},{16,26},{18,8},{24,30},{26,16},{28,22},... | collective-permute-start | bytes 344072 | tf_op jit(solution)/shard_map/ppermute | solution.py:605
  23.5 0.0 collective-permute-done.42.refs_2_
  23.5 0.5 collective-permute-start.45
  24.1 0.0 collective-permute-done.47.refs_12_
  24.1 3.2 %collective-permute-done.43.refs_8_ = bf16[7,64,128]{2,1,0:T(8,128)(2,1)S(1)} collective-permute-done((bf16[7,64,128]{2,1,0:T(8,128)(2,1)S(1)}, bf16[7,64,128]{2,1,0:T(8,128)(2,1)S(1)}, u32[]{:S(2)}, u32[]{:S(2)}) %collective-permute-start.43) | collective-permute-done | bytes 114720 | tf_op jit(solution)/shard_map/ppermute | solution.py:605
  27.2 7.3 %compute.3 = (bf16[56,64,128]{2,1,0:T(8,128)(2,1)S(1)}, bf16[14,64,128]{2,1,0:T(8,128)(2,1)S(1)}, bf16[42,64,128]{2,1,0:T(8,128)(2,1)S(1)}, bf16[16,128,128]{2,1,0:T(8,128)(2,1)S(1)}, bf16[16,128,128]{2,1,0:T(8,128)(2,1)S(1)}) custom-call(s32[32,128]{1,0:T(8,128)S(1)} %get-tuple-element.74.plan, bf16[128,8192]{1,0:T(8,128)(2,1)} %tokens.1, ...), custom_call_target="tpu_custom_call" | custom-call | flops 1000000000 | bytes 20000000 | tf_op jit(solution)/shard_map/compute/pallas_call | solution.py:532
  34.5 0.1 collective-permute-start.52
  34.6 1.5 %collective-permute-done.52.__1_ = bf16[14,64,128]{2,1,0:T(8,128)(2,1)S(1)} collective-permute-done((bf16[14,64,128]{2,1,0:T(8,128)(2,1)S(1)}, bf16[14,64,128]{2,1,0:T(8,128)(2,1)S(1)}, u32[]{:S(2)}, u32[]{:S(2)}) %collective-permute-start.52) | collective-permute-done | bytes 229408 | tf_op jit(solution)/shard_map/ppermute | solution.py:612
  36.1 0.1 collective-permute-start.53
  36.2 0.1 add_convert_fusion.14
  36.3 0.7 %collective-permute-start.54 = (bf16[7,64,128]{2,1,0:T(8,128)(2,1)S(1)}, bf16[7,64,128]{2,1,0:T(8,128)(2,1)S(1)}, u32[]{:S(2)}, u32[]{:S(2)}) collective-permute-start(bf16[7,64,128]{2,1,0:T(8,128)(2,1)S(1)} %get-tuple-element.81), channel_id=1, source_target_pairs={{0,8},{2,6},{8,16},{10,2},{16,24},{18,10},{24,28},{26,18},{28,20},... | collective-permute-start | bytes 344072 | tf_op jit(solution)/shard_map/ppermute | solution.py:629
  37.0 0.8 %collective-permute-start.55 = (bf16[7,64,128]{2,1,0:T(8,128)(2,1)S(1)}, bf16[7,64,128]{2,1,0:T(8,128)(2,1)S(1)}, u32[]{:S(2)}, u32[]{:S(2)}) collective-permute-start(bf16[7,64,128]{2,1,0:T(8,128)(2,1)S(1)} %get-tuple-element.82), channel_id=1, source_target_pairs={{0,4},{2,10},{8,0},{10,18},{16,8},{18,26},{24,16},{26,30},{28,24},... | collective-permute-start | bytes 344072 | tf_op jit(solution)/shard_map/ppermute | solution.py:629
  37.8 0.0 collective-permute-start.35
  37.8 1.5 %collective-permute-start.51 = (bf16[16,128,128]{2,1,0:T(8,128)(2,1)S(1)}, bf16[16,128,128]{2,1,0:T(8,128)(2,1)S(1)}, u32[]{:S(2)}, u32[]{:S(2)}) collective-permute-start(bf16[16,128,128]{2,1,0:T(8,128)(2,1)S(1)} %get-tuple-element.77), channel_id=1, source_target_pairs={{0,1},{1,0},{2,3},{3,2},{4,5},{5,4},{6,7},{7,6},{8,9},{9,8},{10,11... | collective-permute-start | bytes 1572872 | tf_op jit(solution)/shard_map/ppermute | solution.py:653
  39.3 1.3 %collective-permute-done.54.__0_ = bf16[7,64,128]{2,1,0:T(8,128)(2,1)S(1)} collective-permute-done((bf16[7,64,128]{2,1,0:T(8,128)(2,1)S(1)}, bf16[7,64,128]{2,1,0:T(8,128)(2,1)S(1)}, u32[]{:S(2)}, u32[]{:S(2)}) %collective-permute-start.54) | collective-permute-done | bytes 114720 | tf_op jit(solution)/shard_map/ppermute | solution.py:629
  40.6 1.4 %collective-permute-done.55.__1_ = bf16[7,64,128]{2,1,0:T(8,128)(2,1)S(1)} collective-permute-done((bf16[7,64,128]{2,1,0:T(8,128)(2,1)S(1)}, bf16[7,64,128]{2,1,0:T(8,128)(2,1)S(1)}, u32[]{:S(2)}, u32[]{:S(2)}) %collective-permute-start.55) | collective-permute-done | bytes 114720 | tf_op jit(solution)/shard_map/ppermute | solution.py:629
  42.0 0.0 collective-permute-done.53
  42.0 0.1 add_convert_fusion.11
  42.1 1.1 %collective-permute-start.57 = (bf16[7,64,128]{2,1,0:T(8,128)(2,1)S(1)}, bf16[7,64,128]{2,1,0:T(8,128)(2,1)S(1)}, u32[]{:S(2)}, u32[]{:S(2)}) collective-permute-start(bf16[7,64,128]{2,1,0:T(8,128)(2,1)S(1)} %get-tuple-element.110.__1_), channel_id=1, source_target_pairs={{0,8},{2,6},{8,16},{10,2},{16,24},{18,10},{24,28},{26,18},{28,20},... | collective-permute-start | bytes 344072 | tf_op jit(solution)/shard_map/ppermute | solution.py:629
  43.1 0.0 collective-permute-start.58
  43.2 0.1 add_convert_fusion.12.__1_
  43.2 1.5 %collective-permute-start.56 = (bf16[7,64,128]{2,1,0:T(8,128)(2,1)S(1)}, bf16[7,64,128]{2,1,0:T(8,128)(2,1)S(1)}, u32[]{:S(2)}, u32[]{:S(2)}) collective-permute-start(bf16[7,64,128]{2,1,0:T(8,128)(2,1)S(1)} %add_convert_fusion.12.__1_), channel_id=1, source_target_pairs={{0,4},{2,10},{8,0},{10,18},{16,8},{18,26},{24,16},{26,30},{28,24},... | collective-permute-start | bytes 344072 | tf_op jit(solution)/shard_map/ppermute | solution.py:629
  44.7 0.0 collective-permute-done.35.note.__2_.refs_0_
  44.7 2.5 %prepare.3 = (bf16[128,4096]{1,0:T(8,128)(2,1)}, bf16[128,4096]{1,0:T(8,128)(2,1)}, bf16[16,128,128]{2,1,0:T(8,128)(2,1)S(1)}) custom-call(s32[32,128]{1,0:T(8,128)S(1)} %get-tuple-element.74.plan, s32[1,128]{1,0:T(1,128)S(1)} %collective-permute-done.35.note.__2_.refs_0_, bf16[16,128,128]{2,1,0:T(8,128)(2,1)S(1)} %turn.27.first), custom_call_target="tpu_custom_call" | custom-call | flops 1000000 | bytes 6000000 | tf_op jit(solution)/shard_map/prepare/pallas_call | solution.py:549
  47.2 0.0 collective-permute-done.57.__0_
  47.2 0.1 add_convert_fusion.10.__1_
  47.3 1.3 %collective-permute-start.61 = (bf16[7,64,128]{2,1,0:T(8,128)(2,1)S(1)}, bf16[7,64,128]{2,1,0:T(8,128)(2,1)S(1)}, u32[]{:S(2)}, u32[]{:S(2)}) collective-permute-start(bf16[7,64,128]{2,1,0:T(8,128)(2,1)S(1)} %add_convert_fusion.10.__1_), channel_id=1, source_target_pairs={{0,8},{2,6},{8,16},{10,2},{16,24},{18,10},{24,28},{26,18},{28,20},... | collective-permute-start | bytes 344072 | tf_op jit(solution)/shard_map/ppermute | solution.py:629
  48.5 0.0 collective-permute-done.56.__0_
  48.5 0.1 add_convert_fusion.9.__1_
  48.6 0.3 collective-permute-start.59
  48.9 1.7 %collective-permute-start.60 = (bf16[7,64,128]{2,1,0:T(8,128)(2,1)S(1)}, bf16[7,64,128]{2,1,0:T(8,128)(2,1)S(1)}, u32[]{:S(2)}, u32[]{:S(2)}) collective-permute-start(bf16[7,64,128]{2,1,0:T(8,128)(2,1)S(1)} %add_convert_fusion.9.__1_), channel_id=1, source_target_pairs={{0,6},{2,8},{8,2},{10,16},{16,10},{18,24},{24,18},{26,28},{28,26},... | collective-permute-start | bytes 344072 | tf_op jit(solution)/shard_map/ppermute | solution.py:641
  50.6 0.7 %collective-permute-done.61.__0_ = bf16[7,64,128]{2,1,0:T(8,128)(2,1)S(1)} collective-permute-done((bf16[7,64,128]{2,1,0:T(8,128)(2,1)S(1)}, bf16[7,64,128]{2,1,0:T(8,128)(2,1)S(1)}, u32[]{:S(2)}, u32[]{:S(2)}) %collective-permute-start.61) | collective-permute-done | bytes 114720 | tf_op jit(solution)/shard_map/ppermute | solution.py:629
  51.2 0.1 add_convert_fusion.8
  51.3 1.3 %collective-permute-start.62 = (bf16[7,64,128]{2,1,0:T(8,128)(2,1)S(1)}, bf16[7,64,128]{2,1,0:T(8,128)(2,1)S(1)}, u32[]{:S(2)}, u32[]{:S(2)}) collective-permute-start(bf16[7,64,128]{2,1,0:T(8,128)(2,1)S(1)} %add_convert_fusion.8), channel_id=1, source_target_pairs={{0,8},{2,6},{8,16},{10,2},{16,24},{18,10},{24,28},{26,18},{28,20},... | collective-permute-start | bytes 344072 | tf_op jit(solution)/shard_map/ppermute | solution.py:637
  52.6 3.7 %collective-permute-start.63 = (bf16[7,64,128]{2,1,0:T(8,128)(2,1)S(1)}, bf16[7,64,128]{2,1,0:T(8,128)(2,1)S(1)}, u32[]{:S(2)}, u32[]{:S(2)}) collective-permute-start(bf16[7,64,128]{2,1,0:T(8,128)(2,1)S(1)} %add_convert_fusion.8), channel_id=1, source_target_pairs={{0,10},{2,4},{8,18},{10,0},{16,26},{18,8},{24,30},{26,16},{28,22},... | collective-permute-start | bytes 344072 | tf_op jit(solution)/shard_map/ppermute | solution.py:640
  56.3 0.0 collective-permute-done.59.__1_.refs_2_
  56.3 0.0 collective-permute-done.60.__2_.refs_5_
  56.3 0.0 copy-start.1
  56.3 0.0 copy-start.2
  56.3 1.6 %add.122 = (bf16[128,4096]{1,0:T(8,128)(2,1)}, bf16[128,4096]{1,0:T(8,128)(2,1)}, s32[1]{0:T(128)}) custom-call(s32[32,128]{1,0:T(8,128)S(1)} %get-tuple-element.74.plan, s32[1,128]{1,0:T(1,128)S(1)} %collective-permute-done.35.note.__2_.refs_0_, bf16[16,128,128]{2,1,0:T(8,128)(2,1)S(1)} %turn.30.refs_1_, ...), custom_call_target="tpu_custom_call", output_to_operand_aliasing={{0}: (4, {}), {1}: (5, {})} | custom-call | flops 1000000 | bytes 3000000 | tf_op jit(solution)/shard_map/add/pallas_call | solution.py:562
  58.6 1.4 %collective-permute-done.63.refs_4_ = bf16[7,64,128]{2,1,0:T(8,128)(2,1)S(1)} collective-permute-done((bf16[7,64,128]{2,1,0:T(8,128)(2,1)S(1)}, bf16[7,64,128]{2,1,0:T(8,128)(2,1)S(1)}, u32[]{:S(2)}, u32[]{:S(2)}) %collective-permute-start.63) | collective-permute-done | bytes 114720 | tf_op jit(solution)/shard_map/ppermute | solution.py:640
  60.0 1.6 %last.3 = (bf16[1,2,128,128]{3,2,1,0:T(8,128)(2,1)}, bf16[1,2,128,128]{3,2,1,0:T(8,128)(2,1)}, bf16[1,2,128,128]{3,2,1,0:T(8,128)(2,1)}) custom-call(s32[32,128]{1,0:T(8,128)S(1)} %get-tuple-element.74.plan, bf16[7,64,128]{2,1,0:T(8,128)(2,1)S(1)} %get-tuple-element.109.refs_0_, bf16[7,64,128]{2,1,0:T(8,128)(2,1)S(1)} %collective-permute-done.62.refs_1_, ...), custom_call_target="tpu_custom_call" | custom-call | flops 1000000 | bytes 1000000 | tf_op jit(solution)/shard_map/last/pallas_call | solution.py:581
  (28 shorter events, 0.1 us)
Async XLA Ops:
  0.6 2.0 %collective-permute-start.32 = (bf16[1,2,128,128]{3,2,1,0:T(8,128)(2,1)}, bf16[1,2,128,128]{3,2,1,0:T(8,128)(2,1)S(1)}, u32[]{:S(2)}, u32[]{:S(2)}) collective-permute-start(bf16[1,2,128,128]{3,2,1,0:T(8,128)(2,1)} %refs_0_.1), channel_id=1, source_target_pairs={{0,2},{2,0},{8,10},{10,8},{16,18},{18,16},{24,26},{26,24},{28,30},... | collective-permute-start | bytes 196616 | tf_op jit(solution)/shard_map/ppermute | solution.py:649
  1.4 1.5 %collective-permute-start.33 = (bf16[1,2,128,128]{3,2,1,0:T(8,128)(2,1)}, bf16[1,2,128,128]{3,2,1,0:T(8,128)(2,1)S(1)}, u32[]{:S(2)}, u32[]{:S(2)}) collective-permute-start(bf16[1,2,128,128]{3,2,1,0:T(8,128)(2,1)} %refs_1_.1), channel_id=1, source_target_pairs={{0,2},{2,0},{8,10},{10,8},{16,18},{18,16},{24,26},{26,24},{28,30},... | collective-permute-start | bytes 196616 | tf_op jit(solution)/shard_map/ppermute | solution.py:649
  1.5 1.5 %collective-permute-start.34 = (bf16[1,2,128,128]{3,2,1,0:T(8,128)(2,1)}, bf16[1,2,128,128]{3,2,1,0:T(8,128)(2,1)S(1)}, u32[]{:S(2)}, u32[]{:S(2)}) collective-permute-start(bf16[1,2,128,128]{3,2,1,0:T(8,128)(2,1)} %refs_2_.1), channel_id=1, source_target_pairs={{0,2},{2,0},{8,10},{10,8},{16,18},{18,16},{24,26},{26,24},{28,30},... | collective-permute-start | bytes 196616 | tf_op jit(solution)/shard_map/ppermute | solution.py:649
  3.9 4.2 %collective-permute-start.36 = (bf16[7,64,128]{2,1,0:T(8,128)(2,1)S(1)}, bf16[7,64,128]{2,1,0:T(8,128)(2,1)S(1)}, u32[]{:S(2)}, u32[]{:S(2)}) collective-permute-start(bf16[7,64,128]{2,1,0:T(8,128)(2,1)S(1)} %get-tuple-element.76.refs_7_), channel_id=1, source_target_pairs={{0,8},{2,6},{8,16},{10,2},{16,24},{18,10},{24,28},{26,18},{28,20},... | collective-permute-start | bytes 344072 | tf_op jit(solution)/shard_map/ppermute | solution.py:601
  5.6 4.7 %collective-permute-start.40 = (bf16[7,64,128]{2,1,0:T(8,128)(2,1)S(1)}, bf16[7,64,128]{2,1,0:T(8,128)(2,1)S(1)}, u32[]{:S(2)}, u32[]{:S(2)}) collective-permute-start(bf16[7,64,128]{2,1,0:T(8,128)(2,1)S(1)} %get-tuple-element.76.refs_7_), channel_id=1, source_target_pairs={{0,4},{2,10},{8,0},{10,18},{16,8},{18,26},{24,16},{26,30},{28,24},... | collective-permute-start | bytes 344072 | tf_op jit(solution)/shard_map/ppermute | solution.py:601
  8.1 4.3 %collective-permute-start.37 = (bf16[7,64,128]{2,1,0:T(8,128)(2,1)S(1)}, bf16[7,64,128]{2,1,0:T(8,128)(2,1)S(1)}, u32[]{:S(2)}, u32[]{:S(2)}) collective-permute-start(bf16[7,64,128]{2,1,0:T(8,128)(2,1)S(1)} %collective-permute-done.36.refs_5_), channel_id=1, source_target_pairs={{0,8},{2,6},{8,16},{10,2},{16,24},{18,10},{24,28},{26,18},{28,20},... | collective-permute-start | bytes 344072 | tf_op jit(solution)/shard_map/ppermute | solution.py:601
  10.3 6.0 %collective-permute-start.41 = (bf16[7,64,128]{2,1,0:T(8,128)(2,1)S(1)}, bf16[7,64,128]{2,1,0:T(8,128)(2,1)S(1)}, u32[]{:S(2)}, u32[]{:S(2)}) collective-permute-start(bf16[7,64,128]{2,1,0:T(8,128)(2,1)S(1)} %collective-permute-done.40.refs_6_), channel_id=1, source_target_pairs={{0,4},{2,10},{8,0},{10,18},{16,8},{18,26},{24,16},{26,30},{28,24},... | collective-permute-start | bytes 344072 | tf_op jit(solution)/shard_map/ppermute | solution.py:601
  10.3 7.4 %collective-permute-start.50 = (bf16[7,64,128]{2,1,0:T(8,128)(2,1)S(1)}, bf16[7,64,128]{2,1,0:T(8,128)(2,1)S(1)}, u32[]{:S(2)}, u32[]{:S(2)}) collective-permute-start(bf16[7,64,128]{2,1,0:T(8,128)(2,1)S(1)} %get-tuple-element.76.refs_7_), channel_id=1, source_target_pairs={{0,2},{2,0},{8,10},{10,8},{16,18},{18,16},{24,26},{26,24},{28,30},... | collective-permute-start | bytes 344072 | tf_op jit(solution)/shard_map/ppermute | solution.py:603
  12.4 5.5 %collective-permute-start.48 = (bf16[7,64,128]{2,1,0:T(8,128)(2,1)S(1)}, bf16[7,64,128]{2,1,0:T(8,128)(2,1)S(1)}, u32[]{:S(2)}, u32[]{:S(2)}) collective-permute-start(bf16[7,64,128]{2,1,0:T(8,128)(2,1)S(1)} %collective-permute-done.36.refs_5_), channel_id=1, source_target_pairs={{0,2},{2,0},{8,10},{10,8},{16,18},{18,16},{24,26},{26,24},{28,30},... | collective-permute-start | bytes 344072 | tf_op jit(solution)/shard_map/ppermute | solution.py:603
  12.4 5.9 %collective-permute-start.38 = (bf16[7,64,128]{2,1,0:T(8,128)(2,1)S(1)}, bf16[7,64,128]{2,1,0:T(8,128)(2,1)S(1)}, u32[]{:S(2)}, u32[]{:S(2)}) collective-permute-start(bf16[7,64,128]{2,1,0:T(8,128)(2,1)S(1)} %collective-permute-done.37.refs_3_), channel_id=1, source_target_pairs={{0,8},{2,6},{8,16},{10,2},{16,24},{18,10},{24,28},{26,18},{28,20},... | collective-permute-start | bytes 344072 | tf_op jit(solution)/shard_map/ppermute | solution.py:601
  13.6 5.4 %collective-permute-start.49 = (bf16[7,64,128]{2,1,0:T(8,128)(2,1)S(1)}, bf16[7,64,128]{2,1,0:T(8,128)(2,1)S(1)}, u32[]{:S(2)}, u32[]{:S(2)}) collective-permute-start(bf16[7,64,128]{2,1,0:T(8,128)(2,1)S(1)} %collective-permute-done.40.refs_6_), channel_id=1, source_target_pairs={{0,2},{2,0},{8,10},{10,8},{16,18},{18,16},{24,26},{26,24},{28,30},... | collective-permute-start | bytes 344072 | tf_op jit(solution)/shard_map/ppermute | solution.py:603
  16.4 7.2 %collective-permute-start.42 = (bf16[7,64,128]{2,1,0:T(8,128)(2,1)S(1)}, bf16[7,64,128]{2,1,0:T(8,128)(2,1)S(1)}, u32[]{:S(2)}, u32[]{:S(2)}) collective-permute-start(bf16[7,64,128]{2,1,0:T(8,128)(2,1)S(1)} %collective-permute-done.41.refs_4_), channel_id=1, source_target_pairs={{0,4},{2,10},{8,0},{10,18},{16,8},{18,26},{24,16},{26,30},{28,24},... | collective-permute-start | bytes 344072 | tf_op jit(solution)/shard_map/ppermute | solution.py:601
  17.8 5.8 %collective-permute-start.46 = (bf16[7,64,128]{2,1,0:T(8,128)(2,1)S(1)}, bf16[7,64,128]{2,1,0:T(8,128)(2,1)S(1)}, u32[]{:S(2)}, u32[]{:S(2)}) collective-permute-start(bf16[7,64,128]{2,1,0:T(8,128)(2,1)S(1)} %collective-permute-done.37.refs_3_), channel_id=1, source_target_pairs={{0,2},{2,0},{8,10},{10,8},{16,18},{18,16},{24,26},{26,24},{28,30},... | collective-permute-start | bytes 344072 | tf_op jit(solution)/shard_map/ppermute | solution.py:603
  17.9 6.1 %collective-permute-start.47 = (bf16[7,64,128]{2,1,0:T(8,128)(2,1)S(1)}, bf16[7,64,128]{2,1,0:T(8,128)(2,1)S(1)}, u32[]{:S(2)}, u32[]{:S(2)}) collective-permute-start(bf16[7,64,128]{2,1,0:T(8,128)(2,1)S(1)} %collective-permute-done.41.refs_4_), channel_id=1, source_target_pairs={{0,2},{2,0},{8,10},{10,8},{16,18},{18,16},{24,26},{26,24},{28,30},... | collective-permute-start | bytes 344072 | tf_op jit(solution)/shard_map/ppermute | solution.py:603
  18.3 5.8 %collective-permute-start.39 = (bf16[7,64,128]{2,1,0:T(8,128)(2,1)S(1)}, bf16[7,64,128]{2,1,0:T(8,128)(2,1)S(1)}, u32[]{:S(2)}, u32[]{:S(2)}) collective-permute-start(bf16[7,64,128]{2,1,0:T(8,128)(2,1)S(1)} %collective-permute-done.38.refs_1_), channel_id=1, source_target_pairs={{0,8},{2,6},{8,16},{10,2},{16,24},{18,10},{24,28},{26,18},{28,20},... | collective-permute-start | bytes 344072 | tf_op jit(solution)/shard_map/ppermute | solution.py:604
  19.1 8.2 %collective-permute-start.43 = (bf16[7,64,128]{2,1,0:T(8,128)(2,1)S(1)}, bf16[7,64,128]{2,1,0:T(8,128)(2,1)S(1)}, u32[]{:S(2)}, u32[]{:S(2)}) collective-permute-start(bf16[7,64,128]{2,1,0:T(8,128)(2,1)S(1)} %collective-permute-done.38.refs_1_), channel_id=1, source_target_pairs={{0,10},{2,4},{8,18},{10,0},{16,26},{18,8},{24,30},{26,16},{28,22},... | collective-permute-start | bytes 344072 | tf_op jit(solution)/shard_map/ppermute | solution.py:605
  23.5 3.7 %collective-permute-start.44 = (bf16[7,64,128]{2,1,0:T(8,128)(2,1)S(1)}, bf16[7,64,128]{2,1,0:T(8,128)(2,1)S(1)}, u32[]{:S(2)}, u32[]{:S(2)}) collective-permute-start(bf16[7,64,128]{2,1,0:T(8,128)(2,1)S(1)} %collective-permute-done.38.refs_1_), channel_id=1, source_target_pairs={{0,2},{2,0},{8,10},{10,8},{16,18},{18,16},{24,26},{26,24},{28,30},... | collective-permute-start | bytes 344072 | tf_op jit(solution)/shard_map/ppermute | solution.py:603
  23.5 3.7 %collective-permute-start.45 = (bf16[7,64,128]{2,1,0:T(8,128)(2,1)S(1)}, bf16[7,64,128]{2,1,0:T(8,128)(2,1)S(1)}, u32[]{:S(2)}, u32[]{:S(2)}) collective-permute-start(bf16[7,64,128]{2,1,0:T(8,128)(2,1)S(1)} %collective-permute-done.42.refs_2_), channel_id=1, source_target_pairs={{0,2},{2,0},{8,10},{10,8},{16,18},{18,16},{24,26},{26,24},{28,30},... | collective-permute-start | bytes 344072 | tf_op jit(solution)/shard_map/ppermute | solution.py:603
  34.5 1.6 %collective-permute-start.52 = (bf16[14,64,128]{2,1,0:T(8,128)(2,1)S(1)}, bf16[14,64,128]{2,1,0:T(8,128)(2,1)S(1)}, u32[]{:S(2)}, u32[]{:S(2)}) collective-permute-start(bf16[14,64,128]{2,1,0:T(8,128)(2,1)S(1)} %get-tuple-element.80), channel_id=1, source_target_pairs={{0,2},{2,0},{8,10},{10,8},{16,18},{18,16},{24,26},{26,24},{28,30},... | collective-permute-start | bytes 688136 | tf_op jit(solution)/shard_map/ppermute | solution.py:612
  36.1 5.9 %collective-permute-start.53 = (bf16[42,64,128]{2,1,0:T(8,128)(2,1)S(1)}, bf16[42,64,128]{2,1,0:T(8,128)(2,1)S(1)}, u32[]{:S(2)}, u32[]{:S(2)}) collective-permute-start(bf16[42,64,128]{2,1,0:T(8,128)(2,1)S(1)} %turn.24), channel_id=1, source_target_pairs={{0,2},{2,0},{8,10},{10,8},{16,18},{18,16},{24,26},{26,24},{28,30},... | collective-permute-start | bytes 2064392 | tf_op jit(solution)/shard_map/ppermute | solution.py:613
  36.3 4.3 %collective-permute-start.54 = (bf16[7,64,128]{2,1,0:T(8,128)(2,1)S(1)}, bf16[7,64,128]{2,1,0:T(8,128)(2,1)S(1)}, u32[]{:S(2)}, u32[]{:S(2)}) collective-permute-start(bf16[7,64,128]{2,1,0:T(8,128)(2,1)S(1)} %get-tuple-element.81), channel_id=1, source_target_pairs={{0,8},{2,6},{8,16},{10,2},{16,24},{18,10},{24,28},{26,18},{28,20},... | collective-permute-start | bytes 344072 | tf_op jit(solution)/shard_map/ppermute | solution.py:629
  37.0 5.0 %collective-permute-start.55 = (bf16[7,64,128]{2,1,0:T(8,128)(2,1)S(1)}, bf16[7,64,128]{2,1,0:T(8,128)(2,1)S(1)}, u32[]{:S(2)}, u32[]{:S(2)}) collective-permute-start(bf16[7,64,128]{2,1,0:T(8,128)(2,1)S(1)} %get-tuple-element.82), channel_id=1, source_target_pairs={{0,4},{2,10},{8,0},{10,18},{16,8},{18,26},{24,16},{26,30},{28,24},... | collective-permute-start | bytes 344072 | tf_op jit(solution)/shard_map/ppermute | solution.py:629
  37.8 6.9 %collective-permute-start.35 = (s32[1,128]{1,0:T(1,128)S(1)}, s32[1,128]{1,0:T(1,128)S(1)}, u32[]{:S(2)}, u32[]{:S(2)}) collective-permute-start(s32[1,128]{1,0:T(1,128)S(1)} %get-tuple-element.75), channel_id=1, source_target_pairs={{0,1},{1,0},{2,3},{3,2},{4,5},{5,4},{6,7},{7,6},{8,9},{9,8},{10,11... | collective-permute-start | bytes 1544 | tf_op jit(solution)/shard_map/ppermute | solution.py:653
  37.8 12.7 %collective-permute-start.51 = (bf16[16,128,128]{2,1,0:T(8,128)(2,1)S(1)}, bf16[16,128,128]{2,1,0:T(8,128)(2,1)S(1)}, u32[]{:S(2)}, u32[]{:S(2)}) collective-permute-start(bf16[16,128,128]{2,1,0:T(8,128)(2,1)S(1)} %get-tuple-element.77), channel_id=1, source_target_pairs={{0,1},{1,0},{2,3},{3,2},{4,5},{5,4},{6,7},{7,6},{8,9},{9,8},{10,11... | collective-permute-start | bytes 1572872 | tf_op jit(solution)/shard_map/ppermute | solution.py:653
  42.1 5.1 %collective-permute-start.57 = (bf16[7,64,128]{2,1,0:T(8,128)(2,1)S(1)}, bf16[7,64,128]{2,1,0:T(8,128)(2,1)S(1)}, u32[]{:S(2)}, u32[]{:S(2)}) collective-permute-start(bf16[7,64,128]{2,1,0:T(8,128)(2,1)S(1)} %get-tuple-element.110.__1_), channel_id=1, source_target_pairs={{0,8},{2,6},{8,16},{10,2},{16,24},{18,10},{24,28},{26,18},{28,20},... | collective-permute-start | bytes 344072 | tf_op jit(solution)/shard_map/ppermute | solution.py:629
  43.1 1.5 %collective-permute-start.58 = (bf16[7,64,128]{2,1,0:T(8,128)(2,1)S(1)}, bf16[7,64,128]{2,1,0:T(8,128)(2,1)S(1)}, u32[]{:S(2)}, u32[]{:S(2)}) collective-permute-start(bf16[7,64,128]{2,1,0:T(8,128)(2,1)S(1)} %get-tuple-element.109.refs_0_), channel_id=1, source_target_pairs={{0,2},{2,0},{8,10},{10,8},{16,18},{18,16},{24,26},{26,24},{28,30},... | collective-permute-start | bytes 344072 | tf_op jit(solution)/shard_map/ppermute | solution.py:625
  43.2 5.3 %collective-permute-start.56 = (bf16[7,64,128]{2,1,0:T(8,128)(2,1)S(1)}, bf16[7,64,128]{2,1,0:T(8,128)(2,1)S(1)}, u32[]{:S(2)}, u32[]{:S(2)}) collective-permute-start(bf16[7,64,128]{2,1,0:T(8,128)(2,1)S(1)} %add_convert_fusion.12.__1_), channel_id=1, source_target_pairs={{0,4},{2,10},{8,0},{10,18},{16,8},{18,26},{24,16},{26,30},{28,24},... | collective-permute-start | bytes 344072 | tf_op jit(solution)/shard_map/ppermute | solution.py:629
  47.3 4.0 %collective-permute-start.61 = (bf16[7,64,128]{2,1,0:T(8,128)(2,1)S(1)}, bf16[7,64,128]{2,1,0:T(8,128)(2,1)S(1)}, u32[]{:S(2)}, u32[]{:S(2)}) collective-permute-start(bf16[7,64,128]{2,1,0:T(8,128)(2,1)S(1)} %add_convert_fusion.10.__1_), channel_id=1, source_target_pairs={{0,8},{2,6},{8,16},{10,2},{16,24},{18,10},{24,28},{26,18},{28,20},... | collective-permute-start | bytes 344072 | tf_op jit(solution)/shard_map/ppermute | solution.py:629
  48.6 7.7 %collective-permute-start.59 = (bf16[7,64,128]{2,1,0:T(8,128)(2,1)S(1)}, bf16[7,64,128]{2,1,0:T(8,128)(2,1)S(1)}, u32[]{:S(2)}, u32[]{:S(2)}) collective-permute-start(bf16[7,64,128]{2,1,0:T(8,128)(2,1)S(1)} %add_convert_fusion.9.__1_), channel_id=1, source_target_pairs={{0,4},{2,10},{8,0},{10,18},{16,8},{18,26},{24,16},{26,30},{28,24},... | collective-permute-start | bytes 344072 | tf_op jit(solution)/shard_map/ppermute | solution.py:629
  48.9 7.4 %collective-permute-start.60 = (bf16[7,64,128]{2,1,0:T(8,128)(2,1)S(1)}, bf16[7,64,128]{2,1,0:T(8,128)(2,1)S(1)}, u32[]{:S(2)}, u32[]{:S(2)}) collective-permute-start(bf16[7,64,128]{2,1,0:T(8,128)(2,1)S(1)} %add_convert_fusion.9.__1_), channel_id=1, source_target_pairs={{0,6},{2,8},{8,2},{10,16},{16,10},{18,24},{24,18},{26,28},{28,26},... | collective-permute-start | bytes 344072 | tf_op jit(solution)/shard_map/ppermute | solution.py:641
  51.3 7.3 %collective-permute-start.62 = (bf16[7,64,128]{2,1,0:T(8,128)(2,1)S(1)}, bf16[7,64,128]{2,1,0:T(8,128)(2,1)S(1)}, u32[]{:S(2)}, u32[]{:S(2)}) collective-permute-start(bf16[7,64,128]{2,1,0:T(8,128)(2,1)S(1)} %add_convert_fusion.8), channel_id=1, source_target_pairs={{0,8},{2,6},{8,16},{10,2},{16,24},{18,10},{24,28},{26,18},{28,20},... | collective-permute-start | bytes 344072 | tf_op jit(solution)/shard_map/ppermute | solution.py:637
  52.6 7.4 %collective-permute-start.63 = (bf16[7,64,128]{2,1,0:T(8,128)(2,1)S(1)}, bf16[7,64,128]{2,1,0:T(8,128)(2,1)S(1)}, u32[]{:S(2)}, u32[]{:S(2)}) collective-permute-start(bf16[7,64,128]{2,1,0:T(8,128)(2,1)S(1)} %add_convert_fusion.8), channel_id=1, source_target_pairs={{0,10},{2,4},{8,18},{10,0},{16,26},{18,8},{24,30},{26,16},{28,22},... | collective-permute-start | bytes 344072 | tf_op jit(solution)/shard_map/ppermute | solution.py:640
  56.3 5.2 %copy-start = (bf16[1,2,128,128]{3,2,1,0:T(8,128)(2,1)S(1)}, bf16[1,2,128,128]{3,2,1,0:T(8,128)(2,1)}, u32[]{:S(2)}) copy-start(bf16[1,2,128,128]{3,2,1,0:T(8,128)(2,1)} %refs_0_.1) | copy-start | bytes 196612
  56.3 5.2 %copy-start.1 = (bf16[1,2,128,128]{3,2,1,0:T(8,128)(2,1)S(1)}, bf16[1,2,128,128]{3,2,1,0:T(8,128)(2,1)}, u32[]{:S(2)}) copy-start(bf16[1,2,128,128]{3,2,1,0:T(8,128)(2,1)} %refs_1_.1) | copy-start | bytes 196612
  56.3 5.2 %copy-start.2 = (bf16[1,2,128,128]{3,2,1,0:T(8,128)(2,1)S(1)}, bf16[1,2,128,128]{3,2,1,0:T(8,128)(2,1)}, u32[]{:S(2)}) copy-start(bf16[1,2,128,128]{3,2,1,0:T(8,128)(2,1)} %refs_2_.1) | copy-start | bytes 196612
